TPU v7x, 32 devices: a whole 2x2x4 slice. The times are simulated.
32 devices in a mesh: dp: 8 (over z, core), seq: 4 (over y, x).
Axes of the slice: x: 2, y: 2, z: 4, core: 2. Of those that a mesh axis runs over, the one named last changes fastest.
Arguments:
- byte_ids: int32 [128, 2048], P('dp', 'seq'), may hold values from 0 to 255
- lengths: int32 [128], P('dp'), may hold values from 512 to 2048, as said below
- embed: float32 [256, 768], P('dp'), may hold values from -6 to 6
- conv: float32 [5, 768, 768], P(None, 'dp'), may hold values from -0.09375 to 0.09375
- score: float32 [768], replicated, may hold values from -0.4375 to 0.4375
- out_grad: float32 [128, 1024, 768], P('dp', 'seq'), may hold values from -6 to 6
- embed_left: float32 [256, 256], P('dp')
- embed_right: float32 [768, 768], P('dp')
- conv_left: float32 [5, 768, 768], P(None, 'dp')
- conv_right: float32 [5, 768, 768], P(None, 'dp')
- embed_left_root: float32 [256, 256], P('dp')
- embed_right_root: float32 [768, 768], replicated
- conv_left_root: float32 [5, 768, 768], P(None, 'dp')
- conv_right_root: float32 [5, 768, 768], replicated
- score_second: float32 [768], replicated, may hold values from 20132.66 to 80530.64
Outputs:
- output: float32 [128, 1024, 768], P('dp', 'seq')
- entropy: float32 [], replicated
- embed_grad: float32 [256, 768], P('dp')
- conv_grad: float32 [5, 768, 768], P(None, 'dp')
- score_grad: float32 [768], replicated
- new_embed: float32 [256, 768], P('dp')
- new_conv: float32 [5, 768, 768], P(None, 'dp')
- new_score: float32 [768], replicated
- new_embed_left: float32 [256, 256], P('dp')
- new_embed_right: float32 [768, 768], P('dp')
- new_conv_left: float32 [5, 768, 768], P(None, 'dp')
- new_conv_right: float32 [5, 768, 768], P(None, 'dp')
- new_score_second: float32 [768], replicated
Inputs may be any that keep to these rules, and one draw needn't show every extreme that they name: `lengths`: in each aligned block of 16 rows one row, chosen by the seed, has all 2048 bytes.
All inputs are finite; a program needn't handle non-finite values.
Results may differ from a plain program's by a relative error of at most 0.0007.
The roundings to bfloat16 on the way count: a program that leaves them out, or rounds other values in their place, can miss the bound.
Values may be sent and summed in bfloat16 or wider, within the bound.
No kernel may reach another device: no remote copies, remote signals or barrier semaphores. Data moves between devices by JAX's collectives and lax.ppermute only.
A program may use at most 576 MiB of HBM per device.

v0:
```python
from functools import partial

import jax
import jax.numpy as jnp
from jax import lax
from jax.sharding import PartitionSpec as P

VOCAB = 256
SIZES = 4


BETA_STAT = 0.9
BETA_SECOND = 0.99
RATE_EMBED = 10.0
RATE_CONV = 0.25
RATE_SCORE = 0.012
EPSILON = 1e-08


def padded(cells, sides, width):
    for axis, dim in sides:
        count = lax.axis_size(axis)
        ends = count - 1
        head = lax.slice_in_dim(cells, 0, width, axis=dim)
        tail = lax.slice_in_dim(cells, cells.shape[dim] - width, cells.shape[dim], axis=dim)
        cells = jnp.concatenate(
            [
                lax.ppermute(tail, axis, [(i, (i + 1) % count) for i in range(ends)]),
                cells,
                lax.ppermute(head, axis, [((i + 1) % count, i) for i in range(ends)]),
            ],
            axis=dim,
        )
    return cells


def same_block(places, offset, block_size):
    return ((places + offset) // block_size == places // block_size).astype(jnp.float32)


def rows_of(array, begin, amount, axis_number):
    return lax.dynamic_slice_in_dim(array, begin, amount, axis_number)


def refresh(
    summed, weight, left, right, left_root, right_root, rate, owner_index, sub_count, sub_index
):
    highest = lax.Precision.HIGHEST
    left_cols = left.shape[1] // sub_count
    right_cols = right.shape[1] // sub_count
    left_start = sub_index * left_cols
    right_start = sub_index * right_cols
    weight_part = rows_of(weight, right_start, right_cols, 1)
    left_part = rows_of(left, left_start, left_cols, 1)
    right_part = rows_of(right, right_start, right_cols, 1)
    grad_rows = rows_of(summed, owner_index * left.shape[0], left.shape[0], 0)
    grad_cols = rows_of(summed, owner_index * right.shape[0], right.shape[0], 1)
    other_rows = rows_of(summed, left_start, left_cols, 0)
    other_cols = rows_of(summed, right_start, right_cols, 1)
    outer_left = lax.dot_general(
        grad_rows,
        other_rows,
        (((1,), (1,)), ((), ())),
        precision=highest,
        preferred_element_type=jnp.float32,
    )
    outer_right = lax.dot_general(
        grad_cols,
        other_cols,
        (((0,), (0,)), ((), ())),
        precision=highest,
        preferred_element_type=jnp.float32,
    )
    new_left = BETA_STAT * left_part + (1.0 - BETA_STAT) * outer_left
    new_right = BETA_STAT * right_part + (1.0 - BETA_STAT) * outer_right
    root_cols = rows_of(right_root, right_start, right_cols, 1)
    step = jnp.dot(jnp.dot(left_root, summed, precision=highest), root_cols, precision=highest)
    return (weight_part - rate * step, new_left, new_right)


def shards(
    byte_ids,
    lengths,
    embed,
    conv,
    score,
    out_grad,
    embed_left,
    embed_right,
    conv_left,
    conv_right,
    embed_left_root,
    embed_right_root,
    conv_left_root,
    conv_right_root,
    score_second,
):
    highest = lax.Precision.HIGHEST
    rows_dev, piece_len = byte_ids.shape
    width = embed.shape[1]
    taps = conv.shape[0]
    ext_len = piece_len + 4
    start = lax.axis_index("seq") * piece_len
    embed_all, conv_all = (
        lax.all_gather(embed.astype(jnp.bfloat16), "dp", axis=0, tiled=True),
        lax.all_gather(conv.astype(jnp.bfloat16), "dp", axis=1, tiled=True),
    )
    ids_ext = padded(byte_ids, (("seq", 1),), 4)
    place_ext = start - 4 + jnp.arange(piece_len + 8, dtype=jnp.int32)
    valid_ext = ((place_ext[None, :] >= 0) & (place_ext[None, :] < lengths[:, None])).astype(
        jnp.float32
    )
    valid_hidden = valid_ext[:, 2 : piece_len + 6]
    valid_own = valid_ext[:, 4 : piece_len + 4]
    onehot_ext = (ids_ext[:, :, None] == jnp.arange(VOCAB, dtype=jnp.int32)[None, None, :]).astype(
        jnp.bfloat16
    )
    looked = jnp.dot(onehot_ext, embed_all, preferred_element_type=jnp.float32)
    inputs_ext = (looked * valid_ext[:, :, None]).astype(jnp.bfloat16)
    windows = jnp.concatenate([inputs_ext[:, tap : tap + ext_len] for tap in range(taps)], axis=2)
    hidden = jnp.dot(
        windows, conv_all.reshape(taps * width, width), preferred_element_type=jnp.float32
    )
    hidden = hidden * valid_hidden[:, :, None]
    padded_hidden = jnp.pad(hidden, ((0, 0), (1, 1), (0, 0)))
    own_place = start + jnp.arange(piece_len, dtype=jnp.int32)
    pooled = []
    for block_size in range(1, SIZES + 1):
        summed = jnp.zeros((rows_dev, piece_len, width), jnp.float32)
        for offset in range(1 - block_size, block_size):
            in_block = same_block(own_place, offset, block_size)
            summed = (
                summed
                + in_block[None, :, None] * padded_hidden[:, 3 + offset : 3 + offset + piece_len]
            )
        pooled.append(summed / block_size)
    scores = jnp.stack([jnp.einsum("rtd,d->rt", item, score, precision=highest) for item in pooled])
    size_probs = jax.nn.softmax(scores, axis=0)
    mixed = jnp.zeros((rows_dev, piece_len, width), jnp.float32)
    for level in range(SIZES):
        mixed = mixed + size_probs[level][:, :, None] * pooled[level]
    mixed = valid_own[:, :, None] * mixed
    output = jnp.sum(mixed.reshape(rows_dev, piece_len // 2, 2, width), axis=2) * 0.5
    entropy_part = jnp.sum(valid_own * -jnp.sum(size_probs * jnp.log(size_probs), axis=0))
    entropy_total, count_total = lax.psum((entropy_part, jnp.sum(valid_own)), ("dp", "seq"))
    entropy = entropy_total / count_total
    mixed_grad = valid_own[:, :, None] * jnp.repeat(out_grad * 0.5, 2, axis=1)
    prob_grad = jnp.stack([jnp.sum(mixed_grad * item, axis=2) for item in pooled])
    score_in_grad = size_probs * (
        prob_grad - jnp.sum(size_probs * prob_grad, axis=0, keepdims=True)
    )
    score_part = jnp.zeros((width,), jnp.float32)
    ext_place = start - 2 + jnp.arange(ext_len, dtype=jnp.int32)
    hidden_part = jnp.zeros((rows_dev, ext_len, width), jnp.float32)
    for level in range(SIZES):
        block_size = level + 1
        score_part = score_part + jnp.einsum(
            "rt,rtd->d", score_in_grad[level], pooled[level], precision=highest
        )
        pooled_grad = (
            size_probs[level][:, :, None] * mixed_grad
            + score_in_grad[level][:, :, None] * score[None, None, :]
        )
        padded_grad = jnp.pad(pooled_grad, ((0, 0), (5, 5), (0, 0)))
        for offset in range(1 - block_size, block_size):
            in_block = same_block(ext_place, offset, block_size)
            hidden_part = (
                hidden_part
                + in_block[None, :, None]
                * padded_grad[:, 3 + offset : 3 + offset + ext_len]
                / block_size
            )
    hidden_part = hidden_part * valid_hidden[:, :, None]
    rim_parts = jnp.concatenate([hidden_part[:, :2], hidden_part[:, ext_len - 2 :]], axis=1)
    rim_ext = padded(rim_parts.astype(jnp.bfloat16), (("seq", 1),), 2).astype(rim_parts.dtype)
    inner_part = hidden_part[:, 2 : piece_len + 2]
    inner_part = jnp.concatenate(
        [
            inner_part[:, :2] + rim_ext[:, :2],
            inner_part[:, 2 : piece_len - 2],
            inner_part[:, piece_len - 2 :] + rim_ext[:, 6:],
        ],
        axis=1,
    )
    hidden_grad = inner_part.astype(jnp.bfloat16)
    flat_windows = windows[:, 2 : piece_len + 2].reshape(rows_dev * piece_len, taps * width)
    conv_part = lax.dot_general(
        flat_windows,
        hidden_grad.reshape(rows_dev * piece_len, width),
        (((0,), (0,)), ((), ())),
        preferred_element_type=jnp.float32,
    ).reshape(taps, width, width)
    source = padded(hidden_grad, (("seq", 1),), 2)
    low_edge = 4
    stacked = jnp.stack([source[:, 4 - tap : 4 - tap + piece_len] for tap in range(taps)], axis=2)
    inputs_grad = lax.dot_general(
        stacked, conv_all, (((2, 3), (0, 2)), ((), ())), preferred_element_type=jnp.float32
    )
    inputs_grad = inputs_grad * valid_ext[:, low_edge : low_edge + piece_len][:, :, None]
    onehot_sel = (
        onehot_ext[:, low_edge : low_edge + piece_len]
        .astype(jnp.float32)
        .reshape(rows_dev * piece_len, VOCAB)
    )
    embed_part = lax.dot_general(
        onehot_sel,
        inputs_grad.reshape(rows_dev * piece_len, width),
        (((0,), (0,)), ((), ())),
        precision=highest,
        preferred_element_type=jnp.float32,
    )
    embed_total, conv_total, score_grad = lax.psum(
        (embed_part, conv_part, score_part), ("dp", "seq")
    )
    owner_index = lax.axis_index("dp")
    embed_rows = embed.shape[0]
    conv_rows = conv.shape[1]
    embed_grad = rows_of(embed_total, owner_index * embed_rows, embed_rows, 0)
    conv_grad = rows_of(conv_total, owner_index * conv_rows, conv_rows, 1)
    new_embed, new_embed_left, new_embed_right = refresh(
        embed_total,
        embed,
        embed_left,
        embed_right,
        embed_left_root,
        embed_right_root,
        RATE_EMBED,
        owner_index,
        1,
        0,
    )
    conv_rule = jax.vmap(
        partial(refresh, rate=RATE_CONV, owner_index=owner_index, sub_count=1, sub_index=0)
    )
    new_conv, new_conv_left, new_conv_right = conv_rule(
        conv_total, conv, conv_left, conv_right, conv_left_root, conv_right_root
    )
    new_score_second = BETA_SECOND * score_second + (1.0 - BETA_SECOND) * score_grad * score_grad
    new_score = score - RATE_SCORE * score_grad / (jnp.sqrt(new_score_second) + EPSILON)
    return (
        output,
        entropy,
        embed_grad,
        conv_grad,
        score_grad,
        new_embed,
        new_conv,
        new_score,
        new_embed_left,
        new_embed_right,
        new_conv_left,
        new_conv_right,
        new_score_second,
    )


def solution(mesh):
    placed = (
        P("dp", "seq"),
        P("dp"),
        P("dp", None),
        P(None, "dp", None),
        P(),
        P("dp", "seq", None),
        P("dp", None),
        P("dp", None),
        P(None, "dp", None),
        P(None, "dp", None),
        P("dp", None),
        P(),
        P(None, "dp", None),
        P(),
        P(),
    )
    return jax.shard_map(
        shards,
        mesh=mesh,
        in_specs=placed,
        out_specs=(
            P("dp", "seq", None),
            P(),
            P("dp", None),
            P(None, "dp", None),
            P(),
            P("dp", None),
            P(None, "dp", None),
            P(),
            P("dp", None),
            P("dp", None),
            P(None, "dp", None),
            P(None, "dp", None),
            P(),
        ),
        check_vma=False,
    )
```

profile of v0, /device:TPU:1, one launch (start us, length us, event | category | flops | bytes accessed | tf_op | source)
XLA Modules:
  0.0 1299.0 jit_solution(8697818966488539303)
XLA Ops:
  8.2 3.9 collective-permute-start
  25.5 16.8 %all_gather.6 = bf16[256,768]{1,0:T(8,128)(2,1)S(1)} all-gather(bf16[32,768]{1,0:T(8,128)(2,1)S(1)} %convert_element_type.240), channel_id=1, replica_groups=mesh['dp'=8,'seq'=4] {'dp'}, dimensions={0}, use_global_device_ids=true | all-gather | bytes 442368 | tf_op jit(solution)/shard_map/all_gather | solution.py:105
  42.3 10.6 broadcast_multiply_fusion
  53.5 13.8 %broadcast_in_dim.4 = f32[16,256,2,768]{3,2,1,0:T(2,128)} broadcast(f32[16,256,768]{2,1,0:T(8,128)} %broadcast_multiply_fusion), dimensions={0,1,3} | broadcast | bytes 37748736 | tf_op jit(solution)/shard_map/broadcast_in_dim | solution.py:147
  67.3 30.3 %reshape.619 = f32[16,512,768]{2,1,0:T(8,128)} reshape(f32[16,256,2,768]{3,2,1,0:T(2,128)} %broadcast_in_dim.4) | data formatting | bytes 50331648 | tf_op jit(solution)/shard_map/reshape | solution.py:147
  97.6 5.4 multiply_convert_fusion
  103.1 5.8 slice_dynamic-update-slice_fusion.4
  108.8 7.0 slice_dynamic-update-slice_fusion.3
  115.8 7.1 slice_dynamic-update-slice_fusion.2
  123.0 7.0 slice_dynamic-update-slice_fusion.1
  129.9 7.1 slice_dynamic-update-slice_fusion
  137.0 42.4 %slice.305 = bf16[16,512,3840]{2,1,0:T(8,128)(2,1)} slice(bf16[16,516,3840]{2,1,0:T(8,128)(2,1)} %slice_dynamic-update-slice_fusion), slice={[0:16], [2:514], [0:3840]} | slice | bytes 125829120 | tf_op jit(solution)/shard_map/slice | solution.py:186
  179.4 73.1 %copy.29 = bf16[3840,8192]{1,0:T(8,128)(2,1)} copy(bf16[3840,8192]{0,1:T(8,128)(2,1)} %bitcast.121) | data formatting | bytes 125829120 | tf_op jit(solution)/shard_map/dot_general | solution.py:187
  252.5 3.0 iota_compare_fusion
  255.5 58.6 %convolution_multiply_fusion = f32[16,516,768]{2,1,0:T(8,128)} fusion(bf16[16,516,3840]{2,1,0:T(8,128)(2,1)} %slice_dynamic-update-slice_fusion, bf16[3840,768,1]{1,0,2:T(8,128)(2,1)} %bitcast.139, f32[16,516]{1,0:T(8,128)S(1)} %slice.285), kind=kOutput, calls=%fused_computation.49 | convolution fusion | flops 48702210048 | bytes 94699776 | tf_op jit(solution)/shard_map/dot_general | solution.py:121
  314.3 26.1 %fusion.31 = f32[1,16,512]{2,0,1:T(1,128)S(1)} fusion(f32[768,1,1]{0,1,2:T(1,128)S(1)} %copy-done.19, f32[16,516,768]{2,1,0:T(8,128)} %convolution_multiply_fusion), kind=kOutput, calls=%fused_computation.47 | convolution fusion | flops 75497472 | bytes 25201664 | tf_op jit(solution)/shard_map/rtd,d->rt/dot_general | solution.py:137
  340.5 95.3 %multiply_reduce_fusion.3 = (f32[16,512]{1,0:T(8,128)S(1)}, f32[16,512]{1,0:T(8,128)S(1)}, f32[16,512]{1,0:T(8,128)S(1)}, f32[16,512]{1,0:T(8,128)S(1)}, f32[16,...) fusion(f32[16,516,768]{2,1,0:T(8,128)} %convolution_multiply_fusion, ...), kind=kLoop, calls=%fused_computation.28 | loop fusion | flops 226459648 | bytes 252239872 | tf_op jit(solution)/shard_map/reduce_sum | solution.py:148
  435.9 25.2 %fusion.27 = f32[1,16,512]{2,0,1:T(1,128)S(1)} fusion(f32[768,1,1]{0,1,2:T(1,128)S(1)} %copy-done.19, f32[16,512,768]{2,1,0:T(8,128)} %get-tuple-element.53), kind=kOutput, calls=%fused_computation.43 | convolution fusion | flops 81788928 | bytes 25201664 | tf_op jit(solution)/shard_map/rtd,d->rt/dot_general | solution.py:137
  461.1 25.4 %fusion.23 = f32[1,16,512]{2,0,1:T(1,128)S(1)} fusion(f32[768,1,1]{0,1,2:T(1,128)S(1)} %copy-done.19, f32[16,512,768]{2,1,0:T(8,128)} %get-tuple-element.54), kind=kOutput, calls=%fused_computation.39 | convolution fusion | flops 81788928 | bytes 25201664 | tf_op jit(solution)/shard_map/rtd,d->rt/dot_general | solution.py:137
  486.5 25.6 %fusion.19 = f32[1,16,512]{2,0,1:T(1,128)S(1)} fusion(f32[768,1,1]{0,1,2:T(1,128)S(1)} %copy-done.19, f32[16,512,768]{2,1,0:T(8,128)} %get-tuple-element.55), kind=kOutput, calls=%fused_computation.35 | convolution fusion | flops 81788928 | bytes 25201664 | tf_op jit(solution)/shard_map/rtd,d->rt/dot_general | solution.py:137
  513.8 78.8 %multiply_add_fusion.3 = (f32[16,512,768]{2,1,0:T(8,128)}, f32[16,512,768]{2,1,0:T(8,128)}, f32[16,512,768]{2,1,0:T(8,128)}, f32[16,512,768]{2,1,0:T(8,128)}, f32[16,512,768]{2,1,0:T(8,128)}) fusion(f32[16,512,768]{2,1,0:T(8,128)} %reshape.619, f32[768]{0:T(1024)S(1)} %copy-done.22, f32[16,512]{1,0:T(8,128)S(1)} %get-tuple-element.64, ...), kind=kLoop, calls=%fused_computation.24 | loop fusion | flops 132120576 | bytes 252054528 | tf_op jit(solution)/shard_map/add | solution.py:161
  592.7 179.4 %fusion.221 = (bf16[16,516,768]{2,1,0:T(8,128)(2,1)}, f32[16,516,768]{2,1,0:T(8,128)}) fusion(f32[16,516]{1,0:T(8,128)S(1)} %copy-done.13, f32[516]{0:T(1024)S(1)} %copy-done.31, f32[516]{0:T(1024)S(1)} %copy-done.33, f32[516]{0:T(1024)S(1)} %copy-done.25, f32[516]{0:T(1024)S(1)} %copy-done.26, f32[516]{0:T(1024)S(1)} %copy-done.34, ...), kind=kLoop, calls=%fused_computation.399 | loop fusion | flops 278986752 | bytes 138764736 | tf_op jit(solution)/shard_map/convert.11
  773.2 4.7 collective-permute-start.2
  779.3 13.9 %slice_bitcast_fusion.12 = bf16[16,508,1,768]{3,1,0,2:T(8,128)(2,1)} fusion(f32[16,516,768]{2,1,0:T(8,128)} %get-tuple-element.51), kind=kLoop, calls=%fused_computation.402 | loop fusion | bytes 24969216 | tf_op jit(solution)/shard_map/concatenate | solution.py:177
  793.2 9.8 slice.443
  805.2 4.9 collective-permute-start.5
  811.5 7.5 pad_maximum_fusion.6
  819.0 58.6 %fusion.225 = f32[5,768,768]{2,1,0:T(8,128)} fusion(bf16[5,768,8192]{2,1,0:T(8,128)(2,1)} %bitcast.124, bf16[8192,768,1]{1,0,2:T(8,128)(2,1)} %bitcast.127), kind=kOutput, calls=%fused_computation.403 | convolution fusion | flops 48318382080 | bytes 87293952 | tf_op jit(solution)/shard_map/dot_general | solution.py:187
  877.5 12.4 fusion.37
  889.9 7.8 fusion.36
  898.7 7.0 maximum_dynamic-update-slice_fusion
  905.8 7.5 fusion.34
  913.2 7.2 fusion.38
  920.4 55.5 %fusion.47 = f32[16,512,768,1]{2,1,0,3:T(8,128)} fusion(bf16[16,512,5,768]{3,1,0,2:T(8,128)(2,1)} %fusion.38, bf16[5,768,768]{2,1,0:T(8,128)(2,1)S(1)} %bitcast.141), kind=kOutput, calls=%fused_computation.82 | convolution fusion | flops 48318382080 | bytes 93978624 | tf_op jit(solution)/shard_map/dot_general | solution.py:196
  976.0 20.1 %fusion.57 = f32[256,768]{1,0:T(8,128)} fusion(f32[16,512,768,1]{2,1,0,3:T(8,128)} %fusion.47, f32[16,512]{1,0:T(8,128)S(1)} %copy-done.6, pred[16,520,256]{1,2,0:T(32,128)(4,1)S(1)} %copy-done.3), kind=kOutput, calls=%fused_computation.91 | convolution fusion | flops 19333644288 | bytes 28082176 | tf_op jit(solution)/shard_map/dot_general | solution.py:205
  997.5 15.9 %fusion.63 = f32[768]{0:T(1024)S(1)} fusion(f32[16,512,768]{2,1,0:T(8,128)} %get-tuple-element.53, f32[16,512,1]{1,0,2:T(8,128)S(1)} %copy-done.17), kind=kOutput, calls=%fused_computation.98 | convolution fusion | flops 81788928 | bytes 25201664 | tf_op jit(solution)/shard_map/rt,rtd->d/dot_general | solution.py:157
  1013.5 16.4 %fusion.66 = f32[768]{0:T(1024)S(1)} fusion(f32[16,512,768]{2,1,0:T(8,128)} %get-tuple-element.54, f32[16,512,1]{1,0,2:T(8,128)S(1)} %copy-done.16), kind=kOutput, calls=%fused_computation.99 | convolution fusion | flops 81788928 | bytes 25201664 | tf_op jit(solution)/shard_map/rt,rtd->d/dot_general | solution.py:157
  1029.9 15.9 %fusion.69 = f32[768]{0:T(1024)S(1)} fusion(f32[16,512,768]{2,1,0:T(8,128)} %get-tuple-element.55, f32[16,512,1]{1,0,2:T(8,128)S(1)} %copy-done.15), kind=kOutput, calls=%fused_computation.100 | convolution fusion | flops 81788928 | bytes 25201664 | tf_op jit(solution)/shard_map/rt,rtd->d/dot_general | solution.py:157
  1045.8 16.7 %fusion.72 = f32[768]{0:T(1024)S(1)} fusion(f32[16,516,768]{2,1,0:T(8,128)} %convolution_multiply_fusion, f32[16,512,1]{1,0,2:T(8,128)S(1)} %copy-done.14), kind=kOutput, calls=%fused_computation.101 | convolution fusion | flops 75497472 | bytes 25201664 | tf_op jit(solution)/shard_map/rt,rtd->d/dot_general | solution.py:157
  1062.5 43.3 %all-reduce.5 = (f32[]{:T(128)}, f32[]{:T(128)}, f32[768]{0:T(1024)S(1)}) all-reduce(f32[]{:T(128)} %get-tuple-element.42, f32[]{:T(128)} %get-tuple-element.41, f32[768]{0:T(1024)S(1)} %add_add_fusion), channel_id=1, replica_groups=mesh['dp'=8,'seq'=4] {'dp','seq'}, use_global_device_ids=true, to_apply=%region_4.5 | all-reduce | flops 770 | bytes 6160 | tf_op jit(solution)/shard_map/psum | solution.py:145
  1105.8 29.3 %reshape.618 = f32[16,256,2,768]{3,2,1,0:T(2,128)} reshape(f32[16,512,768]{2,1,0:T(8,128)} %get-tuple-element.79) | data formatting | bytes 50331648 | tf_op jit(solution)/shard_map/reshape | solution.py:143
  1136.5 37.4 %reduce_sum.91 = f32[16,256,768]{2,1,0:T(8,128)} reduce(f32[16,256,2,768]{3,2,1,0:T(2,128)} %reshape.618, f32[]{:T(128)} %constant.352.clone.1), dimensions={2}, to_apply=%region_1.2 | reduce | flops 3145728 | bytes 37748740 | tf_op jit(solution)/shard_map/reduce_sum | solution.py:143
  1174.6 10.6 broadcast_multiply_fusion.1
  1185.2 45.1 %all-reduce.9.cloned.1.call-done = (f32[256,768]{1,0:T(8,128)}, f32[5,768,768]{2,1,0:T(8,128)}) async-done(((f32[256,768]{1,0:T(8,128)}, f32[5,768,768]{2,1,0:T(8,128)}), (f32[256,768]{1,0:T(8,128)}, f32[5,768,768]{2,1,0:T(8,128)})) %all-reduce.9.cloned.1.call-update) | async-done | bytes 12582928 | tf_op jit(solution)/shard_map/psum | solution.py:212
  1239.4 10.9 fusion.227
  1255.2 14.1 %multiply_add_fusion.8 = f32[5,96,768]{2,1,0:T(8,128)} fusion(f32[5,96,768]{2,1,0:T(8,128)} %param.23, f32[5,768,768]{2,1,0:T(8,128)S(1)} %bitcast.123, s32[]{:T(128)S(1)} %bitcast.138), kind=kOutput, calls=%fused_computation.89 | convolution fusion | flops 3398492160 | bytes 16220672 | tf_op jit(solution)/shard_map/vmap()/dot_general | solution.py:60
  1269.3 10.7 multiply_add_fusion.7
  1280.1 10.5 multiply_subtract_fusion
  (181 shorter events, 39.5 us)
Async XLA Ops:
  7.2 1245.8 %copy-start = (f32[768,768]{1,0:T(8,128)S(1)}, f32[768,768]{1,0:T(8,128)}, u32[]{:S(2)}) copy-start(f32[768,768]{1,0:T(8,128)} %param.26) | copy-start | bytes 7077892
  7.2 45.7 %copy-start.21 = (f32[768]{0:T(1024)S(1)}, f32[768]{0:T(1024)}, u32[]{:S(2)}) copy-start(f32[768]{0:T(1024)} %param.19) | copy-start | bytes 9220
  7.2 248.3 %all-gather.2.cloned.1.call-start = ((), (), s32[]{:S(2)}) async-start(), calls=%async_computation | async-start | bytes 6635520 | tf_op jit(solution)/shard_map/all_gather | solution.py:106
  8.2 89.3 %collective-permute-start = (s32[16,4]{1,0:T(8,128)S(1)}, s32[16,4]{1,0:T(8,128)S(1)}, u32[]{:S(2)}, u32[]{:S(2)}) collective-permute-start(s32[16,4]{1,0:T(8,128)S(1)} %get-tuple-element.80), channel_id=1, source_target_pairs={{0,1},{1,2},{2,3},{4,5},{5,6},{6,7},{8,9},{9,10},{10,11},{12,13},{... | collective-permute-start | bytes 776 | tf_op jit(solution)/shard_map/ppermute | solution.py:28
  12.1 85.4 %collective-permute-start.1 = (s32[16,4]{1,0:T(8,128)S(1)}, s32[16,4]{1,0:T(8,128)S(1)}, u32[]{:S(2)}, u32[]{:S(2)}) collective-permute-start(s32[16,4]{1,0:T(8,128)S(1)} %get-tuple-element.81), channel_id=1, source_target_pairs={{1,0},{2,1},{3,2},{5,4},{6,5},{7,6},{9,8},{10,9},{11,10},{13,12},{... | collective-permute-start | bytes 776 | tf_op jit(solution)/shard_map/ppermute | solution.py:30
  15.8 1214.6 %all-reduce.9.cloned.1.call-start = ((), (), s32[]{:S(2)}) async-start(), calls=%async_computation.1 | async-start | bytes 25165824 | tf_op jit(solution)/shard_map/psum | solution.py:212
  23.9 73.8 %copy-start.7 = (f32[16,520]{1,0:T(8,128)}, f32[16,520]{1,0:T(8,128)S(1)}, u32[]{:S(2)}) copy-start(f32[16,520]{1,0:T(8,128)S(1)} %and_convert_fusion) | copy-start | bytes 99844
  52.9 202.6 %copy-start.12 = (f32[16,516]{1,0:T(8,128)}, f32[16,516]{1,0:T(8,128)S(1)}, u32[]{:S(2)}) copy-start(f32[16,516]{1,0:T(8,128)S(1)} %slice.285) | copy-start | bytes 99076
  67.3 30.3 %copy-start.20 = (s32[16,512]{1,0:T(8,128)S(1)}, s32[16,512]{1,0:T(8,128)}, u32[]{:S(2)}) copy-start(s32[16,512]{1,0:T(8,128)} %param.15) | copy-start | bytes 98308
  255.5 58.6 %copy-start.19 = (f32[768,1,1]{0,1,2:T(1,128)S(1)}, f32[768,1,1]{0,1,2:T(1,128)}, u32[]{:S(2)}) copy-start(f32[768,1,1]{0,1,2:T(1,128)} %reshape.671) | copy-start | bytes 9220
  314.2 26.2 %copy-start.38 = (f32[512]{0:T(512)S(1)}, f32[512]{0:T(512)}, u32[]{:S(2)}) copy-start(f32[512]{0:T(512)} %get-tuple-element.89) | copy-start | bytes 6148
  314.2 26.2 %copy-start.39 = (f32[512]{0:T(512)S(1)}, f32[512]{0:T(512)}, u32[]{:S(2)}) copy-start(f32[512]{0:T(512)} %get-tuple-element.90) | copy-start | bytes 6148
  314.2 26.2 %copy-start.40 = (f32[512]{0:T(512)S(1)}, f32[512]{0:T(512)}, u32[]{:S(2)}) copy-start(f32[512]{0:T(512)} %get-tuple-element.91) | copy-start | bytes 6148
  314.2 26.2 %copy-start.41 = (f32[512]{0:T(512)S(1)}, f32[512]{0:T(512)}, u32[]{:S(2)}) copy-start(f32[512]{0:T(512)} %get-tuple-element.86) | copy-start | bytes 6148
  314.2 26.2 %copy-start.42 = (f32[512]{0:T(512)S(1)}, f32[512]{0:T(512)}, u32[]{:S(2)}) copy-start(f32[512]{0:T(512)} %get-tuple-element.87) | copy-start | bytes 6148
  314.2 26.2 %copy-start.43 = (f32[512]{0:T(512)S(1)}, f32[512]{0:T(512)}, u32[]{:S(2)}) copy-start(f32[512]{0:T(512)} %get-tuple-element.82) | copy-start | bytes 6148
  314.2 26.2 %copy-start.44 = (f32[512]{0:T(512)S(1)}, f32[512]{0:T(512)}, u32[]{:S(2)}) copy-start(f32[512]{0:T(512)} %get-tuple-element.83) | copy-start | bytes 6148
  314.2 26.2 %copy-start.45 = (f32[512]{0:T(512)S(1)}, f32[512]{0:T(512)}, u32[]{:S(2)}) copy-start(f32[512]{0:T(512)} %get-tuple-element.92) | copy-start | bytes 6148
  461.1 52.5 %copy-start.22 = (f32[768]{0:T(1024)S(1)}, f32[768]{0:T(1024)}, u32[]{:S(2)}) copy-start(f32[768]{0:T(1024)} %param.19) | copy-start | bytes 9220
  513.6 78.9 %copy-start.13 = (f32[16,516]{1,0:T(8,128)S(1)}, f32[16,516]{1,0:T(8,128)}, u32[]{:S(2)}) copy-start(f32[16,516]{1,0:T(8,128)} %copy-done.12) | copy-start | bytes 99076
  513.6 78.9 %copy-start.25 = (f32[516]{0:T(1024)S(1)}, f32[516]{0:T(1024)}, u32[]{:S(2)}) copy-start(f32[516]{0:T(1024)} %get-tuple-element.104) | copy-start | bytes 6196
  513.6 78.9 %copy-start.26 = (f32[516]{0:T(1024)S(1)}, f32[516]{0:T(1024)}, u32[]{:S(2)}) copy-start(f32[516]{0:T(1024)} %get-tuple-element.105) | copy-start | bytes 6196
  513.6 78.9 %copy-start.27 = (f32[516]{0:T(1024)S(1)}, f32[516]{0:T(1024)}, u32[]{:S(2)}) copy-start(f32[516]{0:T(1024)} %get-tuple-element.102) | copy-start | bytes 6196
  513.7 78.9 %copy-start.28 = (f32[516]{0:T(1024)S(1)}, f32[516]{0:T(1024)}, u32[]{:S(2)}) copy-start(f32[516]{0:T(1024)} %get-tuple-element.103) | copy-start | bytes 6196
  513.7 78.9 %copy-start.29 = (f32[516]{0:T(1024)S(1)}, f32[516]{0:T(1024)}, u32[]{:S(2)}) copy-start(f32[516]{0:T(1024)} %get-tuple-element.100) | copy-start | bytes 6196
  513.7 78.9 %copy-start.30 = (f32[516]{0:T(1024)S(1)}, f32[516]{0:T(1024)}, u32[]{:S(2)}) copy-start(f32[516]{0:T(1024)} %get-tuple-element.101) | copy-start | bytes 6196
  513.7 78.9 %copy-start.31 = (f32[516]{0:T(1024)S(1)}, f32[516]{0:T(1024)}, u32[]{:S(2)}) copy-start(f32[516]{0:T(1024)} %get-tuple-element.96) | copy-start | bytes 6196
  513.7 78.9 %copy-start.32 = (f32[516]{0:T(1024)S(1)}, f32[516]{0:T(1024)}, u32[]{:S(2)}) copy-start(f32[516]{0:T(1024)} %get-tuple-element.97) | copy-start | bytes 6196
  513.7 78.9 %copy-start.33 = (f32[516]{0:T(1024)S(1)}, f32[516]{0:T(1024)}, u32[]{:S(2)}) copy-start(f32[516]{0:T(1024)} %get-tuple-element.98) | copy-start | bytes 6196
  513.7 78.9 %copy-start.34 = (f32[516]{0:T(1024)S(1)}, f32[516]{0:T(1024)}, u32[]{:S(2)}) copy-start(f32[516]{0:T(1024)} %get-tuple-element.99) | copy-start | bytes 6196
  513.7 78.9 %copy-start.35 = (f32[516]{0:T(1024)S(1)}, f32[516]{0:T(1024)}, u32[]{:S(2)}) copy-start(f32[516]{0:T(1024)} %get-tuple-element.106) | copy-start | bytes 6196
  513.7 78.9 %copy-start.36 = (f32[516]{0:T(1024)S(1)}, f32[516]{0:T(1024)}, u32[]{:S(2)}) copy-start(f32[516]{0:T(1024)} %get-tuple-element.107) | copy-start | bytes 6196
  773.2 29.8 %collective-permute-start.2 = (bf16[16,2,768]{2,1,0:T(2,128)(2,1)S(1)}, bf16[16,2,768]{2,1,0:T(2,128)(2,1)S(1)}, u32[]{:S(2)}, u32[]{:S(2)}) collective-permute-start(bf16[16,2,768]{2,1,0:T(2,128)(2,1)S(1)} %get-tuple-element.62), channel_id=1, source_target_pairs={{0,1},{1,2},{2,3},{4,5},{5,6},{6,7},{8,9},{9,10},{10,11},{12,13},{... | collective-permute-start | bytes 147464 | tf_op jit(solution)/shard_map/ppermute | solution.py:28
  778.0 25.1 %collective-permute-start.3 = (bf16[16,2,768]{2,1,0:T(2,128)(2,1)S(1)}, bf16[16,2,768]{2,1,0:T(2,128)(2,1)S(1)}, u32[]{:S(2)}, u32[]{:S(2)}) collective-permute-start(bf16[16,2,768]{2,1,0:T(2,128)(2,1)S(1)} %get-tuple-element.63), channel_id=1, source_target_pairs={{1,0},{2,1},{3,2},{5,4},{6,5},{7,6},{9,8},{10,9},{11,10},{13,12},{... | collective-permute-start | bytes 147464 | tf_op jit(solution)/shard_map/ppermute | solution.py:30
  805.2 100.5 %collective-permute-start.5 = (bf16[16,2,768]{2,1,0:T(2,128)(2,1)S(1)}, bf16[16,2,768]{2,1,0:T(2,128)(2,1)S(1)}, u32[]{:S(2)}, u32[]{:S(2)}) collective-permute-start(bf16[16,2,768]{2,1,0:T(2,128)(2,1)S(1)} %get-tuple-element.56), channel_id=1, source_target_pairs={{0,1},{1,2},{2,3},{4,5},{5,6},{6,7},{8,9},{9,10},{10,11},{12,13},{... | collective-permute-start | bytes 147464 | tf_op jit(solution)/shard_map/ppermute | solution.py:28
  810.2 67.4 %collective-permute-start.4 = (bf16[16,2,768]{2,1,0:T(2,128)(2,1)S(1)}, bf16[16,2,768]{2,1,0:T(2,128)(2,1)S(1)}, u32[]{:S(2)}, u32[]{:S(2)}) collective-permute-start(bf16[16,2,768]{2,1,0:T(2,128)(2,1)S(1)} %get-tuple-element.57), channel_id=1, source_target_pairs={{1,0},{2,1},{3,2},{5,4},{6,5},{7,6},{9,8},{10,9},{11,10},{13,12},{... | collective-permute-start | bytes 147464 | tf_op jit(solution)/shard_map/ppermute | solution.py:30
  920.4 55.5 %copy-start.3 = (pred[16,520,256]{1,2,0:T(32,128)(4,1)S(1)}, pred[16,520,256]{1,2,0:T(32,128)(4,1)}, u32[]{:S(2)}) copy-start(pred[16,520,256]{1,2,0:T(32,128)(4,1)} %iota_compare_fusion) | copy-start | bytes 6389764
  920.4 55.5 %copy-start.6 = (f32[16,512]{1,0:T(8,128)S(1)}, f32[16,512]{1,0:T(8,128)}, u32[]{:S(2)}) copy-start(f32[16,512]{1,0:T(8,128)} %slice.279) | copy-start | bytes 98308
  997.5 32.4 %copy-start.15 = (f32[16,512,1]{1,0,2:T(8,128)S(1)}, f32[16,512,1]{1,0,2:T(8,128)}, u32[]{:S(2)}) copy-start(f32[16,512,1]{1,0,2:T(8,128)} %get-tuple-element.68) | copy-start | bytes 98308
  1013.5 32.3 %copy-start.14 = (f32[16,512,1]{1,0,2:T(8,128)S(1)}, f32[16,512,1]{1,0,2:T(8,128)}, u32[]{:S(2)}) copy-start(f32[16,512,1]{1,0,2:T(8,128)} %get-tuple-element.65) | copy-start | bytes 98308
  1105.8 68.1 %copy-start.50 = (f32[768]{0:T(1024)}, f32[768]{0:T(1024)S(1)}, u32[]{:S(2)}) copy-start(f32[768]{0:T(1024)S(1)} %get-tuple-element.45) | copy-start | bytes 9220
  1135.1 38.8 %copy-start.23 = (f32[768]{0:T(1024)S(1)}, f32[768]{0:T(1024)}, u32[]{:S(2)}) copy-start(f32[768]{0:T(1024)} %param.19) | copy-start | bytes 9220
  1135.1 38.8 %copy-start.49 = (f32[768]{0:T(1024)S(1)}, f32[768]{0:T(1024)}, u32[]{:S(2)}) copy-start(f32[768]{0:T(1024)} %param.29) | copy-start | bytes 9220
  1136.5 94.9 %copy-start.11 = (f32[96,768]{1,0:T(8,128)S(1)}, f32[96,768]{1,0:T(8,128)}, u32[]{:S(2)}) copy-start(f32[96,768]{1,0:T(8,128)} %param.22) | copy-start | bytes 884740
  1136.5 97.7 %copy-start.24 = (f32[32,256]{1,0:T(8,128)S(1)}, f32[32,256]{1,0:T(8,128)}, u32[]{:S(2)}) copy-start(f32[32,256]{1,0:T(8,128)} %param.25) | copy-start | bytes 98308
  1173.9 79.1 %copy-start.9 = (f32[32,768]{1,0:T(8,128)S(1)}, f32[32,768]{1,0:T(8,128)}, u32[]{:S(2)}) copy-start(f32[32,768]{1,0:T(8,128)} %param.17) | copy-start | bytes 294916
  1231.4 48.7 %copy-start.10 = (f32[32,768]{1,0:T(8,128)}, f32[32,768]{1,0:T(8,128)S(1)}, u32[]{:S(2)}) copy-start(f32[32,768]{1,0:T(8,128)S(1)} %constant_dynamic-slice_fusion.1) | copy-start | bytes 294916
  1250.3 29.7 %copy-start.4 = (f32[5,96,768]{2,1,0:T(8,128)S(1)}, f32[5,96,768]{2,1,0:T(8,128)}, u32[]{:S(2)}) copy-start(f32[5,96,768]{2,1,0:T(8,128)} %param.18) | copy-start | bytes 4423684
  (19 other events, 374.9 us)
Sparse Core Ops, SparseCore 0:
  15.9 67.6 all-gather.1
  996.2 234.0 all-reduce.8
where the time goes:
time: 1310 us; the launch traced here: 1300 us
  other arithmetic  480 us (37%)
  matrix products  422 us (32%)
  local copies, waits for them, and re-layouts  256 us (20%)
  blocking collectives  60.1 us (5%)
  waiting for transfers between devices  45.2 us (3%)
  between operations  17.8 us (1%)
  starting transfers between devices  17.5 us (1%)
    another operation x1, other arithmetic  179 us
    dot_general x4, matrix products, shards(): jnp.einsum('rtd,d->rt', item, score, precision=highest)  102 us
    reduce_sum x1, other arithmetic, shards(): jnp.sum(mixed_grad * item, axis=2)  95.3 us
    add x1, other arithmetic, shards(): size_probs[level][:, :, None] * mixed_grad  78.8 us
    dot_general x1, local copies, waits for them, and re-layouts, shards(): lax.dot_general(flat_windows, hidden_grad.reshape(rows_dev * piece_len, w...  73.1 us
    dot_general x4, matrix products, shards(): jnp.einsum('rt,rtd->d', score_in_grad[level], pooled[level], precision=hi...  64.9 us
    dot_general x1, matrix products, shards(): jnp.dot(windows, conv_all.reshape(taps * width, width), preferred_element...  58.6 us
    dot_general x1, matrix products, shards(): lax.dot_general(flat_windows, hidden_grad.reshape(rows_dev * piece_len, w...  58.6 us
  transfers between devices with their start and end apart: 8, of which 1 were waited for; matrix products, arithmetic and copies ran while one was open for 37% of the time, Pallas kernels for 0%

commit v1 on v0

v1 whole, which is shorter than its diff:
```python
from functools import partial

import jax
import jax.numpy as jnp
from jax import lax
from jax.experimental import pallas as pl
from jax.experimental.pallas import tpu as pltpu
from jax.sharding import PartitionSpec as P

VOCAB = 256
SIZES = 4
BETA_STAT = 0.9
BETA_SECOND = 0.99
RATE_EMBED = 10.0
RATE_CONV = 0.25
RATE_SCORE = 0.012
EPSILON = 1e-08
TILE = 128
HALO = 8
BLOCKS = 32
WIN = TILE // 2 + 16
BF = jnp.bfloat16
F32 = jnp.float32


def split(v):
    high = v.astype(BF)
    return high, (v - high.astype(F32)).astype(BF)


def roll_to(v, offset):
    width = v.shape[-1]
    return v if offset == 0 else pltpu.roll(v, (-offset) % width, v.ndim - 1)


def lookup_body(where_ref, mid_ref, g_ref, gh_ref, score_ref, near_ref, far_ref, hid_ref, rim_ref, band_ref, gext, table_ref, *, masks, taps):
    length = hid_ref.shape[1] * TILE
    half = length // 2
    blocks = table_ref.shape[1] // TILE
    slots = near_ref.shape[1] // len(masks[0])

    @pl.when(pl.program_id(0) == 0)
    def _():
        for h in range(2):
            for spot in range(near_ref.shape[1]):
                for other, source in enumerate((near_ref, far_ref)):
                    group = 2 * (where_ref[1] ^ masks[h][spot // slots]) + ((where_ref[0] & 1) ^ other)
                    unit = group * slots + spot % slots

                    @pl.when(unit < taps * blocks)
                    def _():
                        row = pl.multiple_of((h * taps + unit // blocks) * VOCAB, VOCAB)
                        column = pl.multiple_of(unit % blocks * TILE, TILE)
                        table_ref[pl.ds(row, VOCAB), pl.ds(column, TILE)] = source[h, spot]

    gext[0:8] = gh_ref[0, 0:8]
    gext[8 : half + 8] = g_ref[0]
    gext[half + 8 : half + 16] = gh_ref[0, 8:16]
    nt = (((1,), (1,)), ((), ()))
    tiles = length // TILE
    mid = mid_ref[0]
    rim = jnp.where(lax.broadcasted_iota(jnp.int32, (8, TILE), 1) < TILE // 2, mid[:, TILE + length :], mid[:, 0:TILE])
    mid = jnp.concatenate([mid[:, TILE : TILE + length], pltpu.roll(rim, HALO, 1)], axis=1)
    cells = lax.broadcasted_iota(jnp.int32, (VOCAB, length + TILE), 0)
    hits = [(mid[k : k + 1] == cells).astype(F32).astype(BF) for k in range(taps)]
    onehot = jnp.concatenate(hits + hits, axis=0)[:, 0 : length + 2 * HALO]
    for n in range(0, table_ref.shape[1], 256):
        h_high, h_low = split(
            lax.dot_general(onehot, table_ref[:, n : n + 256], (((0,), (0,)), ((), ())), preferred_element_type=F32)
        )
        for i in range(tiles):
            hid_ref[0, i, 0:TILE, n : n + 256] = h_high[i * TILE : (i + 1) * TILE]
            hid_ref[0, i, TILE : 2 * TILE, n : n + 256] = h_low[i * TILE : (i + 1) * TILE]
        rim_ref[0, 0:16, n : n + 256] = h_high[length:]
        rim_ref[0, 16:32, n : n + 256] = h_low[length:]
    for i in range(length // TILE):
        g_high, g_low = split(gext[i * TILE // 2 : i * TILE // 2 + WIN])
        left = jnp.concatenate([g_high, g_low, score_ref[0:16]], axis=0)
        gram = lax.dot_general(left, hid_ref[0, i], nt, preferred_element_type=F32)
        band = gram[0:WIN, 0:TILE] + gram[WIN : 2 * WIN, 0:TILE] + gram[0:WIN, TILE:]
        dots = gram[2 * WIN : 2 * WIN + 1, 0:TILE] + gram[2 * WIN + 1 : 2 * WIN + 2, 0:TILE] + gram[2 * WIN : 2 * WIN + 1, TILE:]
        place = lax.broadcasted_iota(jnp.int32, (WIN, TILE), 0) - 8
        gap = place - (lax.broadcasted_iota(jnp.int32, (WIN, TILE), 1) >> 1)
        rows = [jnp.sum(jnp.where(gap == d, band, 0.0), axis=0, keepdims=True) for d in (-1, 0, 1)]
        band_ref[0, :, TILE * (i + 1) : TILE * (i + 2)] = jnp.concatenate(rows + [dots, jnp.zeros((4, TILE), F32)], axis=0)
    rims = rim_ref[0]
    g_high, g_low = split(jnp.concatenate([gext[0:16], gext[half : half + 16]], axis=0))
    gram = lax.dot_general(jnp.concatenate([g_high, g_low, score_ref[0:16]], axis=0), rims, nt, preferred_element_type=F32)
    band = gram[0:32, 0:16] + gram[32:64, 0:16] + gram[0:32, 16:32]
    dots = gram[64:65, 0:16] + gram[65:66, 0:16] + gram[64:65, 16:32]
    row = lax.broadcasted_iota(jnp.int32, (32, 16), 0)
    lane = lax.broadcasted_iota(jnp.int32, (32, 16), 1)
    place = jnp.where(row < 16, row - 8, half - 24 + row)
    spot = jnp.where(lane < 8, lane - 8, length + lane - 8)
    gap = place - (spot >> 1)
    rows = [jnp.sum(jnp.where(gap == d, band, 0.0), axis=0, keepdims=True) for d in (-1, 0, 1)]
    both = jnp.concatenate(rows + [dots, jnp.zeros((4, 16), F32)], axis=0)
    both = pltpu.roll(jnp.concatenate([both, jnp.zeros((8, TILE - 16), F32)], axis=1), TILE - 8, 1)
    band_ref[0, :, 0:TILE] = both
    band_ref[0, :, TILE + length :] = both


def lookup(where, mid, out_grad, grad_rim, score_rows, near, far, masks, taps):
    rows, _, span = mid.shape
    half, width = out_grad.shape[1:]
    tiles = 2 * half // TILE
    whole = lambda *shape: pl.BlockSpec(shape, lambda r: (0,) * len(shape), pipeline_mode=pl.Buffered(1))
    by_row = lambda *shape: pl.BlockSpec((1, *shape), lambda r: (r,) + (0,) * len(shape))
    return pl.pallas_call(
        partial(lookup_body, masks=masks, taps=taps),
        grid=(rows,),
        in_specs=[
            pl.BlockSpec(memory_space=pltpu.SMEM),
            by_row(8, span),
            by_row(half, width),
            by_row(16, width),
            whole(*score_rows.shape),
            whole(*near.shape),
            whole(*far.shape),
        ],
        out_specs=[by_row(tiles, 2 * TILE, width), by_row(32, width), by_row(8, span)],
        out_shape=[
            jax.ShapeDtypeStruct((rows, tiles, 2 * TILE, width), BF),
            jax.ShapeDtypeStruct((rows, 32, width), BF),
            jax.ShapeDtypeStruct((rows, 8, span), F32),
        ],
        scratch_shapes=[
            pltpu.VMEM((half + 16, width), F32),
            pltpu.VMEM((2 * taps * VOCAB, width), BF),
        ],
        compiler_params=pltpu.CompilerParams(vmem_limit_bytes=56 << 20),
    )(where, mid, out_grad, grad_rim, score_rows, near, far)


def weigh_body(band_ref, lengths_ref, start_ref, out_ref, sums_ref):
    rows, _, span = band_ref.shape
    length = span - 2 * TILE
    start = start_ref[0]
    lane = lax.broadcasted_iota(jnp.int32, (rows, span), 1)
    place = start + lane - TILE
    valid = ((place >= 0) & (place < lengths_ref[...])).astype(F32)
    phase3 = lax.rem(place + 3 * TILE, 3)
    phase4 = place & 3
    even = (place & 1) == 0
    inside = {
        1: {0: None},
        2: {0: None, 1: even, -1: ~even},
        3: {0: None, 1: phase3 <= 1, 2: phase3 == 0, -1: phase3 >= 1, -2: phase3 == 2},
        4: {0: None, **{d: phase4 <= 3 - d for d in (1, 2, 3)}, **{-d: phase4 >= d for d in (1, 2, 3)}},
    }

    def over_block(size, pick):
        total = pick(0)
        for d, mask in inside[size].items():
            if d != 0:
                total = total + jnp.where(mask, pick(d), 0.0)
        return total

    def shifts(v):
        return {d: roll_to(v, d) for d in range(-3, 4)}

    dots = shifts(band_ref[:, 3, :] * valid)
    scores = [over_block(b, lambda d: dots[d]) * (1.0 / b) for b in range(1, SIZES + 1)]
    highest = jnp.maximum(jnp.maximum(scores[0], scores[1]), jnp.maximum(scores[2], scores[3]))
    powers = [jnp.exp(item - highest) for item in scores]
    total = powers[0] + powers[1] + powers[2] + powers[3]
    probs = [item / total for item in powers]
    log_total = jnp.log(total)
    entropy = jnp.zeros_like(total)
    for b in range(SIZES):
        entropy = entropy - probs[b] * (scores[b] - highest - log_total)
    own = (lane >= TILE) & (lane < TILE + length)
    own_valid = jnp.where(own, valid, 0.0)
    entropy = jnp.sum(jnp.where(own, entropy * valid, 0.0), axis=1, keepdims=True)
    count = jnp.sum(own_valid, axis=1, keepdims=True)
    sums_ref[...] = jnp.where(lax.broadcasted_iota(jnp.int32, (rows, TILE), 1) == 0, entropy, count)
    below, same, above = (shifts(band_ref[:, d, :] * valid) for d in range(3))
    near = {0: same[0], 1: jnp.where(even, same[1], below[1]), 2: below[2], 3: below[3]}
    near.update({-1: jnp.where(even, above[-1], same[-1]), -2: above[-2], -3: above[-3]})
    inner = [over_block(b, lambda d: near[d]) * (valid * (0.5 / b)) for b in range(1, SIZES + 1)]
    mean = probs[0] * inner[0] + probs[1] * inner[1] + probs[2] * inner[2] + probs[3] * inner[3]
    score_in = [probs[b] * (inner[b] - mean) for b in range(SIZES)]
    pull = jnp.zeros_like(total)
    for b in range(1, SIZES + 1):
        moved = shifts(score_in[b - 1])
        pull = pull + over_block(b, lambda d: moved[d]) * (1.0 / b)
    weight = {d: jnp.zeros_like(total) for d in range(-3, 4)}
    for b in range(1, SIZES + 1):
        moved = shifts(probs[b - 1] * valid * (0.5 / b))
        for d, mask in inside[b].items():
            weight[d] = weight[d] + (moved[d] if mask is None else jnp.where(mask, moved[d], 0.0))
    out_ref[:, 0, :] = valid * (weight[-2] + jnp.where(even, weight[-1], weight[-3]))
    out_ref[:, 1, :] = valid * (weight[0] + jnp.where(even, weight[1], weight[-1]))
    out_ref[:, 2, :] = valid * (weight[2] + jnp.where(even, weight[3], weight[1]))
    out_ref[:, 3, :] = valid * pull
    for d in range(4, 8):
        out_ref[:, d, :] = jnp.zeros_like(total)


def weigh(band, lengths, start):
    rows, _, span = band.shape
    vmem = pl.BlockSpec(memory_space=pltpu.VMEM)
    return pl.pallas_call(
        weigh_body,
        in_specs=[vmem, vmem, pl.BlockSpec(memory_space=pltpu.SMEM)],
        out_specs=[vmem, vmem],
        out_shape=[jax.ShapeDtypeStruct(band.shape, F32), jax.ShapeDtypeStruct((rows, TILE), F32)],
    )(band, lengths.reshape(rows, 1), start.reshape(1))


def apply_body(
    me_ref, mid_ref, g_ref, gh_ref, score_ref, hid_ref, rim_ref, weight_ref, sums_ref,
    out_ref, keep_ref, send_ref, extra_ref, onehot, hgrad, gext, total, table_ref, pull_ref,
):
    length = hid_ref.shape[1] * TILE
    half = length // 2
    taps = table_ref.shape[0] // VOCAB

    @pl.when(pl.program_id(0) == 0)
    def _():
        table_ref[...] = jnp.zeros_like(table_ref)
        pull_ref[...] = jnp.zeros_like(pull_ref)

    cells = lax.broadcasted_iota(jnp.int32, (VOCAB, length), 0)
    for tap in range(taps):
        hit = mid_ref[0, tap : tap + 1, TILE : TILE + length] == cells
        onehot[tap * VOCAB : (tap + 1) * VOCAB] = hit.astype(F32).astype(BF)
    gext[0:8] = gh_ref[0, 0:8]
    gext[8 : half + 8] = g_ref[0]
    gext[half + 8 : half + 16] = gh_ref[0, 8:16]
    total[...] = jnp.zeros_like(total)
    pulled = jnp.zeros((1, total.shape[1]), F32)
    for i in range(length // TILE):
        w = weight_ref[0, :, TILE * (i + 1) : TILE * (i + 2)]
        place = lax.broadcasted_iota(jnp.int32, (WIN, TILE), 0) - 8
        gap = place - (lax.broadcasted_iota(jnp.int32, (WIN, TILE), 1) >> 1)
        a = jnp.where(gap == 0, w[1:2], 0.0)
        a = jnp.where(gap == -1, w[0:1], a)
        a = jnp.where(gap == 1, w[2:3], a)
        a_high, a_low = split(a)
        q_high, q_low = split(w[3:4])
        sub = lax.broadcasted_iota(jnp.int32, (16, TILE), 0)
        q = jnp.where(sub < 2, q_high.astype(F32), jnp.where(sub == 2, q_low.astype(F32), 0.0)).astype(BF)
        g_high, g_low = split(gext[i * TILE // 2 : i * TILE // 2 + WIN])
        stack = jnp.concatenate([g_high, g_low, g_high, score_ref[16:32]], axis=0)
        left = jnp.concatenate([a_high, a_high, a_low, q], axis=0)
        hg = lax.dot_general(left, stack, (((0,), (0,)), ((), ())), preferred_element_type=F32)
        hgrad[i * TILE : (i + 1) * TILE] = hg.astype(BF)
        left = jnp.concatenate([a_high, a_low, q], axis=0)
        res = jnp.dot(jnp.concatenate([left, left], axis=1), hid_ref[0, i], preferred_element_type=F32)
        total[i * TILE // 2 : i * TILE // 2 + WIN] += res[0:WIN] + res[WIN : 2 * WIN]
        pulled = pulled + res[2 * WIN : 2 * WIN + 1] + res[2 * WIN + 2 : 2 * WIN + 3]
    lane = lax.broadcasted_iota(jnp.int32, (8, TILE), 1)
    w = jnp.where(lane < 64, weight_ref[0, :, TILE + length :], weight_ref[0, :, 0:TILE])
    w = pltpu.roll(w, 8, 1)[:, 0:16]
    row = lax.broadcasted_iota(jnp.int32, (32, 16), 0)
    lane = lax.broadcasted_iota(jnp.int32, (32, 16), 1)
    place = jnp.where(row < 16, row - 8, half - 24 + row)
    spot = jnp.where(lane < 8, lane - 8, length + lane - 8)
    gap = place - (spot >> 1)
    a = jnp.where(gap == 0, w[1:2], 0.0)
    a = jnp.where(gap == -1, w[0:1], a)
    a = jnp.where(gap == 1, w[2:3], a)
    a_high, a_low = split(a)
    left = jnp.concatenate([a_high, a_low], axis=0)
    res = jnp.dot(jnp.concatenate([left, left], axis=1), rim_ref[0], preferred_element_type=F32)
    res = res[0:32] + res[32:64]
    total[8:16] += res[8:16]
    total[half : half + 8] += res[16:24]
    out_ref[0] = total[8 : half + 8]
    pull_ref[0:1] += pulled
    table_ref[...] += jnp.dot(onehot[...], hgrad[...], preferred_element_type=F32)

    @pl.when(pl.program_id(0) == pl.num_programs(0) - 1)
    def _():
        row = lax.broadcasted_iota(jnp.int32, pull_ref.shape, 0)
        lane = lax.broadcasted_iota(jnp.int32, pull_ref.shape, 1)
        counts = jnp.sum(sums_ref[...], axis=0, keepdims=True)
        counts = jnp.concatenate([counts] + [jnp.zeros_like(counts)] * (pull_ref.shape[1] // TILE - 1), axis=1)
        extra = jnp.where((row == 1) & (lane < 2), counts, pull_ref[...])
        part = extra.shape[1] // 2
        block = table_ref.shape[0] // BLOCKS
        for h in range(2):
            extra_ref[h] = extra[:, h * part : (h + 1) * part]
            send_ref[h, BLOCKS // 2 * block :] = extra[:, h * part : (h + 1) * part]
            for p in range(BLOCKS):
                source = pl.multiple_of((me_ref[h] ^ p) * block, 8)
                rows = table_ref[pl.ds(source, block), h * part : (h + 1) * part]
                target = keep_ref if p < BLOCKS // 2 else send_ref
                target[h, p % (BLOCKS // 2) * block : (p % (BLOCKS // 2) + 1) * block] = rows


def apply_weights(me, mid, out_grad, grad_rim, score_rows, hid, rim, weight, sums, taps):
    rows, _, span = mid.shape
    half, width = out_grad.shape[1:]
    tiles = 2 * half // TILE
    whole = lambda *shape: pl.BlockSpec(shape, lambda r: (0,) * len(shape), pipeline_mode=pl.Buffered(1))
    by_row = lambda *shape: pl.BlockSpec((1, *shape), lambda r: (r,) + (0,) * len(shape))
    return pl.pallas_call(
        apply_body,
        grid=(rows,),
        in_specs=[
            pl.BlockSpec(memory_space=pltpu.SMEM),
            by_row(8, span),
            by_row(half, width),
            by_row(16, width),
            whole(*score_rows.shape),
            by_row(tiles, 2 * TILE, width),
            by_row(32, width),
            by_row(8, span),
            whole(*sums.shape),
        ],
        out_specs=[
            by_row(half, width),
            whole(2, taps * VOCAB // 2, width // 2),
            whole(2, taps * VOCAB // 2 + 8, width // 2),
            whole(2, 8, width // 2),
        ],
        out_shape=[
            jax.ShapeDtypeStruct((rows, half, width), F32),
            jax.ShapeDtypeStruct((2, taps * VOCAB // 2, width // 2), F32),
            jax.ShapeDtypeStruct((2, taps * VOCAB // 2 + 8, width // 2), F32),
            jax.ShapeDtypeStruct((2, 8, width // 2), F32),
        ],
        scratch_shapes=[
            pltpu.VMEM((taps * VOCAB, 2 * half), BF),
            pltpu.VMEM((2 * half, width), BF),
            pltpu.VMEM((half + 16, width), F32),
            pltpu.VMEM((half + 16, width), F32),
            pltpu.VMEM((taps * VOCAB, width), F32),
            pltpu.VMEM((8, width), F32),
        ],
        compiler_params=pltpu.CompilerParams(vmem_limit_bytes=56 << 20),
    )(me, mid, out_grad, grad_rim, score_rows, hid, rim, weight, sums)


def shifted_rim(cells, width):
    count = lax.axis_size("seq")
    head, tail = cells[:, :width], cells[:, cells.shape[1] - width :]
    left = lax.ppermute(tail, "seq", [(i, i + 1) for i in range(count - 1)])
    right = lax.ppermute(head, "seq", [(i + 1, i) for i in range(count - 1)])
    return left, right


def marked_ids(byte_ids, lengths, start, taps):
    rows, length = byte_ids.shape
    left, right = shifted_rim(byte_ids, HALO)
    near = jnp.concatenate([left, byte_ids, right], axis=1)
    place = start - HALO + jnp.arange(length + 2 * HALO, dtype=jnp.int32)
    valid = (place[None, :] >= 0) & (place[None, :] < lengths[:, None])
    near = jnp.where(valid, near, -1)
    near = jnp.pad(near, ((0, 0), (TILE - HALO + 2, TILE - HALO + 2)), constant_values=-1)
    span = length + 2 * TILE
    lists = [near[:, k : k + span] for k in range(taps)]
    lists += [jnp.full((rows, span), -1, jnp.int32)] * (8 - taps)
    return jnp.stack(lists, axis=1)


NN = (((1,), (0,)), ((), ()))
NT = (((1,), (1,)), ((), ()))
TN = (((0,), (0,)), ((), ()))


def dot(a, b, dims):
    return lax.dot_general(a, b, dims, preferred_element_type=F32)


def dot2(a, pair, dims):
    return dot(a, pair[0], dims) + dot(a, pair[1], dims)


def dot3(left, right, dims):
    return dot(left[0], right[0], dims) + dot(left[0], right[1], dims) + dot(left[1], right[0], dims)


def bits_of(count):
    return [1 << i for i in range(count.bit_length() - 1)]


def exchange_plan(seq_size, dp_size):
    across = bits_of(seq_size)
    half = len(across) // 2
    along = [("dp", 2 * bit) for bit in reversed(bits_of(dp_size // 2))]
    orders = [across, across[half:] + across[:half]]
    return [[("dp", 1)] + [("seq", bit) for bit in order] + along for order in orders]


def block_index(plan):
    index = jnp.int32(0)
    for axis, bit in plan[: BLOCKS.bit_length() - 1]:
        index = 2 * index + ((lax.axis_index(axis) & bit) != 0).astype(jnp.int32)
    return index


def swap(cells, axis, bit):
    return lax.ppermute(cells, axis, [(i, i ^ bit) for i in range(lax.axis_size(axis))])


def pack_body(where_ref, conv_ref, embed_ref, out_ref, *, slots):
    taps, own, width = conv_ref.shape
    rows = embed_ref.shape[0]
    blocks = width // TILE
    for j in range(blocks):
        out_ref[j * rows : (j + 1) * rows] = embed_ref[:, j * TILE : (j + 1) * TILE].astype(BF)
    for i in range(2 * slots):
        group = 2 * where_ref[1] + ((where_ref[0] & 1) ^ (i // slots))
        unit = jnp.minimum(group * slots + i % slots, taps * blocks - 1)
        column = pl.multiple_of(unit % blocks * TILE, TILE)
        first = blocks * rows + i * own
        out_ref[first : first + own] = conv_ref[unit // blocks, :, pl.ds(column, TILE)].astype(BF)


def pack_weights(where, conv, embed, slots):
    vmem = pl.BlockSpec(memory_space=pltpu.VMEM)
    rows = embed.shape[0] * embed.shape[1] // TILE + 2 * slots * conv.shape[1]
    return pl.pallas_call(
        partial(pack_body, slots=slots),
        in_specs=[pl.BlockSpec(memory_space=pltpu.SMEM), vmem, vmem],
        out_specs=vmem,
        out_shape=jax.ShapeDtypeStruct((rows, TILE), BF),
    )(where, conv, embed)


def tables_body(where_ref, score_ref, *refs, slots, own, rows):
    *near, far_ref, embed_ref, stack_ref, high_ref, low_ref, units = refs
    blocks = embed_ref.shape[1] // TILE
    first = blocks * rows
    for m, near_ref in enumerate(near):
        for other in range(2):
            source = far_ref.at[m] if other else near_ref
            place = where_ref[0] ^ (2 * m + other)
            for j in range(blocks):
                embed_ref[pl.ds(pl.multiple_of(place * rows, 16), rows), j * TILE : (j + 1) * TILE] = source[
                    j * rows : (j + 1) * rows
                ]
            for t in range(slots):
                units[t, pl.ds(pl.multiple_of(place * own, 16), own)] = source[first + t * own : first + (t + 1) * own]
    for t in range(slots):
        high, low = split(jnp.dot(embed_ref[...], units[t], preferred_element_type=F32))
        high_ref[t], low_ref[t] = high, low
    high, low = (part.astype(F32) for part in split(score_ref[...]))
    row = lax.broadcasted_iota(jnp.int32, stack_ref.shape, 0)
    highs, lows = (row == 0) | (row == 16) | (row == 18), (row == 1) | (row == 17)
    stack_ref[...] = jnp.where(highs, high, jnp.where(lows, low, 0.0)).astype(BF)


def make_tables(where, score, near, far, slots, own, rows):
    width = score.shape[0]
    vmem = pl.BlockSpec(memory_space=pltpu.VMEM)
    unit = jax.ShapeDtypeStruct((slots, VOCAB, TILE), BF)
    return pl.pallas_call(
        partial(tables_body, slots=slots, own=own, rows=rows),
        in_specs=[pl.BlockSpec(memory_space=pltpu.SMEM)] + [vmem] * (len(near) + 2),
        out_specs=[vmem] * 4,
        out_shape=[jax.ShapeDtypeStruct((VOCAB, width), BF), jax.ShapeDtypeStruct((32, width), BF), unit, unit],
        scratch_shapes=[pltpu.VMEM((slots, width, TILE), BF)],
    )(where, score.reshape(1, width), *near, far)


def gather_tables(where, embed, conv, score, rims):
    taps, own, width = conv.shape
    rows = embed.shape[0]
    seq, chips = lax.axis_size("seq"), lax.axis_size("dp") // 2
    slots = -(-taps * (width // TILE) // (2 * seq))
    pack = pack_weights(where, conv, embed, slots)
    near = [pack] + [swap(pack, "dp", 2 * m) for m in range(1, chips)]
    first = rows * width // TILE
    other = first + slots * own
    far = swap(jnp.stack([jnp.concatenate([item[:first], item[other:]], axis=0) for item in near]), "dp", 1)
    far, rims = lax.optimization_barrier((far, rims))
    embed_all, score_rows, *parts = make_tables(where, score, near, far, slots, own, rows)
    across = bits_of(seq)
    masks = []
    for h in range(2):
        found = [0]
        half = len(across) // 2
        for bit in across[half:] + across[:half] if h else across:
            parts[h] = jnp.concatenate([parts[h], swap(parts[h], "seq", bit)], axis=0)
            found = found + [mask ^ bit for mask in found]
        masks.append(found)
    units = jnp.stack(parts)
    return embed_all, score_rows, units, swap(units, "dp", 1), masks, rims


def sum_over_devices(keep, send, extra, plans, ready):
    block = keep.shape[1] // (BLOCKS // 2)
    depth = BLOCKS.bit_length() - 1
    got = swap(send, "dp", 1)
    cells = keep + got[:, : keep.shape[1]]
    extra = extra + got[:, keep.shape[1] :]
    across = len([axis for axis, _ in plans[0] if axis == "seq"])
    parts, extras = [], []
    for h in range(2):
        part, more = cells[h], extra[h]
        for step, (axis, bit) in enumerate(plans[h][1 : 1 + across]):
            if step == 1 and h == 0:
                part, ready = lax.optimization_barrier((part, ready))
            rest = part.shape[0] // 2
            got = swap(jnp.concatenate([part[rest:], more], axis=0), axis, bit)
            part, more = part[:rest] + got[:rest], more + got[rest:]
        parts.append(part)
        extras.append(more)
    cells, extra = jnp.stack(parts), jnp.stack(extras)
    along = 1 << (depth - 1 - across)
    if along > 1:
        got = [
            swap(jnp.concatenate([cells[:, m * block : (m + 1) * block], extra], axis=1), "dp", 2 * m)
            for m in range(1, along)
        ]
        cells, extra = cells[:, :block], extra
        for item in got:
            cells, extra = cells + item[:, :block], extra + item[:, block:]
    for axis, bit in plans[0][depth:]:
        got = swap(jnp.concatenate([cells, extra], axis=1), axis, bit)
        cells, extra = cells + got[:, :block], extra + got[:, block:]
    if along > 1:
        cells = jnp.concatenate([cells] + [swap(cells, "dp", 2 * m) for m in range(1, along)], axis=1)
    parts = []
    for h in range(2):
        part = cells[h]
        for axis, bit in reversed(plans[h][1 : 1 + across]):
            part = jnp.concatenate([part, swap(part, axis, bit)], axis=0)
        parts.append(part)
    cells = jnp.stack(parts)
    return cells, swap(cells, "dp", 1), extra, ready


def pick_rows(count, total, first):
    row = lax.broadcasted_iota(jnp.int32, (count, total), 0)
    return (lax.broadcasted_iota(jnp.int32, (count, total), 1) == row + first).astype(F32).astype(BF)


def order_body(me_ref, near_ref, far_ref, conv_ref, high_ref, low_ref, grad_ref, table):
    block = table.shape[0] // BLOCKS
    part = table.shape[1] // 2
    for h in range(2):
        for p in range(BLOCKS):
            source = near_ref if p < BLOCKS // 2 else far_ref
            rows = source[h, p % (BLOCKS // 2) * block : (p % (BLOCKS // 2) + 1) * block]
            table[pl.ds(pl.multiple_of((me_ref[h] ^ p) * block, 8), block), h * part : (h + 1) * part] = rows
    taps = conv_ref.shape[0]
    total = jnp.zeros(grad_ref.shape, F32)
    for k in range(taps):
        pair = split(table[k * VOCAB : (k + 1) * VOCAB])
        high_ref[k], low_ref[k] = pair
        total = total + dot2(conv_ref[k], pair, NT)
    grad_ref[...] = total


def order_table(me, near, far, conv_low):
    taps, own, width = conv_low.shape
    vmem = pl.BlockSpec(memory_space=pltpu.VMEM)
    table = jax.ShapeDtypeStruct((taps, VOCAB, width), BF)
    return pl.pallas_call(
        order_body,
        in_specs=[pl.BlockSpec(memory_space=pltpu.SMEM), vmem, vmem, vmem],
        out_specs=[vmem, vmem, vmem],
        out_shape=[table, table, jax.ShapeDtypeStruct((own, VOCAB), F32)],
        scratch_shapes=[pltpu.VMEM((taps * VOCAB, width), F32)],
        compiler_params=pltpu.CompilerParams(vmem_limit_bytes=60 << 20),
    )(me, near, far, conv_low)


def dot2_left(pair, b, dims):
    return dot(pair[0], b, dims) + dot(pair[1], b, dims)


def both(left, right, dims):
    count = left[0].shape[0]
    first = dot(jnp.concatenate(left, axis=0), right[0], dims)
    return first[:count] + first[count:] + dot(left[0], right[1], dims)


def ready_body(where_ref, embed_ref, left_root_ref, right_root_ref, square_high, square_low, columns_ref, rooted_high, rooted_low, right_high, right_low):
    own, width = left_root_ref.shape[1:]
    embed = embed_ref[...]

    @pl.when(pl.program_id(0) == 0)
    def _():
        square_high[...], square_low[...] = split(dot(embed, embed, NT))
        columns_ref[...] = dot(pick_rows(own, width, where_ref[0] * own), embed, NT).astype(BF)

    rooted_high[0], rooted_low[0] = split(dot2_left(split(left_root_ref[0]), embed, NT))
    right_high[0], right_low[0] = split(right_root_ref[0])


def make_ready(where, embed_all, left_root, right_root):
    taps, own, width = left_root.shape
    by_tap = lambda *shape: pl.BlockSpec((1, *shape), lambda k: (k,) + (0,) * len(shape))
    whole = lambda *shape: pl.BlockSpec(shape, lambda k: (0,) * len(shape))
    like = lambda *shape: jax.ShapeDtypeStruct(shape, BF)
    return pl.pallas_call(
        ready_body,
        grid=(taps,),
        in_specs=[
            pl.BlockSpec(memory_space=pltpu.SMEM),
            whole(VOCAB, width),
            by_tap(own, width),
            by_tap(width, width),
        ],
        out_specs=[whole(VOCAB, VOCAB)] * 2 + [whole(own, VOCAB)] + [by_tap(own, VOCAB)] * 2 + [by_tap(width, width)] * 2,
        out_shape=[like(VOCAB, VOCAB)] * 2
        + [like(own, VOCAB)]
        + [like(taps, own, VOCAB)] * 2
        + [like(taps, width, width)] * 2,
        compiler_params=pltpu.CompilerParams(vmem_limit_bytes=60 << 20),
        cost_estimate=pl.CostEstimate(flops=4 << 30, bytes_accessed=32 << 20, transcendentals=0),
    )(where, embed_all, left_root, right_root)


def conv_body(
    where_ref, high_ref, low_ref, embed_ref, square_high, square_low, columns_ref, rooted_high, rooted_low, right_high, right_low,
    weight_ref, left_ref, right_ref, grad_out, weight_out, left_out, right_out,
):
    own, width = weight_ref.shape[1:]
    table = high_ref[0], low_ref[0]
    columns = columns_ref[...]
    pick = pick_rows(own, width, where_ref[0] * own)
    high = dot(jnp.concatenate([columns, rooted_high[0], rooted_low[0]], axis=0), table[0], NN)
    low = dot(jnp.concatenate([columns, rooted_high[0]], axis=0), table[1], NN)
    grad = high[:own] + low[:own]
    inner = high[own : 2 * own] + high[2 * own :] + low[own:]
    grad_out[0] = grad
    grad = split(grad)
    high = dot(jnp.concatenate([grad[0], grad[1], pick], axis=0), table[0], NT)
    low = dot(jnp.concatenate([grad[0], pick], axis=0), table[1], NT)
    crossed = split(high[:own] + high[own : 2 * own] + low[:own])
    mine = split(high[2 * own :] + low[own:])
    step = both(split(inner), (right_high[0], right_low[0]), NN)
    weight_out[0] = weight_ref[0] - RATE_CONV * step
    outer = dot(jnp.concatenate(crossed, axis=0), embed_ref[...], NN)
    left_out[0] = BETA_STAT * left_ref[0] + (1.0 - BETA_STAT) * (outer[:own] + outer[own:])
    outer = both(split(both(mine, (square_high[...], square_low[...]), NN)), table, NN)
    right_out[0] = BETA_STAT * right_ref[0] + (1.0 - BETA_STAT) * outer


def renew_conv(where, high, low, embed_all, ready, conv, left, right):
    taps, own, width = conv.shape
    by_tap = lambda *shape: pl.BlockSpec((1, *shape), lambda k: (k,) + (0,) * len(shape))
    whole = lambda *shape: pl.BlockSpec(shape, lambda k: (0,) * len(shape))
    rows = by_tap(own, width)
    return pl.pallas_call(
        conv_body,
        grid=(taps,),
        in_specs=[
            pl.BlockSpec(memory_space=pltpu.SMEM),
            by_tap(VOCAB, width),
            by_tap(VOCAB, width),
            whole(VOCAB, width),
            whole(VOCAB, VOCAB),
            whole(VOCAB, VOCAB),
            whole(own, VOCAB),
            by_tap(own, VOCAB),
            by_tap(own, VOCAB),
            by_tap(width, width),
            by_tap(width, width),
            rows,
            rows,
            rows,
        ],
        out_specs=[rows] * 4,
        out_shape=[jax.ShapeDtypeStruct(conv.shape, F32)] * 4,
        compiler_params=pltpu.CompilerParams(vmem_limit_bytes=60 << 20),
        cost_estimate=pl.CostEstimate(flops=8 << 30, bytes_accessed=32 << 20, transcendentals=0),
    )(where, high, low, embed_all, *ready, conv, left, right)


def embed_body(
    owner_ref, near_ref, far_ref, weight_ref, left_ref, right_ref, left_root_ref, right_root_ref,
    grad_out, weight_out, left_out, right_out, table,
):
    count, own, _ = near_ref.shape
    rows = weight_ref.shape[0]
    owner = owner_ref[0]
    for m in range(count):
        table[pl.ds(pl.multiple_of((owner ^ (2 * m)) * own, 8), own)] = near_ref[m]
        table[pl.ds(pl.multiple_of((owner ^ (2 * m + 1)) * own, 8), own)] = far_ref[m]
    pair = split(table[...])
    grad = dot2(pick_rows(rows, VOCAB, owner * rows), pair, NT)
    grad_out[...] = grad
    left_out[...] = BETA_STAT * left_ref[...] + (1.0 - BETA_STAT) * dot3(split(grad), pair, NN)
    right_out[...] = BETA_STAT * right_ref[...] + (1.0 - BETA_STAT) * dot3(split(near_ref[0]), pair, NT)
    step = dot3(split(dot3(split(left_root_ref[...]), pair, NT)), split(right_root_ref[...]), NN)
    weight_out[...] = weight_ref[...] - RATE_EMBED * step


def renew_embed(owner, near, far, embed, left, right, left_root, right_root):
    vmem = pl.BlockSpec(memory_space=pltpu.VMEM)
    shapes = [jax.ShapeDtypeStruct(item.shape, F32) for item in (embed, embed, left, right)]
    return pl.pallas_call(
        embed_body,
        in_specs=[pl.BlockSpec(memory_space=pltpu.SMEM)] + [vmem] * 7,
        out_specs=[vmem] * 4,
        out_shape=shapes,
        scratch_shapes=[pltpu.VMEM((embed.shape[1], VOCAB), F32)],
        compiler_params=pltpu.CompilerParams(vmem_limit_bytes=60 << 20),
    )(owner, near, far, embed, left, right, left_root, right_root)


def shards(
    byte_ids,
    lengths,
    embed,
    conv,
    score,
    out_grad,
    embed_left,
    embed_right,
    conv_left,
    conv_right,
    embed_left_root,
    embed_right_root,
    conv_left_root,
    conv_right_root,
    score_second,
):
    length = byte_ids.shape[1]
    width = embed.shape[1]
    taps = conv.shape[0]
    owner = lax.axis_index("dp")
    start = lax.axis_index("seq") * length
    conv_low = conv.astype(BF)
    where = jnp.stack([owner, lax.axis_index("seq")]).astype(jnp.int32)
    mid = marked_ids(byte_ids, lengths, start, taps)
    left, right = shifted_rim(out_grad, 1)
    zero = jnp.zeros((byte_ids.shape[0], 7, width), F32)
    grad_rim = jnp.concatenate([zero, left, right, zero], axis=1)
    embed_all, scores, near, far, masks, (mid, grad_rim) = gather_tables(where, embed, conv, score, (mid, grad_rim))
    hidden, rim, band = lookup(where, mid, out_grad, grad_rim, scores, near, far, masks, taps)
    weights, sums = weigh(band, lengths, start)
    plans = exchange_plan(lax.axis_size("seq"), lax.axis_size("dp"))
    me = jnp.stack([block_index(plan) for plan in plans])
    output, keep, send, extra = apply_weights(
        me, mid, out_grad, grad_rim, scores, hidden, rim, weights, sums, taps
    )
    ready = make_ready(where, embed_all, conv_left_root, conv_right_root)
    near, far, extra, ready = sum_over_devices(keep, send, extra, plans, ready)
    score_grad = extra[:, 0].reshape(width)
    entropy = extra[0, 1, 0] / extra[0, 1, 1]
    high, low, columns = order_table(me, near, far, conv_low)
    near = jnp.stack([columns] + [swap(columns, "dp", 2 * m) for m in range(1, lax.axis_size("dp") // 2)])
    conv_grad, new_conv, new_conv_left, new_conv_right = renew_conv(
        where, high, low, embed_all, ready, conv, conv_left, conv_right
    )
    near, conv_grad = lax.optimization_barrier((near, conv_grad))
    far = swap(near, "dp", 1)
    embed_grad, new_embed, new_embed_left, new_embed_right = renew_embed(
        where, near, far, embed, embed_left, embed_right, embed_left_root, embed_right_root
    )
    new_score_second = BETA_SECOND * score_second + (1.0 - BETA_SECOND) * score_grad * score_grad
    new_score = score - RATE_SCORE * score_grad / (jnp.sqrt(new_score_second) + EPSILON)
    return (
        output,
        entropy,
        embed_grad,
        conv_grad,
        score_grad,
        new_embed,
        new_conv,
        new_score,
        new_embed_left,
        new_embed_right,
        new_conv_left,
        new_conv_right,
        new_score_second,
    )


def solution(mesh):
    placed = (
        P("dp", "seq"),
        P("dp"),
        P("dp", None),
        P(None, "dp", None),
        P(),
        P("dp", "seq", None),
        P("dp", None),
        P("dp", None),
        P(None, "dp", None),
        P(None, "dp", None),
        P("dp", None),
        P(),
        P(None, "dp", None),
        P(),
        P(),
    )
    return jax.shard_map(
        shards,
        mesh=mesh,
        in_specs=placed,
        out_specs=(
            P("dp", "seq", None),
            P(),
            P("dp", None),
            P(None, "dp", None),
            P(),
            P("dp", None),
            P(None, "dp", None),
            P(),
            P("dp", None),
            P("dp", None),
            P(None, "dp", None),
            P(None, "dp", None),
            P(),
        ),
        check_vma=False,
    )
```

time: 1310 us -> 299 us (0.23)
  other arithmetic: 480 us -> 9.11 us
  matrix products: 422 us -> 0 us
  local copies, waits for them, and re-layouts: 256 us -> 9.68 us
  Pallas kernels: 0 us -> 145 us
  blocking collectives: 60.1 us -> 0 us
  starting transfers between devices: 17.5 us -> 56.3 us
  waiting for transfers between devices: 45.2 us -> 74.2 us
  between operations: 17.8 us -> 3.72 us
    dot_general x21 -> x0, matrix products: 422 us -> none  [the longest x4 102 us: shards(): jnp.einsum('rtd,d->rt', item, score, precision=highest)]
    another operation x2 -> x19, other arithmetic: 187 us -> 2.12 us  [the longest x1 0.62 us: shards(): where = jnp.stack([owner, lax.axis_index('seq')]).astype(jnp.int32)]
    pallas_call x0 -> x9, Pallas kernels: none -> 145 us  [the longest x1 66.3 us: lookup(): pl.pallas_call(partial(lookup_body, masks=masks, taps=taps), grid=(rows,)...]
    reduce_sum x5 -> x0, other arithmetic: 134 us -> none  [the longest x1 95.3 us: shards(): jnp.sum(mixed_grad * item, axis=2)]
    add x3 -> x7, other arithmetic: 78.8 us -> 2.06 us  [the longest x1 1.86 us: sum_over_devices(): cells = keep + got[:, :keep.shape[1]]]
    ppermute x6 -> x33, waiting for transfers between devices: 0.02 us -> 74.2 us  [the longest x29 74.2 us: swap(): lax.ppermute(cells, axis, [(i, i ^ bit) for i in range(lax.axis_size(axis...]
    dot_general x5 -> x0, local copies, waits for them, and re-layouts: 73.1 us -> none  [the longest x1 73.1 us: shards(): lax.dot_general(flat_windows, hidden_grad.reshape(rows_dev * piece_len, w...]
    reshape x2 -> x1, local copies, waits for them, and re-layouts: 59.6 us -> 0.58 us  [make_tables(): score.reshape(1, width)]
  transfers between devices with their start and end apart: 8 -> 33, of which waited for: 1 -> 17; matrix products, arithmetic and copies ran while one was open for 37% -> 4% of each run, Pallas kernels for 0% -> 9%
where the time goes in v1:
time: 299 us; the launch traced here: 298 us
  Pallas kernels  145 us (48%)
  waiting for transfers between devices  74.2 us (25%)
  starting transfers between devices  56.3 us (19%)
  local copies, waits for them, and re-layouts  9.68 us (3%)
  other arithmetic  9.11 us (3%)
  between operations  3.72 us (1%)
    ppermute x29, waiting for transfers between devices, swap(): lax.ppermute(cells, axis, [(i, i ^ bit) for i in range(lax.axis_size(axis...  74.2 us
    pallas_call x1, Pallas kernels, lookup(): pl.pallas_call(partial(lookup_body, masks=masks, taps=taps), grid=(rows,)...  66.3 us
    ppermute x29, starting transfers between devices, swap(): lax.ppermute(cells, axis, [(i, i ^ bit) for i in range(lax.axis_size(axis...  46.6 us
    pallas_call x1, Pallas kernels, apply_weights(): pl.pallas_call(apply_body, grid=(rows,), in_specs=[pl.BlockSpec(memory_sp...  35 us
    pallas_call x1, Pallas kernels, renew_conv(): pl.pallas_call(conv_body, grid=(taps,), in_specs=[pl.BlockSpec(memory_spa...  13.1 us
    pallas_call x1, Pallas kernels, make_ready(): pl.pallas_call(ready_body, grid=(taps,), in_specs=[pl.BlockSpec(memory_sp...  12.3 us
    ppermute x2, starting transfers between devices, shifted_rim(): left = lax.ppermute(tail, 'seq', [(i, i + 1) for i in range(count - 1)])  7.09 us
  transfers between devices with their start and end apart: 33, of which 17 were waited for; matrix products, arithmetic and copies ran while one was open for 4% of the time, Pallas kernels for 9%

profile of v1, /device:TPU:1, one launch (start us, length us, event | category | flops | bytes accessed | tf_op | source)
XLA Modules:
  0.0 297.5 jit_solution(11610406961567454374)
XLA Ops:
  1.3 2.2 shard_map.246.refs_0_
  3.4 2.2 collective-permute-start
  5.6 2.3 collective-permute-start.1
  8.7 3.1 %collective-permute-start.4 = (s32[16,8]{1,0:T(8,128)S(1)}, s32[16,8]{1,0:T(8,128)S(1)}, u32[]{:S(2)}, u32[]{:S(2)}) collective-permute-start(s32[16,8]{1,0:T(8,128)S(1)} %get-tuple-element.119), channel_id=1, source_target_pairs={{0,1},{1,2},{2,3},{4,5},{5,6},{6,7},{8,9},{9,10},{10,11},{12,13},{... | collective-permute-start | bytes 1544 | tf_op jit(solution)/shard_map/ppermute | solution.py:340
  11.8 1.3 collective-permute-start.5
  14.8 1.2 fusion.16
  16.1 4.0 %collective-permute-start.6 = (f32[16,1,768]{2,1,0:T(1,128)S(1)}, f32[16,1,768]{2,1,0:T(1,128)S(1)}, u32[]{:S(2)}, u32[]{:S(2)}) collective-permute-start(f32[16,1,768]{2,1,0:T(1,128)S(1)} %get-tuple-element.103), channel_id=1, source_target_pairs={{0,1},{1,2},{2,3},{4,5},{5,6},{6,7},{8,9},{9,10},{10,11},{12,13},{... | collective-permute-start | bytes 147464 | tf_op jit(solution)/shard_map/ppermute | solution.py:340
  20.1 1.3 collective-permute-start.7
  21.5 2.5 collective-permute-done.2.refs_3_
  24.1 4.6 %collective-permute-start.3 = (bf16[4,576,128]{2,1,0:T(8,128)(2,1)S(1)}, bf16[4,576,128]{2,1,0:T(8,128)(2,1)S(1)}, u32[]{:S(2)}, u32[]{:S(2)}) collective-permute-start(bf16[4,576,128]{2,1,0:T(8,128)(2,1)S(1)} %pad_maximum_fusion.3), channel_id=1, source_target_pairs={{0,4},{4,0},{8,12},{12,8},{16,20},{20,16},{24,28},{28,24},{1,5},{5... | collective-permute-start | bytes 1769480 | tf_op jit(solution)/shard_map/ppermute | solution.py:396
  29.9 1.2 stack.122.mid_ref
  33.0 3.0 %shard_map.247 = (bf16[256,768]{1,0:T(8,128)(2,1)}, bf16[32,768]{1,0:T(8,128)(2,1)}, bf16[4,256,128]{2,1,0:T(8,128)(2,1)}, bf16[4,256,128]{2,1,0:T(8,128)(2,1)}) custom-call(s32[2]{0:T(128)} %pad_add_fusion.1.where_ref.owner_ref, f32[1,768]{1,0:T(1,128)} %reshape.47.score_ref, bf16[960,128]{1,0:T(8,128)(2,1)} %shard_map.246.refs_0_, ...), custom_call_target="tpu_custom_call" | custom-call | tf_op jit(solution)/shard_map/pallas_call | solution.py:451
  36.0 2.4 collective-permute-start.8
  38.4 1.2 collective-permute-start.10
  39.6 4.0 %collective-permute-done.8 = bf16[4,256,128]{2,1,0:T(8,128)(2,1)S(1)} collective-permute-done((bf16[4,256,128]{2,1,0:T(8,128)(2,1)}, bf16[4,256,128]{2,1,0:T(8,128)(2,1)S(1)}, u32[]{:S(2)}, u32[]{:S(2)}) %collective-permute-start.8) | collective-permute-done | bytes 262176 | tf_op jit(solution)/shard_map/ppermute | solution.py:396
  44.6 3.9 %collective-permute-start.9 = (bf16[8,256,128]{2,1,0:T(8,128)(2,1)S(1)}, bf16[8,256,128]{2,1,0:T(8,128)(2,1)S(1)}, u32[]{:S(2)}, u32[]{:S(2)}) collective-permute-start(bf16[8,256,128]{2,1,0:T(8,128)(2,1)S(1)} %pad_maximum_fusion.4), channel_id=1, source_target_pairs={{0,2},{1,3},{2,0},{3,1},{4,6},{5,7},{6,4},{7,5},{8,10},{9,11},{10,... | collective-permute-start | bytes 1572872 | tf_op jit(solution)/shard_map/ppermute | solution.py:396
  49.9 10.1 %collective-permute-done.9 = bf16[8,256,128]{2,1,0:T(8,128)(2,1)S(1)} collective-permute-done((bf16[8,256,128]{2,1,0:T(8,128)(2,1)S(1)}, bf16[8,256,128]{2,1,0:T(8,128)(2,1)S(1)}, u32[]{:S(2)}, u32[]{:S(2)}) %collective-permute-start.9) | collective-permute-done | bytes 524320 | tf_op jit(solution)/shard_map/ppermute | solution.py:396
  60.1 1.8 collective-permute-done.11
  62.2 2.1 collective-permute-start.12
  65.6 2.7 collective-permute-done.12.far_ref
  68.2 66.3 %shard_map.248 = (bf16[16,4,256,768]{3,2,1,0:T(8,128)(2,1)}, bf16[16,32,768]{2,1,0:T(8,128)(2,1)}, f32[16,8,768]{2,1,0:T(8,128)}) custom-call(s32[2]{0:T(128)} %pad_add_fusion.1.where_ref.owner_ref, s32[16,8,768]{2,1,0:T(8,128)} %stack.122.mid_ref, f32[16,256,768]{2,1,0:T(8,128)} %g_ref.3, f32[16,16,768]{2,1,0:T(8,128)} %pad_maximum_fusion.2.gh_ref, ...), custom_call_target="tpu_custom_call" | custom-call | tf_op jit(solution)/shard_map/pallas_call | solution.py:109
  134.5 2.7 shard_map.249
  137.2 35.0 %shard_map.250 = (f32[16,256,768]{2,1,0:T(8,128)}, f32[2,640,384]{2,1,0:T(8,128)}, f32[2,648,384]{2,1,0:T(8,128)}, f32[2,8,384]{2,1,0:T(8,128)}) custom-call(s32[2]{0:T(128)} %pad_add_fusion.me_ref, s32[16,8,768]{2,1,0:T(8,128)} %stack.122.mid_ref, f32[16,256,768]{2,1,0:T(8,128)} %g_ref.3, f32[16,16,768]{2,1,0:T(8,128)} %pad_maximum_fusion.2.gh_ref, ...), custom_call_target="tpu_custom_call" | custom-call | tf_op jit(solution)/shard_map/pallas_call | solution.py:299
  172.6 3.8 %collective-permute-done.13 = f32[2,648,384]{2,1,0:T(8,128)S(1)} collective-permute-done((f32[2,648,384]{2,1,0:T(8,128)}, f32[2,648,384]{2,1,0:T(8,128)S(1)}, u32[]{:S(2)}, u32[]{:S(2)}) %collective-permute-start.13) | collective-permute-done | bytes 1990688 | tf_op jit(solution)/shard_map/ppermute | solution.py:396
  176.4 1.9 slice_add_fusion
  179.6 12.3 %collective-permute-done.16 = f32[328,384]{1,0:T(8,128)S(1)} collective-permute-done((f32[328,384]{1,0:T(8,128)S(1)}, f32[328,384]{1,0:T(8,128)S(1)}, u32[]{:S(2)}, u32[]{:S(2)}) %collective-permute-start.16) | collective-permute-done | bytes 503840 | tf_op jit(solution)/shard_map/ppermute | solution.py:396
  192.4 12.3 %shard_map.251 = (bf16[256,256]{1,0:T(8,128)(2,1)}, bf16[256,256]{1,0:T(8,128)(2,1)}, bf16[96,256]{1,0:T(8,128)(2,1)}, bf16[5,96,256]{2,1,0:T(8,128)(2,1)}, bf16...) custom-call(s32[2]{0:T(128)} %pad_add_fusion.1.where_ref.owner_ref, ...), custom_call_target="tpu_custom_call" | custom-call | flops 4294967296 | bytes 33554432 | tf_op jit(solution)/shard_map/pallas_call | solution.py:592
  204.7 1.3 collective-permute-start.15
  206.1 4.8 %collective-permute-done.15 = f32[168,384]{1,0:T(8,128)S(1)} collective-permute-done((f32[168,384]{1,0:T(8,128)S(1)}, f32[168,384]{1,0:T(8,128)S(1)}, u32[]{:S(2)}, u32[]{:S(2)}) %collective-permute-start.15) | collective-permute-done | bytes 258080 | tf_op jit(solution)/shard_map/ppermute | solution.py:396
  211.1 1.5 collective-permute-start.18
  215.1 4.1 %collective-permute-done.19 = f32[2,48,384]{2,1,0:T(8,128)S(1)} collective-permute-done((f32[2,48,384]{2,1,0:T(8,128)S(1)}, f32[2,48,384]{2,1,0:T(8,128)S(1)}, u32[]{:S(2)}, u32[]{:S(2)}) %collective-permute-start.19) | collective-permute-done | bytes 147488 | tf_op jit(solution)/shard_map/ppermute | solution.py:396
  219.2 2.7 collective-permute-done.20
  222.0 5.2 %collective-permute-start.21 = (f32[2,40,384]{2,1,0:T(8,128)S(1)}, f32[2,40,384]{2,1,0:T(8,128)S(1)}, u32[]{:S(2)}, u32[]{:S(2)}) collective-permute-start(f32[2,40,384]{2,1,0:T(8,128)S(1)} %slice_add_fusion.5), channel_id=1, source_target_pairs={{0,8},{4,12},{8,0},{12,4},{16,24},{20,28},{24,16},{28,20},{1,9},{5... | collective-permute-start | bytes 368648 | tf_op jit(solution)/shard_map/ppermute | solution.py:396
  227.2 2.0 collective-permute-start.22
  229.1 1.1 collective-permute-start.23
  230.3 1.6 collective-permute-done.22
  231.9 5.1 %collective-permute-done.23 = f32[2,40,384]{2,1,0:T(8,128)S(1)} collective-permute-done((f32[2,40,384]{2,1,0:T(8,128)S(1)}, f32[2,40,384]{2,1,0:T(8,128)S(1)}, u32[]{:S(2)}, u32[]{:S(2)}) %collective-permute-start.23) | collective-permute-done | bytes 122912 | tf_op jit(solution)/shard_map/ppermute | solution.py:396
  237.1 1.3 collective-permute-start.24
  238.5 3.8 %collective-permute-done.24 = f32[160,384]{1,0:T(8,128)S(1)} collective-permute-done((f32[160,384]{1,0:T(8,128)S(1)}, f32[160,384]{1,0:T(8,128)S(1)}, u32[]{:S(2)}, u32[]{:S(2)}) %collective-permute-start.24) | collective-permute-done | bytes 245792 | tf_op jit(solution)/shard_map/ppermute | solution.py:396
  242.4 1.2 collective-permute-done.26
  243.8 10.4 %collective-permute-done.25 = f32[320,384]{1,0:T(8,128)S(1)} collective-permute-done((f32[320,384]{1,0:T(8,128)S(1)}, f32[320,384]{1,0:T(8,128)S(1)}, u32[]{:S(2)}, u32[]{:S(2)}) %collective-permute-start.25) | collective-permute-done | bytes 491552 | tf_op jit(solution)/shard_map/ppermute | solution.py:396
  254.5 6.3 %collective-permute-start.28 = (f32[2,640,384]{2,1,0:T(8,128)S(1)}, f32[2,640,384]{2,1,0:T(8,128)}, u32[]{:S(2)}, u32[]{:S(2)}) collective-permute-start(f32[2,640,384]{2,1,0:T(8,128)S(1)} %pad_maximum_fusion.1.near_ref), channel_id=1, source_target_pairs={{0,4},{4,0},{8,12},{12,8},{16,20},{20,16},{24,28},{28,24},{1,5},{5... | collective-permute-start | bytes 5898248 | tf_op jit(solution)/shard_map/ppermute | solution.py:396
  261.8 2.8 collective-permute-done.28.far_ref
  264.6 5.4 %shard_map.252 = (bf16[5,256,768]{2,1,0:T(8,128)(2,1)}, bf16[5,256,768]{2,1,0:T(8,128)(2,1)}, f32[96,256]{1,0:T(8,128)}) custom-call(s32[2]{0:T(128)} %pad_add_fusion.me_ref, f32[2,640,384]{2,1,0:T(8,128)} %copy-done.1, f32[2,640,384]{2,1,0:T(8,128)} %collective-permute-done.28.far_ref, bf16[5,96,768]{2,1,0:T(8,128)(2,1)} %convert_element_type.25.conv_ref), custom_call_target="tpu_custom_call" | custom-call | tf_op jit(solution)/shard_map/pallas_call | solution.py:554
  270.6 2.2 collective-permute-start.30
  272.9 1.2 collective-permute-start.31
  274.0 13.1 %shard_map.253 = (f32[5,96,768]{2,1,0:T(8,128)}, f32[5,96,768]{2,1,0:T(8,128)}, f32[5,96,768]{2,1,0:T(8,128)}, f32[5,96,768]{2,1,0:T(8,128)}) custom-call(s32[2]{0:T(128)} %pad_add_fusion.1.where_ref.owner_ref, bf16[5,256,768]{2,1,0:T(8,128)(2,1)} %get-tuple-element.82.high_ref, bf16[5,256,768]{2,1,0:T(8,128)(2,1)} %get-tuple-element.83.low_ref, ...), custom_call_target="tpu_custom_call" | custom-call | flops 8589934592 | bytes 33554432 | tf_op jit(solution)/shard_map/pallas_call | solution.py:642
  291.5 4.9 %shard_map.254 = (f32[32,768]{1,0:T(8,128)}, f32[32,768]{1,0:T(8,128)}, f32[32,256]{1,0:T(8,128)}, f32[96,768]{1,0:T(8,128)}) custom-call(s32[2]{0:T(128)} %pad_add_fusion.1.where_ref.owner_ref, f32[4,96,256]{2,1,0:T(8,128)} %copy-done.3, f32[4,96,256]{2,1,0:T(8,128)} %copy-done.10, f32[32,768]{1,0:T(8,128)} %weight_ref.3, f32[32,256]{1,0:T(8,128)} %left_ref.3, ...), custom_call_target="tpu_custom_call" | custom-call | tf_op jit(solution)/shard_map/pallas_call | solution.py:690
  (134 shorter events, 20.8 us)
Async XLA Ops:
  3.4 25.3 %copy-start.14 = (f32[768]{0:T(1024)S(1)}, f32[768]{0:T(1024)}, u32[]{:S(2)}) copy-start(f32[768]{0:T(1024)} %param.19) | copy-start | bytes 9220
  3.4 25.9 %copy-start.12 = (s32[16,512]{1,0:T(8,128)S(1)}, s32[16,512]{1,0:T(8,128)}, u32[]{:S(2)}) copy-start(s32[16,512]{1,0:T(8,128)} %param.15) | copy-start | bytes 98308
  3.4 25.9 %copy-start.17 = (s32[16]{0:T(128)S(1)}, s32[16]{0:T(128)}, u32[]{:S(2)}) copy-start(s32[16]{0:T(128)} %param.16) | copy-start | bytes 196
  3.4 12.6 %collective-permute-start = (bf16[960,128]{1,0:T(8,128)(2,1)}, bf16[960,128]{1,0:T(8,128)(2,1)S(1)}, u32[]{:S(2)}, u32[]{:S(2)}) collective-permute-start(bf16[960,128]{1,0:T(8,128)(2,1)} %shard_map.246.refs_0_), channel_id=1, source_target_pairs={{0,8},{4,12},{8,0},{12,4},{16,24},{20,28},{24,16},{28,20},{1,9},{5... | collective-permute-start | bytes 737288 | tf_op jit(solution)/shard_map/ppermute | solution.py:396
  5.6 14.5 %collective-permute-start.1 = (bf16[960,128]{1,0:T(8,128)(2,1)}, bf16[960,128]{1,0:T(8,128)(2,1)S(1)}, u32[]{:S(2)}, u32[]{:S(2)}) collective-permute-start(bf16[960,128]{1,0:T(8,128)(2,1)} %shard_map.246.refs_0_), channel_id=1, source_target_pairs={{0,16},{4,20},{8,24},{12,28},{16,0},{20,4},{24,8},{28,12},{1,17},{... | collective-permute-start | bytes 737288 | tf_op jit(solution)/shard_map/ppermute | solution.py:396
  7.9 16.0 %collective-permute-start.2 = (bf16[960,128]{1,0:T(8,128)(2,1)}, bf16[960,128]{1,0:T(8,128)(2,1)S(1)}, u32[]{:S(2)}, u32[]{:S(2)}) collective-permute-start(bf16[960,128]{1,0:T(8,128)(2,1)} %shard_map.246.refs_0_), channel_id=1, source_target_pairs={{0,24},{4,28},{8,16},{12,20},{16,8},{20,12},{24,0},{28,4},{1,25},{... | collective-permute-start | bytes 737288 | tf_op jit(solution)/shard_map/ppermute | solution.py:396
  8.7 20.6 %collective-permute-start.4 = (s32[16,8]{1,0:T(8,128)S(1)}, s32[16,8]{1,0:T(8,128)S(1)}, u32[]{:S(2)}, u32[]{:S(2)}) collective-permute-start(s32[16,8]{1,0:T(8,128)S(1)} %get-tuple-element.119), channel_id=1, source_target_pairs={{0,1},{1,2},{2,3},{4,5},{5,6},{6,7},{8,9},{9,10},{10,11},{12,13},{... | collective-permute-start | bytes 1544 | tf_op jit(solution)/shard_map/ppermute | solution.py:340
  11.8 17.5 %collective-permute-start.5 = (s32[16,8]{1,0:T(8,128)S(1)}, s32[16,8]{1,0:T(8,128)S(1)}, u32[]{:S(2)}, u32[]{:S(2)}) collective-permute-start(s32[16,8]{1,0:T(8,128)S(1)} %get-tuple-element.120), channel_id=1, source_target_pairs={{1,0},{2,1},{3,2},{5,4},{6,5},{7,6},{9,8},{10,9},{11,10},{13,12},{... | collective-permute-start | bytes 1544 | tf_op jit(solution)/shard_map/ppermute | solution.py:341
  16.1 13.8 %copy-start.6 = (bf16[960,128]{1,0:T(8,128)(2,1)}, bf16[960,128]{1,0:T(8,128)(2,1)S(1)}, u32[]{:S(2)}) copy-start(bf16[960,128]{1,0:T(8,128)(2,1)S(1)} %collective-permute-done.refs_1_) | copy-start | bytes 737284
  16.1 15.1 %collective-permute-start.6 = (f32[16,1,768]{2,1,0:T(1,128)S(1)}, f32[16,1,768]{2,1,0:T(1,128)S(1)}, u32[]{:S(2)}, u32[]{:S(2)}) collective-permute-start(f32[16,1,768]{2,1,0:T(1,128)S(1)} %get-tuple-element.103), channel_id=1, source_target_pairs={{0,1},{1,2},{2,3},{4,5},{5,6},{6,7},{8,9},{9,10},{10,11},{12,13},{... | collective-permute-start | bytes 147464 | tf_op jit(solution)/shard_map/ppermute | solution.py:340
  20.1 11.0 %copy-start.7 = (bf16[960,128]{1,0:T(8,128)(2,1)}, bf16[960,128]{1,0:T(8,128)(2,1)S(1)}, u32[]{:S(2)}) copy-start(bf16[960,128]{1,0:T(8,128)(2,1)S(1)} %collective-permute-done.1.refs_2_) | copy-start | bytes 737284
  20.1 11.0 %collective-permute-start.7 = (f32[16,1,768]{2,1,0:T(1,128)S(1)}, f32[16,1,768]{2,1,0:T(1,128)S(1)}, u32[]{:S(2)}, u32[]{:S(2)}) collective-permute-start(f32[16,1,768]{2,1,0:T(1,128)S(1)} %get-tuple-element.104), channel_id=1, source_target_pairs={{1,0},{2,1},{3,2},{5,4},{6,5},{7,6},{9,8},{10,9},{11,10},{13,12},{... | collective-permute-start | bytes 147464 | tf_op jit(solution)/shard_map/ppermute | solution.py:341
  24.0 7.2 %copy-start.8 = (bf16[960,128]{1,0:T(8,128)(2,1)}, bf16[960,128]{1,0:T(8,128)(2,1)S(1)}, u32[]{:S(2)}) copy-start(bf16[960,128]{1,0:T(8,128)(2,1)S(1)} %collective-permute-done.2.refs_3_) | copy-start | bytes 737284
  24.1 8.1 %collective-permute-start.3 = (bf16[4,576,128]{2,1,0:T(8,128)(2,1)S(1)}, bf16[4,576,128]{2,1,0:T(8,128)(2,1)S(1)}, u32[]{:S(2)}, u32[]{:S(2)}) collective-permute-start(bf16[4,576,128]{2,1,0:T(8,128)(2,1)S(1)} %pad_maximum_fusion.3), channel_id=1, source_target_pairs={{0,4},{4,0},{8,12},{12,8},{16,20},{20,16},{24,28},{28,24},{1,5},{5... | collective-permute-start | bytes 1769480 | tf_op jit(solution)/shard_map/ppermute | solution.py:396
  36.0 24.0 %copy-start.5 = (bf16[4,256,128]{2,1,0:T(8,128)(2,1)S(1)}, bf16[4,256,128]{2,1,0:T(8,128)(2,1)}, u32[]{:S(2)}) copy-start(bf16[4,256,128]{2,1,0:T(8,128)(2,1)} %get-tuple-element.61) | copy-start | bytes 786436
  36.0 7.6 %collective-permute-start.8 = (bf16[4,256,128]{2,1,0:T(8,128)(2,1)}, bf16[4,256,128]{2,1,0:T(8,128)(2,1)S(1)}, u32[]{:S(2)}, u32[]{:S(2)}) collective-permute-start(bf16[4,256,128]{2,1,0:T(8,128)(2,1)} %get-tuple-element.61), channel_id=1, source_target_pairs={{0,1},{1,0},{2,3},{3,2},{4,5},{5,4},{6,7},{7,6},{8,9},{9,8},{10,11... | collective-permute-start | bytes 786440 | tf_op jit(solution)/shard_map/ppermute | solution.py:396
  38.4 23.5 %copy-start.4 = (bf16[4,256,128]{2,1,0:T(8,128)(2,1)S(1)}, bf16[4,256,128]{2,1,0:T(8,128)(2,1)}, u32[]{:S(2)}) copy-start(bf16[4,256,128]{2,1,0:T(8,128)(2,1)} %get-tuple-element.62) | copy-start | bytes 786436
  38.4 10.1 %collective-permute-start.10 = (bf16[4,256,128]{2,1,0:T(8,128)(2,1)}, bf16[4,256,128]{2,1,0:T(8,128)(2,1)S(1)}, u32[]{:S(2)}, u32[]{:S(2)}) collective-permute-start(bf16[4,256,128]{2,1,0:T(8,128)(2,1)} %get-tuple-element.62), channel_id=1, source_target_pairs={{0,2},{1,3},{2,0},{3,1},{4,6},{5,7},{6,4},{7,5},{8,10},{9,11},{10,... | collective-permute-start | bytes 786440 | tf_op jit(solution)/shard_map/ppermute | solution.py:396
  44.6 15.4 %collective-permute-start.9 = (bf16[8,256,128]{2,1,0:T(8,128)(2,1)S(1)}, bf16[8,256,128]{2,1,0:T(8,128)(2,1)S(1)}, u32[]{:S(2)}, u32[]{:S(2)}) collective-permute-start(bf16[8,256,128]{2,1,0:T(8,128)(2,1)S(1)} %pad_maximum_fusion.4), channel_id=1, source_target_pairs={{0,2},{1,3},{2,0},{3,1},{4,6},{5,7},{6,4},{7,5},{8,10},{9,11},{10,... | collective-permute-start | bytes 1572872 | tf_op jit(solution)/shard_map/ppermute | solution.py:396
  49.5 12.4 %collective-permute-start.11 = (bf16[8,256,128]{2,1,0:T(8,128)(2,1)S(1)}, bf16[8,256,128]{2,1,0:T(8,128)(2,1)S(1)}, u32[]{:S(2)}, u32[]{:S(2)}) collective-permute-start(bf16[8,256,128]{2,1,0:T(8,128)(2,1)S(1)} %pad_maximum_fusion.5), channel_id=1, source_target_pairs={{0,1},{1,0},{2,3},{3,2},{4,5},{5,4},{6,7},{7,6},{8,9},{9,8},{10,11... | collective-permute-start | bytes 1572872 | tf_op jit(solution)/shard_map/ppermute | solution.py:396
  62.2 6.0 %copy-start = (bf16[2,16,256,128]{3,2,1,0:T(8,128)(2,1)}, bf16[2,16,256,128]{3,2,1,0:T(8,128)(2,1)S(1)}, u32[]{:S(2)}) copy-start(bf16[2,16,256,128]{3,2,1,0:T(8,128)(2,1)S(1)} %pad_maximum_fusion.near_ref) | copy-start | bytes 6291460
  62.2 6.0 %collective-permute-start.12 = (bf16[2,16,256,128]{3,2,1,0:T(8,128)(2,1)S(1)}, bf16[2,16,256,128]{3,2,1,0:T(8,128)(2,1)}, u32[]{:S(2)}, u32[]{:S(2)}) collective-permute-start(bf16[2,16,256,128]{3,2,1,0:T(8,128)(2,1)S(1)} %pad_maximum_fusion.near_ref), channel_id=1, source_target_pairs={{0,4},{4,0},{8,12},{12,8},{16,20},{20,16},{24,28},{28,24},{1,5},{5... | collective-permute-start | bytes 6291464 | tf_op jit(solution)/shard_map/ppermute | solution.py:396
  172.2 4.3 %collective-permute-start.13 = (f32[2,648,384]{2,1,0:T(8,128)}, f32[2,648,384]{2,1,0:T(8,128)S(1)}, u32[]{:S(2)}, u32[]{:S(2)}) collective-permute-start(f32[2,648,384]{2,1,0:T(8,128)} %get-tuple-element.70), channel_id=1, source_target_pairs={{0,4},{4,0},{8,12},{12,8},{16,20},{20,16},{24,28},{28,24},{1,5},{5... | collective-permute-start | bytes 5971976 | tf_op jit(solution)/shard_map/ppermute | solution.py:396
  179.1 12.8 %collective-permute-start.16 = (f32[328,384]{1,0:T(8,128)S(1)}, f32[328,384]{1,0:T(8,128)S(1)}, u32[]{:S(2)}, u32[]{:S(2)}) collective-permute-start(f32[328,384]{1,0:T(8,128)S(1)} %pad_maximum_fusion.7), channel_id=1, source_target_pairs={{0,2},{1,3},{2,0},{3,1},{4,6},{5,7},{6,4},{7,5},{8,10},{9,11},{10,... | collective-permute-start | bytes 1511432 | tf_op jit(solution)/shard_map/ppermute | solution.py:396
  179.2 12.6 %collective-permute-start.14 = (f32[328,384]{1,0:T(8,128)S(1)}, f32[328,384]{1,0:T(8,128)S(1)}, u32[]{:S(2)}, u32[]{:S(2)}) collective-permute-start(f32[328,384]{1,0:T(8,128)S(1)} %pad_maximum_fusion.6), channel_id=1, source_target_pairs={{0,1},{1,0},{2,3},{3,2},{4,5},{5,4},{6,7},{7,6},{8,9},{9,8},{10,11... | collective-permute-start | bytes 1511432 | tf_op jit(solution)/shard_map/ppermute | solution.py:396
  192.1 14.0 %collective-permute-start.17 = (f32[168,384]{1,0:T(8,128)S(1)}, f32[168,384]{1,0:T(8,128)S(1)}, u32[]{:S(2)}, u32[]{:S(2)}) collective-permute-start(f32[168,384]{1,0:T(8,128)S(1)} %pad_maximum_fusion.13), channel_id=1, source_target_pairs={{0,1},{1,0},{2,3},{3,2},{4,5},{5,4},{6,7},{7,6},{8,9},{9,8},{10,11... | collective-permute-start | bytes 774152 | tf_op jit(solution)/shard_map/ppermute | solution.py:396
  204.7 6.2 %collective-permute-start.15 = (f32[168,384]{1,0:T(8,128)S(1)}, f32[168,384]{1,0:T(8,128)S(1)}, u32[]{:S(2)}, u32[]{:S(2)}) collective-permute-start(f32[168,384]{1,0:T(8,128)S(1)} %pad_maximum_fusion.12), channel_id=1, source_target_pairs={{0,2},{1,3},{2,0},{3,1},{4,6},{5,7},{6,4},{7,5},{8,10},{9,11},{10,... | collective-permute-start | bytes 774152 | tf_op jit(solution)/shard_map/ppermute | solution.py:396
  211.1 4.1 %collective-permute-start.18 = (f32[2,48,384]{2,1,0:T(8,128)S(1)}, f32[2,48,384]{2,1,0:T(8,128)S(1)}, u32[]{:S(2)}, u32[]{:S(2)}) collective-permute-start(f32[2,48,384]{2,1,0:T(8,128)S(1)} %get-tuple-element.123), channel_id=1, source_target_pairs={{0,8},{4,12},{8,0},{12,4},{16,24},{20,28},{24,16},{28,20},{1,9},{5... | collective-permute-start | bytes 442376 | tf_op jit(solution)/shard_map/ppermute | solution.py:396
  212.5 6.7 %collective-permute-start.19 = (f32[2,48,384]{2,1,0:T(8,128)S(1)}, f32[2,48,384]{2,1,0:T(8,128)S(1)}, u32[]{:S(2)}, u32[]{:S(2)}) collective-permute-start(f32[2,48,384]{2,1,0:T(8,128)S(1)} %get-tuple-element.124), channel_id=1, source_target_pairs={{0,16},{4,20},{8,24},{12,28},{16,0},{20,4},{24,8},{28,12},{1,17},{... | collective-permute-start | bytes 442376 | tf_op jit(solution)/shard_map/ppermute | solution.py:396
  213.6 8.4 %collective-permute-start.20 = (f32[2,48,384]{2,1,0:T(8,128)S(1)}, f32[2,48,384]{2,1,0:T(8,128)S(1)}, u32[]{:S(2)}, u32[]{:S(2)}) collective-permute-start(f32[2,48,384]{2,1,0:T(8,128)S(1)} %get-tuple-element.125), channel_id=1, source_target_pairs={{0,24},{4,28},{8,16},{12,20},{16,8},{20,12},{24,0},{28,4},{1,25},{... | collective-permute-start | bytes 442376 | tf_op jit(solution)/shard_map/ppermute | solution.py:396
  222.0 8.3 %collective-permute-start.21 = (f32[2,40,384]{2,1,0:T(8,128)S(1)}, f32[2,40,384]{2,1,0:T(8,128)S(1)}, u32[]{:S(2)}, u32[]{:S(2)}) collective-permute-start(f32[2,40,384]{2,1,0:T(8,128)S(1)} %slice_add_fusion.5), channel_id=1, source_target_pairs={{0,8},{4,12},{8,0},{12,4},{16,24},{20,28},{24,16},{28,20},{1,9},{5... | collective-permute-start | bytes 368648 | tf_op jit(solution)/shard_map/ppermute | solution.py:396
  227.2 4.7 %collective-permute-start.22 = (f32[2,40,384]{2,1,0:T(8,128)S(1)}, f32[2,40,384]{2,1,0:T(8,128)S(1)}, u32[]{:S(2)}, u32[]{:S(2)}) collective-permute-start(f32[2,40,384]{2,1,0:T(8,128)S(1)} %slice_add_fusion.5), channel_id=1, source_target_pairs={{0,16},{4,20},{8,24},{12,28},{16,0},{20,4},{24,8},{28,12},{1,17},{... | collective-permute-start | bytes 368648 | tf_op jit(solution)/shard_map/ppermute | solution.py:396
  229.1 7.9 %collective-permute-start.23 = (f32[2,40,384]{2,1,0:T(8,128)S(1)}, f32[2,40,384]{2,1,0:T(8,128)S(1)}, u32[]{:S(2)}, u32[]{:S(2)}) collective-permute-start(f32[2,40,384]{2,1,0:T(8,128)S(1)} %slice_add_fusion.5), channel_id=1, source_target_pairs={{0,24},{4,28},{8,16},{12,20},{16,8},{20,12},{24,0},{28,4},{1,25},{... | collective-permute-start | bytes 368648 | tf_op jit(solution)/shard_map/ppermute | solution.py:396
  237.1 5.1 %collective-permute-start.24 = (f32[160,384]{1,0:T(8,128)S(1)}, f32[160,384]{1,0:T(8,128)S(1)}, u32[]{:S(2)}, u32[]{:S(2)}) collective-permute-start(f32[160,384]{1,0:T(8,128)S(1)} %get-tuple-element.109), channel_id=1, source_target_pairs={{0,2},{1,3},{2,0},{3,1},{4,6},{5,7},{6,4},{7,5},{8,10},{9,11},{10,... | collective-permute-start | bytes 737288 | tf_op jit(solution)/shard_map/ppermute | solution.py:396
  238.5 5.0 %collective-permute-start.26 = (f32[160,384]{1,0:T(8,128)S(1)}, f32[160,384]{1,0:T(8,128)S(1)}, u32[]{:S(2)}, u32[]{:S(2)}) collective-permute-start(f32[160,384]{1,0:T(8,128)S(1)} %get-tuple-element.110), channel_id=1, source_target_pairs={{0,1},{1,0},{2,3},{3,2},{4,5},{5,4},{6,7},{7,6},{8,9},{9,8},{10,11... | collective-permute-start | bytes 737288 | tf_op jit(solution)/shard_map/ppermute | solution.py:396
  242.3 12.0 %collective-permute-start.25 = (f32[320,384]{1,0:T(8,128)S(1)}, f32[320,384]{1,0:T(8,128)S(1)}, u32[]{:S(2)}, u32[]{:S(2)}) collective-permute-start(f32[320,384]{1,0:T(8,128)S(1)} %pad_maximum_fusion.9), channel_id=1, source_target_pairs={{0,1},{1,0},{2,3},{3,2},{4,5},{5,4},{6,7},{7,6},{8,9},{9,8},{10,11... | collective-permute-start | bytes 1474568 | tf_op jit(solution)/shard_map/ppermute | solution.py:396
  243.6 10.8 %collective-permute-start.27 = (f32[320,384]{1,0:T(8,128)S(1)}, f32[320,384]{1,0:T(8,128)S(1)}, u32[]{:S(2)}, u32[]{:S(2)}) collective-permute-start(f32[320,384]{1,0:T(8,128)S(1)} %pad_maximum_fusion.10), channel_id=1, source_target_pairs={{0,2},{1,3},{2,0},{3,1},{4,6},{5,7},{6,4},{7,5},{8,10},{9,11},{10,... | collective-permute-start | bytes 1474568 | tf_op jit(solution)/shard_map/ppermute | solution.py:396
  254.4 6.4 %copy-start.2 = (f32[5,96,768]{2,1,0:T(8,128)S(1)}, f32[5,96,768]{2,1,0:T(8,128)}, u32[]{:S(2)}) copy-start(f32[5,96,768]{2,1,0:T(8,128)} %weight_ref.2) | copy-start | bytes 4423684
  254.5 10.0 %copy-start.1 = (f32[2,640,384]{2,1,0:T(8,128)}, f32[2,640,384]{2,1,0:T(8,128)S(1)}, u32[]{:S(2)}) copy-start(f32[2,640,384]{2,1,0:T(8,128)S(1)} %pad_maximum_fusion.1.near_ref) | copy-start | bytes 5898244
  254.5 10.0 %collective-permute-start.28 = (f32[2,640,384]{2,1,0:T(8,128)S(1)}, f32[2,640,384]{2,1,0:T(8,128)}, u32[]{:S(2)}, u32[]{:S(2)}) collective-permute-start(f32[2,640,384]{2,1,0:T(8,128)S(1)} %pad_maximum_fusion.1.near_ref), channel_id=1, source_target_pairs={{0,4},{4,0},{8,12},{12,8},{16,20},{20,16},{24,28},{28,24},{1,5},{5... | collective-permute-start | bytes 5898248 | tf_op jit(solution)/shard_map/ppermute | solution.py:396
  270.0 17.2 %collective-permute-start.29 = (f32[96,256]{1,0:T(8,128)}, f32[96,256]{1,0:T(8,128)S(1)}, u32[]{:S(2)}, u32[]{:S(2)}) collective-permute-start(f32[96,256]{1,0:T(8,128)} %get-tuple-element.81), channel_id=1, source_target_pairs={{0,8},{4,12},{8,0},{12,4},{16,24},{20,28},{24,16},{28,20},{1,9},{5... | collective-permute-start | bytes 294920 | tf_op jit(solution)/shard_map/ppermute | solution.py:396
  270.6 16.5 %collective-permute-start.30 = (f32[96,256]{1,0:T(8,128)}, f32[96,256]{1,0:T(8,128)S(1)}, u32[]{:S(2)}, u32[]{:S(2)}) collective-permute-start(f32[96,256]{1,0:T(8,128)} %get-tuple-element.81), channel_id=1, source_target_pairs={{0,16},{4,20},{8,24},{12,28},{16,0},{20,4},{24,8},{28,12},{1,17},{... | collective-permute-start | bytes 294920 | tf_op jit(solution)/shard_map/ppermute | solution.py:396
  272.9 14.3 %collective-permute-start.31 = (f32[96,256]{1,0:T(8,128)}, f32[96,256]{1,0:T(8,128)S(1)}, u32[]{:S(2)}, u32[]{:S(2)}) collective-permute-start(f32[96,256]{1,0:T(8,128)} %get-tuple-element.81), channel_id=1, source_target_pairs={{0,24},{4,28},{8,16},{12,20},{16,8},{20,12},{24,0},{28,4},{1,25},{... | collective-permute-start | bytes 294920 | tf_op jit(solution)/shard_map/ppermute | solution.py:396
  274.0 13.1 %copy-start.11 = (f32[96,256]{1,0:T(8,128)S(1)}, f32[96,256]{1,0:T(8,128)}, u32[]{:S(2)}) copy-start(f32[96,256]{1,0:T(8,128)} %get-tuple-element.81) | copy-start | bytes 294916
  274.0 16.1 %copy-start.16 = (f32[768]{0:T(1024)S(1)}, f32[768]{0:T(1024)}, u32[]{:S(2)}) copy-start(f32[768]{0:T(1024)} %param.29) | copy-start | bytes 9220
  287.2 3.6 %copy-start.3 = (f32[4,96,256]{2,1,0:T(8,128)}, f32[4,96,256]{2,1,0:T(8,128)S(1)}, u32[]{:S(2)}) copy-start(f32[4,96,256]{2,1,0:T(8,128)S(1)} %pad_maximum_fusion.11.near_ref) | copy-start | bytes 1179652
  287.2 3.6 %collective-permute-start.32 = (f32[4,96,256]{2,1,0:T(8,128)S(1)}, f32[4,96,256]{2,1,0:T(8,128)S(1)}, u32[]{:S(2)}, u32[]{:S(2)}) collective-permute-start(f32[4,96,256]{2,1,0:T(8,128)S(1)} %pad_maximum_fusion.11.near_ref), channel_id=1, source_target_pairs={{0,4},{4,0},{8,12},{12,8},{16,20},{20,16},{24,28},{28,24},{1,5},{5... | collective-permute-start | bytes 1179656 | tf_op jit(solution)/shard_map/ppermute | solution.py:396
  288.2 8.2 %copy-start.15 = (f32[768]{0:T(1024)}, f32[768]{0:T(1024)S(1)}, u32[]{:S(2)}) copy-start(f32[768]{0:T(1024)S(1)} %reshape_squeeze.3) | copy-start | bytes 9220
  (3 other events, 2.3 us)

commit v2 on v1

--- a/solution.py
+++ b/solution.py
@@ -28,14 +28,71 @@
     return high, (v - high.astype(F32)).astype(BF)
 
 
+def exponent_of(v):
+    return jnp.clip(jnp.floor(jnp.log2(jnp.maximum(v, 1e-30))) + 1.0, -90.0, 120.0)
+
+
+def to_code(v, exponent):
+    scaled = v * jnp.exp2(15.0 - exponent)
+    code = jnp.clip(jnp.floor(scaled + 0.5), -32767.0, 32767.0)
+    return code, scaled - code
+
+
+def as_short(v):
+    return v.astype(jnp.int32).astype(jnp.int16)
+
+
+def as_float(v):
+    return v.astype(jnp.int32).astype(F32)
+
+
+def encode(rows, extra):
+    exponent = exponent_of(jnp.max(jnp.abs(rows), axis=0, keepdims=True))
+    code, _ = to_code(rows, exponent)
+    few = extra[0:2]
+    powers = exponent_of(jnp.abs(few))
+    high, rest = to_code(few, powers)
+    low = jnp.floor(rest * 16384.0 + 0.5)
+    blank = jnp.zeros((9, rows.shape[1]), F32)
+    return as_short(jnp.concatenate([code, exponent, high, low, powers, blank], axis=0))
+
+
+def decode(cells):
+    cells = as_float(cells)
+    count = cells.shape[0] - 16
+    more = cells[count:]
+    extra = (more[1:3] + more[3:5] * (1.0 / 16384.0)) * jnp.exp2(more[5:7] - 15.0)
+    extra = jnp.concatenate([extra, jnp.zeros((6, extra.shape[1]), F32)], axis=0)
+    return cells[:count] * jnp.exp2(more[0:1] - 15.0), extra
+
+
 def roll_to(v, offset):
     width = v.shape[-1]
     return v if offset == 0 else pltpu.roll(v, (-offset) % width, v.ndim - 1)
 
 
-def lookup_body(where_ref, mid_ref, g_ref, gh_ref, score_ref, near_ref, far_ref, hid_ref, rim_ref, band_ref, gext, table_ref, *, masks, taps):
+def score_rows(score_ref):
+    high, low = (part.astype(F32) for part in split(score_ref[...]))
+    row = lax.broadcasted_iota(jnp.int32, (16, high.shape[1]), 0)
+    return jnp.where((row == 0) | (row == 2), high, jnp.where(row == 1, low, 0.0)).astype(BF)
+
+
+def grad_window(g_ref, gh_ref, i, tiles):
+    half = tiles * TILE // 2
+    first, last = i * TILE // 2 - 8, (i + 1) * TILE // 2 + 8
+    parts = [g_ref[0, max(first, 0) : min(last, half)]]
+    if i == 0:
+        parts = [gh_ref[0, 0:8]] + parts
+    if i == tiles - 1:
+        parts = parts + [gh_ref[0, 8:16]]
+    return split(jnp.concatenate(parts, axis=0))
+
+
+def lookup_body(
+    where_ref, mid_ref, next_ref, g_ref, gh_ref, score_ref, near_ref, far_ref, hid_ref, rim_ref, band_ref, table_ref, onehot_ref,
+    *, masks, taps,
+):
     length = hid_ref.shape[1] * TILE
-    half = length // 2
     blocks = table_ref.shape[1] // TILE
     slots = near_ref.shape[1] // len(masks[0])
 
@@ -53,29 +110,33 @@
                         column = pl.multiple_of(unit % blocks * TILE, TILE)
                         table_ref[pl.ds(row, VOCAB), pl.ds(column, TILE)] = source[h, spot]
 
-    gext[0:8] = gh_ref[0, 0:8]
-    gext[8 : half + 8] = g_ref[0]
-    gext[half + 8 : half + 16] = gh_ref[0, 8:16]
     nt = (((1,), (1,)), ((), ()))
     tiles = length // TILE
-    mid = mid_ref[0]
-    rim = jnp.where(lax.broadcasted_iota(jnp.int32, (8, TILE), 1) < TILE // 2, mid[:, TILE + length :], mid[:, 0:TILE])
-    mid = jnp.concatenate([mid[:, TILE : TILE + length], pltpu.roll(rim, HALO, 1)], axis=1)
-    cells = lax.broadcasted_iota(jnp.int32, (VOCAB, length + TILE), 0)
-    hits = [(mid[k : k + 1] == cells).astype(F32).astype(BF) for k in range(taps)]
-    onehot = jnp.concatenate(hits + hits, axis=0)[:, 0 : length + 2 * HALO]
+    lanes = lax.broadcasted_iota(jnp.int32, (1, VOCAB), 1).astype(F32)
+
+    def mark(ref):
+        columns = jnp.transpose(ref[0].astype(F32))
+        ids = [columns[TILE : TILE + length], columns[TILE - HALO : TILE], columns[TILE + length : TILE + length + HALO]]
+        ids = jnp.concatenate(ids, axis=0)
+        for k in range(taps):
+            onehot_ref[:, k * VOCAB : (k + 1) * VOCAB] = (ids[:, k : k + 1] == lanes).astype(F32).astype(BF)
+
+    @pl.when(pl.program_id(0) == 0)
+    def _():
+        mark(mid_ref)
+
+    onehot = onehot_ref[...]
+    onehot = jnp.concatenate([onehot, onehot], axis=1)
     for n in range(0, table_ref.shape[1], 256):
-        h_high, h_low = split(
-            lax.dot_general(onehot, table_ref[:, n : n + 256], (((0,), (0,)), ((), ())), preferred_element_type=F32)
-        )
+        hidden = jnp.dot(onehot, table_ref[:, n : n + 256], preferred_element_type=F32)
+        h_high, h_low = split(hidden[0:length])
         for i in range(tiles):
             hid_ref[0, i, 0:TILE, n : n + 256] = h_high[i * TILE : (i + 1) * TILE]
             hid_ref[0, i, TILE : 2 * TILE, n : n + 256] = h_low[i * TILE : (i + 1) * TILE]
-        rim_ref[0, 0:16, n : n + 256] = h_high[length:]
-        rim_ref[0, 16:32, n : n + 256] = h_low[length:]
-    for i in range(length // TILE):
-        g_high, g_low = split(gext[i * TILE // 2 : i * TILE // 2 + WIN])
-        left = jnp.concatenate([g_high, g_low, score_ref[0:16]], axis=0)
+        rim_ref[0, :, n : n + 256] = hidden[length:]
+    score = score_rows(score_ref)
+    for i in range(tiles):
+        left = jnp.concatenate([*grad_window(g_ref, gh_ref, i, tiles), score], axis=0)
         gram = lax.dot_general(left, hid_ref[0, i], nt, preferred_element_type=F32)
         band = gram[0:WIN, 0:TILE] + gram[WIN : 2 * WIN, 0:TILE] + gram[0:WIN, TILE:]
         dots = gram[2 * WIN : 2 * WIN + 1, 0:TILE] + gram[2 * WIN + 1 : 2 * WIN + 2, 0:TILE] + gram[2 * WIN : 2 * WIN + 1, TILE:]
@@ -83,27 +144,17 @@
         gap = place - (lax.broadcasted_iota(jnp.int32, (WIN, TILE), 1) >> 1)
         rows = [jnp.sum(jnp.where(gap == d, band, 0.0), axis=0, keepdims=True) for d in (-1, 0, 1)]
         band_ref[0, :, TILE * (i + 1) : TILE * (i + 2)] = jnp.concatenate(rows + [dots, jnp.zeros((4, TILE), F32)], axis=0)
-    rims = rim_ref[0]
-    g_high, g_low = split(jnp.concatenate([gext[0:16], gext[half : half + 16]], axis=0))
-    gram = lax.dot_general(jnp.concatenate([g_high, g_low, score_ref[0:16]], axis=0), rims, nt, preferred_element_type=F32)
-    band = gram[0:32, 0:16] + gram[32:64, 0:16] + gram[0:32, 16:32]
-    dots = gram[64:65, 0:16] + gram[65:66, 0:16] + gram[64:65, 16:32]
-    row = lax.broadcasted_iota(jnp.int32, (32, 16), 0)
-    lane = lax.broadcasted_iota(jnp.int32, (32, 16), 1)
-    place = jnp.where(row < 16, row - 8, half - 24 + row)
-    spot = jnp.where(lane < 8, lane - 8, length + lane - 8)
-    gap = place - (spot >> 1)
-    rows = [jnp.sum(jnp.where(gap == d, band, 0.0), axis=0, keepdims=True) for d in (-1, 0, 1)]
-    both = jnp.concatenate(rows + [dots, jnp.zeros((4, 16), F32)], axis=0)
-    both = pltpu.roll(jnp.concatenate([both, jnp.zeros((8, TILE - 16), F32)], axis=1), TILE - 8, 1)
-    band_ref[0, :, 0:TILE] = both
-    band_ref[0, :, TILE + length :] = both
-
-
-def lookup(where, mid, out_grad, grad_rim, score_rows, near, far, masks, taps):
+    mark(next_ref)
+    blank = jnp.zeros((8, TILE), F32)
+    band_ref[0, :, 0:TILE] = blank
+    band_ref[0, :, TILE + length :] = blank
+
+
+def lookup(where, mid, out_grad, grad_rim, score, near, far, masks, taps):
     rows, _, span = mid.shape
     half, width = out_grad.shape[1:]
-    tiles = 2 * half // TILE
+    length = 2 * half
+    tiles = length // TILE
     whole = lambda *shape: pl.BlockSpec(shape, lambda r: (0,) * len(shape), pipeline_mode=pl.Buffered(1))
     by_row = lambda *shape: pl.BlockSpec((1, *shape), lambda r: (r,) + (0,) * len(shape))
     return pl.pallas_call(
@@ -112,27 +163,28 @@
         in_specs=[
             pl.BlockSpec(memory_space=pltpu.SMEM),
             by_row(8, span),
+            pl.BlockSpec((1, 8, span), lambda r: (jnp.minimum(r + 1, rows - 1), 0, 0)),
             by_row(half, width),
             by_row(16, width),
-            whole(*score_rows.shape),
+            whole(1, width),
             whole(*near.shape),
             whole(*far.shape),
         ],
-        out_specs=[by_row(tiles, 2 * TILE, width), by_row(32, width), by_row(8, span)],
+        out_specs=[by_row(tiles, 2 * TILE, width), by_row(16, width), by_row(8, span)],
         out_shape=[
             jax.ShapeDtypeStruct((rows, tiles, 2 * TILE, width), BF),
-            jax.ShapeDtypeStruct((rows, 32, width), BF),
+            jax.ShapeDtypeStruct((rows, 16, width), F32),
             jax.ShapeDtypeStruct((rows, 8, span), F32),
         ],
         scratch_shapes=[
-            pltpu.VMEM((half + 16, width), F32),
             pltpu.VMEM((2 * taps * VOCAB, width), BF),
+            pltpu.VMEM((length + 2 * HALO, taps * VOCAB), BF),
         ],
         compiler_params=pltpu.CompilerParams(vmem_limit_bytes=56 << 20),
-    )(where, mid, out_grad, grad_rim, score_rows, near, far)
-
-
-def weigh_body(band_ref, lengths_ref, start_ref, out_ref, sums_ref):
+    )(where, mid, mid, out_grad, grad_rim, score.reshape(1, width), near, far)
+
+
+def weigh_body(band_ref, lengths_ref, start_ref, score_ref, rim_ref, edge_ref, out_ref, sums_ref, spill_ref):
     rows, _, span = band_ref.shape
     length = span - 2 * TILE
     start = start_ref[0]
@@ -159,7 +211,18 @@
     def shifts(v):
         return {d: roll_to(v, d) for d in range(-3, 4)}
 
-    dots = shifts(band_ref[:, 3, :] * valid)
+    base = [band_ref[:, d, :] for d in range(4)]
+    edges = [edge_ref[j] for j in range(4)]
+    meets = {4: {2: 0}, 5: {2: 0}, 6: {1: 0, 2: 1}, 7: {1: 0, 2: 1}}
+    meets.update({8: {1: 3, 0: 2}, 9: {1: 3, 0: 2}, 10: {0: 3}, 11: {0: 3}})
+    spots = {spot: TILE - 8 + spot + (length if spot >= 8 else 0) for spot in meets}
+    near = {spot: rim_ref[:, spot, :] for spot in meets}
+    for spot, pairs in meets.items():
+        here = lane == spots[spot]
+        base[3] = jnp.where(here, jnp.sum(near[spot] * score_ref[...], axis=1, keepdims=True), base[3])
+        for d, j in pairs.items():
+            base[d] = jnp.where(here, jnp.sum(near[spot] * edges[j], axis=1, keepdims=True), base[d])
+    dots = shifts(base[3] * valid)
     scores = [over_block(b, lambda d: dots[d]) * (1.0 / b) for b in range(1, SIZES + 1)]
     highest = jnp.maximum(jnp.maximum(scores[0], scores[1]), jnp.maximum(scores[2], scores[3]))
     powers = [jnp.exp(item - highest) for item in scores]
@@ -174,10 +237,10 @@
     entropy = jnp.sum(jnp.where(own, entropy * valid, 0.0), axis=1, keepdims=True)
     count = jnp.sum(own_valid, axis=1, keepdims=True)
     sums_ref[...] = jnp.where(lax.broadcasted_iota(jnp.int32, (rows, TILE), 1) == 0, entropy, count)
-    below, same, above = (shifts(band_ref[:, d, :] * valid) for d in range(3))
-    near = {0: same[0], 1: jnp.where(even, same[1], below[1]), 2: below[2], 3: below[3]}
-    near.update({-1: jnp.where(even, above[-1], same[-1]), -2: above[-2], -3: above[-3]})
-    inner = [over_block(b, lambda d: near[d]) * (valid * (0.5 / b)) for b in range(1, SIZES + 1)]
+    below, same, above = (shifts(base[d] * valid) for d in range(3))
+    close = {0: same[0], 1: jnp.where(even, same[1], below[1]), 2: below[2], 3: below[3]}
+    close.update({-1: jnp.where(even, above[-1], same[-1]), -2: above[-2], -3: above[-3]})
+    inner = [over_block(b, lambda d: close[d]) * (valid * (0.5 / b)) for b in range(1, SIZES + 1)]
     mean = probs[0] * inner[0] + probs[1] * inner[1] + probs[2] * inner[2] + probs[3] * inner[3]
     score_in = [probs[b] * (inner[b] - mean) for b in range(SIZES)]
     pull = jnp.zeros_like(total)
@@ -189,28 +252,38 @@
         moved = shifts(probs[b - 1] * valid * (0.5 / b))
         for d, mask in inside[b].items():
             weight[d] = weight[d] + (moved[d] if mask is None else jnp.where(mask, moved[d], 0.0))
-    out_ref[:, 0, :] = valid * (weight[-2] + jnp.where(even, weight[-1], weight[-3]))
+    below = valid * (weight[-2] + jnp.where(even, weight[-1], weight[-3]))
+    above = valid * (weight[2] + jnp.where(even, weight[3], weight[1]))
+    pick = lambda v, spot: jnp.sum(jnp.where(lane == spots[spot], v, 0.0), axis=1, keepdims=True) * near[spot]
+    spill_ref[...] = jnp.zeros_like(spill_ref)
+    spill_ref[:, 0, :] = pick(above, 6) + pick(above, 7)
+    spill_ref[:, 7, :] = pick(below, 8) + pick(below, 9)
+    out_ref[:, 0, :] = below
     out_ref[:, 1, :] = valid * (weight[0] + jnp.where(even, weight[1], weight[-1]))
-    out_ref[:, 2, :] = valid * (weight[2] + jnp.where(even, weight[3], weight[1]))
+    out_ref[:, 2, :] = above
     out_ref[:, 3, :] = valid * pull
     for d in range(4, 8):
         out_ref[:, d, :] = jnp.zeros_like(total)
 
 
-def weigh(band, lengths, start):
+def weigh(band, lengths, start, score, rim, edges):
     rows, _, span = band.shape
     vmem = pl.BlockSpec(memory_space=pltpu.VMEM)
     return pl.pallas_call(
         weigh_body,
-        in_specs=[vmem, vmem, pl.BlockSpec(memory_space=pltpu.SMEM)],
-        out_specs=[vmem, vmem],
-        out_shape=[jax.ShapeDtypeStruct(band.shape, F32), jax.ShapeDtypeStruct((rows, TILE), F32)],
-    )(band, lengths.reshape(rows, 1), start.reshape(1))
+        in_specs=[vmem, vmem, pl.BlockSpec(memory_space=pltpu.SMEM), vmem, vmem, vmem],
+        out_specs=[vmem, vmem, vmem],
+        out_shape=[
+            jax.ShapeDtypeStruct(band.shape, F32),
+            jax.ShapeDtypeStruct((rows, TILE), F32),
+            jax.ShapeDtypeStruct((rows, 8, rim.shape[2]), F32),
+        ],
+    )(band, lengths.reshape(rows, 1), start.reshape(1), score.reshape(1, -1), rim, edges)
 
 
 def apply_body(
-    me_ref, mid_ref, g_ref, gh_ref, score_ref, hid_ref, rim_ref, weight_ref, sums_ref,
-    out_ref, keep_ref, send_ref, extra_ref, onehot, hgrad, gext, total, table_ref, pull_ref,
+    me_ref, mid_ref, g_ref, gh_ref, score_ref, hid_ref, spill_ref, weight_ref, sums_ref,
+    out_ref, keep_ref, send_ref, extra_ref, onehot, hgrad, total, table_ref, pull_ref, staged,
 ):
     length = hid_ref.shape[1] * TILE
     half = length // 2
@@ -225,11 +298,9 @@
     for tap in range(taps):
         hit = mid_ref[0, tap : tap + 1, TILE : TILE + length] == cells
         onehot[tap * VOCAB : (tap + 1) * VOCAB] = hit.astype(F32).astype(BF)
-    gext[0:8] = gh_ref[0, 0:8]
-    gext[8 : half + 8] = g_ref[0]
-    gext[half + 8 : half + 16] = gh_ref[0, 8:16]
     total[...] = jnp.zeros_like(total)
     pulled = jnp.zeros((1, total.shape[1]), F32)
+    score = score_rows(score_ref)
     for i in range(length // TILE):
         w = weight_ref[0, :, TILE * (i + 1) : TILE * (i + 2)]
         place = lax.broadcasted_iota(jnp.int32, (WIN, TILE), 0) - 8
@@ -241,8 +312,8 @@
         q_high, q_low = split(w[3:4])
         sub = lax.broadcasted_iota(jnp.int32, (16, TILE), 0)
         q = jnp.where(sub < 2, q_high.astype(F32), jnp.where(sub == 2, q_low.astype(F32), 0.0)).astype(BF)
-        g_high, g_low = split(gext[i * TILE // 2 : i * TILE // 2 + WIN])
-        stack = jnp.concatenate([g_high, g_low, g_high, score_ref[16:32]], axis=0)
+        g_high, g_low = grad_window(g_ref, gh_ref, i, length // TILE)
+        stack = jnp.concatenate([g_high, g_low, g_high, score], axis=0)
         left = jnp.concatenate([a_high, a_high, a_low, q], axis=0)
         hg = lax.dot_general(left, stack, (((0,), (0,)), ((), ())), preferred_element_type=F32)
         hgrad[i * TILE : (i + 1) * TILE] = hg.astype(BF)
@@ -250,23 +321,8 @@
         res = jnp.dot(jnp.concatenate([left, left], axis=1), hid_ref[0, i], preferred_element_type=F32)
         total[i * TILE // 2 : i * TILE // 2 + WIN] += res[0:WIN] + res[WIN : 2 * WIN]
         pulled = pulled + res[2 * WIN : 2 * WIN + 1] + res[2 * WIN + 2 : 2 * WIN + 3]
-    lane = lax.broadcasted_iota(jnp.int32, (8, TILE), 1)
-    w = jnp.where(lane < 64, weight_ref[0, :, TILE + length :], weight_ref[0, :, 0:TILE])
-    w = pltpu.roll(w, 8, 1)[:, 0:16]
-    row = lax.broadcasted_iota(jnp.int32, (32, 16), 0)
-    lane = lax.broadcasted_iota(jnp.int32, (32, 16), 1)
-    place = jnp.where(row < 16, row - 8, half - 24 + row)
-    spot = jnp.where(lane < 8, lane - 8, length + lane - 8)
-    gap = place - (spot >> 1)
-    a = jnp.where(gap == 0, w[1:2], 0.0)
-    a = jnp.where(gap == -1, w[0:1], a)
-    a = jnp.where(gap == 1, w[2:3], a)
-    a_high, a_low = split(a)
-    left = jnp.concatenate([a_high, a_low], axis=0)
-    res = jnp.dot(jnp.concatenate([left, left], axis=1), rim_ref[0], preferred_element_type=F32)
-    res = res[0:32] + res[32:64]
-    total[8:16] += res[8:16]
-    total[half : half + 8] += res[16:24]
+    total[8:16] += jnp.where(lax.broadcasted_iota(jnp.int32, spill_ref.shape[1:], 0) == 0, spill_ref[0], 0.0)
+    total[half : half + 8] += jnp.where(lax.broadcasted_iota(jnp.int32, spill_ref.shape[1:], 0) == 7, spill_ref[0], 0.0)
     out_ref[0] = total[8 : half + 8]
     pull_ref[0:1] += pulled
     table_ref[...] += jnp.dot(onehot[...], hgrad[...], preferred_element_type=F32)
@@ -280,17 +336,21 @@
         extra = jnp.where((row == 1) & (lane < 2), counts, pull_ref[...])
         part = extra.shape[1] // 2
         block = table_ref.shape[0] // BLOCKS
+        half_rows = BLOCKS // 2 * block
         for h in range(2):
-            extra_ref[h] = extra[:, h * part : (h + 1) * part]
-            send_ref[h, BLOCKS // 2 * block :] = extra[:, h * part : (h + 1) * part]
+            mine = extra[:, h * part : (h + 1) * part]
+            extra_ref[h] = mine
             for p in range(BLOCKS):
                 source = pl.multiple_of((me_ref[h] ^ p) * block, 8)
                 rows = table_ref[pl.ds(source, block), h * part : (h + 1) * part]
-                target = keep_ref if p < BLOCKS // 2 else send_ref
-                target[h, p % (BLOCKS // 2) * block : (p % (BLOCKS // 2) + 1) * block] = rows
-
-
-def apply_weights(me, mid, out_grad, grad_rim, score_rows, hid, rim, weight, sums, taps):
+                if p < BLOCKS // 2:
+                    keep_ref[h, p * block : (p + 1) * block] = rows
+                else:
+                    staged[p * block - half_rows : (p + 1) * block - half_rows] = rows
+            send_ref[h] = encode(staged[...], mine)
+
+
+def apply_weights(me, mid, out_grad, grad_rim, score, hid, spill, weight, sums, taps):
     rows, _, span = mid.shape
     half, width = out_grad.shape[1:]
     tiles = 2 * half // TILE
@@ -304,34 +364,34 @@
             by_row(8, span),
             by_row(half, width),
             by_row(16, width),
-            whole(*score_rows.shape),
+            whole(1, width),
             by_row(tiles, 2 * TILE, width),
-            by_row(32, width),
+            by_row(8, width),
             by_row(8, span),
             whole(*sums.shape),
         ],
         out_specs=[
             by_row(half, width),
             whole(2, taps * VOCAB // 2, width // 2),
-            whole(2, taps * VOCAB // 2 + 8, width // 2),
+            whole(2, taps * VOCAB // 2 + 16, width // 2),
             whole(2, 8, width // 2),
         ],
         out_shape=[
             jax.ShapeDtypeStruct((rows, half, width), F32),
             jax.ShapeDtypeStruct((2, taps * VOCAB // 2, width // 2), F32),
-            jax.ShapeDtypeStruct((2, taps * VOCAB // 2 + 8, width // 2), F32),
+            jax.ShapeDtypeStruct((2, taps * VOCAB // 2 + 16, width // 2), jnp.int16),
             jax.ShapeDtypeStruct((2, 8, width // 2), F32),
         ],
         scratch_shapes=[
             pltpu.VMEM((taps * VOCAB, 2 * half), BF),
             pltpu.VMEM((2 * half, width), BF),
             pltpu.VMEM((half + 16, width), F32),
-            pltpu.VMEM((half + 16, width), F32),
             pltpu.VMEM((taps * VOCAB, width), F32),
             pltpu.VMEM((8, width), F32),
+            pltpu.VMEM((taps * VOCAB // 2, width // 2), F32),
         ],
         compiler_params=pltpu.CompilerParams(vmem_limit_bytes=56 << 20),
-    )(me, mid, out_grad, grad_rim, score_rows, hid, rim, weight, sums)
+    )(me, mid, out_grad, grad_rim, score.reshape(1, width), hid, spill, weight, sums)
 
 
 def shifted_rim(cells, width):
@@ -421,8 +481,8 @@
     )(where, conv, embed)
 
 
-def tables_body(where_ref, score_ref, *refs, slots, own, rows):
-    *near, far_ref, embed_ref, stack_ref, high_ref, low_ref, units = refs
+def tables_body(where_ref, *refs, slots, own, rows):
+    *near, far_ref, embed_ref, high_ref, low_ref, units = refs
     blocks = embed_ref.shape[1] // TILE
     first = blocks * rows
     for m, near_ref in enumerate(near):
@@ -438,26 +498,22 @@
     for t in range(slots):
         high, low = split(jnp.dot(embed_ref[...], units[t], preferred_element_type=F32))
         high_ref[t], low_ref[t] = high, low
-    high, low = (part.astype(F32) for part in split(score_ref[...]))
-    row = lax.broadcasted_iota(jnp.int32, stack_ref.shape, 0)
-    highs, lows = (row == 0) | (row == 16) | (row == 18), (row == 1) | (row == 17)
-    stack_ref[...] = jnp.where(highs, high, jnp.where(lows, low, 0.0)).astype(BF)
-
-
-def make_tables(where, score, near, far, slots, own, rows):
-    width = score.shape[0]
+
+
+def make_tables(where, near, far, slots, own, rows):
+    width = 2 * len(near) * own
     vmem = pl.BlockSpec(memory_space=pltpu.VMEM)
     unit = jax.ShapeDtypeStruct((slots, VOCAB, TILE), BF)
     return pl.pallas_call(
         partial(tables_body, slots=slots, own=own, rows=rows),
-        in_specs=[pl.BlockSpec(memory_space=pltpu.SMEM)] + [vmem] * (len(near) + 2),
-        out_specs=[vmem] * 4,
-        out_shape=[jax.ShapeDtypeStruct((VOCAB, width), BF), jax.ShapeDtypeStruct((32, width), BF), unit, unit],
+        in_specs=[pl.BlockSpec(memory_space=pltpu.SMEM)] + [vmem] * (len(near) + 1),
+        out_specs=[vmem] * 3,
+        out_shape=[jax.ShapeDtypeStruct((VOCAB, width), BF), unit, unit],
         scratch_shapes=[pltpu.VMEM((slots, width, TILE), BF)],
-    )(where, score.reshape(1, width), *near, far)
-
-
-def gather_tables(where, embed, conv, score, rims):
+    )(where, *near, far)
+
+
+def gather_tables(where, embed, conv, left_root, rims):
     taps, own, width = conv.shape
     rows = embed.shape[0]
     seq, chips = lax.axis_size("seq"), lax.axis_size("dp") // 2
@@ -468,7 +524,8 @@
     other = first + slots * own
     far = swap(jnp.stack([jnp.concatenate([item[:first], item[other:]], axis=0) for item in near]), "dp", 1)
     far, rims = lax.optimization_barrier((far, rims))
-    embed_all, score_rows, *parts = make_tables(where, score, near, far, slots, own, rows)
+    embed_all, *parts = make_tables(where, near, far, slots, own, rows)
+    ready = make_ready(where, embed_all, left_root)
     across = bits_of(seq)
     masks = []
     for h in range(2):
@@ -478,41 +535,76 @@
             parts[h] = jnp.concatenate([parts[h], swap(parts[h], "seq", bit)], axis=0)
             found = found + [mask ^ bit for mask in found]
         masks.append(found)
-    units = jnp.stack(parts)
-    return embed_all, score_rows, units, swap(units, "dp", 1), masks, rims
-
-
-def sum_over_devices(keep, send, extra, plans, ready):
-    block = keep.shape[1] // (BLOCKS // 2)
+    units, ready = lax.optimization_barrier((jnp.stack(parts), ready))
+    return embed_all, units, swap(units, "dp", 1), masks, ready, rims
+
+
+def fold_body(keep_ref, extra_ref, *refs, gots, pieces, joint):
+    got_refs, keep_out, extra_out, *sends = refs[:gots], refs[gots], refs[gots + 1], *refs[gots + 2 :]
+    rest = keep_ref.shape[1] // pieces
+    for h in range(2):
+        total, extra = keep_ref[h], extra_ref[h]
+        for ref in got_refs if got_refs[0].ndim == 3 else got_refs[h : h + 1]:
+            cells, more = decode(ref[h] if ref.ndim == 3 else ref[...])
+            total, extra = total + cells, extra + more
+        keep_out[h] = total[:rest]
+        extra_out[h] = extra
+        for m in range(1, pieces):
+            code = encode(total[m * rest : (m + 1) * rest], extra)
+            if joint:
+                sends[m - 1][h] = code
+            else:
+                sends[h][...] = code
+
+
+def fold(keep, extra, got, pieces, joint):
+    _, count, width = keep.shape
+    rest = count // pieces
+    cells = jax.ShapeDtypeStruct((2, rest + 16, width) if joint else (rest + 16, width), jnp.int16)
+    sends = 0 if pieces == 1 else pieces - 1 if joint else 2
+    vmem = pl.BlockSpec(memory_space=pltpu.VMEM)
+    return pl.pallas_call(
+        partial(fold_body, gots=len(got), pieces=pieces, joint=joint),
+        in_specs=[vmem] * (2 + len(got)),
+        out_specs=[vmem] * (2 + sends),
+        out_shape=[jax.ShapeDtypeStruct((2, rest, width), F32), jax.ShapeDtypeStruct(extra.shape, F32)] + [cells] * sends,
+    )(keep, extra, *got)
+
+
+def finish_body(cells_ref, out_ref):
+    count = cells_ref.shape[1]
+    for h in range(2):
+        rows = cells_ref[h]
+        exponent = exponent_of(jnp.max(jnp.abs(rows), axis=0, keepdims=True))
+        code, _ = to_code(rows, exponent)
+        out_ref[h] = as_short(jnp.concatenate([code, jnp.broadcast_to(exponent, (8, rows.shape[1]))], axis=0))
+
+
+def finish(cells):
+    vmem = pl.BlockSpec(memory_space=pltpu.VMEM)
+    return pl.pallas_call(
+        finish_body,
+        in_specs=[vmem],
+        out_specs=vmem,
+        out_shape=jax.ShapeDtypeStruct((2, cells.shape[1] + 8, cells.shape[2]), jnp.int16),
+    )(cells)
+
+
+def sum_over_devices(keep, send, extra, plans):
     depth = BLOCKS.bit_length() - 1
-    got = swap(send, "dp", 1)
-    cells = keep + got[:, : keep.shape[1]]
-    extra = extra + got[:, keep.shape[1] :]
     across = len([axis for axis, _ in plans[0] if axis == "seq"])
-    parts, extras = [], []
-    for h in range(2):
-        part, more = cells[h], extra[h]
-        for step, (axis, bit) in enumerate(plans[h][1 : 1 + across]):
-            if step == 1 and h == 0:
-                part, ready = lax.optimization_barrier((part, ready))
-            rest = part.shape[0] // 2
-            got = swap(jnp.concatenate([part[rest:], more], axis=0), axis, bit)
-            part, more = part[:rest] + got[:rest], more + got[rest:]
-        parts.append(part)
-        extras.append(more)
-    cells, extra = jnp.stack(parts), jnp.stack(extras)
     along = 1 << (depth - 1 - across)
+    got = [swap(send, "dp", 1)]
+    for step in range(1, 1 + across):
+        keep, extra, *sends = fold(keep, extra, got, 2, False)
+        got = [swap(sends[h], *plans[h][step]) for h in range(2)]
+    keep, extra, *sends = fold(keep, extra, got, along, True)
     if along > 1:
-        got = [
-            swap(jnp.concatenate([cells[:, m * block : (m + 1) * block], extra], axis=1), "dp", 2 * m)
-            for m in range(1, along)
-        ]
-        cells, extra = cells[:, :block], extra
-        for item in got:
-            cells, extra = cells + item[:, :block], extra + item[:, block:]
+        got = [swap(item, "dp", 2 * m) for m, item in enumerate(sends, 1)]
+        keep, extra = fold(keep, extra, got, 1, True)
     for axis, bit in plans[0][depth:]:
-        got = swap(jnp.concatenate([cells, extra], axis=1), axis, bit)
-        cells, extra = cells + got[:, :block], extra + got[:, block:]
+        keep, extra = keep + swap(keep, axis, bit), extra + swap(extra, axis, bit)
+    cells = finish(keep)
     if along > 1:
         cells = jnp.concatenate([cells] + [swap(cells, "dp", 2 * m) for m in range(1, along)], axis=1)
     parts = []
@@ -522,7 +614,7 @@
             part = jnp.concatenate([part, swap(part, axis, bit)], axis=0)
         parts.append(part)
     cells = jnp.stack(parts)
-    return cells, swap(cells, "dp", 1), extra, ready
+    return cells, swap(cells, "dp", 1), extra
 
 
 def pick_rows(count, total, first):
@@ -536,7 +628,9 @@
     for h in range(2):
         for p in range(BLOCKS):
             source = near_ref if p < BLOCKS // 2 else far_ref
-            rows = source[h, p % (BLOCKS // 2) * block : (p % (BLOCKS // 2) + 1) * block]
+            first = p % (BLOCKS // 2) * (block + 8)
+            cells = as_float(source[h, first : first + block + 8])
+            rows = cells[:block] * jnp.exp2(cells[block : block + 1] - 15.0)
             table[pl.ds(pl.multiple_of((me_ref[h] ^ p) * block, 8), block), h * part : (h + 1) * part] = rows
     taps = conv_ref.shape[0]
     total = jnp.zeros(grad_ref.shape, F32)
@@ -571,7 +665,7 @@
     return first[:count] + first[count:] + dot(left[0], right[1], dims)
 
 
-def ready_body(where_ref, embed_ref, left_root_ref, right_root_ref, square_high, square_low, columns_ref, rooted_high, rooted_low, right_high, right_low):
+def ready_body(where_ref, embed_ref, left_root_ref, square_high, square_low, columns_ref, rooted_high, rooted_low):
     own, width = left_root_ref.shape[1:]
     embed = embed_ref[...]
 
@@ -581,10 +675,9 @@
         columns_ref[...] = dot(pick_rows(own, width, where_ref[0] * own), embed, NT).astype(BF)
 
     rooted_high[0], rooted_low[0] = split(dot2_left(split(left_root_ref[0]), embed, NT))
-    right_high[0], right_low[0] = split(right_root_ref[0])
-
-
-def make_ready(where, embed_all, left_root, right_root):
+
+
+def make_ready(where, embed_all, left_root):
     taps, own, width = left_root.shape
     by_tap = lambda *shape: pl.BlockSpec((1, *shape), lambda k: (k,) + (0,) * len(shape))
     whole = lambda *shape: pl.BlockSpec(shape, lambda k: (0,) * len(shape))
@@ -596,20 +689,18 @@
             pl.BlockSpec(memory_space=pltpu.SMEM),
             whole(VOCAB, width),
             by_tap(own, width),
-            by_tap(width, width),
-        ],
-        out_specs=[whole(VOCAB, VOCAB)] * 2 + [whole(own, VOCAB)] + [by_tap(own, VOCAB)] * 2 + [by_tap(width, width)] * 2,
+        ],
+        out_specs=[whole(VOCAB, VOCAB)] * 2 + [whole(own, VOCAB)] + [by_tap(own, VOCAB)] * 2,
         out_shape=[like(VOCAB, VOCAB)] * 2
         + [like(own, VOCAB)]
-        + [like(taps, own, VOCAB)] * 2
-        + [like(taps, width, width)] * 2,
+        + [like(taps, own, VOCAB)] * 2,
         compiler_params=pltpu.CompilerParams(vmem_limit_bytes=60 << 20),
-        cost_estimate=pl.CostEstimate(flops=4 << 30, bytes_accessed=32 << 20, transcendentals=0),
-    )(where, embed_all, left_root, right_root)
+        cost_estimate=pl.CostEstimate(flops=1 << 30, bytes_accessed=3 << 20, transcendentals=0),
+    )(where, embed_all, left_root)
 
 
 def conv_body(
-    where_ref, high_ref, low_ref, embed_ref, square_high, square_low, columns_ref, rooted_high, rooted_low, right_high, right_low,
+    where_ref, high_ref, low_ref, embed_ref, square_high, square_low, columns_ref, rooted_high, rooted_low, right_root_ref,
     weight_ref, left_ref, right_ref, grad_out, weight_out, left_out, right_out,
 ):
     own, width = weight_ref.shape[1:]
@@ -626,7 +717,7 @@
     low = dot(jnp.concatenate([grad[0], pick], axis=0), table[1], NT)
     crossed = split(high[:own] + high[own : 2 * own] + low[:own])
     mine = split(high[2 * own :] + low[own:])
-    step = both(split(inner), (right_high[0], right_low[0]), NN)
+    step = both(split(inner), split(right_root_ref[0]), NN)
     weight_out[0] = weight_ref[0] - RATE_CONV * step
     outer = dot(jnp.concatenate(crossed, axis=0), embed_ref[...], NN)
     left_out[0] = BETA_STAT * left_ref[0] + (1.0 - BETA_STAT) * (outer[:own] + outer[own:])
@@ -634,7 +725,7 @@
     right_out[0] = BETA_STAT * right_ref[0] + (1.0 - BETA_STAT) * outer
 
 
-def renew_conv(where, high, low, embed_all, ready, conv, left, right):
+def renew_conv(where, high, low, embed_all, ready, right_root, conv, left, right):
     taps, own, width = conv.shape
     by_tap = lambda *shape: pl.BlockSpec((1, *shape), lambda k: (k,) + (0,) * len(shape))
     whole = lambda *shape: pl.BlockSpec(shape, lambda k: (0,) * len(shape))
@@ -653,7 +744,6 @@
             by_tap(own, VOCAB),
             by_tap(own, VOCAB),
             by_tap(width, width),
-            by_tap(width, width),
             rows,
             rows,
             rows,
@@ -662,7 +752,7 @@
         out_shape=[jax.ShapeDtypeStruct(conv.shape, F32)] * 4,
         compiler_params=pltpu.CompilerParams(vmem_limit_bytes=60 << 20),
         cost_estimate=pl.CostEstimate(flops=8 << 30, bytes_accessed=32 << 20, transcendentals=0),
-    )(where, high, low, embed_all, *ready, conv, left, right)
+    )(where, high, low, embed_all, *ready, right_root, conv, left, right)
 
 
 def embed_body(
@@ -725,22 +815,24 @@
     left, right = shifted_rim(out_grad, 1)
     zero = jnp.zeros((byte_ids.shape[0], 7, width), F32)
     grad_rim = jnp.concatenate([zero, left, right, zero], axis=1)
-    embed_all, scores, near, far, masks, (mid, grad_rim) = gather_tables(where, embed, conv, score, (mid, grad_rim))
-    hidden, rim, band = lookup(where, mid, out_grad, grad_rim, scores, near, far, masks, taps)
-    weights, sums = weigh(band, lengths, start)
+    edges = jnp.stack([left[:, 0], out_grad[:, 0], out_grad[:, -1], right[:, 0]])
+    embed_all, near, far, masks, ready, (mid, grad_rim) = gather_tables(
+        where, embed, conv, conv_left_root, (mid, grad_rim)
+    )
+    hidden, rim, band = lookup(where, mid, out_grad, grad_rim, score, near, far, masks, taps)
+    weights, sums, spill = weigh(band, lengths, start, score, rim, edges)
     plans = exchange_plan(lax.axis_size("seq"), lax.axis_size("dp"))
     me = jnp.stack([block_index(plan) for plan in plans])
     output, keep, send, extra = apply_weights(
-        me, mid, out_grad, grad_rim, scores, hidden, rim, weights, sums, taps
+        me, mid, out_grad, grad_rim, score, hidden, spill, weights, sums, taps
     )
-    ready = make_ready(where, embed_all, conv_left_root, conv_right_root)
-    near, far, extra, ready = sum_over_devices(keep, send, extra, plans, ready)
+    near, far, extra = sum_over_devices(keep, send, extra, plans)
     score_grad = extra[:, 0].reshape(width)
     entropy = extra[0, 1, 0] / extra[0, 1, 1]
     high, low, columns = order_table(me, near, far, conv_low)
     near = jnp.stack([columns] + [swap(columns, "dp", 2 * m) for m in range(1, lax.axis_size("dp") // 2)])
     conv_grad, new_conv, new_conv_left, new_conv_right = renew_conv(
-        where, high, low, embed_all, ready, conv, conv_left, conv_right
+        where, high, low, embed_all, ready, conv_right_root, conv, conv_left, conv_right
     )
     near, conv_grad = lax.optimization_barrier((near, conv_grad))
     far = swap(near, "dp", 1)

time: 299 us -> 273 us (0.913)
  waiting for transfers between devices: 74.2 us -> 44.6 us
  local copies, waits for them, and re-layouts: 9.68 us -> 15.2 us
    ppermute x29, waiting for transfers between devices: 74.2 us -> 44.5 us  [swap(): lax.ppermute(cells, axis, [(i, i ^ bit) for i in range(lax.axis_size(axis...]
    pallas_call x0 -> x5, Pallas kernels: none -> 11.4 us  [the longest x4 9.78 us: fold(): pl.pallas_call(partial(fold_body, gots=len(got), pieces=pieces, joint=joi...]
    pallas_call x1, Pallas kernels: 12.3 us -> 5.45 us  [make_ready(): pl.pallas_call(ready_body, grid=(taps,), in_specs=[pl.BlockSpec(memory_sp...]
    pallas_call x1, Pallas kernels: 66.3 us -> 61.4 us  [lookup(): pl.pallas_call(partial(lookup_body, masks=masks, taps=taps), grid=(rows,)...]
    unnamed x36 -> x52, local copies, waits for them, and re-layouts: 2.27 us -> 5.61 us
  transfers between devices with their start and end apart: 33 -> 33, of which waited for: 17 -> 18; matrix products, arithmetic and copies ran while one was open for 4% -> 6% of each run, Pallas kernels for 9% -> 7%
where the time goes in v2:
time: 273 us; the launch traced here: 272 us
  Pallas kernels  145 us (53%)
  starting transfers between devices  55.7 us (20%)
  waiting for transfers between devices  44.6 us (16%)
  local copies, waits for them, and re-layouts  15.2 us (6%)
  other arithmetic  7.85 us (3%)
  between operations  3.63 us (1%)
    pallas_call x1, Pallas kernels, lookup(): pl.pallas_call(partial(lookup_body, masks=masks, taps=taps), grid=(rows,)...  61.4 us
    ppermute x29, starting transfers between devices, swap(): lax.ppermute(cells, axis, [(i, i ^ bit) for i in range(lax.axis_size(axis...  46 us
    ppermute x29, waiting for transfers between devices, swap(): lax.ppermute(cells, axis, [(i, i ^ bit) for i in range(lax.axis_size(axis...  44.5 us
    pallas_call x1, Pallas kernels, apply_weights(): pl.pallas_call(apply_body, grid=(rows,), in_specs=[pl.BlockSpec(memory_sp...  34.7 us
    pallas_call x1, Pallas kernels, renew_conv(): pl.pallas_call(conv_body, grid=(taps,), in_specs=[pl.BlockSpec(memory_spa...  13.1 us
    pallas_call x4, Pallas kernels, fold(): pl.pallas_call(partial(fold_body, gots=len(got), pieces=pieces, joint=joi...  9.78 us
    ppermute x2, starting transfers between devices, shifted_rim(): left = lax.ppermute(tail, 'seq', [(i, i + 1) for i in range(count - 1)])  7.09 us
    unnamed x52, local copies, waits for them, and re-layouts  5.61 us
  transfers between devices with their start and end apart: 33, of which 18 were waited for; matrix products, arithmetic and copies ran while one was open for 6% of the time, Pallas kernels for 7%

profile of v2, /device:TPU:1, one launch (start us, length us, event | category | flops | bytes accessed | tf_op | source)
XLA Modules:
  0.0 271.5 jit_solution(9895021078694686919)
XLA Ops:
  1.3 2.2 shard_map.246.refs_0_
  3.4 2.1 collective-permute-start
  5.5 2.3 collective-permute-start.1
  8.6 3.1 %collective-permute-start.4 = (s32[16,8]{1,0:T(8,128)S(1)}, s32[16,8]{1,0:T(8,128)S(1)}, u32[]{:S(2)}, u32[]{:S(2)}) collective-permute-start(s32[16,8]{1,0:T(8,128)S(1)} %get-tuple-element.136), channel_id=1, source_target_pairs={{0,1},{1,2},{2,3},{4,5},{5,6},{6,7},{8,9},{9,10},{10,11},{12,13},{... | collective-permute-start | bytes 1544 | tf_op jit(solution)/shard_map/ppermute | solution.py:400
  11.8 1.3 collective-permute-start.5
  16.0 4.0 %collective-permute-start.6 = (f32[16,1,768]{2,1,0:T(1,128)S(1)}, f32[16,1,768]{2,1,0:T(1,128)S(1)}, u32[]{:S(2)}, u32[]{:S(2)}) collective-permute-start(f32[16,1,768]{2,1,0:T(1,128)S(1)} %get-tuple-element.128), channel_id=1, source_target_pairs={{0,1},{1,2},{2,3},{4,5},{5,6},{6,7},{8,9},{9,10},{10,11},{12,13},{... | collective-permute-start | bytes 147464 | tf_op jit(solution)/shard_map/ppermute | solution.py:400
  20.1 1.3 collective-permute-start.7
  21.4 2.4 collective-permute-done.2.refs_3_
  24.0 4.6 %collective-permute-start.3 = (bf16[4,576,128]{2,1,0:T(8,128)(2,1)S(1)}, bf16[4,576,128]{2,1,0:T(8,128)(2,1)S(1)}, u32[]{:S(2)}, u32[]{:S(2)}) collective-permute-start(bf16[4,576,128]{2,1,0:T(8,128)(2,1)S(1)} %pad_maximum_fusion.2), channel_id=1, source_target_pairs={{0,4},{4,0},{8,12},{12,8},{16,20},{20,16},{24,28},{28,24},{1,5},{5... | collective-permute-start | bytes 1769480 | tf_op jit(solution)/shard_map/ppermute | solution.py:456
  32.4 3.0 %shard_map.247 = (bf16[256,768]{1,0:T(8,128)(2,1)}, bf16[4,256,128]{2,1,0:T(8,128)(2,1)}, bf16[4,256,128]{2,1,0:T(8,128)(2,1)}) custom-call(s32[2]{0:T(128)} %pad_add_fusion.5.where_ref.owner_ref, bf16[960,128]{1,0:T(8,128)(2,1)} %shard_map.246.refs_0_, bf16[960,128]{1,0:T(8,128)(2,1)} %copy-done.8, bf16[960,128]{1,0:T(8,128)(2,1)} %copy-done.9, ...), custom_call_target="tpu_custom_call" | custom-call | tf_op jit(solution)/shard_map/pallas_call | solution.py:507
  35.4 2.4 collective-permute-start.8
  37.7 1.2 collective-permute-start.10
  39.0 3.3 %collective-permute-done.8 = bf16[4,256,128]{2,1,0:T(8,128)(2,1)S(1)} collective-permute-done((bf16[4,256,128]{2,1,0:T(8,128)(2,1)}, bf16[4,256,128]{2,1,0:T(8,128)(2,1)S(1)}, u32[]{:S(2)}, u32[]{:S(2)}) %collective-permute-start.8) | collective-permute-done | bytes 262176 | tf_op jit(solution)/shard_map/ppermute | solution.py:456
  43.3 4.1 %collective-permute-start.9 = (bf16[8,256,128]{2,1,0:T(8,128)(2,1)S(1)}, bf16[8,256,128]{2,1,0:T(8,128)(2,1)S(1)}, u32[]{:S(2)}, u32[]{:S(2)}) collective-permute-start(bf16[8,256,128]{2,1,0:T(8,128)(2,1)S(1)} %pad_maximum_fusion.3), channel_id=1, source_target_pairs={{0,2},{1,3},{2,0},{3,1},{4,6},{5,7},{6,4},{7,5},{8,10},{9,11},{10,... | collective-permute-start | bytes 1572872 | tf_op jit(solution)/shard_map/ppermute | solution.py:456
  49.2 5.5 %shard_map.248 = (bf16[256,256]{1,0:T(8,128)(2,1)}, bf16[256,256]{1,0:T(8,128)(2,1)}, bf16[96,256]{1,0:T(8,128)(2,1)}, bf16[5,96,256]{2,1,0:T(8,128)(2,1)}, bf16[5,96,256]{2,1,0:T(8,128)(2,1)}) custom-call(s32[2]{0:T(128)} %pad_add_fusion.5.where_ref.owner_ref, bf16[256,768]{1,0:T(8,128)(2,1)} %get-tuple-element.73.embed_ref, f32[5,96,768]{2,1,0:T(8,128)} %left_root_ref.2), custom_call_target="tpu_custom_call" | custom-call | flops 1073741824 | bytes 3145728 | tf_op jit(solution)/shard_map/pallas_call | solution.py:685
  54.7 3.6 %collective-permute-done.9 = bf16[8,256,128]{2,1,0:T(8,128)(2,1)S(1)} collective-permute-done((bf16[8,256,128]{2,1,0:T(8,128)(2,1)S(1)}, bf16[8,256,128]{2,1,0:T(8,128)(2,1)S(1)}, u32[]{:S(2)}, u32[]{:S(2)}) %collective-permute-start.9) | collective-permute-done | bytes 524320 | tf_op jit(solution)/shard_map/ppermute | solution.py:456
  58.4 1.9 collective-permute-done.11
  60.6 2.6 collective-permute-start.12
  67.1 61.4 %shard_map.249 = (bf16[16,4,256,768]{3,2,1,0:T(8,128)(2,1)}, f32[16,16,768]{2,1,0:T(8,128)}, f32[16,8,768]{2,1,0:T(8,128)}) custom-call(s32[2]{0:T(128)} %pad_add_fusion.5.where_ref.owner_ref, s32[16,8,768]{2,1,0:T(8,128)} %stack.107.mid_ref.next_ref, s32[16,8,768]{2,1,0:T(8,128)} %stack.107.mid_ref.next_ref, f32[16,256,768]{2,1,0:T(8,128)} %g_ref.3, ...), custom_call_target="tpu_custom_call" | custom-call | tf_op jit(solution)/shard_map/pallas_call | solution.py:160
  128.5 3.4 %shard_map.250 = (f32[16,8,768]{2,1,0:T(8,128)}, f32[16,128]{1,0:T(8,128)}, f32[16,8,768]{2,1,0:T(8,128)}) custom-call(f32[16,8,768]{2,1,0:T(8,128)} %get-tuple-element.81.band_ref, s32[16,1]{1,0:T(8,128)} %copy.32.lengths_ref, s32[1]{0:T(128)} %bitcast.15.start_ref, f32[1,768]{1,0:T(1,128)} %reshape.45.score_ref, f32[16,16,768]{2,1,0:T(8,128)} %get-tuple-element.82.rim_ref, ...), custom_call_target="tpu_custom_call" | custom-call | tf_op jit(solution)/shard_map/pallas_call | solution.py:272
  131.9 34.7 %shard_map.251 = (f32[16,256,768]{2,1,0:T(8,128)}, f32[2,640,384]{2,1,0:T(8,128)}, s16[2,656,384]{2,1,0:T(8,128)(2,1)}, f32[2,8,384]{2,1,0:T(8,128)}) custom-call(s32[2]{0:T(128)} %pad_add_fusion.4.me_ref, s32[16,8,768]{2,1,0:T(8,128)} %stack.107.mid_ref.next_ref, f32[16,256,768]{2,1,0:T(8,128)} %g_ref.3, f32[16,16,768]{2,1,0:T(8,128)} %pad_maximum_fusion.1.gh_ref, ...), custom_call_target="tpu_custom_call" | custom-call | tf_op jit(solution)/shard_map/pallas_call | solution.py:359
  167.1 2.4 collective-permute-done.13.refs_0_
  170.5 3.5 %shard_map.252 = (f32[2,320,384]{2,1,0:T(8,128)}, f32[2,8,384]{2,1,0:T(8,128)}, s16[336,384]{1,0:T(8,128)(2,1)}, s16[336,384]{1,0:T(8,128)(2,1)}) custom-call(f32[2,640,384]{2,1,0:T(8,128)} %get-tuple-element.87.keep_ref, f32[2,8,384]{2,1,0:T(8,128)} %get-tuple-element.88.extra_ref, s16[2,656,384]{2,1,0:T(8,128)(2,1)} %copy-done.7), custom_call_target="tpu_custom_call" | custom-call | tf_op jit(solution)/shard_map/pallas_call | solution.py:566
  174.8 6.8 %collective-permute-done.14.refs_0_ = s16[336,384]{1,0:T(8,128)(2,1)S(1)} collective-permute-done((s16[336,384]{1,0:T(8,128)(2,1)}, s16[336,384]{1,0:T(8,128)(2,1)S(1)}, u32[]{:S(2)}, u32[]{:S(2)}) %collective-permute-start.14) | collective-permute-done | bytes 258080 | tf_op jit(solution)/shard_map/ppermute | solution.py:456
  182.8 2.4 shard_map.253
  186.0 3.4 %collective-permute-done.16.refs_0_ = s16[176,384]{1,0:T(8,128)(2,1)S(1)} collective-permute-done((s16[176,384]{1,0:T(8,128)(2,1)}, s16[176,384]{1,0:T(8,128)(2,1)S(1)}, u32[]{:S(2)}, u32[]{:S(2)}) %collective-permute-start.16) | collective-permute-done | bytes 135200 | tf_op jit(solution)/shard_map/ppermute | solution.py:456
  190.0 2.1 shard_map.254
  192.1 1.7 collective-permute-start.18
  196.1 2.2 collective-permute-done.19.refs_1_
  198.2 2.1 collective-permute-done.20.refs_2_
  201.0 1.8 shard_map.255
  202.8 1.6 shard_map.256
  204.3 1.3 collective-permute-start.21
  205.6 1.6 collective-permute-start.22
  208.5 1.5 collective-permute-done.22
  209.9 2.7 %collective-permute-done.23 = s16[2,48,384]{2,1,0:T(8,128)(2,1)S(1)} collective-permute-done((s16[2,48,384]{2,1,0:T(8,128)(2,1)}, s16[2,48,384]{2,1,0:T(8,128)(2,1)S(1)}, u32[]{:S(2)}, u32[]{:S(2)}) %collective-permute-start.23) | collective-permute-done | bytes 73760 | tf_op jit(solution)/shard_map/ppermute | solution.py:456
  213.6 2.8 %collective-permute-start.24 = (s16[192,384]{1,0:T(8,128)(2,1)S(1)}, s16[192,384]{1,0:T(8,128)(2,1)S(1)}, u32[]{:S(2)}, u32[]{:S(2)}) collective-permute-start(s16[192,384]{1,0:T(8,128)(2,1)S(1)} %get-tuple-element.129), channel_id=1, source_target_pairs={{0,2},{1,3},{2,0},{3,1},{4,6},{5,7},{6,4},{7,5},{8,10},{9,11},{10,... | collective-permute-start | bytes 442376 | tf_op jit(solution)/shard_map/ppermute | solution.py:456
  216.7 2.3 collective-permute-done.24
  220.9 5.1 %collective-permute-done.25 = s16[384,384]{1,0:T(8,128)(2,1)S(1)} collective-permute-done((s16[384,384]{1,0:T(8,128)(2,1)S(1)}, s16[384,384]{1,0:T(8,128)(2,1)S(1)}, u32[]{:S(2)}, u32[]{:S(2)}) %collective-permute-start.25) | collective-permute-done | bytes 294944 | tf_op jit(solution)/shard_map/ppermute | solution.py:456
  226.7 7.3 %collective-permute-start.28 = (s16[2,768,384]{2,1,0:T(8,128)(2,1)S(1)}, s16[2,768,384]{2,1,0:T(8,128)(2,1)S(1)}, u32[]{:S(2)}, u32[]{:S(2)}) collective-permute-start(s16[2,768,384]{2,1,0:T(8,128)(2,1)S(1)} %pad_add_fusion.near_ref), channel_id=1, source_target_pairs={{0,4},{4,0},{8,12},{12,8},{16,20},{20,16},{24,28},{28,24},{1,5},{5... | collective-permute-start | bytes 3538952 | tf_op jit(solution)/shard_map/ppermute | solution.py:456
  235.0 1.5 collective-permute-done.28.far_ref
  237.5 5.2 %shard_map.257 = (bf16[5,256,768]{2,1,0:T(8,128)(2,1)}, bf16[5,256,768]{2,1,0:T(8,128)(2,1)}, f32[96,256]{1,0:T(8,128)}) custom-call(s32[2]{0:T(128)} %pad_add_fusion.4.me_ref, s16[2,768,384]{2,1,0:T(8,128)(2,1)} %copy-done.2, s16[2,768,384]{2,1,0:T(8,128)(2,1)} %copy-done.4, bf16[5,96,768]{2,1,0:T(8,128)(2,1)} %convert_element_type.25.conv_ref), custom_call_target="tpu_custom_call" | custom-call | tf_op jit(solution)/shard_map/pallas_call | solution.py:648
  242.7 1.6 collective-permute-start.30
  244.3 1.9 collective-permute-start.31
  246.2 13.1 %shard_map.258 = (f32[5,96,768]{2,1,0:T(8,128)}, f32[5,96,768]{2,1,0:T(8,128)}, f32[5,96,768]{2,1,0:T(8,128)}, f32[5,96,768]{2,1,0:T(8,128)}) custom-call(s32[2]{0:T(128)} %pad_add_fusion.5.where_ref.owner_ref, bf16[5,256,768]{2,1,0:T(8,128)(2,1)} %get-tuple-element.106.high_ref, bf16[5,256,768]{2,1,0:T(8,128)(2,1)} %get-tuple-element.107.low_ref, ...), custom_call_target="tpu_custom_call" | custom-call | flops 8589934592 | bytes 33554432 | tf_op jit(solution)/shard_map/pallas_call | solution.py:733
  259.4 1.3 collective-permute-start.32
  261.4 1.3 fusion.7
  265.5 4.9 %shard_map.259 = (f32[32,768]{1,0:T(8,128)}, f32[32,768]{1,0:T(8,128)}, f32[32,256]{1,0:T(8,128)}, f32[96,768]{1,0:T(8,128)}) custom-call(s32[2]{0:T(128)} %pad_add_fusion.5.where_ref.owner_ref, f32[4,96,256]{2,1,0:T(8,128)} %copy-done.3, f32[4,96,256]{2,1,0:T(8,128)} %copy-done.12, f32[32,768]{1,0:T(8,128)} %weight_ref.3, f32[32,256]{1,0:T(8,128)} %left_ref.3, ...), custom_call_target="tpu_custom_call" | custom-call | tf_op jit(solution)/shard_map/pallas_call | solution.py:780
  (137 shorter events, 32.3 us)
Async XLA Ops:
  3.4 25.2 %copy-start.21 = (s32[16,512]{1,0:T(8,128)S(1)}, s32[16,512]{1,0:T(8,128)}, u32[]{:S(2)}) copy-start(s32[16,512]{1,0:T(8,128)} %param.15) | copy-start | bytes 98308
  3.4 25.2 %copy-start.25 = (s32[16]{0:T(128)S(1)}, s32[16]{0:T(128)}, u32[]{:S(2)}) copy-start(s32[16]{0:T(128)} %param.16) | copy-start | bytes 196
  3.4 12.6 %collective-permute-start = (bf16[960,128]{1,0:T(8,128)(2,1)}, bf16[960,128]{1,0:T(8,128)(2,1)S(1)}, u32[]{:S(2)}, u32[]{:S(2)}) collective-permute-start(bf16[960,128]{1,0:T(8,128)(2,1)} %shard_map.246.refs_0_), channel_id=1, source_target_pairs={{0,8},{4,12},{8,0},{12,4},{16,24},{20,28},{24,16},{28,20},{1,9},{5... | collective-permute-start | bytes 737288 | tf_op jit(solution)/shard_map/ppermute | solution.py:456
  5.5 14.5 %collective-permute-start.1 = (bf16[960,128]{1,0:T(8,128)(2,1)}, bf16[960,128]{1,0:T(8,128)(2,1)S(1)}, u32[]{:S(2)}, u32[]{:S(2)}) collective-permute-start(bf16[960,128]{1,0:T(8,128)(2,1)} %shard_map.246.refs_0_), channel_id=1, source_target_pairs={{0,16},{4,20},{8,24},{12,28},{16,0},{20,4},{24,8},{28,12},{1,17},{... | collective-permute-start | bytes 737288 | tf_op jit(solution)/shard_map/ppermute | solution.py:456
  7.9 16.0 %collective-permute-start.2 = (bf16[960,128]{1,0:T(8,128)(2,1)}, bf16[960,128]{1,0:T(8,128)(2,1)S(1)}, u32[]{:S(2)}, u32[]{:S(2)}) collective-permute-start(bf16[960,128]{1,0:T(8,128)(2,1)} %shard_map.246.refs_0_), channel_id=1, source_target_pairs={{0,24},{4,28},{8,16},{12,20},{16,8},{20,12},{24,0},{28,4},{1,25},{... | collective-permute-start | bytes 737288 | tf_op jit(solution)/shard_map/ppermute | solution.py:456
  8.6 20.0 %collective-permute-start.4 = (s32[16,8]{1,0:T(8,128)S(1)}, s32[16,8]{1,0:T(8,128)S(1)}, u32[]{:S(2)}, u32[]{:S(2)}) collective-permute-start(s32[16,8]{1,0:T(8,128)S(1)} %get-tuple-element.136), channel_id=1, source_target_pairs={{0,1},{1,2},{2,3},{4,5},{5,6},{6,7},{8,9},{9,10},{10,11},{12,13},{... | collective-permute-start | bytes 1544 | tf_op jit(solution)/shard_map/ppermute | solution.py:400
  11.8 16.9 %collective-permute-start.5 = (s32[16,8]{1,0:T(8,128)S(1)}, s32[16,8]{1,0:T(8,128)S(1)}, u32[]{:S(2)}, u32[]{:S(2)}) collective-permute-start(s32[16,8]{1,0:T(8,128)S(1)} %get-tuple-element.137), channel_id=1, source_target_pairs={{1,0},{2,1},{3,2},{5,4},{6,5},{7,6},{9,8},{10,9},{11,10},{13,12},{... | collective-permute-start | bytes 1544 | tf_op jit(solution)/shard_map/ppermute | solution.py:401
  16.0 13.2 %copy-start.8 = (bf16[960,128]{1,0:T(8,128)(2,1)}, bf16[960,128]{1,0:T(8,128)(2,1)S(1)}, u32[]{:S(2)}) copy-start(bf16[960,128]{1,0:T(8,128)(2,1)S(1)} %collective-permute-done.refs_1_) | copy-start | bytes 737284
  16.0 14.4 %collective-permute-start.6 = (f32[16,1,768]{2,1,0:T(1,128)S(1)}, f32[16,1,768]{2,1,0:T(1,128)S(1)}, u32[]{:S(2)}, u32[]{:S(2)}) collective-permute-start(f32[16,1,768]{2,1,0:T(1,128)S(1)} %get-tuple-element.128), channel_id=1, source_target_pairs={{0,1},{1,2},{2,3},{4,5},{5,6},{6,7},{8,9},{9,10},{10,11},{12,13},{... | collective-permute-start | bytes 147464 | tf_op jit(solution)/shard_map/ppermute | solution.py:400
  20.1 10.4 %copy-start.9 = (bf16[960,128]{1,0:T(8,128)(2,1)}, bf16[960,128]{1,0:T(8,128)(2,1)S(1)}, u32[]{:S(2)}) copy-start(bf16[960,128]{1,0:T(8,128)(2,1)S(1)} %collective-permute-done.1.refs_2_) | copy-start | bytes 737284
  20.1 10.4 %collective-permute-start.7 = (f32[16,1,768]{2,1,0:T(1,128)S(1)}, f32[16,1,768]{2,1,0:T(1,128)S(1)}, u32[]{:S(2)}, u32[]{:S(2)}) collective-permute-start(f32[16,1,768]{2,1,0:T(1,128)S(1)} %get-tuple-element.127), channel_id=1, source_target_pairs={{1,0},{2,1},{3,2},{5,4},{6,5},{7,6},{9,8},{10,9},{11,10},{13,12},{... | collective-permute-start | bytes 147464 | tf_op jit(solution)/shard_map/ppermute | solution.py:401
  23.9 6.6 %copy-start.10 = (bf16[960,128]{1,0:T(8,128)(2,1)}, bf16[960,128]{1,0:T(8,128)(2,1)S(1)}, u32[]{:S(2)}) copy-start(bf16[960,128]{1,0:T(8,128)(2,1)S(1)} %collective-permute-done.2.refs_3_) | copy-start | bytes 737284
  24.0 7.6 %collective-permute-start.3 = (bf16[4,576,128]{2,1,0:T(8,128)(2,1)S(1)}, bf16[4,576,128]{2,1,0:T(8,128)(2,1)S(1)}, u32[]{:S(2)}, u32[]{:S(2)}) collective-permute-start(bf16[4,576,128]{2,1,0:T(8,128)(2,1)S(1)} %pad_maximum_fusion.2), channel_id=1, source_target_pairs={{0,4},{4,0},{8,12},{12,8},{16,20},{20,16},{24,28},{28,24},{1,5},{5... | collective-permute-start | bytes 1769480 | tf_op jit(solution)/shard_map/ppermute | solution.py:456
  35.4 6.9 %collective-permute-start.8 = (bf16[4,256,128]{2,1,0:T(8,128)(2,1)}, bf16[4,256,128]{2,1,0:T(8,128)(2,1)S(1)}, u32[]{:S(2)}, u32[]{:S(2)}) collective-permute-start(bf16[4,256,128]{2,1,0:T(8,128)(2,1)} %get-tuple-element.71), channel_id=1, source_target_pairs={{0,1},{1,0},{2,3},{3,2},{4,5},{5,4},{6,7},{7,6},{8,9},{9,8},{10,11... | collective-permute-start | bytes 786440 | tf_op jit(solution)/shard_map/ppermute | solution.py:456
  37.7 9.6 %collective-permute-start.10 = (bf16[4,256,128]{2,1,0:T(8,128)(2,1)}, bf16[4,256,128]{2,1,0:T(8,128)(2,1)S(1)}, u32[]{:S(2)}, u32[]{:S(2)}) collective-permute-start(bf16[4,256,128]{2,1,0:T(8,128)(2,1)} %get-tuple-element.72), channel_id=1, source_target_pairs={{0,2},{1,3},{2,0},{3,1},{4,6},{5,7},{6,4},{7,5},{8,10},{9,11},{10,... | collective-permute-start | bytes 786440 | tf_op jit(solution)/shard_map/ppermute | solution.py:456
  43.3 15.0 %collective-permute-start.9 = (bf16[8,256,128]{2,1,0:T(8,128)(2,1)S(1)}, bf16[8,256,128]{2,1,0:T(8,128)(2,1)S(1)}, u32[]{:S(2)}, u32[]{:S(2)}) collective-permute-start(bf16[8,256,128]{2,1,0:T(8,128)(2,1)S(1)} %pad_maximum_fusion.3), channel_id=1, source_target_pairs={{0,2},{1,3},{2,0},{3,1},{4,6},{5,7},{6,4},{7,5},{8,10},{9,11},{10,... | collective-permute-start | bytes 1572872 | tf_op jit(solution)/shard_map/ppermute | solution.py:456
  48.4 11.9 %collective-permute-start.11 = (bf16[8,256,128]{2,1,0:T(8,128)(2,1)S(1)}, bf16[8,256,128]{2,1,0:T(8,128)(2,1)S(1)}, u32[]{:S(2)}, u32[]{:S(2)}) collective-permute-start(bf16[8,256,128]{2,1,0:T(8,128)(2,1)S(1)} %pad_maximum_fusion.4), channel_id=1, source_target_pairs={{0,1},{1,0},{2,3},{3,2},{4,5},{5,4},{6,7},{7,6},{8,9},{9,8},{10,11... | collective-permute-start | bytes 1572872 | tf_op jit(solution)/shard_map/ppermute | solution.py:456
  49.2 9.1 %copy-start.6 = (bf16[4,256,128]{2,1,0:T(8,128)(2,1)S(1)}, bf16[4,256,128]{2,1,0:T(8,128)(2,1)}, u32[]{:S(2)}) copy-start(bf16[4,256,128]{2,1,0:T(8,128)(2,1)} %get-tuple-element.71) | copy-start | bytes 786436
  54.7 5.6 %copy-start.5 = (bf16[4,256,128]{2,1,0:T(8,128)(2,1)S(1)}, bf16[4,256,128]{2,1,0:T(8,128)(2,1)}, u32[]{:S(2)}) copy-start(bf16[4,256,128]{2,1,0:T(8,128)(2,1)} %get-tuple-element.72) | copy-start | bytes 786436
  60.6 6.5 %copy-start = (bf16[2,16,256,128]{3,2,1,0:T(8,128)(2,1)}, bf16[2,16,256,128]{3,2,1,0:T(8,128)(2,1)S(1)}, u32[]{:S(2)}) copy-start(bf16[2,16,256,128]{3,2,1,0:T(8,128)(2,1)S(1)} %pad_maximum_fusion.near_ref) | copy-start | bytes 6291460
  60.6 6.5 %collective-permute-start.12 = (bf16[2,16,256,128]{3,2,1,0:T(8,128)(2,1)S(1)}, bf16[2,16,256,128]{3,2,1,0:T(8,128)(2,1)}, u32[]{:S(2)}, u32[]{:S(2)}) collective-permute-start(bf16[2,16,256,128]{3,2,1,0:T(8,128)(2,1)S(1)} %pad_maximum_fusion.near_ref), channel_id=1, source_target_pairs={{0,4},{4,0},{8,12},{12,8},{16,20},{20,16},{24,28},{28,24},{1,5},{5... | collective-permute-start | bytes 6291464 | tf_op jit(solution)/shard_map/ppermute | solution.py:456
  166.6 2.9 %collective-permute-start.13 = (s16[2,656,384]{2,1,0:T(8,128)(2,1)}, s16[2,656,384]{2,1,0:T(8,128)(2,1)S(1)}, u32[]{:S(2)}, u32[]{:S(2)}) collective-permute-start(s16[2,656,384]{2,1,0:T(8,128)(2,1)} %get-tuple-element.89), channel_id=1, source_target_pairs={{0,4},{4,0},{8,12},{12,8},{16,20},{20,16},{24,28},{28,24},{1,5},{5... | collective-permute-start | bytes 3022856 | tf_op jit(solution)/shard_map/ppermute | solution.py:456
  174.0 7.6 %collective-permute-start.14 = (s16[336,384]{1,0:T(8,128)(2,1)}, s16[336,384]{1,0:T(8,128)(2,1)S(1)}, u32[]{:S(2)}, u32[]{:S(2)}) collective-permute-start(s16[336,384]{1,0:T(8,128)(2,1)} %get-tuple-element.92), channel_id=1, source_target_pairs={{0,1},{1,0},{2,3},{3,2},{4,5},{5,4},{6,7},{7,6},{8,9},{9,8},{10,11... | collective-permute-start | bytes 774152 | tf_op jit(solution)/shard_map/ppermute | solution.py:456
  174.8 7.3 %collective-permute-start.15 = (s16[336,384]{1,0:T(8,128)(2,1)}, s16[336,384]{1,0:T(8,128)(2,1)S(1)}, u32[]{:S(2)}, u32[]{:S(2)}) collective-permute-start(s16[336,384]{1,0:T(8,128)(2,1)} %get-tuple-element.93), channel_id=1, source_target_pairs={{0,2},{1,3},{2,0},{3,1},{4,6},{5,7},{6,4},{7,5},{8,10},{9,11},{10,... | collective-permute-start | bytes 774152 | tf_op jit(solution)/shard_map/ppermute | solution.py:456
  185.2 4.1 %collective-permute-start.16 = (s16[176,384]{1,0:T(8,128)(2,1)}, s16[176,384]{1,0:T(8,128)(2,1)S(1)}, u32[]{:S(2)}, u32[]{:S(2)}) collective-permute-start(s16[176,384]{1,0:T(8,128)(2,1)} %get-tuple-element.96), channel_id=1, source_target_pairs={{0,2},{1,3},{2,0},{3,1},{4,6},{5,7},{6,4},{7,5},{8,10},{9,11},{10,... | collective-permute-start | bytes 405512 | tf_op jit(solution)/shard_map/ppermute | solution.py:456
  185.3 4.1 %collective-permute-start.17 = (s16[176,384]{1,0:T(8,128)(2,1)}, s16[176,384]{1,0:T(8,128)(2,1)S(1)}, u32[]{:S(2)}, u32[]{:S(2)}) collective-permute-start(s16[176,384]{1,0:T(8,128)(2,1)} %get-tuple-element.97), channel_id=1, source_target_pairs={{0,1},{1,0},{2,3},{3,2},{4,5},{5,4},{6,7},{7,6},{8,9},{9,8},{10,11... | collective-permute-start | bytes 405512 | tf_op jit(solution)/shard_map/ppermute | solution.py:456
  192.1 4.0 %collective-permute-start.18 = (s16[2,56,384]{2,1,0:T(8,128)(2,1)}, s16[2,56,384]{2,1,0:T(8,128)(2,1)S(1)}, u32[]{:S(2)}, u32[]{:S(2)}) collective-permute-start(s16[2,56,384]{2,1,0:T(8,128)(2,1)} %get-tuple-element.100), channel_id=1, source_target_pairs={{0,8},{4,12},{8,0},{12,4},{16,24},{20,28},{24,16},{28,20},{1,9},{5... | collective-permute-start | bytes 258056 | tf_op jit(solution)/shard_map/ppermute | solution.py:456
  193.8 4.5 %collective-permute-start.19 = (s16[2,56,384]{2,1,0:T(8,128)(2,1)}, s16[2,56,384]{2,1,0:T(8,128)(2,1)S(1)}, u32[]{:S(2)}, u32[]{:S(2)}) collective-permute-start(s16[2,56,384]{2,1,0:T(8,128)(2,1)} %get-tuple-element.101), channel_id=1, source_target_pairs={{0,16},{4,20},{8,24},{12,28},{16,0},{20,4},{24,8},{28,12},{1,17},{... | collective-permute-start | bytes 258056 | tf_op jit(solution)/shard_map/ppermute | solution.py:456
  194.9 5.4 %collective-permute-start.20 = (s16[2,56,384]{2,1,0:T(8,128)(2,1)}, s16[2,56,384]{2,1,0:T(8,128)(2,1)S(1)}, u32[]{:S(2)}, u32[]{:S(2)}) collective-permute-start(s16[2,56,384]{2,1,0:T(8,128)(2,1)} %get-tuple-element.102), channel_id=1, source_target_pairs={{0,24},{4,28},{8,16},{12,20},{16,8},{20,12},{24,0},{28,4},{1,25},{... | collective-permute-start | bytes 258056 | tf_op jit(solution)/shard_map/ppermute | solution.py:456
  196.1 4.3 %copy-start.18 = (s16[2,56,384]{2,1,0:T(8,128)(2,1)}, s16[2,56,384]{2,1,0:T(8,128)(2,1)S(1)}, u32[]{:S(2)}) copy-start(s16[2,56,384]{2,1,0:T(8,128)(2,1)S(1)} %collective-permute-done.18.refs_0_) | copy-start | bytes 258052
  204.3 4.1 %collective-permute-start.21 = (s16[2,48,384]{2,1,0:T(8,128)(2,1)}, s16[2,48,384]{2,1,0:T(8,128)(2,1)S(1)}, u32[]{:S(2)}, u32[]{:S(2)}) collective-permute-start(s16[2,48,384]{2,1,0:T(8,128)(2,1)} %shard_map.256), channel_id=1, source_target_pairs={{0,8},{4,12},{8,0},{12,4},{16,24},{20,28},{24,16},{28,20},{1,9},{5... | collective-permute-start | bytes 221192 | tf_op jit(solution)/shard_map/ppermute | solution.py:456
  205.6 4.3 %collective-permute-start.22 = (s16[2,48,384]{2,1,0:T(8,128)(2,1)}, s16[2,48,384]{2,1,0:T(8,128)(2,1)S(1)}, u32[]{:S(2)}, u32[]{:S(2)}) collective-permute-start(s16[2,48,384]{2,1,0:T(8,128)(2,1)} %shard_map.256), channel_id=1, source_target_pairs={{0,16},{4,20},{8,24},{12,28},{16,0},{20,4},{24,8},{28,12},{1,17},{... | collective-permute-start | bytes 221192 | tf_op jit(solution)/shard_map/ppermute | solution.py:456
  207.3 5.4 %collective-permute-start.23 = (s16[2,48,384]{2,1,0:T(8,128)(2,1)}, s16[2,48,384]{2,1,0:T(8,128)(2,1)S(1)}, u32[]{:S(2)}, u32[]{:S(2)}) collective-permute-start(s16[2,48,384]{2,1,0:T(8,128)(2,1)} %shard_map.256), channel_id=1, source_target_pairs={{0,24},{4,28},{8,16},{12,20},{16,8},{20,12},{24,0},{28,4},{1,25},{... | collective-permute-start | bytes 221192 | tf_op jit(solution)/shard_map/ppermute | solution.py:456
  213.6 5.4 %collective-permute-start.24 = (s16[192,384]{1,0:T(8,128)(2,1)S(1)}, s16[192,384]{1,0:T(8,128)(2,1)S(1)}, u32[]{:S(2)}, u32[]{:S(2)}) collective-permute-start(s16[192,384]{1,0:T(8,128)(2,1)S(1)} %get-tuple-element.129), channel_id=1, source_target_pairs={{0,2},{1,3},{2,0},{3,1},{4,6},{5,7},{6,4},{7,5},{8,10},{9,11},{10,... | collective-permute-start | bytes 442376 | tf_op jit(solution)/shard_map/ppermute | solution.py:456
  216.5 4.0 %collective-permute-start.26 = (s16[192,384]{1,0:T(8,128)(2,1)S(1)}, s16[192,384]{1,0:T(8,128)(2,1)S(1)}, u32[]{:S(2)}, u32[]{:S(2)}) collective-permute-start(s16[192,384]{1,0:T(8,128)(2,1)S(1)} %get-tuple-element.130), channel_id=1, source_target_pairs={{0,1},{1,0},{2,3},{3,2},{4,5},{5,4},{6,7},{7,6},{8,9},{9,8},{10,11... | collective-permute-start | bytes 442376 | tf_op jit(solution)/shard_map/ppermute | solution.py:456
  219.0 6.9 %collective-permute-start.25 = (s16[384,384]{1,0:T(8,128)(2,1)S(1)}, s16[384,384]{1,0:T(8,128)(2,1)S(1)}, u32[]{:S(2)}, u32[]{:S(2)}) collective-permute-start(s16[384,384]{1,0:T(8,128)(2,1)S(1)} %pad_add_fusion.2), channel_id=1, source_target_pairs={{0,1},{1,0},{2,3},{3,2},{4,5},{5,4},{6,7},{7,6},{8,9},{9,8},{10,11... | collective-permute-start | bytes 884744 | tf_op jit(solution)/shard_map/ppermute | solution.py:456
  220.5 6.1 %collective-permute-start.27 = (s16[384,384]{1,0:T(8,128)(2,1)S(1)}, s16[384,384]{1,0:T(8,128)(2,1)S(1)}, u32[]{:S(2)}, u32[]{:S(2)}) collective-permute-start(s16[384,384]{1,0:T(8,128)(2,1)S(1)} %pad_add_fusion.3), channel_id=1, source_target_pairs={{0,2},{1,3},{2,0},{3,1},{4,6},{5,7},{6,4},{7,5},{8,10},{9,11},{10,... | collective-permute-start | bytes 884744 | tf_op jit(solution)/shard_map/ppermute | solution.py:456
  226.0 8.0 %copy-start.1 = (f32[5,96,768]{2,1,0:T(8,128)S(1)}, f32[5,96,768]{2,1,0:T(8,128)}, u32[]{:S(2)}) copy-start(f32[5,96,768]{2,1,0:T(8,128)} %weight_ref.2) | copy-start | bytes 4423684
  226.7 9.8 %copy-start.2 = (s16[2,768,384]{2,1,0:T(8,128)(2,1)}, s16[2,768,384]{2,1,0:T(8,128)(2,1)S(1)}, u32[]{:S(2)}) copy-start(s16[2,768,384]{2,1,0:T(8,128)(2,1)S(1)} %pad_add_fusion.near_ref) | copy-start | bytes 3538948
  226.7 9.8 %collective-permute-start.28 = (s16[2,768,384]{2,1,0:T(8,128)(2,1)S(1)}, s16[2,768,384]{2,1,0:T(8,128)(2,1)S(1)}, u32[]{:S(2)}, u32[]{:S(2)}) collective-permute-start(s16[2,768,384]{2,1,0:T(8,128)(2,1)S(1)} %pad_add_fusion.near_ref), channel_id=1, source_target_pairs={{0,4},{4,0},{8,12},{12,8},{16,20},{20,16},{24,28},{28,24},{1,5},{5... | collective-permute-start | bytes 3538952 | tf_op jit(solution)/shard_map/ppermute | solution.py:456
  242.7 16.6 %collective-permute-start.29 = (f32[96,256]{1,0:T(8,128)}, f32[96,256]{1,0:T(8,128)S(1)}, u32[]{:S(2)}, u32[]{:S(2)}) collective-permute-start(f32[96,256]{1,0:T(8,128)} %get-tuple-element.105), channel_id=1, source_target_pairs={{0,8},{4,12},{8,0},{12,4},{16,24},{20,28},{24,16},{28,20},{1,9},{5... | collective-permute-start | bytes 294920 | tf_op jit(solution)/shard_map/ppermute | solution.py:456
  242.7 16.6 %collective-permute-start.30 = (f32[96,256]{1,0:T(8,128)}, f32[96,256]{1,0:T(8,128)S(1)}, u32[]{:S(2)}, u32[]{:S(2)}) collective-permute-start(f32[96,256]{1,0:T(8,128)} %get-tuple-element.105), channel_id=1, source_target_pairs={{0,16},{4,20},{8,24},{12,28},{16,0},{20,4},{24,8},{28,12},{1,17},{... | collective-permute-start | bytes 294920 | tf_op jit(solution)/shard_map/ppermute | solution.py:456
  244.3 15.0 %collective-permute-start.31 = (f32[96,256]{1,0:T(8,128)}, f32[96,256]{1,0:T(8,128)S(1)}, u32[]{:S(2)}, u32[]{:S(2)}) collective-permute-start(f32[96,256]{1,0:T(8,128)} %get-tuple-element.105), channel_id=1, source_target_pairs={{0,24},{4,28},{8,16},{12,20},{16,8},{20,12},{24,0},{28,4},{1,25},{... | collective-permute-start | bytes 294920 | tf_op jit(solution)/shard_map/ppermute | solution.py:456
  246.2 13.1 %copy-start.17 = (f32[96,256]{1,0:T(8,128)S(1)}, f32[96,256]{1,0:T(8,128)}, u32[]{:S(2)}) copy-start(f32[96,256]{1,0:T(8,128)} %get-tuple-element.105) | copy-start | bytes 294916
  246.2 17.9 %copy-start.24 = (f32[768]{0:T(1024)S(1)}, f32[768]{0:T(1024)}, u32[]{:S(2)}) copy-start(f32[768]{0:T(1024)} %param.29) | copy-start | bytes 9220
  259.4 5.4 %copy-start.3 = (f32[4,96,256]{2,1,0:T(8,128)}, f32[4,96,256]{2,1,0:T(8,128)S(1)}, u32[]{:S(2)}) copy-start(f32[4,96,256]{2,1,0:T(8,128)S(1)} %pad_maximum_fusion.5.near_ref) | copy-start | bytes 1179652
  259.4 5.3 %collective-permute-start.32 = (f32[4,96,256]{2,1,0:T(8,128)S(1)}, f32[4,96,256]{2,1,0:T(8,128)S(1)}, u32[]{:S(2)}, u32[]{:S(2)}) collective-permute-start(f32[4,96,256]{2,1,0:T(8,128)S(1)} %pad_maximum_fusion.5.near_ref), channel_id=1, source_target_pairs={{0,4},{4,0},{8,12},{12,8},{16,20},{20,16},{24,28},{28,24},{1,5},{5... | collective-permute-start | bytes 1179656 | tf_op jit(solution)/shard_map/ppermute | solution.py:456
  261.4 9.0 %copy-start.23 = (f32[768]{0:T(1024)}, f32[768]{0:T(1024)S(1)}, u32[]{:S(2)}) copy-start(f32[768]{0:T(1024)S(1)} %reshape_squeeze.3) | copy-start | bytes 9220
  (11 other events, 11.8 us)

commit v3 on v2

--- a/solution.py
+++ b/solution.py
@@ -18,6 +18,7 @@
 TILE = 128
 HALO = 8
 BLOCKS = 32
+GROUP = 2
 WIN = TILE // 2 + 16
 BF = jnp.bfloat16
 F32 = jnp.float32
@@ -77,19 +78,19 @@
     return jnp.where((row == 0) | (row == 2), high, jnp.where(row == 1, low, 0.0)).astype(BF)
 
 
-def grad_window(g_ref, gh_ref, i, tiles):
+def grad_window(g_ref, gh_ref, r, i, tiles):
     half = tiles * TILE // 2
     first, last = i * TILE // 2 - 8, (i + 1) * TILE // 2 + 8
-    parts = [g_ref[0, max(first, 0) : min(last, half)]]
+    parts = [g_ref[r, max(first, 0) : min(last, half)]]
     if i == 0:
-        parts = [gh_ref[0, 0:8]] + parts
+        parts = [gh_ref[r, 0:8]] + parts
     if i == tiles - 1:
-        parts = parts + [gh_ref[0, 8:16]]
+        parts = parts + [gh_ref[r, 8:16]]
     return split(jnp.concatenate(parts, axis=0))
 
 
 def lookup_body(
-    where_ref, mid_ref, next_ref, g_ref, gh_ref, score_ref, near_ref, far_ref, hid_ref, rim_ref, band_ref, table_ref, onehot_ref,
+    where_ref, mid_ref, next_ref, g_ref, gh_ref, score_ref, near_ref, far_ref, hid_ref, rim_ref, band_ref, table_ref, onehot_ref, spread, hidden,
     *, masks, taps,
 ):
     length = hid_ref.shape[1] * TILE
@@ -127,24 +128,33 @@
 
     onehot = onehot_ref[...]
     onehot = jnp.concatenate([onehot, onehot], axis=1)
+    for m in range(spread.shape[0]):
+        at = slice(m * TILE, (m + 1) * TILE)
+        spread[m, 0:8] = jnp.broadcast_to(gh_ref[0, 7:8, at], (8, TILE))
+        spread[m, 8 + length :] = jnp.broadcast_to(gh_ref[0, 8:9, at], (8, TILE))
+        rows = g_ref[0, :, at]
+        spread[m, pl.ds(8, length // 2, stride=2)] = rows
+        spread[m, pl.ds(9, length // 2, stride=2)] = rows
     for n in range(0, table_ref.shape[1], 256):
-        hidden = jnp.dot(onehot, table_ref[:, n : n + 256], preferred_element_type=F32)
-        h_high, h_low = split(hidden[0:length])
+        cells = jnp.dot(onehot, table_ref[:, n : n + 256], preferred_element_type=F32)
+        hidden[:, n : n + 256] = cells
+        h_high, h_low = split(cells[0:length])
         for i in range(tiles):
             hid_ref[0, i, 0:TILE, n : n + 256] = h_high[i * TILE : (i + 1) * TILE]
             hid_ref[0, i, TILE : 2 * TILE, n : n + 256] = h_low[i * TILE : (i + 1) * TILE]
-        rim_ref[0, :, n : n + 256] = hidden[length:]
-    score = score_rows(score_ref)
-    for i in range(tiles):
-        left = jnp.concatenate([*grad_window(g_ref, gh_ref, i, tiles), score], axis=0)
-        gram = lax.dot_general(left, hid_ref[0, i], nt, preferred_element_type=F32)
-        band = gram[0:WIN, 0:TILE] + gram[WIN : 2 * WIN, 0:TILE] + gram[0:WIN, TILE:]
-        dots = gram[2 * WIN : 2 * WIN + 1, 0:TILE] + gram[2 * WIN + 1 : 2 * WIN + 2, 0:TILE] + gram[2 * WIN : 2 * WIN + 1, TILE:]
-        place = lax.broadcasted_iota(jnp.int32, (WIN, TILE), 0) - 8
-        gap = place - (lax.broadcasted_iota(jnp.int32, (WIN, TILE), 1) >> 1)
-        rows = [jnp.sum(jnp.where(gap == d, band, 0.0), axis=0, keepdims=True) for d in (-1, 0, 1)]
-        band_ref[0, :, TILE * (i + 1) : TILE * (i + 2)] = jnp.concatenate(rows + [dots, jnp.zeros((4, TILE), F32)], axis=0)
+        rim_ref[0, :, n : n + 256] = cells[length:]
     mark(next_ref)
+    columns = []
+    for t in range(0, length, 64):
+        sums = [jnp.zeros((64, TILE), F32)] * 4
+        for m in range(spread.shape[0]):
+            part = hidden[t : t + 64, m * TILE : (m + 1) * TILE]
+            for d in range(3):
+                sums[d] = sums[d] + part * spread[m, 6 + 2 * d + t : 6 + 2 * d + t + 64]
+            sums[3] = sums[3] + part * score_ref[:, m * TILE : (m + 1) * TILE]
+        row = [jnp.sum(item, axis=1, keepdims=True) for item in sums]
+        columns.append(jnp.concatenate(row + [jnp.zeros((64, 4), F32)], axis=1))
+    band_ref[0, :, TILE : TILE + length] = jnp.transpose(jnp.concatenate(columns, axis=0))
     blank = jnp.zeros((8, TILE), F32)
     band_ref[0, :, 0:TILE] = blank
     band_ref[0, :, TILE + length :] = blank
@@ -179,6 +189,8 @@
         scratch_shapes=[
             pltpu.VMEM((2 * taps * VOCAB, width), BF),
             pltpu.VMEM((length + 2 * HALO, taps * VOCAB), BF),
+            pltpu.VMEM((width // TILE, length + 16, TILE), F32),
+            pltpu.VMEM((length + 2 * HALO, width), F32),
         ],
         compiler_params=pltpu.CompilerParams(vmem_limit_bytes=56 << 20),
     )(where, mid, mid, out_grad, grad_rim, score.reshape(1, width), near, far)
@@ -294,37 +306,38 @@
         table_ref[...] = jnp.zeros_like(table_ref)
         pull_ref[...] = jnp.zeros_like(pull_ref)
 
-    cells = lax.broadcasted_iota(jnp.int32, (VOCAB, length), 0)
-    for tap in range(taps):
-        hit = mid_ref[0, tap : tap + 1, TILE : TILE + length] == cells
-        onehot[tap * VOCAB : (tap + 1) * VOCAB] = hit.astype(F32).astype(BF)
-    total[...] = jnp.zeros_like(total)
-    pulled = jnp.zeros((1, total.shape[1]), F32)
     score = score_rows(score_ref)
-    for i in range(length // TILE):
-        w = weight_ref[0, :, TILE * (i + 1) : TILE * (i + 2)]
-        place = lax.broadcasted_iota(jnp.int32, (WIN, TILE), 0) - 8
-        gap = place - (lax.broadcasted_iota(jnp.int32, (WIN, TILE), 1) >> 1)
-        a = jnp.where(gap == 0, w[1:2], 0.0)
-        a = jnp.where(gap == -1, w[0:1], a)
-        a = jnp.where(gap == 1, w[2:3], a)
-        a_high, a_low = split(a)
-        q_high, q_low = split(w[3:4])
-        sub = lax.broadcasted_iota(jnp.int32, (16, TILE), 0)
-        q = jnp.where(sub < 2, q_high.astype(F32), jnp.where(sub == 2, q_low.astype(F32), 0.0)).astype(BF)
-        g_high, g_low = grad_window(g_ref, gh_ref, i, length // TILE)
-        stack = jnp.concatenate([g_high, g_low, g_high, score], axis=0)
-        left = jnp.concatenate([a_high, a_high, a_low, q], axis=0)
-        hg = lax.dot_general(left, stack, (((0,), (0,)), ((), ())), preferred_element_type=F32)
-        hgrad[i * TILE : (i + 1) * TILE] = hg.astype(BF)
-        left = jnp.concatenate([a_high, a_low, q], axis=0)
-        res = jnp.dot(jnp.concatenate([left, left], axis=1), hid_ref[0, i], preferred_element_type=F32)
-        total[i * TILE // 2 : i * TILE // 2 + WIN] += res[0:WIN] + res[WIN : 2 * WIN]
-        pulled = pulled + res[2 * WIN : 2 * WIN + 1] + res[2 * WIN + 2 : 2 * WIN + 3]
-    total[8:16] += jnp.where(lax.broadcasted_iota(jnp.int32, spill_ref.shape[1:], 0) == 0, spill_ref[0], 0.0)
-    total[half : half + 8] += jnp.where(lax.broadcasted_iota(jnp.int32, spill_ref.shape[1:], 0) == 7, spill_ref[0], 0.0)
-    out_ref[0] = total[8 : half + 8]
-    pull_ref[0:1] += pulled
+    for r in range(mid_ref.shape[0]):
+        cells = lax.broadcasted_iota(jnp.int32, (VOCAB, length), 0)
+        for tap in range(taps):
+            hit = mid_ref[r, tap : tap + 1, TILE : TILE + length] == cells
+            onehot[tap * VOCAB : (tap + 1) * VOCAB, r * length : (r + 1) * length] = hit.astype(F32).astype(BF)
+        total[...] = jnp.zeros_like(total)
+        pulled = jnp.zeros((1, total.shape[1]), F32)
+        for i in range(length // TILE):
+            w = weight_ref[r, :, TILE * (i + 1) : TILE * (i + 2)]
+            place = lax.broadcasted_iota(jnp.int32, (WIN, TILE), 0) - 8
+            gap = place - (lax.broadcasted_iota(jnp.int32, (WIN, TILE), 1) >> 1)
+            a = jnp.where(gap == 0, w[1:2], 0.0)
+            a = jnp.where(gap == -1, w[0:1], a)
+            a = jnp.where(gap == 1, w[2:3], a)
+            a_high, a_low = split(a)
+            q_high, q_low = split(w[3:4])
+            sub = lax.broadcasted_iota(jnp.int32, (16, TILE), 0)
+            q = jnp.where(sub < 2, q_high.astype(F32), jnp.where(sub == 2, q_low.astype(F32), 0.0)).astype(BF)
+            g_high, g_low = grad_window(g_ref, gh_ref, r, i, length // TILE)
+            stack = jnp.concatenate([g_high, g_low, g_high, score], axis=0)
+            left = jnp.concatenate([a_high, a_high, a_low, q], axis=0)
+            hg = lax.dot_general(left, stack, (((0,), (0,)), ((), ())), preferred_element_type=F32)
+            hgrad[r * length + i * TILE : r * length + (i + 1) * TILE] = hg.astype(BF)
+            left = jnp.concatenate([a_high, a_low, q], axis=0)
+            res = jnp.dot(jnp.concatenate([left, left], axis=1), hid_ref[r, i], preferred_element_type=F32)
+            total[i * TILE // 2 : i * TILE // 2 + WIN] += res[0:WIN] + res[WIN : 2 * WIN]
+            pulled = pulled + res[2 * WIN : 2 * WIN + 1] + res[2 * WIN + 2 : 2 * WIN + 3]
+        total[8:16] += jnp.where(lax.broadcasted_iota(jnp.int32, spill_ref.shape[1:], 0) == 0, spill_ref[r], 0.0)
+        total[half : half + 8] += jnp.where(lax.broadcasted_iota(jnp.int32, spill_ref.shape[1:], 0) == 7, spill_ref[r], 0.0)
+        out_ref[r] = total[8 : half + 8]
+        pull_ref[0:1] += pulled
     table_ref[...] += jnp.dot(onehot[...], hgrad[...], preferred_element_type=F32)
 
     @pl.when(pl.program_id(0) == pl.num_programs(0) - 1)
@@ -355,10 +368,10 @@
     half, width = out_grad.shape[1:]
     tiles = 2 * half // TILE
     whole = lambda *shape: pl.BlockSpec(shape, lambda r: (0,) * len(shape), pipeline_mode=pl.Buffered(1))
-    by_row = lambda *shape: pl.BlockSpec((1, *shape), lambda r: (r,) + (0,) * len(shape))
+    by_row = lambda *shape: pl.BlockSpec((GROUP, *shape), lambda r: (r,) + (0,) * len(shape))
     return pl.pallas_call(
         apply_body,
-        grid=(rows,),
+        grid=(rows // GROUP,),
         in_specs=[
             pl.BlockSpec(memory_space=pltpu.SMEM),
             by_row(8, span),
@@ -383,8 +396,8 @@
             jax.ShapeDtypeStruct((2, 8, width // 2), F32),
         ],
         scratch_shapes=[
-            pltpu.VMEM((taps * VOCAB, 2 * half), BF),
-            pltpu.VMEM((2 * half, width), BF),
+            pltpu.VMEM((taps * VOCAB, GROUP * 2 * half), BF),
+            pltpu.VMEM((GROUP * 2 * half, width), BF),
             pltpu.VMEM((half + 16, width), F32),
             pltpu.VMEM((taps * VOCAB, width), F32),
             pltpu.VMEM((8, width), F32),
@@ -622,7 +635,17 @@
     return (lax.broadcasted_iota(jnp.int32, (count, total), 1) == row + first).astype(F32).astype(BF)
 
 
-def order_body(me_ref, near_ref, far_ref, conv_ref, high_ref, low_ref, grad_ref, table):
+def order_body(
+    me_ref, near_ref, far_ref, conv_ref, extra_ref, score_ref, second_ref,
+    high_ref, low_ref, grad_ref, entropy_ref, score_grad_ref, score_out_ref, second_out_ref, table,
+):
+    sums = jnp.concatenate([extra_ref[0], extra_ref[1]], axis=1)
+    entropy_ref[...] = sums[1:2, 0:1] / sums[1:2, 1:2]
+    score_grad = sums[0:1]
+    second = BETA_SECOND * second_ref[...] + (1.0 - BETA_SECOND) * score_grad * score_grad
+    score_grad_ref[...] = score_grad
+    second_out_ref[...] = second
+    score_out_ref[...] = score_ref[...] - RATE_SCORE * score_grad / (jnp.sqrt(second) + EPSILON)
     block = table.shape[0] // BLOCKS
     part = table.shape[1] // 2
     for h in range(2):
@@ -637,22 +660,31 @@
     for k in range(taps):
         pair = split(table[k * VOCAB : (k + 1) * VOCAB])
         high_ref[k], low_ref[k] = pair
-        total = total + dot2(conv_ref[k], pair, NT)
+        total = total + dot2(conv_ref[k].astype(BF), pair, NT)
     grad_ref[...] = total
 
 
-def order_table(me, near, far, conv_low):
-    taps, own, width = conv_low.shape
+def order_table(me, near, far, conv, extra, score, second):
+    taps, own, width = conv.shape
     vmem = pl.BlockSpec(memory_space=pltpu.VMEM)
     table = jax.ShapeDtypeStruct((taps, VOCAB, width), BF)
+    row = jax.ShapeDtypeStruct((1, width), F32)
     return pl.pallas_call(
         order_body,
-        in_specs=[pl.BlockSpec(memory_space=pltpu.SMEM), vmem, vmem, vmem],
-        out_specs=[vmem, vmem, vmem],
-        out_shape=[table, table, jax.ShapeDtypeStruct((own, VOCAB), F32)],
+        in_specs=[pl.BlockSpec(memory_space=pltpu.SMEM)] + [vmem] * 6,
+        out_specs=[vmem] * 7,
+        out_shape=[
+            table,
+            table,
+            jax.ShapeDtypeStruct((own, VOCAB), F32),
+            jax.ShapeDtypeStruct((1, 1), F32),
+            row,
+            row,
+            row,
+        ],
         scratch_shapes=[pltpu.VMEM((taps * VOCAB, width), F32)],
         compiler_params=pltpu.CompilerParams(vmem_limit_bytes=60 << 20),
-    )(me, near, far, conv_low)
+    )(me, near, far, conv, extra, score.reshape(1, width), second.reshape(1, width))
 
 
 def dot2_left(pair, b, dims):
@@ -809,7 +841,6 @@
     taps = conv.shape[0]
     owner = lax.axis_index("dp")
     start = lax.axis_index("seq") * length
-    conv_low = conv.astype(BF)
     where = jnp.stack([owner, lax.axis_index("seq")]).astype(jnp.int32)
     mid = marked_ids(byte_ids, lengths, start, taps)
     left, right = shifted_rim(out_grad, 1)
@@ -827,9 +858,9 @@
         me, mid, out_grad, grad_rim, score, hidden, spill, weights, sums, taps
     )
     near, far, extra = sum_over_devices(keep, send, extra, plans)
-    score_grad = extra[:, 0].reshape(width)
-    entropy = extra[0, 1, 0] / extra[0, 1, 1]
-    high, low, columns = order_table(me, near, far, conv_low)
+    high, low, columns, entropy, score_grad, new_score, new_score_second = order_table(
+        me, near, far, conv, extra, score, score_second
+    )
     near = jnp.stack([columns] + [swap(columns, "dp", 2 * m) for m in range(1, lax.axis_size("dp") // 2)])
     conv_grad, new_conv, new_conv_left, new_conv_right = renew_conv(
         where, high, low, embed_all, ready, conv_right_root, conv, conv_left, conv_right
@@ -839,22 +870,20 @@
     embed_grad, new_embed, new_embed_left, new_embed_right = renew_embed(
         where, near, far, embed, embed_left, embed_right, embed_left_root, embed_right_root
     )
-    new_score_second = BETA_SECOND * score_second + (1.0 - BETA_SECOND) * score_grad * score_grad
-    new_score = score - RATE_SCORE * score_grad / (jnp.sqrt(new_score_second) + EPSILON)
     return (
         output,
-        entropy,
+        entropy.reshape(()),
         embed_grad,
         conv_grad,
-        score_grad,
+        score_grad.reshape(width),
         new_embed,
         new_conv,
-        new_score,
+        new_score.reshape(width),
         new_embed_left,
         new_embed_right,
         new_conv_left,
         new_conv_right,
-        new_score_second,
+        new_score_second.reshape(width),
     )
 
 

time: 273 us -> 257 us (0.941)
  Pallas kernels: 145 us -> 133 us
    pallas_call x1, Pallas kernels: 61.4 us -> 50.7 us  [lookup(): pl.pallas_call(partial(lookup_body, masks=masks, taps=taps), grid=(rows,)...]
    unnamed x52 -> x54, local copies, waits for them, and re-layouts: 5.61 us -> 5.62 us
  transfers between devices with their start and end apart: 33 -> 33, of which waited for: 18 -> 18; matrix products, arithmetic and copies ran while one was open for 6% -> 5% of each run, Pallas kernels for 7% -> 7%
where the time goes in v3:
time: 257 us
  Pallas kernels  133 us (52%)
  starting transfers between devices  55.7 us (22%)
  waiting for transfers between devices  45.1 us (18%)
  local copies, waits for them, and re-layouts  13.6 us (5%)
  other arithmetic  8.09 us (3%)
    pallas_call x1, Pallas kernels, lookup(): pl.pallas_call(partial(lookup_body, masks=masks, taps=taps), grid=(rows,)...  50.7 us
    ppermute x29, starting transfers between devices, swap(): lax.ppermute(cells, axis, [(i, i ^ bit) for i in range(lax.axis_size(axis...  46 us
    ppermute x29, waiting for transfers between devices, swap(): lax.ppermute(cells, axis, [(i, i ^ bit) for i in range(lax.axis_size(axis...  45.1 us
    pallas_call x1, Pallas kernels, apply_weights(): pl.pallas_call(apply_body, grid=(rows // GROUP,), in_specs=[pl.BlockSpec(...  33.6 us
    pallas_call x1, Pallas kernels, renew_conv(): pl.pallas_call(conv_body, grid=(taps,), in_specs=[pl.BlockSpec(memory_spa...  13.1 us
    pallas_call x4, Pallas kernels, fold(): pl.pallas_call(partial(fold_body, gots=len(got), pieces=pieces, joint=joi...  9.77 us
    ppermute x2, starting transfers between devices, shifted_rim(): left = lax.ppermute(tail, 'seq', [(i, i + 1) for i in range(count - 1)])  7.09 us
    unnamed x54, local copies, waits for them, and re-layouts  5.62 us
  transfers between devices with their start and end apart: 33, of which 18 were waited for; matrix products, arithmetic and copies ran while one was open for 5% of the time, Pallas kernels for 7%

profile of v3, /device:TPU:1, one launch (start us, length us, event | category | flops | bytes accessed | tf_op | source)
XLA Modules:
  0.0 256.6 jit_solution(12951957979503299943)
XLA Ops:
  1.2 2.2 shard_map.246.refs_0_
  3.4 2.1 collective-permute-start
  5.5 2.3 collective-permute-start.1
  8.6 3.1 %collective-permute-start.4 = (s32[16,8]{1,0:T(8,128)S(1)}, s32[16,8]{1,0:T(8,128)S(1)}, u32[]{:S(2)}, u32[]{:S(2)}) collective-permute-start(s32[16,8]{1,0:T(8,128)S(1)} %get-tuple-element.142), channel_id=1, source_target_pairs={{0,1},{1,2},{2,3},{4,5},{5,6},{6,7},{8,9},{9,10},{10,11},{12,13},{... | collective-permute-start | bytes 1544 | tf_op jit(solution)/shard_map/ppermute | solution.py:413
  11.7 1.3 collective-permute-start.5
  16.0 4.0 %collective-permute-start.6 = (f32[16,1,768]{2,1,0:T(1,128)S(1)}, f32[16,1,768]{2,1,0:T(1,128)S(1)}, u32[]{:S(2)}, u32[]{:S(2)}) collective-permute-start(f32[16,1,768]{2,1,0:T(1,128)S(1)} %get-tuple-element.134), channel_id=1, source_target_pairs={{0,1},{1,2},{2,3},{4,5},{5,6},{6,7},{8,9},{9,10},{10,11},{12,13},{... | collective-permute-start | bytes 147464 | tf_op jit(solution)/shard_map/ppermute | solution.py:413
  20.0 1.3 collective-permute-start.7
  21.4 2.4 collective-permute-done.2.refs_3_
  24.0 4.6 %collective-permute-start.3 = (bf16[4,576,128]{2,1,0:T(8,128)(2,1)S(1)}, bf16[4,576,128]{2,1,0:T(8,128)(2,1)S(1)}, u32[]{:S(2)}, u32[]{:S(2)}) collective-permute-start(bf16[4,576,128]{2,1,0:T(8,128)(2,1)S(1)} %pad_maximum_fusion.2), channel_id=1, source_target_pairs={{0,4},{4,0},{8,12},{12,8},{16,20},{20,16},{24,28},{28,24},{1,5},{5... | collective-permute-start | bytes 1769480 | tf_op jit(solution)/shard_map/ppermute | solution.py:469
  29.2 1.2 stack.107.mid_ref.next_ref
  32.3 3.0 %shard_map.247 = (bf16[256,768]{1,0:T(8,128)(2,1)}, bf16[4,256,128]{2,1,0:T(8,128)(2,1)}, bf16[4,256,128]{2,1,0:T(8,128)(2,1)}) custom-call(s32[2]{0:T(128)} %pad_add_fusion.5.where_ref.owner_ref, bf16[960,128]{1,0:T(8,128)(2,1)} %shard_map.246.refs_0_, bf16[960,128]{1,0:T(8,128)(2,1)} %copy-done.7, bf16[960,128]{1,0:T(8,128)(2,1)} %copy-done.8, ...), custom_call_target="tpu_custom_call" | custom-call | tf_op jit(solution)/shard_map/pallas_call | solution.py:520
  35.3 2.4 collective-permute-start.8
  37.7 1.2 collective-permute-start.10
  38.9 3.3 %collective-permute-done.8 = bf16[4,256,128]{2,1,0:T(8,128)(2,1)S(1)} collective-permute-done((bf16[4,256,128]{2,1,0:T(8,128)(2,1)}, bf16[4,256,128]{2,1,0:T(8,128)(2,1)S(1)}, u32[]{:S(2)}, u32[]{:S(2)}) %collective-permute-start.8) | collective-permute-done | bytes 262176 | tf_op jit(solution)/shard_map/ppermute | solution.py:469
  43.2 4.1 %collective-permute-start.9 = (bf16[8,256,128]{2,1,0:T(8,128)(2,1)S(1)}, bf16[8,256,128]{2,1,0:T(8,128)(2,1)S(1)}, u32[]{:S(2)}, u32[]{:S(2)}) collective-permute-start(bf16[8,256,128]{2,1,0:T(8,128)(2,1)S(1)} %pad_maximum_fusion.3), channel_id=1, source_target_pairs={{0,2},{1,3},{2,0},{3,1},{4,6},{5,7},{6,4},{7,5},{8,10},{9,11},{10,... | collective-permute-start | bytes 1572872 | tf_op jit(solution)/shard_map/ppermute | solution.py:469
  49.2 5.5 %shard_map.248 = (bf16[256,256]{1,0:T(8,128)(2,1)}, bf16[256,256]{1,0:T(8,128)(2,1)}, bf16[96,256]{1,0:T(8,128)(2,1)}, bf16[5,96,256]{2,1,0:T(8,128)(2,1)}, bf16[5,96,256]{2,1,0:T(8,128)(2,1)}) custom-call(s32[2]{0:T(128)} %pad_add_fusion.5.where_ref.owner_ref, bf16[256,768]{1,0:T(8,128)(2,1)} %get-tuple-element.77.embed_ref, f32[5,96,768]{2,1,0:T(8,128)} %left_root_ref.2), custom_call_target="tpu_custom_call" | custom-call | flops 1073741824 | bytes 3145728 | tf_op jit(solution)/shard_map/pallas_call | solution.py:717
  54.6 3.6 %collective-permute-done.9 = bf16[8,256,128]{2,1,0:T(8,128)(2,1)S(1)} collective-permute-done((bf16[8,256,128]{2,1,0:T(8,128)(2,1)S(1)}, bf16[8,256,128]{2,1,0:T(8,128)(2,1)S(1)}, u32[]{:S(2)}, u32[]{:S(2)}) %collective-permute-start.9) | collective-permute-done | bytes 524320 | tf_op jit(solution)/shard_map/ppermute | solution.py:469
  58.3 1.9 collective-permute-done.11
  60.5 2.6 %collective-permute-start.12 = (bf16[2,16,256,128]{3,2,1,0:T(8,128)(2,1)S(1)}, bf16[2,16,256,128]{3,2,1,0:T(8,128)(2,1)}, u32[]{:S(2)}, u32[]{:S(2)}) collective-permute-start(bf16[2,16,256,128]{3,2,1,0:T(8,128)(2,1)S(1)} %pad_maximum_fusion.near_ref), channel_id=1, source_target_pairs={{0,4},{4,0},{8,12},{12,8},{16,20},{20,16},{24,28},{28,24},{1,5},{5... | collective-permute-start | bytes 6291464 | tf_op jit(solution)/shard_map/ppermute | solution.py:469
  67.0 50.7 %shard_map.249 = (bf16[16,4,256,768]{3,2,1,0:T(8,128)(2,1)}, f32[16,16,768]{2,1,0:T(8,128)}, f32[16,8,768]{2,1,0:T(8,128)}) custom-call(s32[2]{0:T(128)} %pad_add_fusion.5.where_ref.owner_ref, s32[16,8,768]{2,1,0:T(8,128)} %stack.107.mid_ref.next_ref, s32[16,8,768]{2,1,0:T(8,128)} %stack.107.mid_ref.next_ref, f32[16,256,768]{2,1,0:T(8,128)} %g_ref.3, ...), custom_call_target="tpu_custom_call" | custom-call | tf_op jit(solution)/shard_map/pallas_call | solution.py:170
  117.7 3.4 %shard_map.250 = (f32[16,8,768]{2,1,0:T(8,128)}, f32[16,128]{1,0:T(8,128)}, f32[16,8,768]{2,1,0:T(8,128)}) custom-call(f32[16,8,768]{2,1,0:T(8,128)} %get-tuple-element.85.band_ref, s32[16,1]{1,0:T(8,128)} %copy.32.lengths_ref, s32[1]{0:T(128)} %bitcast.15.start_ref, f32[1,768]{1,0:T(1,128)} %reshape.60.score_ref, f32[16,16,768]{2,1,0:T(8,128)} %get-tuple-element.86.rim_ref, ...), custom_call_target="tpu_custom_call" | custom-call | tf_op jit(solution)/shard_map/pallas_call | solution.py:284
  121.2 33.6 %shard_map.251 = (f32[16,256,768]{2,1,0:T(8,128)}, f32[2,640,384]{2,1,0:T(8,128)}, s16[2,656,384]{2,1,0:T(8,128)(2,1)}, f32[2,8,384]{2,1,0:T(8,128)}) custom-call(s32[2]{0:T(128)} %pad_add_fusion.4.me_ref, s32[16,8,768]{2,1,0:T(8,128)} %stack.107.mid_ref.next_ref, f32[16,256,768]{2,1,0:T(8,128)} %g_ref.3, f32[16,16,768]{2,1,0:T(8,128)} %pad_maximum_fusion.1.gh_ref, ...), custom_call_target="tpu_custom_call" | custom-call | tf_op jit(solution)/shard_map/pallas_call | solution.py:372
  155.2 2.4 collective-permute-done.13.refs_0_
  158.6 3.5 %shard_map.252 = (f32[2,320,384]{2,1,0:T(8,128)}, f32[2,8,384]{2,1,0:T(8,128)}, s16[336,384]{1,0:T(8,128)(2,1)}, s16[336,384]{1,0:T(8,128)(2,1)}) custom-call(f32[2,640,384]{2,1,0:T(8,128)} %get-tuple-element.91.keep_ref, f32[2,8,384]{2,1,0:T(8,128)} %get-tuple-element.92.extra_ref, s16[2,656,384]{2,1,0:T(8,128)(2,1)} %copy-done.6), custom_call_target="tpu_custom_call" | custom-call | tf_op jit(solution)/shard_map/pallas_call | solution.py:579
  163.0 6.8 %collective-permute-done.14.refs_0_ = s16[336,384]{1,0:T(8,128)(2,1)S(1)} collective-permute-done((s16[336,384]{1,0:T(8,128)(2,1)}, s16[336,384]{1,0:T(8,128)(2,1)S(1)}, u32[]{:S(2)}, u32[]{:S(2)}) %collective-permute-start.14) | collective-permute-done | bytes 258080 | tf_op jit(solution)/shard_map/ppermute | solution.py:469
  171.0 2.4 shard_map.253
  174.0 3.4 %collective-permute-done.16.refs_0_ = s16[176,384]{1,0:T(8,128)(2,1)S(1)} collective-permute-done((s16[176,384]{1,0:T(8,128)(2,1)}, s16[176,384]{1,0:T(8,128)(2,1)S(1)}, u32[]{:S(2)}, u32[]{:S(2)}) %collective-permute-start.16) | collective-permute-done | bytes 135200 | tf_op jit(solution)/shard_map/ppermute | solution.py:469
  178.2 2.1 shard_map.254
  180.2 1.6 collective-permute-start.18
  184.2 2.1 collective-permute-done.19.refs_1_
  186.3 2.1 collective-permute-done.20.refs_2_
  189.1 1.8 shard_map.255
  190.9 1.6 shard_map.256
  192.4 1.3 collective-permute-start.21
  193.7 1.6 collective-permute-start.22
  196.6 1.5 collective-permute-done.22
  198.1 2.7 %collective-permute-done.23 = s16[2,48,384]{2,1,0:T(8,128)(2,1)S(1)} collective-permute-done((s16[2,48,384]{2,1,0:T(8,128)(2,1)}, s16[2,48,384]{2,1,0:T(8,128)(2,1)S(1)}, u32[]{:S(2)}, u32[]{:S(2)}) %collective-permute-start.23) | collective-permute-done | bytes 73760 | tf_op jit(solution)/shard_map/ppermute | solution.py:469
  201.7 3.0 %collective-permute-start.24 = (s16[192,384]{1,0:T(8,128)(2,1)S(1)}, s16[192,384]{1,0:T(8,128)(2,1)S(1)}, u32[]{:S(2)}, u32[]{:S(2)}) collective-permute-start(s16[192,384]{1,0:T(8,128)(2,1)S(1)} %get-tuple-element.135), channel_id=1, source_target_pairs={{0,2},{1,3},{2,0},{3,1},{4,6},{5,7},{6,4},{7,5},{8,10},{9,11},{10,... | collective-permute-start | bytes 442376 | tf_op jit(solution)/shard_map/ppermute | solution.py:469
  204.9 2.3 collective-permute-done.24
  209.1 5.2 %collective-permute-done.25 = s16[384,384]{1,0:T(8,128)(2,1)S(1)} collective-permute-done((s16[384,384]{1,0:T(8,128)(2,1)S(1)}, s16[384,384]{1,0:T(8,128)(2,1)S(1)}, u32[]{:S(2)}, u32[]{:S(2)}) %collective-permute-start.25) | collective-permute-done | bytes 294944 | tf_op jit(solution)/shard_map/ppermute | solution.py:469
  215.0 7.3 %collective-permute-start.28 = (s16[2,768,384]{2,1,0:T(8,128)(2,1)S(1)}, s16[2,768,384]{2,1,0:T(8,128)(2,1)S(1)}, u32[]{:S(2)}, u32[]{:S(2)}) collective-permute-start(s16[2,768,384]{2,1,0:T(8,128)(2,1)S(1)} %pad_add_fusion.near_ref), channel_id=1, source_target_pairs={{0,4},{4,0},{8,12},{12,8},{16,20},{20,16},{24,28},{28,24},{1,5},{5... | collective-permute-start | bytes 3538952 | tf_op jit(solution)/shard_map/ppermute | solution.py:469
  222.8 1.9 collective-permute-done.28.far_ref
  225.7 5.5 %shard_map.257 = (bf16[5,256,768]{2,1,0:T(8,128)(2,1)}, bf16[5,256,768]{2,1,0:T(8,128)(2,1)}, f32[96,256]{1,0:T(8,128)}, f32[1,1]{1,0:T(1,128)}, f32[1,768]{1,0:...) custom-call(s32[2]{0:T(128)} %pad_add_fusion.4.me_ref, s16[2,768,384]{2,1,0:T(8,128)(2,1)} %copy-done.1, ...), custom_call_target="tpu_custom_call" | custom-call | tf_op jit(solution)/shard_map/pallas_call | solution.py:672
  231.2 1.6 collective-permute-start.30
  232.8 1.9 collective-permute-start.31
  234.8 13.1 %shard_map.258 = (f32[5,96,768]{2,1,0:T(8,128)}, f32[5,96,768]{2,1,0:T(8,128)}, f32[5,96,768]{2,1,0:T(8,128)}, f32[5,96,768]{2,1,0:T(8,128)}) custom-call(s32[2]{0:T(128)} %pad_add_fusion.5.where_ref.owner_ref, bf16[5,256,768]{2,1,0:T(8,128)(2,1)} %get-tuple-element.111.high_ref, bf16[5,256,768]{2,1,0:T(8,128)(2,1)} %get-tuple-element.112.low_ref, ...), custom_call_target="tpu_custom_call" | custom-call | flops 8589934592 | bytes 33554432 | tf_op jit(solution)/shard_map/pallas_call | solution.py:765
  247.9 1.3 collective-permute-start.32
  251.8 4.9 %shard_map.259 = (f32[32,768]{1,0:T(8,128)}, f32[32,768]{1,0:T(8,128)}, f32[32,256]{1,0:T(8,128)}, f32[96,768]{1,0:T(8,128)}) custom-call(s32[2]{0:T(128)} %pad_add_fusion.5.where_ref.owner_ref, f32[4,96,256]{2,1,0:T(8,128)} %copy-done.2, f32[4,96,256]{2,1,0:T(8,128)} %copy-done.11, f32[32,768]{1,0:T(8,128)} %weight_ref.3, f32[32,256]{1,0:T(8,128)} %left_ref.3, ...), custom_call_target="tpu_custom_call" | custom-call | tf_op jit(solution)/shard_map/pallas_call | solution.py:812
  (138 shorter events, 30.8 us)
Async XLA Ops:
  3.4 25.2 %copy-start.20 = (s32[16,512]{1,0:T(8,128)S(1)}, s32[16,512]{1,0:T(8,128)}, u32[]{:S(2)}) copy-start(s32[16,512]{1,0:T(8,128)} %param.15) | copy-start | bytes 98308
  3.4 25.2 %copy-start.26 = (s32[16]{0:T(128)S(1)}, s32[16]{0:T(128)}, u32[]{:S(2)}) copy-start(s32[16]{0:T(128)} %param.16) | copy-start | bytes 196
  3.4 12.6 %collective-permute-start = (bf16[960,128]{1,0:T(8,128)(2,1)}, bf16[960,128]{1,0:T(8,128)(2,1)S(1)}, u32[]{:S(2)}, u32[]{:S(2)}) collective-permute-start(bf16[960,128]{1,0:T(8,128)(2,1)} %shard_map.246.refs_0_), channel_id=1, source_target_pairs={{0,8},{4,12},{8,0},{12,4},{16,24},{20,28},{24,16},{28,20},{1,9},{5... | collective-permute-start | bytes 737288 | tf_op jit(solution)/shard_map/ppermute | solution.py:469
  5.5 14.5 %collective-permute-start.1 = (bf16[960,128]{1,0:T(8,128)(2,1)}, bf16[960,128]{1,0:T(8,128)(2,1)S(1)}, u32[]{:S(2)}, u32[]{:S(2)}) collective-permute-start(bf16[960,128]{1,0:T(8,128)(2,1)} %shard_map.246.refs_0_), channel_id=1, source_target_pairs={{0,16},{4,20},{8,24},{12,28},{16,0},{20,4},{24,8},{28,12},{1,17},{... | collective-permute-start | bytes 737288 | tf_op jit(solution)/shard_map/ppermute | solution.py:469
  7.8 16.0 %collective-permute-start.2 = (bf16[960,128]{1,0:T(8,128)(2,1)}, bf16[960,128]{1,0:T(8,128)(2,1)S(1)}, u32[]{:S(2)}, u32[]{:S(2)}) collective-permute-start(bf16[960,128]{1,0:T(8,128)(2,1)} %shard_map.246.refs_0_), channel_id=1, source_target_pairs={{0,24},{4,28},{8,16},{12,20},{16,8},{20,12},{24,0},{28,4},{1,25},{... | collective-permute-start | bytes 737288 | tf_op jit(solution)/shard_map/ppermute | solution.py:469
  8.6 20.0 %collective-permute-start.4 = (s32[16,8]{1,0:T(8,128)S(1)}, s32[16,8]{1,0:T(8,128)S(1)}, u32[]{:S(2)}, u32[]{:S(2)}) collective-permute-start(s32[16,8]{1,0:T(8,128)S(1)} %get-tuple-element.142), channel_id=1, source_target_pairs={{0,1},{1,2},{2,3},{4,5},{5,6},{6,7},{8,9},{9,10},{10,11},{12,13},{... | collective-permute-start | bytes 1544 | tf_op jit(solution)/shard_map/ppermute | solution.py:413
  11.7 16.9 %collective-permute-start.5 = (s32[16,8]{1,0:T(8,128)S(1)}, s32[16,8]{1,0:T(8,128)S(1)}, u32[]{:S(2)}, u32[]{:S(2)}) collective-permute-start(s32[16,8]{1,0:T(8,128)S(1)} %get-tuple-element.143), channel_id=1, source_target_pairs={{1,0},{2,1},{3,2},{5,4},{6,5},{7,6},{9,8},{10,9},{11,10},{13,12},{... | collective-permute-start | bytes 1544 | tf_op jit(solution)/shard_map/ppermute | solution.py:414
  16.0 13.2 %copy-start.7 = (bf16[960,128]{1,0:T(8,128)(2,1)}, bf16[960,128]{1,0:T(8,128)(2,1)S(1)}, u32[]{:S(2)}) copy-start(bf16[960,128]{1,0:T(8,128)(2,1)S(1)} %collective-permute-done.refs_1_) | copy-start | bytes 737284
  16.0 14.4 %collective-permute-start.6 = (f32[16,1,768]{2,1,0:T(1,128)S(1)}, f32[16,1,768]{2,1,0:T(1,128)S(1)}, u32[]{:S(2)}, u32[]{:S(2)}) collective-permute-start(f32[16,1,768]{2,1,0:T(1,128)S(1)} %get-tuple-element.134), channel_id=1, source_target_pairs={{0,1},{1,2},{2,3},{4,5},{5,6},{6,7},{8,9},{9,10},{10,11},{12,13},{... | collective-permute-start | bytes 147464 | tf_op jit(solution)/shard_map/ppermute | solution.py:413
  20.0 10.4 %copy-start.8 = (bf16[960,128]{1,0:T(8,128)(2,1)}, bf16[960,128]{1,0:T(8,128)(2,1)S(1)}, u32[]{:S(2)}) copy-start(bf16[960,128]{1,0:T(8,128)(2,1)S(1)} %collective-permute-done.1.refs_2_) | copy-start | bytes 737284
  20.0 10.4 %collective-permute-start.7 = (f32[16,1,768]{2,1,0:T(1,128)S(1)}, f32[16,1,768]{2,1,0:T(1,128)S(1)}, u32[]{:S(2)}, u32[]{:S(2)}) collective-permute-start(f32[16,1,768]{2,1,0:T(1,128)S(1)} %get-tuple-element.133), channel_id=1, source_target_pairs={{1,0},{2,1},{3,2},{5,4},{6,5},{7,6},{9,8},{10,9},{11,10},{13,12},{... | collective-permute-start | bytes 147464 | tf_op jit(solution)/shard_map/ppermute | solution.py:414
  23.8 6.6 %copy-start.9 = (bf16[960,128]{1,0:T(8,128)(2,1)}, bf16[960,128]{1,0:T(8,128)(2,1)S(1)}, u32[]{:S(2)}) copy-start(bf16[960,128]{1,0:T(8,128)(2,1)S(1)} %collective-permute-done.2.refs_3_) | copy-start | bytes 737284
  24.0 7.6 %collective-permute-start.3 = (bf16[4,576,128]{2,1,0:T(8,128)(2,1)S(1)}, bf16[4,576,128]{2,1,0:T(8,128)(2,1)S(1)}, u32[]{:S(2)}, u32[]{:S(2)}) collective-permute-start(bf16[4,576,128]{2,1,0:T(8,128)(2,1)S(1)} %pad_maximum_fusion.2), channel_id=1, source_target_pairs={{0,4},{4,0},{8,12},{12,8},{16,20},{20,16},{24,28},{28,24},{1,5},{5... | collective-permute-start | bytes 1769480 | tf_op jit(solution)/shard_map/ppermute | solution.py:469
  35.3 6.9 %collective-permute-start.8 = (bf16[4,256,128]{2,1,0:T(8,128)(2,1)}, bf16[4,256,128]{2,1,0:T(8,128)(2,1)S(1)}, u32[]{:S(2)}, u32[]{:S(2)}) collective-permute-start(bf16[4,256,128]{2,1,0:T(8,128)(2,1)} %get-tuple-element.75), channel_id=1, source_target_pairs={{0,1},{1,0},{2,3},{3,2},{4,5},{5,4},{6,7},{7,6},{8,9},{9,8},{10,11... | collective-permute-start | bytes 786440 | tf_op jit(solution)/shard_map/ppermute | solution.py:469
  37.7 9.6 %collective-permute-start.10 = (bf16[4,256,128]{2,1,0:T(8,128)(2,1)}, bf16[4,256,128]{2,1,0:T(8,128)(2,1)S(1)}, u32[]{:S(2)}, u32[]{:S(2)}) collective-permute-start(bf16[4,256,128]{2,1,0:T(8,128)(2,1)} %get-tuple-element.76), channel_id=1, source_target_pairs={{0,2},{1,3},{2,0},{3,1},{4,6},{5,7},{6,4},{7,5},{8,10},{9,11},{10,... | collective-permute-start | bytes 786440 | tf_op jit(solution)/shard_map/ppermute | solution.py:469
  43.2 15.0 %collective-permute-start.9 = (bf16[8,256,128]{2,1,0:T(8,128)(2,1)S(1)}, bf16[8,256,128]{2,1,0:T(8,128)(2,1)S(1)}, u32[]{:S(2)}, u32[]{:S(2)}) collective-permute-start(bf16[8,256,128]{2,1,0:T(8,128)(2,1)S(1)} %pad_maximum_fusion.3), channel_id=1, source_target_pairs={{0,2},{1,3},{2,0},{3,1},{4,6},{5,7},{6,4},{7,5},{8,10},{9,11},{10,... | collective-permute-start | bytes 1572872 | tf_op jit(solution)/shard_map/ppermute | solution.py:469
  48.3 11.9 %collective-permute-start.11 = (bf16[8,256,128]{2,1,0:T(8,128)(2,1)S(1)}, bf16[8,256,128]{2,1,0:T(8,128)(2,1)S(1)}, u32[]{:S(2)}, u32[]{:S(2)}) collective-permute-start(bf16[8,256,128]{2,1,0:T(8,128)(2,1)S(1)} %pad_maximum_fusion.4), channel_id=1, source_target_pairs={{0,1},{1,0},{2,3},{3,2},{4,5},{5,4},{6,7},{7,6},{8,9},{9,8},{10,11... | collective-permute-start | bytes 1572872 | tf_op jit(solution)/shard_map/ppermute | solution.py:469
  49.2 9.0 %copy-start.5 = (bf16[4,256,128]{2,1,0:T(8,128)(2,1)S(1)}, bf16[4,256,128]{2,1,0:T(8,128)(2,1)}, u32[]{:S(2)}) copy-start(bf16[4,256,128]{2,1,0:T(8,128)(2,1)} %get-tuple-element.75) | copy-start | bytes 786436
  54.6 5.5 %copy-start.4 = (bf16[4,256,128]{2,1,0:T(8,128)(2,1)S(1)}, bf16[4,256,128]{2,1,0:T(8,128)(2,1)}, u32[]{:S(2)}) copy-start(bf16[4,256,128]{2,1,0:T(8,128)(2,1)} %get-tuple-element.76) | copy-start | bytes 786436
  60.5 6.5 %copy-start = (bf16[2,16,256,128]{3,2,1,0:T(8,128)(2,1)}, bf16[2,16,256,128]{3,2,1,0:T(8,128)(2,1)S(1)}, u32[]{:S(2)}) copy-start(bf16[2,16,256,128]{3,2,1,0:T(8,128)(2,1)S(1)} %pad_maximum_fusion.near_ref) | copy-start | bytes 6291460
  60.5 6.5 %collective-permute-start.12 = (bf16[2,16,256,128]{3,2,1,0:T(8,128)(2,1)S(1)}, bf16[2,16,256,128]{3,2,1,0:T(8,128)(2,1)}, u32[]{:S(2)}, u32[]{:S(2)}) collective-permute-start(bf16[2,16,256,128]{3,2,1,0:T(8,128)(2,1)S(1)} %pad_maximum_fusion.near_ref), channel_id=1, source_target_pairs={{0,4},{4,0},{8,12},{12,8},{16,20},{20,16},{24,28},{28,24},{1,5},{5... | collective-permute-start | bytes 6291464 | tf_op jit(solution)/shard_map/ppermute | solution.py:469
  154.7 2.9 %collective-permute-start.13 = (s16[2,656,384]{2,1,0:T(8,128)(2,1)}, s16[2,656,384]{2,1,0:T(8,128)(2,1)S(1)}, u32[]{:S(2)}, u32[]{:S(2)}) collective-permute-start(s16[2,656,384]{2,1,0:T(8,128)(2,1)} %get-tuple-element.93), channel_id=1, source_target_pairs={{0,4},{4,0},{8,12},{12,8},{16,20},{20,16},{24,28},{28,24},{1,5},{5... | collective-permute-start | bytes 3022856 | tf_op jit(solution)/shard_map/ppermute | solution.py:469
  162.1 7.6 %collective-permute-start.14 = (s16[336,384]{1,0:T(8,128)(2,1)}, s16[336,384]{1,0:T(8,128)(2,1)S(1)}, u32[]{:S(2)}, u32[]{:S(2)}) collective-permute-start(s16[336,384]{1,0:T(8,128)(2,1)} %get-tuple-element.96), channel_id=1, source_target_pairs={{0,1},{1,0},{2,3},{3,2},{4,5},{5,4},{6,7},{7,6},{8,9},{9,8},{10,11... | collective-permute-start | bytes 774152 | tf_op jit(solution)/shard_map/ppermute | solution.py:469
  162.9 7.3 %collective-permute-start.15 = (s16[336,384]{1,0:T(8,128)(2,1)}, s16[336,384]{1,0:T(8,128)(2,1)S(1)}, u32[]{:S(2)}, u32[]{:S(2)}) collective-permute-start(s16[336,384]{1,0:T(8,128)(2,1)} %get-tuple-element.97), channel_id=1, source_target_pairs={{0,2},{1,3},{2,0},{3,1},{4,6},{5,7},{6,4},{7,5},{8,10},{9,11},{10,... | collective-permute-start | bytes 774152 | tf_op jit(solution)/shard_map/ppermute | solution.py:469
  173.4 4.1 %collective-permute-start.16 = (s16[176,384]{1,0:T(8,128)(2,1)}, s16[176,384]{1,0:T(8,128)(2,1)S(1)}, u32[]{:S(2)}, u32[]{:S(2)}) collective-permute-start(s16[176,384]{1,0:T(8,128)(2,1)} %get-tuple-element.100), channel_id=1, source_target_pairs={{0,2},{1,3},{2,0},{3,1},{4,6},{5,7},{6,4},{7,5},{8,10},{9,11},{10,... | collective-permute-start | bytes 405512 | tf_op jit(solution)/shard_map/ppermute | solution.py:469
  173.4 4.1 %collective-permute-start.17 = (s16[176,384]{1,0:T(8,128)(2,1)}, s16[176,384]{1,0:T(8,128)(2,1)S(1)}, u32[]{:S(2)}, u32[]{:S(2)}) collective-permute-start(s16[176,384]{1,0:T(8,128)(2,1)} %get-tuple-element.101), channel_id=1, source_target_pairs={{0,1},{1,0},{2,3},{3,2},{4,5},{5,4},{6,7},{7,6},{8,9},{9,8},{10,11... | collective-permute-start | bytes 405512 | tf_op jit(solution)/shard_map/ppermute | solution.py:469
  180.2 3.9 %collective-permute-start.18 = (s16[2,56,384]{2,1,0:T(8,128)(2,1)}, s16[2,56,384]{2,1,0:T(8,128)(2,1)S(1)}, u32[]{:S(2)}, u32[]{:S(2)}) collective-permute-start(s16[2,56,384]{2,1,0:T(8,128)(2,1)} %get-tuple-element.104), channel_id=1, source_target_pairs={{0,8},{4,12},{8,0},{12,4},{16,24},{20,28},{24,16},{28,20},{1,9},{5... | collective-permute-start | bytes 258056 | tf_op jit(solution)/shard_map/ppermute | solution.py:469
  181.9 4.5 %collective-permute-start.19 = (s16[2,56,384]{2,1,0:T(8,128)(2,1)}, s16[2,56,384]{2,1,0:T(8,128)(2,1)S(1)}, u32[]{:S(2)}, u32[]{:S(2)}) collective-permute-start(s16[2,56,384]{2,1,0:T(8,128)(2,1)} %get-tuple-element.105), channel_id=1, source_target_pairs={{0,16},{4,20},{8,24},{12,28},{16,0},{20,4},{24,8},{28,12},{1,17},{... | collective-permute-start | bytes 258056 | tf_op jit(solution)/shard_map/ppermute | solution.py:469
  183.0 5.4 %collective-permute-start.20 = (s16[2,56,384]{2,1,0:T(8,128)(2,1)}, s16[2,56,384]{2,1,0:T(8,128)(2,1)S(1)}, u32[]{:S(2)}, u32[]{:S(2)}) collective-permute-start(s16[2,56,384]{2,1,0:T(8,128)(2,1)} %get-tuple-element.106), channel_id=1, source_target_pairs={{0,24},{4,28},{8,16},{12,20},{16,8},{20,12},{24,0},{28,4},{1,25},{... | collective-permute-start | bytes 258056 | tf_op jit(solution)/shard_map/ppermute | solution.py:469
  184.2 4.3 %copy-start.17 = (s16[2,56,384]{2,1,0:T(8,128)(2,1)}, s16[2,56,384]{2,1,0:T(8,128)(2,1)S(1)}, u32[]{:S(2)}) copy-start(s16[2,56,384]{2,1,0:T(8,128)(2,1)S(1)} %collective-permute-done.18.refs_0_) | copy-start | bytes 258052
  192.4 4.1 %collective-permute-start.21 = (s16[2,48,384]{2,1,0:T(8,128)(2,1)}, s16[2,48,384]{2,1,0:T(8,128)(2,1)S(1)}, u32[]{:S(2)}, u32[]{:S(2)}) collective-permute-start(s16[2,48,384]{2,1,0:T(8,128)(2,1)} %shard_map.256), channel_id=1, source_target_pairs={{0,8},{4,12},{8,0},{12,4},{16,24},{20,28},{24,16},{28,20},{1,9},{5... | collective-permute-start | bytes 221192 | tf_op jit(solution)/shard_map/ppermute | solution.py:469
  193.7 4.3 %collective-permute-start.22 = (s16[2,48,384]{2,1,0:T(8,128)(2,1)}, s16[2,48,384]{2,1,0:T(8,128)(2,1)S(1)}, u32[]{:S(2)}, u32[]{:S(2)}) collective-permute-start(s16[2,48,384]{2,1,0:T(8,128)(2,1)} %shard_map.256), channel_id=1, source_target_pairs={{0,16},{4,20},{8,24},{12,28},{16,0},{20,4},{24,8},{28,12},{1,17},{... | collective-permute-start | bytes 221192 | tf_op jit(solution)/shard_map/ppermute | solution.py:469
  195.4 5.4 %collective-permute-start.23 = (s16[2,48,384]{2,1,0:T(8,128)(2,1)}, s16[2,48,384]{2,1,0:T(8,128)(2,1)S(1)}, u32[]{:S(2)}, u32[]{:S(2)}) collective-permute-start(s16[2,48,384]{2,1,0:T(8,128)(2,1)} %shard_map.256), channel_id=1, source_target_pairs={{0,24},{4,28},{8,16},{12,20},{16,8},{20,12},{24,0},{28,4},{1,25},{... | collective-permute-start | bytes 221192 | tf_op jit(solution)/shard_map/ppermute | solution.py:469
  201.7 5.5 %collective-permute-start.24 = (s16[192,384]{1,0:T(8,128)(2,1)S(1)}, s16[192,384]{1,0:T(8,128)(2,1)S(1)}, u32[]{:S(2)}, u32[]{:S(2)}) collective-permute-start(s16[192,384]{1,0:T(8,128)(2,1)S(1)} %get-tuple-element.135), channel_id=1, source_target_pairs={{0,2},{1,3},{2,0},{3,1},{4,6},{5,7},{6,4},{7,5},{8,10},{9,11},{10,... | collective-permute-start | bytes 442376 | tf_op jit(solution)/shard_map/ppermute | solution.py:469
  204.7 4.0 %collective-permute-start.26 = (s16[192,384]{1,0:T(8,128)(2,1)S(1)}, s16[192,384]{1,0:T(8,128)(2,1)S(1)}, u32[]{:S(2)}, u32[]{:S(2)}) collective-permute-start(s16[192,384]{1,0:T(8,128)(2,1)S(1)} %get-tuple-element.136), channel_id=1, source_target_pairs={{0,1},{1,0},{2,3},{3,2},{4,5},{5,4},{6,7},{7,6},{8,9},{9,8},{10,11... | collective-permute-start | bytes 442376 | tf_op jit(solution)/shard_map/ppermute | solution.py:469
  207.3 7.1 %collective-permute-start.25 = (s16[384,384]{1,0:T(8,128)(2,1)S(1)}, s16[384,384]{1,0:T(8,128)(2,1)S(1)}, u32[]{:S(2)}, u32[]{:S(2)}) collective-permute-start(s16[384,384]{1,0:T(8,128)(2,1)S(1)} %pad_add_fusion.2), channel_id=1, source_target_pairs={{0,1},{1,0},{2,3},{3,2},{4,5},{5,4},{6,7},{7,6},{8,9},{9,8},{10,11... | collective-permute-start | bytes 884744 | tf_op jit(solution)/shard_map/ppermute | solution.py:469
  208.7 6.1 %collective-permute-start.27 = (s16[384,384]{1,0:T(8,128)(2,1)S(1)}, s16[384,384]{1,0:T(8,128)(2,1)S(1)}, u32[]{:S(2)}, u32[]{:S(2)}) collective-permute-start(s16[384,384]{1,0:T(8,128)(2,1)S(1)} %pad_add_fusion.3), channel_id=1, source_target_pairs={{0,2},{1,3},{2,0},{3,1},{4,6},{5,7},{6,4},{7,5},{8,10},{9,11},{10,... | collective-permute-start | bytes 884744 | tf_op jit(solution)/shard_map/ppermute | solution.py:469
  214.4 7.9 %copy-start.22 = (f32[768]{0:T(1024)S(1)}, f32[768]{0:T(1024)}, u32[]{:S(2)}) copy-start(f32[768]{0:T(1024)} %param.29) | copy-start | bytes 9220
  215.0 9.8 %copy-start.1 = (s16[2,768,384]{2,1,0:T(8,128)(2,1)}, s16[2,768,384]{2,1,0:T(8,128)(2,1)S(1)}, u32[]{:S(2)}) copy-start(s16[2,768,384]{2,1,0:T(8,128)(2,1)S(1)} %pad_add_fusion.near_ref) | copy-start | bytes 3538948
  215.0 9.8 %collective-permute-start.28 = (s16[2,768,384]{2,1,0:T(8,128)(2,1)S(1)}, s16[2,768,384]{2,1,0:T(8,128)(2,1)S(1)}, u32[]{:S(2)}, u32[]{:S(2)}) collective-permute-start(s16[2,768,384]{2,1,0:T(8,128)(2,1)S(1)} %pad_add_fusion.near_ref), channel_id=1, source_target_pairs={{0,4},{4,0},{8,12},{12,8},{16,20},{20,16},{24,28},{28,24},{1,5},{5... | collective-permute-start | bytes 3538952 | tf_op jit(solution)/shard_map/ppermute | solution.py:469
  231.2 16.6 %collective-permute-start.29 = (f32[96,256]{1,0:T(8,128)}, f32[96,256]{1,0:T(8,128)S(1)}, u32[]{:S(2)}, u32[]{:S(2)}) collective-permute-start(f32[96,256]{1,0:T(8,128)} %get-tuple-element.110), channel_id=1, source_target_pairs={{0,8},{4,12},{8,0},{12,4},{16,24},{20,28},{24,16},{28,20},{1,9},{5... | collective-permute-start | bytes 294920 | tf_op jit(solution)/shard_map/ppermute | solution.py:469
  231.2 16.6 %collective-permute-start.30 = (f32[96,256]{1,0:T(8,128)}, f32[96,256]{1,0:T(8,128)S(1)}, u32[]{:S(2)}, u32[]{:S(2)}) collective-permute-start(f32[96,256]{1,0:T(8,128)} %get-tuple-element.110), channel_id=1, source_target_pairs={{0,16},{4,20},{8,24},{12,28},{16,0},{20,4},{24,8},{28,12},{1,17},{... | collective-permute-start | bytes 294920 | tf_op jit(solution)/shard_map/ppermute | solution.py:469
  232.8 15.0 %collective-permute-start.31 = (f32[96,256]{1,0:T(8,128)}, f32[96,256]{1,0:T(8,128)S(1)}, u32[]{:S(2)}, u32[]{:S(2)}) collective-permute-start(f32[96,256]{1,0:T(8,128)} %get-tuple-element.110), channel_id=1, source_target_pairs={{0,24},{4,28},{8,16},{12,20},{16,8},{20,12},{24,0},{28,4},{1,25},{... | collective-permute-start | bytes 294920 | tf_op jit(solution)/shard_map/ppermute | solution.py:469
  234.7 13.1 %copy-start.16 = (f32[96,256]{1,0:T(8,128)S(1)}, f32[96,256]{1,0:T(8,128)}, u32[]{:S(2)}) copy-start(f32[96,256]{1,0:T(8,128)} %get-tuple-element.110) | copy-start | bytes 294916
  234.7 14.4 %copy-start.25 = (f32[1,768]{1,0:T(1,128)S(1)}, f32[1,768]{1,0:T(1,128)}, u32[]{:S(2)}) copy-start(f32[1,768]{1,0:T(1,128)} %get-tuple-element.122) | copy-start | bytes 9220
  234.7 15.0 %copy-start.24 = (f32[1,768]{1,0:T(1,128)S(1)}, f32[1,768]{1,0:T(1,128)}, u32[]{:S(2)}) copy-start(f32[1,768]{1,0:T(1,128)} %get-tuple-element.125) | copy-start | bytes 9220
  234.7 15.7 %copy-start.23 = (f32[1,768]{1,0:T(1,128)S(1)}, f32[1,768]{1,0:T(1,128)}, u32[]{:S(2)}) copy-start(f32[1,768]{1,0:T(1,128)} %get-tuple-element.130) | copy-start | bytes 9220
  247.9 3.1 %collective-permute-start.32 = (f32[4,96,256]{2,1,0:T(8,128)S(1)}, f32[4,96,256]{2,1,0:T(8,128)S(1)}, u32[]{:S(2)}, u32[]{:S(2)}) collective-permute-start(f32[4,96,256]{2,1,0:T(8,128)S(1)} %pad_maximum_fusion.5.near_ref), channel_id=1, source_target_pairs={{0,4},{4,0},{8,12},{12,8},{16,20},{20,16},{24,28},{28,24},{1,5},{5... | collective-permute-start | bytes 1179656 | tf_op jit(solution)/shard_map/ppermute | solution.py:469
  (12 other events, 15.0 us)

commit v4 on v3

--- a/solution.py
+++ b/solution.py
@@ -18,7 +18,6 @@
 TILE = 128
 HALO = 8
 BLOCKS = 32
-GROUP = 2
 WIN = TILE // 2 + 16
 BF = jnp.bfloat16
 F32 = jnp.float32
@@ -30,7 +29,7 @@
 
 
 def exponent_of(v):
-    return jnp.clip(jnp.floor(jnp.log2(jnp.maximum(v, 1e-30))) + 1.0, -90.0, 120.0)
+    return jnp.clip(jnp.ceil(jnp.log2(jnp.maximum(v, 1e-30)) * 16.0), -1440.0, 1920.0) * 0.0625
 
 
 def to_code(v, exponent):
@@ -55,16 +54,16 @@
     high, rest = to_code(few, powers)
     low = jnp.floor(rest * 16384.0 + 0.5)
     blank = jnp.zeros((9, rows.shape[1]), F32)
-    return as_short(jnp.concatenate([code, exponent, high, low, powers, blank], axis=0))
+    return as_short(jnp.concatenate([code, exponent * 16.0, high, low, powers * 16.0, blank], axis=0))
 
 
 def decode(cells):
     cells = as_float(cells)
     count = cells.shape[0] - 16
     more = cells[count:]
-    extra = (more[1:3] + more[3:5] * (1.0 / 16384.0)) * jnp.exp2(more[5:7] - 15.0)
+    extra = (more[1:3] + more[3:5] * (1.0 / 16384.0)) * jnp.exp2(more[5:7] * 0.0625 - 15.0)
     extra = jnp.concatenate([extra, jnp.zeros((6, extra.shape[1]), F32)], axis=0)
-    return cells[:count] * jnp.exp2(more[0:1] - 15.0), extra
+    return cells[:count] * jnp.exp2(more[0:1] * 0.0625 - 15.0), extra
 
 
 def roll_to(v, offset):
@@ -99,19 +98,23 @@
 
     @pl.when(pl.program_id(0) == 0)
     def _():
-        for h in range(2):
-            for spot in range(near_ref.shape[1]):
+        spare = 2 * taps * VOCAB
+        for spot in range(near_ref.shape[1]):
+            found = []
+            for h in range(2):
                 for other, source in enumerate((near_ref, far_ref)):
                     group = 2 * (where_ref[1] ^ masks[h][spot // slots]) + ((where_ref[0] & 1) ^ other)
                     unit = group * slots + spot % slots
-
-                    @pl.when(unit < taps * blocks)
-                    def _():
-                        row = pl.multiple_of((h * taps + unit // blocks) * VOCAB, VOCAB)
-                        column = pl.multiple_of(unit % blocks * TILE, TILE)
-                        table_ref[pl.ds(row, VOCAB), pl.ds(column, TILE)] = source[h, spot]
-
-    nt = (((1,), (1,)), ((), ()))
+                    cells = as_float(source[h, spot])
+                    power = jnp.transpose(cells[TILE : TILE + 8])[:, 0:1]
+                    pair = split(cells[:TILE] * jnp.exp2(power * 0.0625 - 15.0))
+                    for low in range(2):
+                        row = (low * taps + unit // blocks) * VOCAB + h * TILE
+                        row = pl.multiple_of(jnp.where(unit < taps * blocks, row, spare), TILE)
+                        found.append((row, pl.multiple_of(unit % blocks * TILE, TILE), pair[low]))
+            for row, column, part in found:
+                table_ref[pl.ds(row, TILE), pl.ds(column, TILE)] = part
+
     tiles = length // TILE
     lanes = lax.broadcasted_iota(jnp.int32, (1, VOCAB), 1).astype(F32)
 
@@ -136,7 +139,7 @@
         spread[m, pl.ds(8, length // 2, stride=2)] = rows
         spread[m, pl.ds(9, length // 2, stride=2)] = rows
     for n in range(0, table_ref.shape[1], 256):
-        cells = jnp.dot(onehot, table_ref[:, n : n + 256], preferred_element_type=F32)
+        cells = jnp.dot(onehot, table_ref[0 : 2 * taps * VOCAB, n : n + 256], preferred_element_type=F32)
         hidden[:, n : n + 256] = cells
         h_high, h_low = split(cells[0:length])
         for i in range(tiles):
@@ -158,42 +161,6 @@
     blank = jnp.zeros((8, TILE), F32)
     band_ref[0, :, 0:TILE] = blank
     band_ref[0, :, TILE + length :] = blank
-
-
-def lookup(where, mid, out_grad, grad_rim, score, near, far, masks, taps):
-    rows, _, span = mid.shape
-    half, width = out_grad.shape[1:]
-    length = 2 * half
-    tiles = length // TILE
-    whole = lambda *shape: pl.BlockSpec(shape, lambda r: (0,) * len(shape), pipeline_mode=pl.Buffered(1))
-    by_row = lambda *shape: pl.BlockSpec((1, *shape), lambda r: (r,) + (0,) * len(shape))
-    return pl.pallas_call(
-        partial(lookup_body, masks=masks, taps=taps),
-        grid=(rows,),
-        in_specs=[
-            pl.BlockSpec(memory_space=pltpu.SMEM),
-            by_row(8, span),
-            pl.BlockSpec((1, 8, span), lambda r: (jnp.minimum(r + 1, rows - 1), 0, 0)),
-            by_row(half, width),
-            by_row(16, width),
-            whole(1, width),
-            whole(*near.shape),
-            whole(*far.shape),
-        ],
-        out_specs=[by_row(tiles, 2 * TILE, width), by_row(16, width), by_row(8, span)],
-        out_shape=[
-            jax.ShapeDtypeStruct((rows, tiles, 2 * TILE, width), BF),
-            jax.ShapeDtypeStruct((rows, 16, width), F32),
-            jax.ShapeDtypeStruct((rows, 8, span), F32),
-        ],
-        scratch_shapes=[
-            pltpu.VMEM((2 * taps * VOCAB, width), BF),
-            pltpu.VMEM((length + 2 * HALO, taps * VOCAB), BF),
-            pltpu.VMEM((width // TILE, length + 16, TILE), F32),
-            pltpu.VMEM((length + 2 * HALO, width), F32),
-        ],
-        compiler_params=pltpu.CompilerParams(vmem_limit_bytes=56 << 20),
-    )(where, mid, mid, out_grad, grad_rim, score.reshape(1, width), near, far)
 
 
 def weigh_body(band_ref, lengths_ref, start_ref, score_ref, rim_ref, edge_ref, out_ref, sums_ref, spill_ref):
@@ -278,30 +245,16 @@
         out_ref[:, d, :] = jnp.zeros_like(total)
 
 
-def weigh(band, lengths, start, score, rim, edges):
-    rows, _, span = band.shape
-    vmem = pl.BlockSpec(memory_space=pltpu.VMEM)
-    return pl.pallas_call(
-        weigh_body,
-        in_specs=[vmem, vmem, pl.BlockSpec(memory_space=pltpu.SMEM), vmem, vmem, vmem],
-        out_specs=[vmem, vmem, vmem],
-        out_shape=[
-            jax.ShapeDtypeStruct(band.shape, F32),
-            jax.ShapeDtypeStruct((rows, TILE), F32),
-            jax.ShapeDtypeStruct((rows, 8, rim.shape[2]), F32),
-        ],
-    )(band, lengths.reshape(rows, 1), start.reshape(1), score.reshape(1, -1), rim, edges)
-
-
 def apply_body(
     me_ref, mid_ref, g_ref, gh_ref, score_ref, hid_ref, spill_ref, weight_ref, sums_ref,
     out_ref, keep_ref, send_ref, extra_ref, onehot, hgrad, total, table_ref, pull_ref, staged,
+    *, first,
 ):
     length = hid_ref.shape[1] * TILE
     half = length // 2
     taps = table_ref.shape[0] // VOCAB
 
-    @pl.when(pl.program_id(0) == 0)
+    @pl.when(pl.program_id(0) == first)
     def _():
         table_ref[...] = jnp.zeros_like(table_ref)
         pull_ref[...] = jnp.zeros_like(pull_ref)
@@ -363,28 +316,63 @@
             send_ref[h] = encode(staged[...], mine)
 
 
-def apply_weights(me, mid, out_grad, grad_rim, score, hid, spill, weight, sums, taps):
+def mix_body(
+    where_ref, me_ref, start_ref, lengths_ref, mid_ref, next_ref, g_ref, gh_ref, score_ref, near_ref, far_ref, edge_ref,
+    out_ref, keep_ref, send_ref, extra_ref,
+    hid, rim, band, weights, sums, spill, table, onehot, spread, hidden, turned, hgrad, total, gathered, pulled, staged,
+    *, masks, taps,
+):
+    step = pl.program_id(0)
+    rows = hid.shape[0]
+
+    @pl.when(step < rows)
+    def _():
+        here = pl.ds(step, 1)
+        lookup_body(
+            where_ref, mid_ref, next_ref, g_ref, gh_ref, score_ref, near_ref, far_ref,
+            hid.at[here], rim.at[here], band.at[here], table, onehot, spread, hidden, masks=masks, taps=taps,
+        )
+
+    @pl.when(step == rows)
+    def _():
+        weigh_body(band, lengths_ref, start_ref, score_ref, rim, edge_ref, weights, sums, spill)
+
+    @pl.when(step >= rows)
+    def _():
+        here = pl.ds(step - rows, 1)
+        apply_body(
+            me_ref, mid_ref, g_ref, gh_ref, score_ref, hid.at[here], spill.at[here], weights.at[here], sums,
+            out_ref, keep_ref, send_ref, extra_ref, turned, hgrad, total, gathered, pulled, staged, first=rows,
+        )
+
+
+def mix(where, me, start, lengths, mid, out_grad, grad_rim, score, near, far, edges, masks, taps):
     rows, _, span = mid.shape
     half, width = out_grad.shape[1:]
-    tiles = 2 * half // TILE
-    whole = lambda *shape: pl.BlockSpec(shape, lambda r: (0,) * len(shape), pipeline_mode=pl.Buffered(1))
-    by_row = lambda *shape: pl.BlockSpec((GROUP, *shape), lambda r: (r,) + (0,) * len(shape))
+    length = 2 * half
+    tiles = length // TILE
+    whole = lambda *shape: pl.BlockSpec(shape, lambda t: (0,) * len(shape), pipeline_mode=pl.Buffered(1))
+    by_row = lambda *shape: pl.BlockSpec((1, *shape), lambda t: (lax.rem(t, rows),) + (0,) * len(shape))
+    smem = pl.BlockSpec(memory_space=pltpu.SMEM)
     return pl.pallas_call(
-        apply_body,
-        grid=(rows // GROUP,),
+        partial(mix_body, masks=masks, taps=taps),
+        grid=(2 * rows,),
         in_specs=[
-            pl.BlockSpec(memory_space=pltpu.SMEM),
+            smem,
+            smem,
+            smem,
+            whole(rows, 1),
             by_row(8, span),
+            pl.BlockSpec((1, 8, span), lambda t: (jnp.minimum(t + 1, rows - 1), 0, 0)),
             by_row(half, width),
             by_row(16, width),
             whole(1, width),
-            by_row(tiles, 2 * TILE, width),
-            by_row(8, width),
-            by_row(8, span),
-            whole(*sums.shape),
+            whole(*near.shape),
+            whole(*far.shape),
+            whole(*edges.shape),
         ],
         out_specs=[
-            by_row(half, width),
+            pl.BlockSpec((1, half, width), lambda t: (jnp.maximum(t - rows, 0), 0, 0)),
             whole(2, taps * VOCAB // 2, width // 2),
             whole(2, taps * VOCAB // 2 + 16, width // 2),
             whole(2, 8, width // 2),
@@ -396,15 +384,27 @@
             jax.ShapeDtypeStruct((2, 8, width // 2), F32),
         ],
         scratch_shapes=[
-            pltpu.VMEM((taps * VOCAB, GROUP * 2 * half), BF),
-            pltpu.VMEM((GROUP * 2 * half, width), BF),
+            pltpu.VMEM((rows, tiles, 2 * TILE, width), BF),
+            pltpu.VMEM((rows, 16, width), F32),
+            pltpu.VMEM((rows, 8, span), F32),
+            pltpu.VMEM((rows, 8, span), F32),
+            pltpu.VMEM((rows, TILE), F32),
+            pltpu.VMEM((rows, 8, width), F32),
+            pltpu.VMEM((2 * taps * VOCAB + TILE, width), BF),
+            pltpu.VMEM((length + 2 * HALO, taps * VOCAB), BF),
+            pltpu.VMEM((width // TILE, length + 16, TILE), F32),
+            pltpu.VMEM((length + 2 * HALO, width), F32),
+            pltpu.VMEM((taps * VOCAB, length), BF),
+            pltpu.VMEM((length, width), BF),
             pltpu.VMEM((half + 16, width), F32),
             pltpu.VMEM((taps * VOCAB, width), F32),
             pltpu.VMEM((8, width), F32),
             pltpu.VMEM((taps * VOCAB // 2, width // 2), F32),
         ],
-        compiler_params=pltpu.CompilerParams(vmem_limit_bytes=56 << 20),
-    )(me, mid, out_grad, grad_rim, score.reshape(1, width), hid, spill, weight, sums)
+        compiler_params=pltpu.CompilerParams(vmem_limit_bytes=60 << 20),
+    )(
+        where, me, start.reshape(1), lengths.reshape(rows, 1), mid, mid, out_grad, grad_rim, score.reshape(1, width), near, far, edges
+    )
 
 
 def shifted_rim(cells, width):
@@ -495,7 +495,7 @@
 
 
 def tables_body(where_ref, *refs, slots, own, rows):
-    *near, far_ref, embed_ref, high_ref, low_ref, units = refs
+    *near, far_ref, embed_ref, upper_ref, lower_ref, units = refs
     blocks = embed_ref.shape[1] // TILE
     first = blocks * rows
     for m, near_ref in enumerate(near):
@@ -509,14 +509,19 @@
             for t in range(slots):
                 units[t, pl.ds(pl.multiple_of(place * own, 16), own)] = source[first + t * own : first + (t + 1) * own]
     for t in range(slots):
-        high, low = split(jnp.dot(embed_ref[...], units[t], preferred_element_type=F32))
-        high_ref[t], low_ref[t] = high, low
+        table = jnp.dot(embed_ref[...], units[t], preferred_element_type=F32)
+        for h, target in enumerate((upper_ref, lower_ref)):
+            rows = table[h * TILE : (h + 1) * TILE]
+            exponent = exponent_of(jnp.max(jnp.abs(rows), axis=1, keepdims=True))
+            code, _ = to_code(rows, exponent)
+            turned = jnp.transpose(jnp.broadcast_to(exponent * 16.0, (TILE, TILE)))[0:16]
+            target[t] = as_short(jnp.concatenate([code, turned], axis=0))
 
 
 def make_tables(where, near, far, slots, own, rows):
     width = 2 * len(near) * own
     vmem = pl.BlockSpec(memory_space=pltpu.VMEM)
-    unit = jax.ShapeDtypeStruct((slots, VOCAB, TILE), BF)
+    unit = jax.ShapeDtypeStruct((slots, TILE + 16, TILE), jnp.int16)
     return pl.pallas_call(
         partial(tables_body, slots=slots, own=own, rows=rows),
         in_specs=[pl.BlockSpec(memory_space=pltpu.SMEM)] + [vmem] * (len(near) + 1),
@@ -552,7 +557,13 @@
     return embed_all, units, swap(units, "dp", 1), masks, ready, rims
 
 
-def fold_body(keep_ref, extra_ref, *refs, gots, pieces, joint):
+def final_code(rows):
+    exponent = exponent_of(jnp.max(jnp.abs(rows), axis=0, keepdims=True))
+    code, _ = to_code(rows, exponent)
+    return as_short(jnp.concatenate([code, jnp.broadcast_to(exponent * 16.0, (8, rows.shape[1]))], axis=0))
+
+
+def fold_body(keep_ref, extra_ref, *refs, gots, pieces, joint, last):
     got_refs, keep_out, extra_out, *sends = refs[:gots], refs[gots], refs[gots + 1], *refs[gots + 2 :]
     rest = keep_ref.shape[1] // pieces
     for h in range(2):
@@ -560,7 +571,7 @@
         for ref in got_refs if got_refs[0].ndim == 3 else got_refs[h : h + 1]:
             cells, more = decode(ref[h] if ref.ndim == 3 else ref[...])
             total, extra = total + cells, extra + more
-        keep_out[h] = total[:rest]
+        keep_out[h] = final_code(total) if last else total[:rest]
         extra_out[h] = extra
         for m in range(1, pieces):
             code = encode(total[m * rest : (m + 1) * rest], extra)
@@ -570,27 +581,26 @@
                 sends[h][...] = code
 
 
-def fold(keep, extra, got, pieces, joint):
+def fold(keep, extra, got, pieces, joint, last=False):
     _, count, width = keep.shape
     rest = count // pieces
     cells = jax.ShapeDtypeStruct((2, rest + 16, width) if joint else (rest + 16, width), jnp.int16)
     sends = 0 if pieces == 1 else pieces - 1 if joint else 2
+    first = jax.ShapeDtypeStruct((2, rest, width), F32)
+    if last:
+        first = jax.ShapeDtypeStruct((2, rest + 8, width), jnp.int16)
     vmem = pl.BlockSpec(memory_space=pltpu.VMEM)
     return pl.pallas_call(
-        partial(fold_body, gots=len(got), pieces=pieces, joint=joint),
+        partial(fold_body, gots=len(got), pieces=pieces, joint=joint, last=last),
         in_specs=[vmem] * (2 + len(got)),
         out_specs=[vmem] * (2 + sends),
-        out_shape=[jax.ShapeDtypeStruct((2, rest, width), F32), jax.ShapeDtypeStruct(extra.shape, F32)] + [cells] * sends,
+        out_shape=[first, jax.ShapeDtypeStruct(extra.shape, F32)] + [cells] * sends,
     )(keep, extra, *got)
 
 
 def finish_body(cells_ref, out_ref):
-    count = cells_ref.shape[1]
     for h in range(2):
-        rows = cells_ref[h]
-        exponent = exponent_of(jnp.max(jnp.abs(rows), axis=0, keepdims=True))
-        code, _ = to_code(rows, exponent)
-        out_ref[h] = as_short(jnp.concatenate([code, jnp.broadcast_to(exponent, (8, rows.shape[1]))], axis=0))
+        out_ref[h] = final_code(cells_ref[h])
 
 
 def finish(cells):
@@ -614,10 +624,10 @@
     keep, extra, *sends = fold(keep, extra, got, along, True)
     if along > 1:
         got = [swap(item, "dp", 2 * m) for m, item in enumerate(sends, 1)]
-        keep, extra = fold(keep, extra, got, 1, True)
+        keep, extra = fold(keep, extra, got, 1, True, last=len(plans[0]) == depth)
     for axis, bit in plans[0][depth:]:
         keep, extra = keep + swap(keep, axis, bit), extra + swap(extra, axis, bit)
-    cells = finish(keep)
+    cells = keep if keep.dtype == jnp.int16 else finish(keep)
     if along > 1:
         cells = jnp.concatenate([cells] + [swap(cells, "dp", 2 * m) for m in range(1, along)], axis=1)
     parts = []
@@ -653,7 +663,7 @@
             source = near_ref if p < BLOCKS // 2 else far_ref
             first = p % (BLOCKS // 2) * (block + 8)
             cells = as_float(source[h, first : first + block + 8])
-            rows = cells[:block] * jnp.exp2(cells[block : block + 1] - 15.0)
+            rows = cells[:block] * jnp.exp2(cells[block : block + 1] * 0.0625 - 15.0)
             table[pl.ds(pl.multiple_of((me_ref[h] ^ p) * block, 8), block), h * part : (h + 1) * part] = rows
     taps = conv_ref.shape[0]
     total = jnp.zeros(grad_ref.shape, F32)
@@ -850,12 +860,10 @@
     embed_all, near, far, masks, ready, (mid, grad_rim) = gather_tables(
         where, embed, conv, conv_left_root, (mid, grad_rim)
     )
-    hidden, rim, band = lookup(where, mid, out_grad, grad_rim, score, near, far, masks, taps)
-    weights, sums, spill = weigh(band, lengths, start, score, rim, edges)
     plans = exchange_plan(lax.axis_size("seq"), lax.axis_size("dp"))
     me = jnp.stack([block_index(plan) for plan in plans])
-    output, keep, send, extra = apply_weights(
-        me, mid, out_grad, grad_rim, score, hidden, spill, weights, sums, taps
+    output, keep, send, extra = mix(
+        where, me, start, lengths, mid, out_grad, grad_rim, score, near, far, edges, masks, taps
     )
     near, far, extra = sum_over_devices(keep, send, extra, plans)
     high, low, columns, entropy, score_grad, new_score, new_score_second = order_table(

time: 257 us -> 245 us (0.953)
  waiting for transfers between devices: 45.1 us -> 37 us
  Pallas kernels: 133 us -> 129 us
    ppermute x29, waiting for transfers between devices: 45.1 us -> 37 us  [swap(): lax.ppermute(cells, axis, [(i, i ^ bit) for i in range(lax.axis_size(axis...]
    pallas_call x4 -> x1, Pallas kernels: 89.3 us -> 85.3 us  [mix(): pl.pallas_call(partial(mix_body, masks=masks, taps=taps), grid=(2 * rows,...]
    unnamed x54 -> x59, local copies, waits for them, and re-layouts: 5.62 us -> 7.58 us
  transfers between devices with their start and end apart: 33 -> 33, of which waited for: 18 -> 17; matrix products, arithmetic and copies ran while one was open for 5% -> 6% of each run, Pallas kernels for 7% -> 8%
where the time goes in v4:
time: 245 us; the launch traced here: 244 us
  Pallas kernels  129 us (53%)
  starting transfers between devices  55.1 us (22%)
  waiting for transfers between devices  37 us (15%)
  local copies, waits for them, and re-layouts  14.3 us (6%)
  other arithmetic  7.39 us (3%)
    pallas_call x1, Pallas kernels, mix(): pl.pallas_call(partial(mix_body, masks=masks, taps=taps), grid=(2 * rows,...  85.3 us
    ppermute x29, starting transfers between devices, swap(): lax.ppermute(cells, axis, [(i, i ^ bit) for i in range(lax.axis_size(axis...  46 us
    ppermute x29, waiting for transfers between devices, swap(): lax.ppermute(cells, axis, [(i, i ^ bit) for i in range(lax.axis_size(axis...  37 us
    pallas_call x1, Pallas kernels, renew_conv(): pl.pallas_call(conv_body, grid=(taps,), in_specs=[pl.BlockSpec(memory_spa...  13.1 us
    pallas_call x4, Pallas kernels, fold(): pl.pallas_call(partial(fold_body, gots=len(got), pieces=pieces, joint=joi...  9.86 us
    unnamed x59, local copies, waits for them, and re-layouts  7.58 us
    ppermute x2, starting transfers between devices, shifted_rim(): left = lax.ppermute(tail, 'seq', [(i, i + 1) for i in range(count - 1)])  6.48 us
    pallas_call x1, Pallas kernels, order_table(): pl.pallas_call(order_body, in_specs=[pl.BlockSpec(memory_space=pltpu.SMEM...  5.48 us
  transfers between devices with their start and end apart: 33, of which 17 were waited for; matrix products, arithmetic and copies ran while one was open for 6% of the time, Pallas kernels for 8%

profile of v4, /device:TPU:1, one launch (start us, length us, event | category | flops | bytes accessed | tf_op | source)
XLA Modules:
  0.0 244.1 jit_solution(17406873900331703360)
XLA Ops:
  1.3 2.2 shard_map.246.refs_0_
  3.4 2.1 collective-permute-start
  5.5 2.3 collective-permute-start.1
  7.9 3.1 %collective-permute-start.4 = (s32[16,8]{1,0:T(8,128)S(1)}, s32[16,8]{1,0:T(8,128)S(1)}, u32[]{:S(2)}, u32[]{:S(2)}) collective-permute-start(s32[16,8]{1,0:T(8,128)S(1)} %get-tuple-element.132), channel_id=1, source_target_pairs={{0,1},{1,2},{2,3},{4,5},{5,6},{6,7},{8,9},{9,10},{10,11},{12,13},{... | collective-permute-start | bytes 1544 | tf_op jit(solution)/shard_map/ppermute | solution.py:413
  11.1 1.3 collective-permute-start.5
  14.1 1.2 fusion.4
  15.9 3.4 %collective-permute-start.6 = (f32[16,1,768]{2,0,1:T(8,128)S(1)}, f32[16,1,768]{2,0,1:T(8,128)S(1)}, u32[]{:S(2)}, u32[]{:S(2)}) collective-permute-start(f32[16,1,768]{2,0,1:T(8,128)S(1)} %copy.44), channel_id=1, source_target_pairs={{0,1},{1,2},{2,3},{4,5},{5,6},{6,7},{8,9},{9,10},{10,11},{12,13},{... | collective-permute-start | bytes 147464 | tf_op jit(solution)/shard_map/ppermute | solution.py:413
  19.4 1.3 collective-permute-start.7
  20.7 3.1 %collective-permute-done.2.refs_3_ = bf16[960,128]{1,0:T(8,128)(2,1)S(1)} collective-permute-done((bf16[960,128]{1,0:T(8,128)(2,1)}, bf16[960,128]{1,0:T(8,128)(2,1)S(1)}, u32[]{:S(2)}, u32[]{:S(2)}) %collective-permute-start.2) | collective-permute-done | bytes 245792 | tf_op jit(solution)/shard_map/ppermute | solution.py:469
  24.0 4.6 %collective-permute-start.3 = (bf16[4,576,128]{2,1,0:T(8,128)(2,1)S(1)}, bf16[4,576,128]{2,1,0:T(8,128)(2,1)S(1)}, u32[]{:S(2)}, u32[]{:S(2)}) collective-permute-start(bf16[4,576,128]{2,1,0:T(8,128)(2,1)S(1)} %pad_maximum_fusion.1), channel_id=1, source_target_pairs={{0,4},{4,0},{8,12},{12,8},{16,20},{20,16},{24,28},{28,24},{1,5},{5... | collective-permute-start | bytes 1769480 | tf_op jit(solution)/shard_map/ppermute | solution.py:469
  29.2 1.2 stack.107.mid_ref.next_ref
  30.6 1.1 pad_maximum_fusion.gh_ref
  32.5 3.1 %shard_map.247 = (bf16[256,768]{1,0:T(8,128)(2,1)}, s16[4,144,128]{2,1,0:T(8,128)(2,1)}, s16[4,144,128]{2,1,0:T(8,128)(2,1)}) custom-call(s32[2]{0:T(128)} %pad_add_fusion.6.where_ref.owner_ref, bf16[960,128]{1,0:T(8,128)(2,1)} %shard_map.246.refs_0_, bf16[960,128]{1,0:T(8,128)(2,1)} %copy-done.6, bf16[960,128]{1,0:T(8,128)(2,1)} %copy-done.7, ...), custom_call_target="tpu_custom_call" | custom-call | tf_op jit(solution)/shard_map/pallas_call | solution.py:525
  35.6 2.4 collective-permute-start.8
  37.9 1.2 collective-permute-start.10
  39.2 1.5 collective-permute-done.8
  41.6 3.5 %collective-permute-start.9 = (s16[8,144,128]{2,1,0:T(8,128)(2,1)S(1)}, s16[8,144,128]{2,1,0:T(8,128)(2,1)S(1)}, u32[]{:S(2)}, u32[]{:S(2)}) collective-permute-start(s16[8,144,128]{2,1,0:T(8,128)(2,1)S(1)} %pad_add_fusion.2), channel_id=1, source_target_pairs={{0,2},{1,3},{2,0},{3,1},{4,6},{5,7},{6,4},{7,5},{8,10},{9,11},{10,... | collective-permute-start | bytes 884744 | tf_op jit(solution)/shard_map/ppermute | solution.py:469
  46.9 5.5 %shard_map.248 = (bf16[256,256]{1,0:T(8,128)(2,1)}, bf16[256,256]{1,0:T(8,128)(2,1)}, bf16[96,256]{1,0:T(8,128)(2,1)}, bf16[5,96,256]{2,1,0:T(8,128)(2,1)}, bf16[5,96,256]{2,1,0:T(8,128)(2,1)}) custom-call(s32[2]{0:T(128)} %pad_add_fusion.6.where_ref.owner_ref, bf16[256,768]{1,0:T(8,128)(2,1)} %get-tuple-element.71.embed_ref, f32[5,96,768]{2,1,0:T(8,128)} %left_root_ref.2), custom_call_target="tpu_custom_call" | custom-call | flops 1073741824 | bytes 3145728 | tf_op jit(solution)/shard_map/pallas_call | solution.py:727
  53.2 2.5 %collective-permute-start.12 = (s16[2,16,144,128]{3,2,1,0:T(8,128)(2,1)S(1)}, s16[2,16,144,128]{3,2,1,0:T(8,128)(2,1)S(1)}, u32[]{:S(2)}, u32[]{:S(2)}) collective-permute-start(s16[2,16,144,128]{3,2,1,0:T(8,128)(2,1)S(1)} %pad_add_fusion.near_ref), channel_id=1, source_target_pairs={{0,4},{4,0},{8,12},{12,8},{16,20},{20,16},{24,28},{28,24},{1,5},{5... | collective-permute-start | bytes 3538952 | tf_op jit(solution)/shard_map/ppermute | solution.py:469
  58.4 1.0 copy-done.3
  59.4 85.3 %shard_map.249 = (f32[16,256,768]{2,1,0:T(8,128)}, f32[2,640,384]{2,1,0:T(8,128)}, s16[2,656,384]{2,1,0:T(8,128)(2,1)}, f32[2,8,384]{2,1,0:T(8,128)}) custom-call(s32[2]{0:T(128)} %pad_add_fusion.6.where_ref.owner_ref, s32[2]{0:T(128)} %pad_add_fusion.7.me_ref, s32[1]{0:T(128)} %bitcast.4.start_ref, s32[16,1]{1,0:T(8,128)} %copy.36.lengths_ref, ...), custom_call_target="tpu_custom_call" | custom-call | tf_op jit(solution)/shard_map/pallas_call | solution.py:357
  145.2 2.4 collective-permute-done.13.refs_0_
  148.6 3.5 %shard_map.250 = (f32[2,320,384]{2,1,0:T(8,128)}, f32[2,8,384]{2,1,0:T(8,128)}, s16[336,384]{1,0:T(8,128)(2,1)}, s16[336,384]{1,0:T(8,128)(2,1)}) custom-call(f32[2,640,384]{2,1,0:T(8,128)} %get-tuple-element.79.keep_ref, f32[2,8,384]{2,1,0:T(8,128)} %get-tuple-element.80.extra_ref, s16[2,656,384]{2,1,0:T(8,128)(2,1)} %copy-done.5), custom_call_target="tpu_custom_call" | custom-call | tf_op jit(solution)/shard_map/pallas_call | solution.py:593
  152.9 6.9 %collective-permute-done.14.refs_0_ = s16[336,384]{1,0:T(8,128)(2,1)S(1)} collective-permute-done((s16[336,384]{1,0:T(8,128)(2,1)}, s16[336,384]{1,0:T(8,128)(2,1)S(1)}, u32[]{:S(2)}, u32[]{:S(2)}) %collective-permute-start.14) | collective-permute-done | bytes 258080 | tf_op jit(solution)/shard_map/ppermute | solution.py:469
  160.9 2.4 shard_map.251
  164.1 3.3 %collective-permute-done.16.refs_0_ = s16[176,384]{1,0:T(8,128)(2,1)S(1)} collective-permute-done((s16[176,384]{1,0:T(8,128)(2,1)}, s16[176,384]{1,0:T(8,128)(2,1)S(1)}, u32[]{:S(2)}, u32[]{:S(2)}) %collective-permute-start.16) | collective-permute-done | bytes 135200 | tf_op jit(solution)/shard_map/ppermute | solution.py:469
  168.1 2.1 shard_map.252
  170.2 1.7 collective-permute-start.18
  171.9 1.1 collective-permute-start.19
  173.1 1.1 collective-permute-start.20
  174.2 3.1 %collective-permute-done.19.refs_1_ = s16[2,56,384]{2,1,0:T(8,128)(2,1)S(1)} collective-permute-done((s16[2,56,384]{2,1,0:T(8,128)(2,1)}, s16[2,56,384]{2,1,0:T(8,128)(2,1)S(1)}, u32[]{:S(2)}, u32[]{:S(2)}) %collective-permute-start.19) | collective-permute-done | bytes 86048 | tf_op jit(solution)/shard_map/ppermute | solution.py:469
  177.3 1.2 collective-permute-done.20.refs_2_
  179.1 1.8 shard_map.253
  180.9 1.3 collective-permute-start.21
  182.2 1.6 collective-permute-start.22
  183.8 1.2 collective-permute-start.23
  186.5 2.7 %collective-permute-done.23 = s16[2,48,384]{2,1,0:T(8,128)(2,1)S(1)} collective-permute-done((s16[2,48,384]{2,1,0:T(8,128)(2,1)}, s16[2,48,384]{2,1,0:T(8,128)(2,1)S(1)}, u32[]{:S(2)}, u32[]{:S(2)}) %collective-permute-start.23) | collective-permute-done | bytes 73760 | tf_op jit(solution)/shard_map/ppermute | solution.py:469
  189.3 2.8 %collective-permute-start.24 = (s16[192,384]{1,0:T(8,128)(2,1)S(1)}, s16[192,384]{1,0:T(8,128)(2,1)S(1)}, u32[]{:S(2)}, u32[]{:S(2)}) collective-permute-start(s16[192,384]{1,0:T(8,128)(2,1)S(1)} %get-tuple-element.121), channel_id=1, source_target_pairs={{0,2},{1,3},{2,0},{3,1},{4,6},{5,7},{6,4},{7,5},{8,10},{9,11},{10,... | collective-permute-start | bytes 442376 | tf_op jit(solution)/shard_map/ppermute | solution.py:469
  192.5 2.1 collective-permute-done.24
  196.7 4.9 %collective-permute-done.25 = s16[384,384]{1,0:T(8,128)(2,1)S(1)} collective-permute-done((s16[384,384]{1,0:T(8,128)(2,1)S(1)}, s16[384,384]{1,0:T(8,128)(2,1)S(1)}, u32[]{:S(2)}, u32[]{:S(2)}) %collective-permute-start.25) | collective-permute-done | bytes 294944 | tf_op jit(solution)/shard_map/ppermute | solution.py:469
  202.4 7.3 %collective-permute-start.28 = (s16[2,768,384]{2,1,0:T(8,128)(2,1)S(1)}, s16[2,768,384]{2,1,0:T(8,128)(2,1)S(1)}, u32[]{:S(2)}, u32[]{:S(2)}) collective-permute-start(s16[2,768,384]{2,1,0:T(8,128)(2,1)S(1)} %pad_add_fusion.1.near_ref), channel_id=1, source_target_pairs={{0,4},{4,0},{8,12},{12,8},{16,20},{20,16},{24,28},{28,24},{1,5},{5... | collective-permute-start | bytes 3538952 | tf_op jit(solution)/shard_map/ppermute | solution.py:469
  210.3 1.9 collective-permute-done.28.far_ref
  213.2 5.5 %shard_map.254 = (bf16[5,256,768]{2,1,0:T(8,128)(2,1)}, bf16[5,256,768]{2,1,0:T(8,128)(2,1)}, f32[96,256]{1,0:T(8,128)}, f32[1,1]{1,0:T(1,128)}, f32[1,768]{1,0:...) custom-call(s32[2]{0:T(128)} %pad_add_fusion.7.me_ref, s16[2,768,384]{2,1,0:T(8,128)(2,1)} %copy-done.1, ...), custom_call_target="tpu_custom_call" | custom-call | tf_op jit(solution)/shard_map/pallas_call | solution.py:682
  218.7 1.7 collective-permute-start.30
  220.4 1.8 collective-permute-start.31
  222.2 13.1 %shard_map.255 = (f32[5,96,768]{2,1,0:T(8,128)}, f32[5,96,768]{2,1,0:T(8,128)}, f32[5,96,768]{2,1,0:T(8,128)}, f32[5,96,768]{2,1,0:T(8,128)}) custom-call(s32[2]{0:T(128)} %pad_add_fusion.6.where_ref.owner_ref, bf16[5,256,768]{2,1,0:T(8,128)(2,1)} %get-tuple-element.99.high_ref, bf16[5,256,768]{2,1,0:T(8,128)(2,1)} %get-tuple-element.100.low_ref, ...), custom_call_target="tpu_custom_call" | custom-call | flops 8589934592 | bytes 33554432 | tf_op jit(solution)/shard_map/pallas_call | solution.py:775
  235.4 1.3 collective-permute-start.32
  239.3 4.9 %shard_map.256 = (f32[32,768]{1,0:T(8,128)}, f32[32,768]{1,0:T(8,128)}, f32[32,256]{1,0:T(8,128)}, f32[96,768]{1,0:T(8,128)}) custom-call(s32[2]{0:T(128)} %pad_add_fusion.6.where_ref.owner_ref, f32[4,96,256]{2,1,0:T(8,128)} %copy-done.2, f32[4,96,256]{2,1,0:T(8,128)} %copy-done.12, f32[32,768]{1,0:T(8,128)} %weight_ref.3, f32[32,256]{1,0:T(8,128)} %left_ref.3, ...), custom_call_target="tpu_custom_call" | custom-call | tf_op jit(solution)/shard_map/pallas_call | solution.py:822
  (143 shorter events, 25.4 us)
Async XLA Ops:
  0.6 7.2 %copy-start.21 = (s32[16,512]{1,0:T(8,128)S(1)}, s32[16,512]{1,0:T(8,128)}, u32[]{:S(2)}) copy-start(s32[16,512]{1,0:T(8,128)} %param.15) | copy-start | bytes 98308
  3.4 12.5 %collective-permute-start = (bf16[960,128]{1,0:T(8,128)(2,1)}, bf16[960,128]{1,0:T(8,128)(2,1)S(1)}, u32[]{:S(2)}, u32[]{:S(2)}) collective-permute-start(bf16[960,128]{1,0:T(8,128)(2,1)} %shard_map.246.refs_0_), channel_id=1, source_target_pairs={{0,8},{4,12},{8,0},{12,4},{16,24},{20,28},{24,16},{28,20},{1,9},{5... | collective-permute-start | bytes 737288 | tf_op jit(solution)/shard_map/ppermute | solution.py:469
  5.5 13.8 %collective-permute-start.1 = (bf16[960,128]{1,0:T(8,128)(2,1)}, bf16[960,128]{1,0:T(8,128)(2,1)S(1)}, u32[]{:S(2)}, u32[]{:S(2)}) collective-permute-start(bf16[960,128]{1,0:T(8,128)(2,1)} %shard_map.246.refs_0_), channel_id=1, source_target_pairs={{0,16},{4,20},{8,24},{12,28},{16,0},{20,4},{24,8},{28,12},{1,17},{... | collective-permute-start | bytes 737288 | tf_op jit(solution)/shard_map/ppermute | solution.py:469
  7.9 16.0 %collective-permute-start.2 = (bf16[960,128]{1,0:T(8,128)(2,1)}, bf16[960,128]{1,0:T(8,128)(2,1)S(1)}, u32[]{:S(2)}, u32[]{:S(2)}) collective-permute-start(bf16[960,128]{1,0:T(8,128)(2,1)} %shard_map.246.refs_0_), channel_id=1, source_target_pairs={{0,24},{4,28},{8,16},{12,20},{16,8},{20,12},{24,0},{28,4},{1,25},{... | collective-permute-start | bytes 737288 | tf_op jit(solution)/shard_map/ppermute | solution.py:469
  7.9 20.7 %collective-permute-start.4 = (s32[16,8]{1,0:T(8,128)S(1)}, s32[16,8]{1,0:T(8,128)S(1)}, u32[]{:S(2)}, u32[]{:S(2)}) collective-permute-start(s32[16,8]{1,0:T(8,128)S(1)} %get-tuple-element.132), channel_id=1, source_target_pairs={{0,1},{1,2},{2,3},{4,5},{5,6},{6,7},{8,9},{9,10},{10,11},{12,13},{... | collective-permute-start | bytes 1544 | tf_op jit(solution)/shard_map/ppermute | solution.py:413
  11.1 17.6 %collective-permute-start.5 = (s32[16,8]{1,0:T(8,128)S(1)}, s32[16,8]{1,0:T(8,128)S(1)}, u32[]{:S(2)}, u32[]{:S(2)}) collective-permute-start(s32[16,8]{1,0:T(8,128)S(1)} %get-tuple-element.133), channel_id=1, source_target_pairs={{1,0},{2,1},{3,2},{5,4},{6,5},{7,6},{9,8},{10,9},{11,10},{13,12},{... | collective-permute-start | bytes 1544 | tf_op jit(solution)/shard_map/ppermute | solution.py:414
  15.3 13.4 %copy-start.27 = (s32[16]{0:T(128)S(1)}, s32[16]{0:T(128)}, u32[]{:S(2)}) copy-start(s32[16]{0:T(128)} %param.16) | copy-start | bytes 196
  15.9 8.1 %copy-start.6 = (bf16[960,128]{1,0:T(8,128)(2,1)}, bf16[960,128]{1,0:T(8,128)(2,1)S(1)}, u32[]{:S(2)}) copy-start(bf16[960,128]{1,0:T(8,128)(2,1)S(1)} %collective-permute-done.refs_1_) | copy-start | bytes 737284
  15.9 14.5 %collective-permute-start.6 = (f32[16,1,768]{2,0,1:T(8,128)S(1)}, f32[16,1,768]{2,0,1:T(8,128)S(1)}, u32[]{:S(2)}, u32[]{:S(2)}) collective-permute-start(f32[16,1,768]{2,0,1:T(8,128)S(1)} %copy.44), channel_id=1, source_target_pairs={{0,1},{1,2},{2,3},{4,5},{5,6},{6,7},{8,9},{9,10},{10,11},{12,13},{... | collective-permute-start | bytes 147464 | tf_op jit(solution)/shard_map/ppermute | solution.py:413
  19.4 9.5 %copy-start.7 = (bf16[960,128]{1,0:T(8,128)(2,1)}, bf16[960,128]{1,0:T(8,128)(2,1)S(1)}, u32[]{:S(2)}) copy-start(bf16[960,128]{1,0:T(8,128)(2,1)S(1)} %collective-permute-done.1.refs_2_) | copy-start | bytes 737284
  19.4 11.2 %collective-permute-start.7 = (f32[16,1,768]{2,0,1:T(8,128)S(1)}, f32[16,1,768]{2,0,1:T(8,128)S(1)}, u32[]{:S(2)}, u32[]{:S(2)}) collective-permute-start(f32[16,1,768]{2,0,1:T(8,128)S(1)} %copy.43), channel_id=1, source_target_pairs={{1,0},{2,1},{3,2},{5,4},{6,5},{7,6},{9,8},{10,9},{11,10},{13,12},{... | collective-permute-start | bytes 147464 | tf_op jit(solution)/shard_map/ppermute | solution.py:414
  23.9 6.6 %copy-start.8 = (bf16[960,128]{1,0:T(8,128)(2,1)}, bf16[960,128]{1,0:T(8,128)(2,1)S(1)}, u32[]{:S(2)}) copy-start(bf16[960,128]{1,0:T(8,128)(2,1)S(1)} %collective-permute-done.2.refs_3_) | copy-start | bytes 737284
  24.0 7.7 %collective-permute-start.3 = (bf16[4,576,128]{2,1,0:T(8,128)(2,1)S(1)}, bf16[4,576,128]{2,1,0:T(8,128)(2,1)S(1)}, u32[]{:S(2)}, u32[]{:S(2)}) collective-permute-start(bf16[4,576,128]{2,1,0:T(8,128)(2,1)S(1)} %pad_maximum_fusion.1), channel_id=1, source_target_pairs={{0,4},{4,0},{8,12},{12,8},{16,20},{20,16},{24,28},{28,24},{1,5},{5... | collective-permute-start | bytes 1769480 | tf_op jit(solution)/shard_map/ppermute | solution.py:469
  35.6 5.1 %collective-permute-start.8 = (s16[4,144,128]{2,1,0:T(8,128)(2,1)}, s16[4,144,128]{2,1,0:T(8,128)(2,1)S(1)}, u32[]{:S(2)}, u32[]{:S(2)}) collective-permute-start(s16[4,144,128]{2,1,0:T(8,128)(2,1)} %get-tuple-element.69), channel_id=1, source_target_pairs={{0,1},{1,0},{2,3},{3,2},{4,5},{5,4},{6,7},{7,6},{8,9},{9,8},{10,11... | collective-permute-start | bytes 442376 | tf_op jit(solution)/shard_map/ppermute | solution.py:469
  37.9 7.2 %collective-permute-start.10 = (s16[4,144,128]{2,1,0:T(8,128)(2,1)}, s16[4,144,128]{2,1,0:T(8,128)(2,1)S(1)}, u32[]{:S(2)}, u32[]{:S(2)}) collective-permute-start(s16[4,144,128]{2,1,0:T(8,128)(2,1)} %get-tuple-element.70), channel_id=1, source_target_pairs={{0,2},{1,3},{2,0},{3,1},{4,6},{5,7},{6,4},{7,5},{8,10},{9,11},{10,... | collective-permute-start | bytes 442376 | tf_op jit(solution)/shard_map/ppermute | solution.py:469
  41.6 10.7 %collective-permute-start.9 = (s16[8,144,128]{2,1,0:T(8,128)(2,1)S(1)}, s16[8,144,128]{2,1,0:T(8,128)(2,1)S(1)}, u32[]{:S(2)}, u32[]{:S(2)}) collective-permute-start(s16[8,144,128]{2,1,0:T(8,128)(2,1)S(1)} %pad_add_fusion.2), channel_id=1, source_target_pairs={{0,2},{1,3},{2,0},{3,1},{4,6},{5,7},{6,4},{7,5},{8,10},{9,11},{10,... | collective-permute-start | bytes 884744 | tf_op jit(solution)/shard_map/ppermute | solution.py:469
  46.0 7.0 %collective-permute-start.11 = (s16[8,144,128]{2,1,0:T(8,128)(2,1)S(1)}, s16[8,144,128]{2,1,0:T(8,128)(2,1)S(1)}, u32[]{:S(2)}, u32[]{:S(2)}) collective-permute-start(s16[8,144,128]{2,1,0:T(8,128)(2,1)S(1)} %pad_add_fusion.3), channel_id=1, source_target_pairs={{0,1},{1,0},{2,3},{3,2},{4,5},{5,4},{6,7},{7,6},{8,9},{9,8},{10,11... | collective-permute-start | bytes 884744 | tf_op jit(solution)/shard_map/ppermute | solution.py:469
  46.9 5.5 %copy-start.10 = (s16[4,144,128]{2,1,0:T(8,128)(2,1)S(1)}, s16[4,144,128]{2,1,0:T(8,128)(2,1)}, u32[]{:S(2)}) copy-start(s16[4,144,128]{2,1,0:T(8,128)(2,1)} %get-tuple-element.69) | copy-start | bytes 442372
  46.9 6.2 %copy-start.9 = (s16[4,144,128]{2,1,0:T(8,128)(2,1)S(1)}, s16[4,144,128]{2,1,0:T(8,128)(2,1)}, u32[]{:S(2)}) copy-start(s16[4,144,128]{2,1,0:T(8,128)(2,1)} %get-tuple-element.70) | copy-start | bytes 442372
  53.2 5.1 %copy-start = (s16[2,16,144,128]{3,2,1,0:T(8,128)(2,1)}, s16[2,16,144,128]{3,2,1,0:T(8,128)(2,1)S(1)}, u32[]{:S(2)}) copy-start(s16[2,16,144,128]{3,2,1,0:T(8,128)(2,1)S(1)} %pad_add_fusion.near_ref) | copy-start | bytes 3538948
  53.2 5.1 %collective-permute-start.12 = (s16[2,16,144,128]{3,2,1,0:T(8,128)(2,1)S(1)}, s16[2,16,144,128]{3,2,1,0:T(8,128)(2,1)S(1)}, u32[]{:S(2)}, u32[]{:S(2)}) collective-permute-start(s16[2,16,144,128]{3,2,1,0:T(8,128)(2,1)S(1)} %pad_add_fusion.near_ref), channel_id=1, source_target_pairs={{0,4},{4,0},{8,12},{12,8},{16,20},{20,16},{24,28},{28,24},{1,5},{5... | collective-permute-start | bytes 3538952 | tf_op jit(solution)/shard_map/ppermute | solution.py:469
  144.6 3.0 %collective-permute-start.13 = (s16[2,656,384]{2,1,0:T(8,128)(2,1)}, s16[2,656,384]{2,1,0:T(8,128)(2,1)S(1)}, u32[]{:S(2)}, u32[]{:S(2)}) collective-permute-start(s16[2,656,384]{2,1,0:T(8,128)(2,1)} %get-tuple-element.81), channel_id=1, source_target_pairs={{0,4},{4,0},{8,12},{12,8},{16,20},{20,16},{24,28},{28,24},{1,5},{5... | collective-permute-start | bytes 3022856 | tf_op jit(solution)/shard_map/ppermute | solution.py:469
  152.1 7.6 %collective-permute-start.14 = (s16[336,384]{1,0:T(8,128)(2,1)}, s16[336,384]{1,0:T(8,128)(2,1)S(1)}, u32[]{:S(2)}, u32[]{:S(2)}) collective-permute-start(s16[336,384]{1,0:T(8,128)(2,1)} %get-tuple-element.84), channel_id=1, source_target_pairs={{0,1},{1,0},{2,3},{3,2},{4,5},{5,4},{6,7},{7,6},{8,9},{9,8},{10,11... | collective-permute-start | bytes 774152 | tf_op jit(solution)/shard_map/ppermute | solution.py:469
  152.9 7.3 %collective-permute-start.15 = (s16[336,384]{1,0:T(8,128)(2,1)}, s16[336,384]{1,0:T(8,128)(2,1)S(1)}, u32[]{:S(2)}, u32[]{:S(2)}) collective-permute-start(s16[336,384]{1,0:T(8,128)(2,1)} %get-tuple-element.85), channel_id=1, source_target_pairs={{0,2},{1,3},{2,0},{3,1},{4,6},{5,7},{6,4},{7,5},{8,10},{9,11},{10,... | collective-permute-start | bytes 774152 | tf_op jit(solution)/shard_map/ppermute | solution.py:469
  163.3 4.1 %collective-permute-start.16 = (s16[176,384]{1,0:T(8,128)(2,1)}, s16[176,384]{1,0:T(8,128)(2,1)S(1)}, u32[]{:S(2)}, u32[]{:S(2)}) collective-permute-start(s16[176,384]{1,0:T(8,128)(2,1)} %get-tuple-element.88), channel_id=1, source_target_pairs={{0,2},{1,3},{2,0},{3,1},{4,6},{5,7},{6,4},{7,5},{8,10},{9,11},{10,... | collective-permute-start | bytes 405512 | tf_op jit(solution)/shard_map/ppermute | solution.py:469
  163.4 4.1 %collective-permute-start.17 = (s16[176,384]{1,0:T(8,128)(2,1)}, s16[176,384]{1,0:T(8,128)(2,1)S(1)}, u32[]{:S(2)}, u32[]{:S(2)}) collective-permute-start(s16[176,384]{1,0:T(8,128)(2,1)} %get-tuple-element.89), channel_id=1, source_target_pairs={{0,1},{1,0},{2,3},{3,2},{4,5},{5,4},{6,7},{7,6},{8,9},{9,8},{10,11... | collective-permute-start | bytes 405512 | tf_op jit(solution)/shard_map/ppermute | solution.py:469
  170.2 4.0 %collective-permute-start.18 = (s16[2,56,384]{2,1,0:T(8,128)(2,1)}, s16[2,56,384]{2,1,0:T(8,128)(2,1)S(1)}, u32[]{:S(2)}, u32[]{:S(2)}) collective-permute-start(s16[2,56,384]{2,1,0:T(8,128)(2,1)} %get-tuple-element.92), channel_id=1, source_target_pairs={{0,8},{4,12},{8,0},{12,4},{16,24},{20,28},{24,16},{28,20},{1,9},{5... | collective-permute-start | bytes 258056 | tf_op jit(solution)/shard_map/ppermute | solution.py:469
  171.9 5.4 %collective-permute-start.19 = (s16[2,56,384]{2,1,0:T(8,128)(2,1)}, s16[2,56,384]{2,1,0:T(8,128)(2,1)S(1)}, u32[]{:S(2)}, u32[]{:S(2)}) collective-permute-start(s16[2,56,384]{2,1,0:T(8,128)(2,1)} %get-tuple-element.93), channel_id=1, source_target_pairs={{0,16},{4,20},{8,24},{12,28},{16,0},{20,4},{24,8},{28,12},{1,17},{... | collective-permute-start | bytes 258056 | tf_op jit(solution)/shard_map/ppermute | solution.py:469
  173.1 5.4 %collective-permute-start.20 = (s16[2,56,384]{2,1,0:T(8,128)(2,1)}, s16[2,56,384]{2,1,0:T(8,128)(2,1)S(1)}, u32[]{:S(2)}, u32[]{:S(2)}) collective-permute-start(s16[2,56,384]{2,1,0:T(8,128)(2,1)} %get-tuple-element.94), channel_id=1, source_target_pairs={{0,24},{4,28},{8,16},{12,20},{16,8},{20,12},{24,0},{28,4},{1,25},{... | collective-permute-start | bytes 258056 | tf_op jit(solution)/shard_map/ppermute | solution.py:469
  174.2 4.3 %copy-start.18 = (s16[2,56,384]{2,1,0:T(8,128)(2,1)}, s16[2,56,384]{2,1,0:T(8,128)(2,1)S(1)}, u32[]{:S(2)}) copy-start(s16[2,56,384]{2,1,0:T(8,128)(2,1)S(1)} %collective-permute-done.18.refs_0_) | copy-start | bytes 258052
  180.9 5.0 %collective-permute-start.21 = (s16[2,48,384]{2,1,0:T(8,128)(2,1)}, s16[2,48,384]{2,1,0:T(8,128)(2,1)S(1)}, u32[]{:S(2)}, u32[]{:S(2)}) collective-permute-start(s16[2,48,384]{2,1,0:T(8,128)(2,1)} %get-tuple-element.95), channel_id=1, source_target_pairs={{0,8},{4,12},{8,0},{12,4},{16,24},{20,28},{24,16},{28,20},{1,9},{5... | collective-permute-start | bytes 221192 | tf_op jit(solution)/shard_map/ppermute | solution.py:469
  182.2 4.3 %collective-permute-start.22 = (s16[2,48,384]{2,1,0:T(8,128)(2,1)}, s16[2,48,384]{2,1,0:T(8,128)(2,1)S(1)}, u32[]{:S(2)}, u32[]{:S(2)}) collective-permute-start(s16[2,48,384]{2,1,0:T(8,128)(2,1)} %get-tuple-element.95), channel_id=1, source_target_pairs={{0,16},{4,20},{8,24},{12,28},{16,0},{20,4},{24,8},{28,12},{1,17},{... | collective-permute-start | bytes 221192 | tf_op jit(solution)/shard_map/ppermute | solution.py:469
  183.8 5.4 %collective-permute-start.23 = (s16[2,48,384]{2,1,0:T(8,128)(2,1)}, s16[2,48,384]{2,1,0:T(8,128)(2,1)S(1)}, u32[]{:S(2)}, u32[]{:S(2)}) collective-permute-start(s16[2,48,384]{2,1,0:T(8,128)(2,1)} %get-tuple-element.95), channel_id=1, source_target_pairs={{0,24},{4,28},{8,16},{12,20},{16,8},{20,12},{24,0},{28,4},{1,25},{... | collective-permute-start | bytes 221192 | tf_op jit(solution)/shard_map/ppermute | solution.py:469
  189.3 5.4 %collective-permute-start.24 = (s16[192,384]{1,0:T(8,128)(2,1)S(1)}, s16[192,384]{1,0:T(8,128)(2,1)S(1)}, u32[]{:S(2)}, u32[]{:S(2)}) collective-permute-start(s16[192,384]{1,0:T(8,128)(2,1)S(1)} %get-tuple-element.121), channel_id=1, source_target_pairs={{0,2},{1,3},{2,0},{3,1},{4,6},{5,7},{6,4},{7,5},{8,10},{9,11},{10,... | collective-permute-start | bytes 442376 | tf_op jit(solution)/shard_map/ppermute | solution.py:469
  192.1 4.0 %collective-permute-start.26 = (s16[192,384]{1,0:T(8,128)(2,1)S(1)}, s16[192,384]{1,0:T(8,128)(2,1)S(1)}, u32[]{:S(2)}, u32[]{:S(2)}) collective-permute-start(s16[192,384]{1,0:T(8,128)(2,1)S(1)} %get-tuple-element.122), channel_id=1, source_target_pairs={{0,1},{1,0},{2,3},{3,2},{4,5},{5,4},{6,7},{7,6},{8,9},{9,8},{10,11... | collective-permute-start | bytes 442376 | tf_op jit(solution)/shard_map/ppermute | solution.py:469
  194.7 6.9 %collective-permute-start.25 = (s16[384,384]{1,0:T(8,128)(2,1)S(1)}, s16[384,384]{1,0:T(8,128)(2,1)S(1)}, u32[]{:S(2)}, u32[]{:S(2)}) collective-permute-start(s16[384,384]{1,0:T(8,128)(2,1)S(1)} %pad_add_fusion.4), channel_id=1, source_target_pairs={{0,1},{1,0},{2,3},{3,2},{4,5},{5,4},{6,7},{7,6},{8,9},{9,8},{10,11... | collective-permute-start | bytes 884744 | tf_op jit(solution)/shard_map/ppermute | solution.py:469
  196.1 6.1 %collective-permute-start.27 = (s16[384,384]{1,0:T(8,128)(2,1)S(1)}, s16[384,384]{1,0:T(8,128)(2,1)S(1)}, u32[]{:S(2)}, u32[]{:S(2)}) collective-permute-start(s16[384,384]{1,0:T(8,128)(2,1)S(1)} %pad_add_fusion.5), channel_id=1, source_target_pairs={{0,2},{1,3},{2,0},{3,1},{4,6},{5,7},{6,4},{7,5},{8,10},{9,11},{10,... | collective-permute-start | bytes 884744 | tf_op jit(solution)/shard_map/ppermute | solution.py:469
  202.3 7.4 %copy-start.23 = (f32[768]{0:T(1024)S(1)}, f32[768]{0:T(1024)}, u32[]{:S(2)}) copy-start(f32[768]{0:T(1024)} %param.29) | copy-start | bytes 9220
  202.4 9.8 %copy-start.1 = (s16[2,768,384]{2,1,0:T(8,128)(2,1)}, s16[2,768,384]{2,1,0:T(8,128)(2,1)S(1)}, u32[]{:S(2)}) copy-start(s16[2,768,384]{2,1,0:T(8,128)(2,1)S(1)} %pad_add_fusion.1.near_ref) | copy-start | bytes 3538948
  202.4 9.8 %collective-permute-start.28 = (s16[2,768,384]{2,1,0:T(8,128)(2,1)S(1)}, s16[2,768,384]{2,1,0:T(8,128)(2,1)S(1)}, u32[]{:S(2)}, u32[]{:S(2)}) collective-permute-start(s16[2,768,384]{2,1,0:T(8,128)(2,1)S(1)} %pad_add_fusion.1.near_ref), channel_id=1, source_target_pairs={{0,4},{4,0},{8,12},{12,8},{16,20},{20,16},{24,28},{28,24},{1,5},{5... | collective-permute-start | bytes 3538952 | tf_op jit(solution)/shard_map/ppermute | solution.py:469
  218.7 16.6 %collective-permute-start.29 = (f32[96,256]{1,0:T(8,128)}, f32[96,256]{1,0:T(8,128)S(1)}, u32[]{:S(2)}, u32[]{:S(2)}) collective-permute-start(f32[96,256]{1,0:T(8,128)} %get-tuple-element.98), channel_id=1, source_target_pairs={{0,8},{4,12},{8,0},{12,4},{16,24},{20,28},{24,16},{28,20},{1,9},{5... | collective-permute-start | bytes 294920 | tf_op jit(solution)/shard_map/ppermute | solution.py:469
  218.7 16.6 %collective-permute-start.30 = (f32[96,256]{1,0:T(8,128)}, f32[96,256]{1,0:T(8,128)S(1)}, u32[]{:S(2)}, u32[]{:S(2)}) collective-permute-start(f32[96,256]{1,0:T(8,128)} %get-tuple-element.98), channel_id=1, source_target_pairs={{0,16},{4,20},{8,24},{12,28},{16,0},{20,4},{24,8},{28,12},{1,17},{... | collective-permute-start | bytes 294920 | tf_op jit(solution)/shard_map/ppermute | solution.py:469
  220.4 14.9 %collective-permute-start.31 = (f32[96,256]{1,0:T(8,128)}, f32[96,256]{1,0:T(8,128)S(1)}, u32[]{:S(2)}, u32[]{:S(2)}) collective-permute-start(f32[96,256]{1,0:T(8,128)} %get-tuple-element.98), channel_id=1, source_target_pairs={{0,24},{4,28},{8,16},{12,20},{16,8},{20,12},{24,0},{28,4},{1,25},{... | collective-permute-start | bytes 294920 | tf_op jit(solution)/shard_map/ppermute | solution.py:469
  222.2 13.1 %copy-start.17 = (f32[96,256]{1,0:T(8,128)S(1)}, f32[96,256]{1,0:T(8,128)}, u32[]{:S(2)}) copy-start(f32[96,256]{1,0:T(8,128)} %get-tuple-element.98) | copy-start | bytes 294916
  222.2 14.5 %copy-start.26 = (f32[1,768]{1,0:T(1,128)S(1)}, f32[1,768]{1,0:T(1,128)}, u32[]{:S(2)}) copy-start(f32[1,768]{1,0:T(1,128)} %get-tuple-element.110) | copy-start | bytes 9220
  222.2 15.1 %copy-start.25 = (f32[1,768]{1,0:T(1,128)S(1)}, f32[1,768]{1,0:T(1,128)}, u32[]{:S(2)}) copy-start(f32[1,768]{1,0:T(1,128)} %get-tuple-element.113) | copy-start | bytes 9220
  222.2 15.7 %copy-start.24 = (f32[1,768]{1,0:T(1,128)S(1)}, f32[1,768]{1,0:T(1,128)}, u32[]{:S(2)}) copy-start(f32[1,768]{1,0:T(1,128)} %get-tuple-element.118) | copy-start | bytes 9220
  235.4 3.1 %collective-permute-start.32 = (f32[4,96,256]{2,1,0:T(8,128)S(1)}, f32[4,96,256]{2,1,0:T(8,128)S(1)}, u32[]{:S(2)}, u32[]{:S(2)}) collective-permute-start(f32[4,96,256]{2,1,0:T(8,128)S(1)} %pad_maximum_fusion.2.near_ref), channel_id=1, source_target_pairs={{0,4},{4,0},{8,12},{12,8},{16,20},{20,16},{24,28},{28,24},{1,5},{5... | collective-permute-start | bytes 1179656 | tf_op jit(solution)/shard_map/ppermute | solution.py:469
  (13 other events, 14.8 us)

commit v5 on v4

--- a/solution.py
+++ b/solution.py
@@ -21,6 +21,7 @@
 WIN = TILE // 2 + 16
 BF = jnp.bfloat16
 F32 = jnp.float32
+LIGHT = jnp.float8_e4m3fn
 
 
 def split(v):
@@ -89,7 +90,7 @@
 
 
 def lookup_body(
-    where_ref, mid_ref, next_ref, g_ref, gh_ref, score_ref, near_ref, far_ref, hid_ref, rim_ref, band_ref, table_ref, onehot_ref, spread, hidden,
+    where_ref, mid_ref, next_ref, g_ref, gh_ref, score_ref, near_ref, far_ref, hid_ref, rim_ref, band_ref, table_ref, onehot_ref, spread, hidden, few_ref, light_ref, scale_ref,
     *, masks, taps,
 ):
     length = hid_ref.shape[1] * TILE
@@ -98,7 +99,15 @@
 
     @pl.when(pl.program_id(0) == 0)
     def _():
-        spare = 2 * taps * VOCAB
+        spare = taps * VOCAB
+        top = jnp.full((1, TILE), -1440.0, F32)
+        for h in range(2):
+            for spot in range(near_ref.shape[1]):
+                for source in (near_ref, far_ref):
+                    top = jnp.maximum(top, as_float(source[h, spot, TILE : TILE + 16])[0:1])
+        top = jnp.ceil(jnp.max(top, axis=1, keepdims=True) * 0.0625)
+        scale_ref[...] = jnp.broadcast_to(jnp.exp2(top - 16.0), scale_ref.shape)
+        grow = jnp.exp2(16.0 - top)
         for spot in range(near_ref.shape[1]):
             found = []
             for h in range(2):
@@ -107,13 +116,15 @@
                     unit = group * slots + spot % slots
                     cells = as_float(source[h, spot])
                     power = jnp.transpose(cells[TILE : TILE + 8])[:, 0:1]
-                    pair = split(cells[:TILE] * jnp.exp2(power * 0.0625 - 15.0))
-                    for low in range(2):
-                        row = (low * taps + unit // blocks) * VOCAB + h * TILE
-                        row = pl.multiple_of(jnp.where(unit < taps * blocks, row, spare), TILE)
-                        found.append((row, pl.multiple_of(unit % blocks * TILE, TILE), pair[low]))
-            for row, column, part in found:
-                table_ref[pl.ds(row, TILE), pl.ds(column, TILE)] = part
+                    rows = cells[:TILE] * jnp.exp2(power * 0.0625 - 15.0)
+                    high = rows.astype(BF)
+                    low = ((rows - high.astype(F32)) * grow).astype(LIGHT)
+                    row = unit // blocks * VOCAB + h * TILE
+                    row = pl.multiple_of(jnp.where(unit < taps * blocks, row, spare), TILE)
+                    found.append((row, pl.multiple_of(unit % blocks * TILE, TILE), high, low))
+            for row, column, high, low in found:
+                table_ref[pl.ds(row, TILE), pl.ds(column, TILE)] = high
+                few_ref[pl.ds(row, TILE), pl.ds(column, TILE)] = low
 
     tiles = length // TILE
     lanes = lax.broadcasted_iota(jnp.int32, (1, VOCAB), 1).astype(F32)
@@ -123,14 +134,16 @@
         ids = [columns[TILE : TILE + length], columns[TILE - HALO : TILE], columns[TILE + length : TILE + length + HALO]]
         ids = jnp.concatenate(ids, axis=0)
         for k in range(taps):
-            onehot_ref[:, k * VOCAB : (k + 1) * VOCAB] = (ids[:, k : k + 1] == lanes).astype(F32).astype(BF)
+            hit = (ids[:, k : k + 1] == lanes).astype(F32)
+            onehot_ref[:, k * VOCAB : (k + 1) * VOCAB] = hit.astype(BF)
+            light_ref[:, k * VOCAB : (k + 1) * VOCAB] = hit.astype(LIGHT)
 
     @pl.when(pl.program_id(0) == 0)
     def _():
         mark(mid_ref)
 
-    onehot = onehot_ref[...]
-    onehot = jnp.concatenate([onehot, onehot], axis=1)
+    onehot, light = onehot_ref[...], light_ref[...]
+    scale = scale_ref[0:1, 0:1]
     for m in range(spread.shape[0]):
         at = slice(m * TILE, (m + 1) * TILE)
         spread[m, 0:8] = jnp.broadcast_to(gh_ref[0, 7:8, at], (8, TILE))
@@ -139,7 +152,8 @@
         spread[m, pl.ds(8, length // 2, stride=2)] = rows
         spread[m, pl.ds(9, length // 2, stride=2)] = rows
     for n in range(0, table_ref.shape[1], 256):
-        cells = jnp.dot(onehot, table_ref[0 : 2 * taps * VOCAB, n : n + 256], preferred_element_type=F32)
+        low = jnp.dot(light, few_ref[0 : taps * VOCAB, n : n + 256], preferred_element_type=F32)
+        cells = jnp.dot(onehot, table_ref[0 : taps * VOCAB, n : n + 256], preferred_element_type=F32) + low * scale
         hidden[:, n : n + 256] = cells
         h_high, h_low = split(cells[0:length])
         for i in range(tiles):
@@ -319,7 +333,7 @@
 def mix_body(
     where_ref, me_ref, start_ref, lengths_ref, mid_ref, next_ref, g_ref, gh_ref, score_ref, near_ref, far_ref, edge_ref,
     out_ref, keep_ref, send_ref, extra_ref,
-    hid, rim, band, weights, sums, spill, table, onehot, spread, hidden, turned, hgrad, total, gathered, pulled, staged,
+    hid, rim, band, weights, sums, spill, table, onehot, spread, hidden, turned, hgrad, total, gathered, pulled, staged, few, light, scale,
     *, masks, taps,
 ):
     step = pl.program_id(0)
@@ -330,7 +344,7 @@
         here = pl.ds(step, 1)
         lookup_body(
             where_ref, mid_ref, next_ref, g_ref, gh_ref, score_ref, near_ref, far_ref,
-            hid.at[here], rim.at[here], band.at[here], table, onehot, spread, hidden, masks=masks, taps=taps,
+            hid.at[here], rim.at[here], band.at[here], table, onehot, spread, hidden, few, light, scale, masks=masks, taps=taps,
         )
 
     @pl.when(step == rows)
@@ -390,7 +404,7 @@
             pltpu.VMEM((rows, 8, span), F32),
             pltpu.VMEM((rows, TILE), F32),
             pltpu.VMEM((rows, 8, width), F32),
-            pltpu.VMEM((2 * taps * VOCAB + TILE, width), BF),
+            pltpu.VMEM((taps * VOCAB + TILE, width), BF),
             pltpu.VMEM((length + 2 * HALO, taps * VOCAB), BF),
             pltpu.VMEM((width // TILE, length + 16, TILE), F32),
             pltpu.VMEM((length + 2 * HALO, width), F32),
@@ -400,6 +414,9 @@
             pltpu.VMEM((taps * VOCAB, width), F32),
             pltpu.VMEM((8, width), F32),
             pltpu.VMEM((taps * VOCAB // 2, width // 2), F32),
+            pltpu.VMEM((taps * VOCAB + TILE, width), LIGHT),
+            pltpu.VMEM((length + 2 * HALO, taps * VOCAB), LIGHT),
+            pltpu.VMEM((8, TILE), F32),
         ],
         compiler_params=pltpu.CompilerParams(vmem_limit_bytes=60 << 20),
     )(

time: 245 us -> 238 us (0.971)
  Pallas kernels: 129 us -> 123 us
    pallas_call x1, Pallas kernels: 85.3 us -> 78.6 us  [mix(): pl.pallas_call(partial(mix_body, masks=masks, taps=taps), grid=(2 * rows,...]
where the time goes in v5:
time: 238 us; the launch traced here: 237 us
  Pallas kernels  123 us (52%)
  starting transfers between devices  55.3 us (23%)
  waiting for transfers between devices  36.8 us (15%)
  local copies, waits for them, and re-layouts  14.3 us (6%)
  other arithmetic  7.39 us (3%)
    pallas_call x1, Pallas kernels, mix(): pl.pallas_call(partial(mix_body, masks=masks, taps=taps), grid=(2 * rows,...  78.6 us
    ppermute x29, starting transfers between devices, swap(): lax.ppermute(cells, axis, [(i, i ^ bit) for i in range(lax.axis_size(axis...  46.2 us
    ppermute x29, waiting for transfers between devices, swap(): lax.ppermute(cells, axis, [(i, i ^ bit) for i in range(lax.axis_size(axis...  36.8 us
    pallas_call x1, Pallas kernels, renew_conv(): pl.pallas_call(conv_body, grid=(taps,), in_specs=[pl.BlockSpec(memory_spa...  13.1 us
    pallas_call x4, Pallas kernels, fold(): pl.pallas_call(partial(fold_body, gots=len(got), pieces=pieces, joint=joi...  9.86 us
    unnamed x59, local copies, waits for them, and re-layouts  7.58 us
    ppermute x2, starting transfers between devices, shifted_rim(): left = lax.ppermute(tail, 'seq', [(i, i + 1) for i in range(count - 1)])  6.48 us
    pallas_call x1, Pallas kernels, order_table(): pl.pallas_call(order_body, in_specs=[pl.BlockSpec(memory_space=pltpu.SMEM...  5.48 us
  transfers between devices with their start and end apart: 33, of which 17 were waited for; matrix products, arithmetic and copies ran while one was open for 6% of the time, Pallas kernels for 8%

profile of v5, /device:TPU:1, one launch (start us, length us, event | category | flops | bytes accessed | tf_op | source)
XLA Modules:
  0.0 237.5 jit_solution(1413789662319950215)
XLA Ops:
  1.3 2.2 shard_map.246.refs_0_
  3.4 2.1 collective-permute-start
  5.5 2.3 collective-permute-start.1
  7.9 3.1 %collective-permute-start.4 = (s32[16,8]{1,0:T(8,128)S(1)}, s32[16,8]{1,0:T(8,128)S(1)}, u32[]{:S(2)}, u32[]{:S(2)}) collective-permute-start(s32[16,8]{1,0:T(8,128)S(1)} %get-tuple-element.132), channel_id=1, source_target_pairs={{0,1},{1,2},{2,3},{4,5},{5,6},{6,7},{8,9},{9,10},{10,11},{12,13},{... | collective-permute-start | bytes 1544 | tf_op jit(solution)/shard_map/ppermute | solution.py:430
  11.1 1.3 collective-permute-start.5
  14.1 1.2 fusion.4
  15.9 3.4 %collective-permute-start.6 = (f32[16,1,768]{2,0,1:T(8,128)S(1)}, f32[16,1,768]{2,0,1:T(8,128)S(1)}, u32[]{:S(2)}, u32[]{:S(2)}) collective-permute-start(f32[16,1,768]{2,0,1:T(8,128)S(1)} %copy.44), channel_id=1, source_target_pairs={{0,1},{1,2},{2,3},{4,5},{5,6},{6,7},{8,9},{9,10},{10,11},{12,13},{... | collective-permute-start | bytes 147464 | tf_op jit(solution)/shard_map/ppermute | solution.py:430
  19.4 1.3 collective-permute-start.7
  20.7 3.1 %collective-permute-done.2.refs_3_ = bf16[960,128]{1,0:T(8,128)(2,1)S(1)} collective-permute-done((bf16[960,128]{1,0:T(8,128)(2,1)}, bf16[960,128]{1,0:T(8,128)(2,1)S(1)}, u32[]{:S(2)}, u32[]{:S(2)}) %collective-permute-start.2) | collective-permute-done | bytes 245792 | tf_op jit(solution)/shard_map/ppermute | solution.py:486
  24.0 4.6 %collective-permute-start.3 = (bf16[4,576,128]{2,1,0:T(8,128)(2,1)S(1)}, bf16[4,576,128]{2,1,0:T(8,128)(2,1)S(1)}, u32[]{:S(2)}, u32[]{:S(2)}) collective-permute-start(bf16[4,576,128]{2,1,0:T(8,128)(2,1)S(1)} %pad_maximum_fusion.1), channel_id=1, source_target_pairs={{0,4},{4,0},{8,12},{12,8},{16,20},{20,16},{24,28},{28,24},{1,5},{5... | collective-permute-start | bytes 1769480 | tf_op jit(solution)/shard_map/ppermute | solution.py:486
  29.2 1.2 stack.107.mid_ref.next_ref
  30.6 1.1 pad_maximum_fusion.gh_ref
  32.5 3.1 %shard_map.247 = (bf16[256,768]{1,0:T(8,128)(2,1)}, s16[4,144,128]{2,1,0:T(8,128)(2,1)}, s16[4,144,128]{2,1,0:T(8,128)(2,1)}) custom-call(s32[2]{0:T(128)} %pad_add_fusion.6.where_ref.owner_ref, bf16[960,128]{1,0:T(8,128)(2,1)} %shard_map.246.refs_0_, bf16[960,128]{1,0:T(8,128)(2,1)} %copy-done.6, bf16[960,128]{1,0:T(8,128)(2,1)} %copy-done.7, ...), custom_call_target="tpu_custom_call" | custom-call | tf_op jit(solution)/shard_map/pallas_call | solution.py:542
  35.6 2.4 collective-permute-start.8
  37.9 1.2 collective-permute-start.10
  39.2 1.5 collective-permute-done.8
  41.6 3.5 %collective-permute-start.9 = (s16[8,144,128]{2,1,0:T(8,128)(2,1)S(1)}, s16[8,144,128]{2,1,0:T(8,128)(2,1)S(1)}, u32[]{:S(2)}, u32[]{:S(2)}) collective-permute-start(s16[8,144,128]{2,1,0:T(8,128)(2,1)S(1)} %pad_add_fusion.2), channel_id=1, source_target_pairs={{0,2},{1,3},{2,0},{3,1},{4,6},{5,7},{6,4},{7,5},{8,10},{9,11},{10,... | collective-permute-start | bytes 884744 | tf_op jit(solution)/shard_map/ppermute | solution.py:486
  46.9 5.5 %shard_map.248 = (bf16[256,256]{1,0:T(8,128)(2,1)}, bf16[256,256]{1,0:T(8,128)(2,1)}, bf16[96,256]{1,0:T(8,128)(2,1)}, bf16[5,96,256]{2,1,0:T(8,128)(2,1)}, bf16[5,96,256]{2,1,0:T(8,128)(2,1)}) custom-call(s32[2]{0:T(128)} %pad_add_fusion.6.where_ref.owner_ref, bf16[256,768]{1,0:T(8,128)(2,1)} %get-tuple-element.71.embed_ref, f32[5,96,768]{2,1,0:T(8,128)} %left_root_ref.2), custom_call_target="tpu_custom_call" | custom-call | flops 1073741824 | bytes 3145728 | tf_op jit(solution)/shard_map/pallas_call | solution.py:744
  53.2 2.5 %collective-permute-start.12 = (s16[2,16,144,128]{3,2,1,0:T(8,128)(2,1)S(1)}, s16[2,16,144,128]{3,2,1,0:T(8,128)(2,1)S(1)}, u32[]{:S(2)}, u32[]{:S(2)}) collective-permute-start(s16[2,16,144,128]{3,2,1,0:T(8,128)(2,1)S(1)} %pad_add_fusion.near_ref), channel_id=1, source_target_pairs={{0,4},{4,0},{8,12},{12,8},{16,20},{20,16},{24,28},{28,24},{1,5},{5... | collective-permute-start | bytes 3538952 | tf_op jit(solution)/shard_map/ppermute | solution.py:486
  58.4 1.0 copy-done.3
  59.4 78.6 %shard_map.249 = (f32[16,256,768]{2,1,0:T(8,128)}, f32[2,640,384]{2,1,0:T(8,128)}, s16[2,656,384]{2,1,0:T(8,128)(2,1)}, f32[2,8,384]{2,1,0:T(8,128)}) custom-call(s32[2]{0:T(128)} %pad_add_fusion.6.where_ref.owner_ref, s32[2]{0:T(128)} %pad_add_fusion.7.me_ref, s32[1]{0:T(128)} %bitcast.4.start_ref, s32[16,1]{1,0:T(8,128)} %copy.36.lengths_ref, ...), custom_call_target="tpu_custom_call" | custom-call | tf_op jit(solution)/shard_map/pallas_call | solution.py:371
  138.6 2.4 %collective-permute-done.13.refs_0_ = s16[2,656,384]{2,1,0:T(8,128)(2,1)S(1)} collective-permute-done((s16[2,656,384]{2,1,0:T(8,128)(2,1)}, s16[2,656,384]{2,1,0:T(8,128)(2,1)S(1)}, u32[]{:S(2)}, u32[]{:S(2)}) %collective-permute-start.13) | collective-permute-done | bytes 1007648 | tf_op jit(solution)/shard_map/ppermute | solution.py:486
  142.0 3.5 %shard_map.250 = (f32[2,320,384]{2,1,0:T(8,128)}, f32[2,8,384]{2,1,0:T(8,128)}, s16[336,384]{1,0:T(8,128)(2,1)}, s16[336,384]{1,0:T(8,128)(2,1)}) custom-call(f32[2,640,384]{2,1,0:T(8,128)} %get-tuple-element.79.keep_ref, f32[2,8,384]{2,1,0:T(8,128)} %get-tuple-element.80.extra_ref, s16[2,656,384]{2,1,0:T(8,128)(2,1)} %copy-done.5), custom_call_target="tpu_custom_call" | custom-call | tf_op jit(solution)/shard_map/pallas_call | solution.py:610
  146.3 6.9 %collective-permute-done.14.refs_0_ = s16[336,384]{1,0:T(8,128)(2,1)S(1)} collective-permute-done((s16[336,384]{1,0:T(8,128)(2,1)}, s16[336,384]{1,0:T(8,128)(2,1)S(1)}, u32[]{:S(2)}, u32[]{:S(2)}) %collective-permute-start.14) | collective-permute-done | bytes 258080 | tf_op jit(solution)/shard_map/ppermute | solution.py:486
  154.3 2.4 %shard_map.251 = (f32[2,160,384]{2,1,0:T(8,128)}, f32[2,8,384]{2,1,0:T(8,128)}, s16[176,384]{1,0:T(8,128)(2,1)}, s16[176,384]{1,0:T(8,128)(2,1)}) custom-call(f32[2,320,384]{2,1,0:T(8,128)} %get-tuple-element.82.keep_ref, f32[2,8,384]{2,1,0:T(8,128)} %get-tuple-element.83.extra_ref, s16[336,384]{1,0:T(8,128)(2,1)} %copy-done.13, s16[336,384]{1,0:T(8,128)(2,1)} %copy-done.14), custom_call_target="tpu_custom_call" | custom-call | tf_op jit(solution)/shard_map/pallas_call | solution.py:610
  157.4 3.3 %collective-permute-done.16.refs_0_ = s16[176,384]{1,0:T(8,128)(2,1)S(1)} collective-permute-done((s16[176,384]{1,0:T(8,128)(2,1)}, s16[176,384]{1,0:T(8,128)(2,1)S(1)}, u32[]{:S(2)}, u32[]{:S(2)}) %collective-permute-start.16) | collective-permute-done | bytes 135200 | tf_op jit(solution)/shard_map/ppermute | solution.py:486
  161.5 2.1 shard_map.252
  163.6 1.7 collective-permute-start.18
  165.3 1.1 collective-permute-start.19
  166.4 1.1 collective-permute-start.20
  167.6 3.1 %collective-permute-done.19.refs_1_ = s16[2,56,384]{2,1,0:T(8,128)(2,1)S(1)} collective-permute-done((s16[2,56,384]{2,1,0:T(8,128)(2,1)}, s16[2,56,384]{2,1,0:T(8,128)(2,1)S(1)}, u32[]{:S(2)}, u32[]{:S(2)}) %collective-permute-start.19) | collective-permute-done | bytes 86048 | tf_op jit(solution)/shard_map/ppermute | solution.py:486
  170.7 1.1 collective-permute-done.20.refs_2_
  172.5 1.8 shard_map.253
  174.3 1.3 collective-permute-start.21
  175.6 1.6 collective-permute-start.22
  177.2 1.2 collective-permute-start.23
  179.9 2.7 %collective-permute-done.23 = s16[2,48,384]{2,1,0:T(8,128)(2,1)S(1)} collective-permute-done((s16[2,48,384]{2,1,0:T(8,128)(2,1)}, s16[2,48,384]{2,1,0:T(8,128)(2,1)S(1)}, u32[]{:S(2)}, u32[]{:S(2)}) %collective-permute-start.23) | collective-permute-done | bytes 73760 | tf_op jit(solution)/shard_map/ppermute | solution.py:486
  182.7 2.8 %collective-permute-start.24 = (s16[192,384]{1,0:T(8,128)(2,1)S(1)}, s16[192,384]{1,0:T(8,128)(2,1)S(1)}, u32[]{:S(2)}, u32[]{:S(2)}) collective-permute-start(s16[192,384]{1,0:T(8,128)(2,1)S(1)} %get-tuple-element.121), channel_id=1, source_target_pairs={{0,2},{1,3},{2,0},{3,1},{4,6},{5,7},{6,4},{7,5},{8,10},{9,11},{10,... | collective-permute-start | bytes 442376 | tf_op jit(solution)/shard_map/ppermute | solution.py:486
  185.9 2.1 collective-permute-done.24
  190.1 4.8 %collective-permute-done.25 = s16[384,384]{1,0:T(8,128)(2,1)S(1)} collective-permute-done((s16[384,384]{1,0:T(8,128)(2,1)S(1)}, s16[384,384]{1,0:T(8,128)(2,1)S(1)}, u32[]{:S(2)}, u32[]{:S(2)}) %collective-permute-start.25) | collective-permute-done | bytes 294944 | tf_op jit(solution)/shard_map/ppermute | solution.py:486
  195.8 7.3 %collective-permute-start.28 = (s16[2,768,384]{2,1,0:T(8,128)(2,1)S(1)}, s16[2,768,384]{2,1,0:T(8,128)(2,1)S(1)}, u32[]{:S(2)}, u32[]{:S(2)}) collective-permute-start(s16[2,768,384]{2,1,0:T(8,128)(2,1)S(1)} %pad_add_fusion.1.near_ref), channel_id=1, source_target_pairs={{0,4},{4,0},{8,12},{12,8},{16,20},{20,16},{24,28},{28,24},{1,5},{5... | collective-permute-start | bytes 3538952 | tf_op jit(solution)/shard_map/ppermute | solution.py:486
  203.6 1.9 collective-permute-done.28.far_ref
  206.5 5.5 %shard_map.254 = (bf16[5,256,768]{2,1,0:T(8,128)(2,1)}, bf16[5,256,768]{2,1,0:T(8,128)(2,1)}, f32[96,256]{1,0:T(8,128)}, f32[1,1]{1,0:T(1,128)}, f32[1,768]{1,0:...) custom-call(s32[2]{0:T(128)} %pad_add_fusion.7.me_ref, s16[2,768,384]{2,1,0:T(8,128)(2,1)} %copy-done.1, ...), custom_call_target="tpu_custom_call" | custom-call | tf_op jit(solution)/shard_map/pallas_call | solution.py:699
  212.1 1.6 collective-permute-start.30
  213.7 1.8 collective-permute-start.31
  215.6 13.1 %shard_map.255 = (f32[5,96,768]{2,1,0:T(8,128)}, f32[5,96,768]{2,1,0:T(8,128)}, f32[5,96,768]{2,1,0:T(8,128)}, f32[5,96,768]{2,1,0:T(8,128)}) custom-call(s32[2]{0:T(128)} %pad_add_fusion.6.where_ref.owner_ref, bf16[5,256,768]{2,1,0:T(8,128)(2,1)} %get-tuple-element.99.high_ref, bf16[5,256,768]{2,1,0:T(8,128)(2,1)} %get-tuple-element.100.low_ref, ...), custom_call_target="tpu_custom_call" | custom-call | flops 8589934592 | bytes 33554432 | tf_op jit(solution)/shard_map/pallas_call | solution.py:792
  228.7 1.3 collective-permute-start.32
  232.6 4.9 %shard_map.256 = (f32[32,768]{1,0:T(8,128)}, f32[32,768]{1,0:T(8,128)}, f32[32,256]{1,0:T(8,128)}, f32[96,768]{1,0:T(8,128)}) custom-call(s32[2]{0:T(128)} %pad_add_fusion.6.where_ref.owner_ref, f32[4,96,256]{2,1,0:T(8,128)} %copy-done.2, f32[4,96,256]{2,1,0:T(8,128)} %copy-done.12, f32[32,768]{1,0:T(8,128)} %weight_ref.3, f32[32,256]{1,0:T(8,128)} %left_ref.3, ...), custom_call_target="tpu_custom_call" | custom-call | tf_op jit(solution)/shard_map/pallas_call | solution.py:839
  (143 shorter events, 25.6 us)
Async XLA Ops:
  0.6 7.2 %copy-start.21 = (s32[16,512]{1,0:T(8,128)S(1)}, s32[16,512]{1,0:T(8,128)}, u32[]{:S(2)}) copy-start(s32[16,512]{1,0:T(8,128)} %param.15) | copy-start | bytes 98308
  3.4 12.5 %collective-permute-start = (bf16[960,128]{1,0:T(8,128)(2,1)}, bf16[960,128]{1,0:T(8,128)(2,1)S(1)}, u32[]{:S(2)}, u32[]{:S(2)}) collective-permute-start(bf16[960,128]{1,0:T(8,128)(2,1)} %shard_map.246.refs_0_), channel_id=1, source_target_pairs={{0,8},{4,12},{8,0},{12,4},{16,24},{20,28},{24,16},{28,20},{1,9},{5... | collective-permute-start | bytes 737288 | tf_op jit(solution)/shard_map/ppermute | solution.py:486
  5.5 13.8 %collective-permute-start.1 = (bf16[960,128]{1,0:T(8,128)(2,1)}, bf16[960,128]{1,0:T(8,128)(2,1)S(1)}, u32[]{:S(2)}, u32[]{:S(2)}) collective-permute-start(bf16[960,128]{1,0:T(8,128)(2,1)} %shard_map.246.refs_0_), channel_id=1, source_target_pairs={{0,16},{4,20},{8,24},{12,28},{16,0},{20,4},{24,8},{28,12},{1,17},{... | collective-permute-start | bytes 737288 | tf_op jit(solution)/shard_map/ppermute | solution.py:486
  7.9 16.0 %collective-permute-start.2 = (bf16[960,128]{1,0:T(8,128)(2,1)}, bf16[960,128]{1,0:T(8,128)(2,1)S(1)}, u32[]{:S(2)}, u32[]{:S(2)}) collective-permute-start(bf16[960,128]{1,0:T(8,128)(2,1)} %shard_map.246.refs_0_), channel_id=1, source_target_pairs={{0,24},{4,28},{8,16},{12,20},{16,8},{20,12},{24,0},{28,4},{1,25},{... | collective-permute-start | bytes 737288 | tf_op jit(solution)/shard_map/ppermute | solution.py:486
  7.9 20.7 %collective-permute-start.4 = (s32[16,8]{1,0:T(8,128)S(1)}, s32[16,8]{1,0:T(8,128)S(1)}, u32[]{:S(2)}, u32[]{:S(2)}) collective-permute-start(s32[16,8]{1,0:T(8,128)S(1)} %get-tuple-element.132), channel_id=1, source_target_pairs={{0,1},{1,2},{2,3},{4,5},{5,6},{6,7},{8,9},{9,10},{10,11},{12,13},{... | collective-permute-start | bytes 1544 | tf_op jit(solution)/shard_map/ppermute | solution.py:430
  11.1 17.6 %collective-permute-start.5 = (s32[16,8]{1,0:T(8,128)S(1)}, s32[16,8]{1,0:T(8,128)S(1)}, u32[]{:S(2)}, u32[]{:S(2)}) collective-permute-start(s32[16,8]{1,0:T(8,128)S(1)} %get-tuple-element.133), channel_id=1, source_target_pairs={{1,0},{2,1},{3,2},{5,4},{6,5},{7,6},{9,8},{10,9},{11,10},{13,12},{... | collective-permute-start | bytes 1544 | tf_op jit(solution)/shard_map/ppermute | solution.py:431
  15.3 13.4 %copy-start.27 = (s32[16]{0:T(128)S(1)}, s32[16]{0:T(128)}, u32[]{:S(2)}) copy-start(s32[16]{0:T(128)} %param.16) | copy-start | bytes 196
  15.9 8.1 %copy-start.6 = (bf16[960,128]{1,0:T(8,128)(2,1)}, bf16[960,128]{1,0:T(8,128)(2,1)S(1)}, u32[]{:S(2)}) copy-start(bf16[960,128]{1,0:T(8,128)(2,1)S(1)} %collective-permute-done.refs_1_) | copy-start | bytes 737284
  15.9 14.5 %collective-permute-start.6 = (f32[16,1,768]{2,0,1:T(8,128)S(1)}, f32[16,1,768]{2,0,1:T(8,128)S(1)}, u32[]{:S(2)}, u32[]{:S(2)}) collective-permute-start(f32[16,1,768]{2,0,1:T(8,128)S(1)} %copy.44), channel_id=1, source_target_pairs={{0,1},{1,2},{2,3},{4,5},{5,6},{6,7},{8,9},{9,10},{10,11},{12,13},{... | collective-permute-start | bytes 147464 | tf_op jit(solution)/shard_map/ppermute | solution.py:430
  19.4 9.5 %copy-start.7 = (bf16[960,128]{1,0:T(8,128)(2,1)}, bf16[960,128]{1,0:T(8,128)(2,1)S(1)}, u32[]{:S(2)}) copy-start(bf16[960,128]{1,0:T(8,128)(2,1)S(1)} %collective-permute-done.1.refs_2_) | copy-start | bytes 737284
  19.4 11.2 %collective-permute-start.7 = (f32[16,1,768]{2,0,1:T(8,128)S(1)}, f32[16,1,768]{2,0,1:T(8,128)S(1)}, u32[]{:S(2)}, u32[]{:S(2)}) collective-permute-start(f32[16,1,768]{2,0,1:T(8,128)S(1)} %copy.43), channel_id=1, source_target_pairs={{1,0},{2,1},{3,2},{5,4},{6,5},{7,6},{9,8},{10,9},{11,10},{13,12},{... | collective-permute-start | bytes 147464 | tf_op jit(solution)/shard_map/ppermute | solution.py:431
  23.9 6.6 %copy-start.8 = (bf16[960,128]{1,0:T(8,128)(2,1)}, bf16[960,128]{1,0:T(8,128)(2,1)S(1)}, u32[]{:S(2)}) copy-start(bf16[960,128]{1,0:T(8,128)(2,1)S(1)} %collective-permute-done.2.refs_3_) | copy-start | bytes 737284
  24.0 7.7 %collective-permute-start.3 = (bf16[4,576,128]{2,1,0:T(8,128)(2,1)S(1)}, bf16[4,576,128]{2,1,0:T(8,128)(2,1)S(1)}, u32[]{:S(2)}, u32[]{:S(2)}) collective-permute-start(bf16[4,576,128]{2,1,0:T(8,128)(2,1)S(1)} %pad_maximum_fusion.1), channel_id=1, source_target_pairs={{0,4},{4,0},{8,12},{12,8},{16,20},{20,16},{24,28},{28,24},{1,5},{5... | collective-permute-start | bytes 1769480 | tf_op jit(solution)/shard_map/ppermute | solution.py:486
  35.6 5.1 %collective-permute-start.8 = (s16[4,144,128]{2,1,0:T(8,128)(2,1)}, s16[4,144,128]{2,1,0:T(8,128)(2,1)S(1)}, u32[]{:S(2)}, u32[]{:S(2)}) collective-permute-start(s16[4,144,128]{2,1,0:T(8,128)(2,1)} %get-tuple-element.69), channel_id=1, source_target_pairs={{0,1},{1,0},{2,3},{3,2},{4,5},{5,4},{6,7},{7,6},{8,9},{9,8},{10,11... | collective-permute-start | bytes 442376 | tf_op jit(solution)/shard_map/ppermute | solution.py:486
  37.9 7.2 %collective-permute-start.10 = (s16[4,144,128]{2,1,0:T(8,128)(2,1)}, s16[4,144,128]{2,1,0:T(8,128)(2,1)S(1)}, u32[]{:S(2)}, u32[]{:S(2)}) collective-permute-start(s16[4,144,128]{2,1,0:T(8,128)(2,1)} %get-tuple-element.70), channel_id=1, source_target_pairs={{0,2},{1,3},{2,0},{3,1},{4,6},{5,7},{6,4},{7,5},{8,10},{9,11},{10,... | collective-permute-start | bytes 442376 | tf_op jit(solution)/shard_map/ppermute | solution.py:486
  41.6 10.7 %collective-permute-start.9 = (s16[8,144,128]{2,1,0:T(8,128)(2,1)S(1)}, s16[8,144,128]{2,1,0:T(8,128)(2,1)S(1)}, u32[]{:S(2)}, u32[]{:S(2)}) collective-permute-start(s16[8,144,128]{2,1,0:T(8,128)(2,1)S(1)} %pad_add_fusion.2), channel_id=1, source_target_pairs={{0,2},{1,3},{2,0},{3,1},{4,6},{5,7},{6,4},{7,5},{8,10},{9,11},{10,... | collective-permute-start | bytes 884744 | tf_op jit(solution)/shard_map/ppermute | solution.py:486
  46.0 7.0 %collective-permute-start.11 = (s16[8,144,128]{2,1,0:T(8,128)(2,1)S(1)}, s16[8,144,128]{2,1,0:T(8,128)(2,1)S(1)}, u32[]{:S(2)}, u32[]{:S(2)}) collective-permute-start(s16[8,144,128]{2,1,0:T(8,128)(2,1)S(1)} %pad_add_fusion.3), channel_id=1, source_target_pairs={{0,1},{1,0},{2,3},{3,2},{4,5},{5,4},{6,7},{7,6},{8,9},{9,8},{10,11... | collective-permute-start | bytes 884744 | tf_op jit(solution)/shard_map/ppermute | solution.py:486
  46.9 5.5 %copy-start.10 = (s16[4,144,128]{2,1,0:T(8,128)(2,1)S(1)}, s16[4,144,128]{2,1,0:T(8,128)(2,1)}, u32[]{:S(2)}) copy-start(s16[4,144,128]{2,1,0:T(8,128)(2,1)} %get-tuple-element.69) | copy-start | bytes 442372
  46.9 6.2 %copy-start.9 = (s16[4,144,128]{2,1,0:T(8,128)(2,1)S(1)}, s16[4,144,128]{2,1,0:T(8,128)(2,1)}, u32[]{:S(2)}) copy-start(s16[4,144,128]{2,1,0:T(8,128)(2,1)} %get-tuple-element.70) | copy-start | bytes 442372
  53.2 5.1 %copy-start = (s16[2,16,144,128]{3,2,1,0:T(8,128)(2,1)}, s16[2,16,144,128]{3,2,1,0:T(8,128)(2,1)S(1)}, u32[]{:S(2)}) copy-start(s16[2,16,144,128]{3,2,1,0:T(8,128)(2,1)S(1)} %pad_add_fusion.near_ref) | copy-start | bytes 3538948
  53.2 5.1 %collective-permute-start.12 = (s16[2,16,144,128]{3,2,1,0:T(8,128)(2,1)S(1)}, s16[2,16,144,128]{3,2,1,0:T(8,128)(2,1)S(1)}, u32[]{:S(2)}, u32[]{:S(2)}) collective-permute-start(s16[2,16,144,128]{3,2,1,0:T(8,128)(2,1)S(1)} %pad_add_fusion.near_ref), channel_id=1, source_target_pairs={{0,4},{4,0},{8,12},{12,8},{16,20},{20,16},{24,28},{28,24},{1,5},{5... | collective-permute-start | bytes 3538952 | tf_op jit(solution)/shard_map/ppermute | solution.py:486
  138.0 3.0 %collective-permute-start.13 = (s16[2,656,384]{2,1,0:T(8,128)(2,1)}, s16[2,656,384]{2,1,0:T(8,128)(2,1)S(1)}, u32[]{:S(2)}, u32[]{:S(2)}) collective-permute-start(s16[2,656,384]{2,1,0:T(8,128)(2,1)} %get-tuple-element.81), channel_id=1, source_target_pairs={{0,4},{4,0},{8,12},{12,8},{16,20},{20,16},{24,28},{28,24},{1,5},{5... | collective-permute-start | bytes 3022856 | tf_op jit(solution)/shard_map/ppermute | solution.py:486
  145.5 7.6 %collective-permute-start.14 = (s16[336,384]{1,0:T(8,128)(2,1)}, s16[336,384]{1,0:T(8,128)(2,1)S(1)}, u32[]{:S(2)}, u32[]{:S(2)}) collective-permute-start(s16[336,384]{1,0:T(8,128)(2,1)} %get-tuple-element.84), channel_id=1, source_target_pairs={{0,1},{1,0},{2,3},{3,2},{4,5},{5,4},{6,7},{7,6},{8,9},{9,8},{10,11... | collective-permute-start | bytes 774152 | tf_op jit(solution)/shard_map/ppermute | solution.py:486
  146.3 7.3 %collective-permute-start.15 = (s16[336,384]{1,0:T(8,128)(2,1)}, s16[336,384]{1,0:T(8,128)(2,1)S(1)}, u32[]{:S(2)}, u32[]{:S(2)}) collective-permute-start(s16[336,384]{1,0:T(8,128)(2,1)} %get-tuple-element.85), channel_id=1, source_target_pairs={{0,2},{1,3},{2,0},{3,1},{4,6},{5,7},{6,4},{7,5},{8,10},{9,11},{10,... | collective-permute-start | bytes 774152 | tf_op jit(solution)/shard_map/ppermute | solution.py:486
  156.7 4.1 %collective-permute-start.16 = (s16[176,384]{1,0:T(8,128)(2,1)}, s16[176,384]{1,0:T(8,128)(2,1)S(1)}, u32[]{:S(2)}, u32[]{:S(2)}) collective-permute-start(s16[176,384]{1,0:T(8,128)(2,1)} %get-tuple-element.88), channel_id=1, source_target_pairs={{0,2},{1,3},{2,0},{3,1},{4,6},{5,7},{6,4},{7,5},{8,10},{9,11},{10,... | collective-permute-start | bytes 405512 | tf_op jit(solution)/shard_map/ppermute | solution.py:486
  156.7 4.1 %collective-permute-start.17 = (s16[176,384]{1,0:T(8,128)(2,1)}, s16[176,384]{1,0:T(8,128)(2,1)S(1)}, u32[]{:S(2)}, u32[]{:S(2)}) collective-permute-start(s16[176,384]{1,0:T(8,128)(2,1)} %get-tuple-element.89), channel_id=1, source_target_pairs={{0,1},{1,0},{2,3},{3,2},{4,5},{5,4},{6,7},{7,6},{8,9},{9,8},{10,11... | collective-permute-start | bytes 405512 | tf_op jit(solution)/shard_map/ppermute | solution.py:486
  163.6 4.0 %collective-permute-start.18 = (s16[2,56,384]{2,1,0:T(8,128)(2,1)}, s16[2,56,384]{2,1,0:T(8,128)(2,1)S(1)}, u32[]{:S(2)}, u32[]{:S(2)}) collective-permute-start(s16[2,56,384]{2,1,0:T(8,128)(2,1)} %get-tuple-element.92), channel_id=1, source_target_pairs={{0,8},{4,12},{8,0},{12,4},{16,24},{20,28},{24,16},{28,20},{1,9},{5... | collective-permute-start | bytes 258056 | tf_op jit(solution)/shard_map/ppermute | solution.py:486
  165.3 5.4 %collective-permute-start.19 = (s16[2,56,384]{2,1,0:T(8,128)(2,1)}, s16[2,56,384]{2,1,0:T(8,128)(2,1)S(1)}, u32[]{:S(2)}, u32[]{:S(2)}) collective-permute-start(s16[2,56,384]{2,1,0:T(8,128)(2,1)} %get-tuple-element.93), channel_id=1, source_target_pairs={{0,16},{4,20},{8,24},{12,28},{16,0},{20,4},{24,8},{28,12},{1,17},{... | collective-permute-start | bytes 258056 | tf_op jit(solution)/shard_map/ppermute | solution.py:486
  166.4 5.4 %collective-permute-start.20 = (s16[2,56,384]{2,1,0:T(8,128)(2,1)}, s16[2,56,384]{2,1,0:T(8,128)(2,1)S(1)}, u32[]{:S(2)}, u32[]{:S(2)}) collective-permute-start(s16[2,56,384]{2,1,0:T(8,128)(2,1)} %get-tuple-element.94), channel_id=1, source_target_pairs={{0,24},{4,28},{8,16},{12,20},{16,8},{20,12},{24,0},{28,4},{1,25},{... | collective-permute-start | bytes 258056 | tf_op jit(solution)/shard_map/ppermute | solution.py:486
  167.6 4.3 %copy-start.18 = (s16[2,56,384]{2,1,0:T(8,128)(2,1)}, s16[2,56,384]{2,1,0:T(8,128)(2,1)S(1)}, u32[]{:S(2)}) copy-start(s16[2,56,384]{2,1,0:T(8,128)(2,1)S(1)} %collective-permute-done.18.refs_0_) | copy-start | bytes 258052
  174.3 5.0 %collective-permute-start.21 = (s16[2,48,384]{2,1,0:T(8,128)(2,1)}, s16[2,48,384]{2,1,0:T(8,128)(2,1)S(1)}, u32[]{:S(2)}, u32[]{:S(2)}) collective-permute-start(s16[2,48,384]{2,1,0:T(8,128)(2,1)} %get-tuple-element.95), channel_id=1, source_target_pairs={{0,8},{4,12},{8,0},{12,4},{16,24},{20,28},{24,16},{28,20},{1,9},{5... | collective-permute-start | bytes 221192 | tf_op jit(solution)/shard_map/ppermute | solution.py:486
  175.6 4.3 %collective-permute-start.22 = (s16[2,48,384]{2,1,0:T(8,128)(2,1)}, s16[2,48,384]{2,1,0:T(8,128)(2,1)S(1)}, u32[]{:S(2)}, u32[]{:S(2)}) collective-permute-start(s16[2,48,384]{2,1,0:T(8,128)(2,1)} %get-tuple-element.95), channel_id=1, source_target_pairs={{0,16},{4,20},{8,24},{12,28},{16,0},{20,4},{24,8},{28,12},{1,17},{... | collective-permute-start | bytes 221192 | tf_op jit(solution)/shard_map/ppermute | solution.py:486
  177.2 5.4 %collective-permute-start.23 = (s16[2,48,384]{2,1,0:T(8,128)(2,1)}, s16[2,48,384]{2,1,0:T(8,128)(2,1)S(1)}, u32[]{:S(2)}, u32[]{:S(2)}) collective-permute-start(s16[2,48,384]{2,1,0:T(8,128)(2,1)} %get-tuple-element.95), channel_id=1, source_target_pairs={{0,24},{4,28},{8,16},{12,20},{16,8},{20,12},{24,0},{28,4},{1,25},{... | collective-permute-start | bytes 221192 | tf_op jit(solution)/shard_map/ppermute | solution.py:486
  182.7 5.3 %collective-permute-start.24 = (s16[192,384]{1,0:T(8,128)(2,1)S(1)}, s16[192,384]{1,0:T(8,128)(2,1)S(1)}, u32[]{:S(2)}, u32[]{:S(2)}) collective-permute-start(s16[192,384]{1,0:T(8,128)(2,1)S(1)} %get-tuple-element.121), channel_id=1, source_target_pairs={{0,2},{1,3},{2,0},{3,1},{4,6},{5,7},{6,4},{7,5},{8,10},{9,11},{10,... | collective-permute-start | bytes 442376 | tf_op jit(solution)/shard_map/ppermute | solution.py:486
  185.5 4.0 %collective-permute-start.26 = (s16[192,384]{1,0:T(8,128)(2,1)S(1)}, s16[192,384]{1,0:T(8,128)(2,1)S(1)}, u32[]{:S(2)}, u32[]{:S(2)}) collective-permute-start(s16[192,384]{1,0:T(8,128)(2,1)S(1)} %get-tuple-element.122), channel_id=1, source_target_pairs={{0,1},{1,0},{2,3},{3,2},{4,5},{5,4},{6,7},{7,6},{8,9},{9,8},{10,11... | collective-permute-start | bytes 442376 | tf_op jit(solution)/shard_map/ppermute | solution.py:486
  188.0 6.9 %collective-permute-start.25 = (s16[384,384]{1,0:T(8,128)(2,1)S(1)}, s16[384,384]{1,0:T(8,128)(2,1)S(1)}, u32[]{:S(2)}, u32[]{:S(2)}) collective-permute-start(s16[384,384]{1,0:T(8,128)(2,1)S(1)} %pad_add_fusion.4), channel_id=1, source_target_pairs={{0,1},{1,0},{2,3},{3,2},{4,5},{5,4},{6,7},{7,6},{8,9},{9,8},{10,11... | collective-permute-start | bytes 884744 | tf_op jit(solution)/shard_map/ppermute | solution.py:486
  189.5 6.1 %collective-permute-start.27 = (s16[384,384]{1,0:T(8,128)(2,1)S(1)}, s16[384,384]{1,0:T(8,128)(2,1)S(1)}, u32[]{:S(2)}, u32[]{:S(2)}) collective-permute-start(s16[384,384]{1,0:T(8,128)(2,1)S(1)} %pad_add_fusion.5), channel_id=1, source_target_pairs={{0,2},{1,3},{2,0},{3,1},{4,6},{5,7},{6,4},{7,5},{8,10},{9,11},{10,... | collective-permute-start | bytes 884744 | tf_op jit(solution)/shard_map/ppermute | solution.py:486
  195.6 7.4 %copy-start.23 = (f32[768]{0:T(1024)S(1)}, f32[768]{0:T(1024)}, u32[]{:S(2)}) copy-start(f32[768]{0:T(1024)} %param.29) | copy-start | bytes 9220
  195.7 9.8 %copy-start.1 = (s16[2,768,384]{2,1,0:T(8,128)(2,1)}, s16[2,768,384]{2,1,0:T(8,128)(2,1)S(1)}, u32[]{:S(2)}) copy-start(s16[2,768,384]{2,1,0:T(8,128)(2,1)S(1)} %pad_add_fusion.1.near_ref) | copy-start | bytes 3538948
  195.8 9.8 %collective-permute-start.28 = (s16[2,768,384]{2,1,0:T(8,128)(2,1)S(1)}, s16[2,768,384]{2,1,0:T(8,128)(2,1)S(1)}, u32[]{:S(2)}, u32[]{:S(2)}) collective-permute-start(s16[2,768,384]{2,1,0:T(8,128)(2,1)S(1)} %pad_add_fusion.1.near_ref), channel_id=1, source_target_pairs={{0,4},{4,0},{8,12},{12,8},{16,20},{20,16},{24,28},{28,24},{1,5},{5... | collective-permute-start | bytes 3538952 | tf_op jit(solution)/shard_map/ppermute | solution.py:486
  212.0 16.6 %collective-permute-start.29 = (f32[96,256]{1,0:T(8,128)}, f32[96,256]{1,0:T(8,128)S(1)}, u32[]{:S(2)}, u32[]{:S(2)}) collective-permute-start(f32[96,256]{1,0:T(8,128)} %get-tuple-element.98), channel_id=1, source_target_pairs={{0,8},{4,12},{8,0},{12,4},{16,24},{20,28},{24,16},{28,20},{1,9},{5... | collective-permute-start | bytes 294920 | tf_op jit(solution)/shard_map/ppermute | solution.py:486
  212.1 16.6 %collective-permute-start.30 = (f32[96,256]{1,0:T(8,128)}, f32[96,256]{1,0:T(8,128)S(1)}, u32[]{:S(2)}, u32[]{:S(2)}) collective-permute-start(f32[96,256]{1,0:T(8,128)} %get-tuple-element.98), channel_id=1, source_target_pairs={{0,16},{4,20},{8,24},{12,28},{16,0},{20,4},{24,8},{28,12},{1,17},{... | collective-permute-start | bytes 294920 | tf_op jit(solution)/shard_map/ppermute | solution.py:486
  213.7 14.9 %collective-permute-start.31 = (f32[96,256]{1,0:T(8,128)}, f32[96,256]{1,0:T(8,128)S(1)}, u32[]{:S(2)}, u32[]{:S(2)}) collective-permute-start(f32[96,256]{1,0:T(8,128)} %get-tuple-element.98), channel_id=1, source_target_pairs={{0,24},{4,28},{8,16},{12,20},{16,8},{20,12},{24,0},{28,4},{1,25},{... | collective-permute-start | bytes 294920 | tf_op jit(solution)/shard_map/ppermute | solution.py:486
  215.6 13.1 %copy-start.17 = (f32[96,256]{1,0:T(8,128)S(1)}, f32[96,256]{1,0:T(8,128)}, u32[]{:S(2)}) copy-start(f32[96,256]{1,0:T(8,128)} %get-tuple-element.98) | copy-start | bytes 294916
  215.6 14.4 %copy-start.26 = (f32[1,768]{1,0:T(1,128)S(1)}, f32[1,768]{1,0:T(1,128)}, u32[]{:S(2)}) copy-start(f32[1,768]{1,0:T(1,128)} %get-tuple-element.110) | copy-start | bytes 9220
  215.6 15.0 %copy-start.25 = (f32[1,768]{1,0:T(1,128)S(1)}, f32[1,768]{1,0:T(1,128)}, u32[]{:S(2)}) copy-start(f32[1,768]{1,0:T(1,128)} %get-tuple-element.113) | copy-start | bytes 9220
  215.6 15.7 %copy-start.24 = (f32[1,768]{1,0:T(1,128)S(1)}, f32[1,768]{1,0:T(1,128)}, u32[]{:S(2)}) copy-start(f32[1,768]{1,0:T(1,128)} %get-tuple-element.118) | copy-start | bytes 9220
  228.7 3.1 %collective-permute-start.32 = (f32[4,96,256]{2,1,0:T(8,128)S(1)}, f32[4,96,256]{2,1,0:T(8,128)S(1)}, u32[]{:S(2)}, u32[]{:S(2)}) collective-permute-start(f32[4,96,256]{2,1,0:T(8,128)S(1)} %pad_maximum_fusion.2.near_ref), channel_id=1, source_target_pairs={{0,4},{4,0},{8,12},{12,8},{16,20},{20,16},{24,28},{28,24},{1,5},{5... | collective-permute-start | bytes 1179656 | tf_op jit(solution)/shard_map/ppermute | solution.py:486
  (13 other events, 14.8 us)

commit v6 on v5

--- a/solution.py
+++ b/solution.py
@@ -725,34 +725,26 @@
 
 
 def ready_body(where_ref, embed_ref, left_root_ref, square_high, square_low, columns_ref, rooted_high, rooted_low):
-    own, width = left_root_ref.shape[1:]
+    taps, own, width = left_root_ref.shape
     embed = embed_ref[...]
-
-    @pl.when(pl.program_id(0) == 0)
-    def _():
-        square_high[...], square_low[...] = split(dot(embed, embed, NT))
-        columns_ref[...] = dot(pick_rows(own, width, where_ref[0] * own), embed, NT).astype(BF)
-
-    rooted_high[0], rooted_low[0] = split(dot2_left(split(left_root_ref[0]), embed, NT))
+    square_high[...], square_low[...] = split(dot(embed, embed, NT))
+    columns_ref[...] = dot(pick_rows(own, width, where_ref[0] * own), embed, NT).astype(BF)
+    high, low = split(left_root_ref[...].reshape(taps * own, width))
+    rooted = dot(jnp.concatenate([high, low], axis=0), embed, NT)
+    high, low = split(rooted[: taps * own] + rooted[taps * own :])
+    rooted_high[...] = high.reshape(rooted_high.shape)
+    rooted_low[...] = low.reshape(rooted_low.shape)
 
 
 def make_ready(where, embed_all, left_root):
     taps, own, width = left_root.shape
-    by_tap = lambda *shape: pl.BlockSpec((1, *shape), lambda k: (k,) + (0,) * len(shape))
-    whole = lambda *shape: pl.BlockSpec(shape, lambda k: (0,) * len(shape))
+    vmem = pl.BlockSpec(memory_space=pltpu.VMEM)
     like = lambda *shape: jax.ShapeDtypeStruct(shape, BF)
     return pl.pallas_call(
         ready_body,
-        grid=(taps,),
-        in_specs=[
-            pl.BlockSpec(memory_space=pltpu.SMEM),
-            whole(VOCAB, width),
-            by_tap(own, width),
-        ],
-        out_specs=[whole(VOCAB, VOCAB)] * 2 + [whole(own, VOCAB)] + [by_tap(own, VOCAB)] * 2,
-        out_shape=[like(VOCAB, VOCAB)] * 2
-        + [like(own, VOCAB)]
-        + [like(taps, own, VOCAB)] * 2,
+        in_specs=[pl.BlockSpec(memory_space=pltpu.SMEM), vmem, vmem],
+        out_specs=[vmem] * 5,
+        out_shape=[like(VOCAB, VOCAB)] * 2 + [like(own, VOCAB)] + [like(taps, own, VOCAB)] * 2,
         compiler_params=pltpu.CompilerParams(vmem_limit_bytes=60 << 20),
         cost_estimate=pl.CostEstimate(flops=1 << 30, bytes_accessed=3 << 20, transcendentals=0),
     )(where, embed_all, left_root)

time: 238 us -> 238 us (level)
  Pallas kernels: 123 us -> 120 us
  transfers between devices with their start and end apart: 33 -> 33, of which waited for: 17 -> 18; matrix products, arithmetic and copies ran while one was open for 6% -> 6% of each run, Pallas kernels for 8% -> 7%
where the time goes in v6:
time: 238 us; the launch traced here: 237 us
  Pallas kernels  120 us (50%)
  starting transfers between devices  55.3 us (23%)
  waiting for transfers between devices  39.1 us (16%)
  local copies, waits for them, and re-layouts  14.3 us (6%)
  other arithmetic  7.38 us (3%)
    pallas_call x1, Pallas kernels, mix(): pl.pallas_call(partial(mix_body, masks=masks, taps=taps), grid=(2 * rows,...  78.6 us
    ppermute x29, starting transfers between devices, swap(): lax.ppermute(cells, axis, [(i, i ^ bit) for i in range(lax.axis_size(axis...  46.2 us
    ppermute x29, waiting for transfers between devices, swap(): lax.ppermute(cells, axis, [(i, i ^ bit) for i in range(lax.axis_size(axis...  39.1 us
    pallas_call x1, Pallas kernels, renew_conv(): pl.pallas_call(conv_body, grid=(taps,), in_specs=[pl.BlockSpec(memory_spa...  13.1 us
    pallas_call x4, Pallas kernels, fold(): pl.pallas_call(partial(fold_body, gots=len(got), pieces=pieces, joint=joi...  9.86 us
    unnamed x59, local copies, waits for them, and re-layouts  7.58 us
    ppermute x2, starting transfers between devices, shifted_rim(): left = lax.ppermute(tail, 'seq', [(i, i + 1) for i in range(count - 1)])  6.48 us
    pallas_call x1, Pallas kernels, order_table(): pl.pallas_call(order_body, in_specs=[pl.BlockSpec(memory_space=pltpu.SMEM...  5.48 us
  transfers between devices with their start and end apart: 33, of which 18 were waited for; matrix products, arithmetic and copies ran while one was open for 6% of the time, Pallas kernels for 7%

profile of v6, /device:TPU:1, one launch (start us, length us, event | category | flops | bytes accessed | tf_op | source)
XLA Modules:
  0.0 237.5 jit_solution(17328826859902107162)
XLA Ops:
  1.3 2.2 shard_map.246.refs_0_
  3.4 2.1 collective-permute-start
  5.5 2.3 collective-permute-start.1
  7.9 3.1 %collective-permute-start.4 = (s32[16,8]{1,0:T(8,128)S(1)}, s32[16,8]{1,0:T(8,128)S(1)}, u32[]{:S(2)}, u32[]{:S(2)}) collective-permute-start(s32[16,8]{1,0:T(8,128)S(1)} %get-tuple-element.132), channel_id=1, source_target_pairs={{0,1},{1,2},{2,3},{4,5},{5,6},{6,7},{8,9},{9,10},{10,11},{12,13},{... | collective-permute-start | bytes 1544 | tf_op jit(solution)/shard_map/ppermute | solution.py:430
  11.1 1.3 collective-permute-start.5
  14.1 1.2 fusion.4
  15.9 3.4 %collective-permute-start.6 = (f32[16,1,768]{2,0,1:T(8,128)S(1)}, f32[16,1,768]{2,0,1:T(8,128)S(1)}, u32[]{:S(2)}, u32[]{:S(2)}) collective-permute-start(f32[16,1,768]{2,0,1:T(8,128)S(1)} %copy.44), channel_id=1, source_target_pairs={{0,1},{1,2},{2,3},{4,5},{5,6},{6,7},{8,9},{9,10},{10,11},{12,13},{... | collective-permute-start | bytes 147464 | tf_op jit(solution)/shard_map/ppermute | solution.py:430
  19.4 1.3 collective-permute-start.7
  20.7 3.1 %collective-permute-done.2.refs_3_ = bf16[960,128]{1,0:T(8,128)(2,1)S(1)} collective-permute-done((bf16[960,128]{1,0:T(8,128)(2,1)}, bf16[960,128]{1,0:T(8,128)(2,1)S(1)}, u32[]{:S(2)}, u32[]{:S(2)}) %collective-permute-start.2) | collective-permute-done | bytes 245792 | tf_op jit(solution)/shard_map/ppermute | solution.py:486
  24.0 4.6 %collective-permute-start.3 = (bf16[4,576,128]{2,1,0:T(8,128)(2,1)S(1)}, bf16[4,576,128]{2,1,0:T(8,128)(2,1)S(1)}, u32[]{:S(2)}, u32[]{:S(2)}) collective-permute-start(bf16[4,576,128]{2,1,0:T(8,128)(2,1)S(1)} %pad_maximum_fusion.1), channel_id=1, source_target_pairs={{0,4},{4,0},{8,12},{12,8},{16,20},{20,16},{24,28},{28,24},{1,5},{5... | collective-permute-start | bytes 1769480 | tf_op jit(solution)/shard_map/ppermute | solution.py:486
  29.2 1.2 stack.107.mid_ref.next_ref
  30.6 1.1 pad_maximum_fusion.gh_ref
  32.5 3.1 %shard_map.247 = (bf16[256,768]{1,0:T(8,128)(2,1)}, s16[4,144,128]{2,1,0:T(8,128)(2,1)}, s16[4,144,128]{2,1,0:T(8,128)(2,1)}) custom-call(s32[2]{0:T(128)} %pad_add_fusion.6.where_ref.owner_ref, bf16[960,128]{1,0:T(8,128)(2,1)} %shard_map.246.refs_0_, bf16[960,128]{1,0:T(8,128)(2,1)} %copy-done.6, bf16[960,128]{1,0:T(8,128)(2,1)} %copy-done.7, ...), custom_call_target="tpu_custom_call" | custom-call | tf_op jit(solution)/shard_map/pallas_call | solution.py:542
  35.6 2.4 collective-permute-start.8
  37.9 1.2 collective-permute-start.10
  39.2 1.5 collective-permute-done.8
  41.6 3.5 %collective-permute-start.9 = (s16[8,144,128]{2,1,0:T(8,128)(2,1)S(1)}, s16[8,144,128]{2,1,0:T(8,128)(2,1)S(1)}, u32[]{:S(2)}, u32[]{:S(2)}) collective-permute-start(s16[8,144,128]{2,1,0:T(8,128)(2,1)S(1)} %pad_add_fusion.2), channel_id=1, source_target_pairs={{0,2},{1,3},{2,0},{3,1},{4,6},{5,7},{6,4},{7,5},{8,10},{9,11},{10,... | collective-permute-start | bytes 884744 | tf_op jit(solution)/shard_map/ppermute | solution.py:486
  46.9 3.2 %shard_map.248 = (bf16[256,256]{1,0:T(8,128)(2,1)}, bf16[256,256]{1,0:T(8,128)(2,1)}, bf16[96,256]{1,0:T(8,128)(2,1)}, bf16[5,96,256]{2,1,0:T(8,128)(2,1)}, bf16[5,96,256]{2,1,0:T(8,128)(2,1)}) custom-call(s32[2]{0:T(128)} %pad_add_fusion.6.where_ref.owner_ref, bf16[256,768]{1,0:T(8,128)(2,1)} %get-tuple-element.71.embed_ref, f32[5,96,768]{2,1,0:T(8,128)} %left_root_ref.2), custom_call_target="tpu_custom_call" | custom-call | flops 1073741824 | bytes 3145728 | tf_op jit(solution)/shard_map/pallas_call | solution.py:743
  51.1 2.0 collective-permute-done.11
  53.2 2.5 %collective-permute-start.12 = (s16[2,16,144,128]{3,2,1,0:T(8,128)(2,1)S(1)}, s16[2,16,144,128]{3,2,1,0:T(8,128)(2,1)S(1)}, u32[]{:S(2)}, u32[]{:S(2)}) collective-permute-start(s16[2,16,144,128]{3,2,1,0:T(8,128)(2,1)S(1)} %pad_add_fusion.near_ref), channel_id=1, source_target_pairs={{0,4},{4,0},{8,12},{12,8},{16,20},{20,16},{24,28},{28,24},{1,5},{5... | collective-permute-start | bytes 3538952 | tf_op jit(solution)/shard_map/ppermute | solution.py:486
  59.4 78.6 %shard_map.249 = (f32[16,256,768]{2,1,0:T(8,128)}, f32[2,640,384]{2,1,0:T(8,128)}, s16[2,656,384]{2,1,0:T(8,128)(2,1)}, f32[2,8,384]{2,1,0:T(8,128)}) custom-call(s32[2]{0:T(128)} %pad_add_fusion.6.where_ref.owner_ref, s32[2]{0:T(128)} %pad_add_fusion.7.me_ref, s32[1]{0:T(128)} %bitcast.4.start_ref, s32[16,1]{1,0:T(8,128)} %copy.36.lengths_ref, ...), custom_call_target="tpu_custom_call" | custom-call | tf_op jit(solution)/shard_map/pallas_call | solution.py:371
  138.6 2.4 %collective-permute-done.13.refs_0_ = s16[2,656,384]{2,1,0:T(8,128)(2,1)S(1)} collective-permute-done((s16[2,656,384]{2,1,0:T(8,128)(2,1)}, s16[2,656,384]{2,1,0:T(8,128)(2,1)S(1)}, u32[]{:S(2)}, u32[]{:S(2)}) %collective-permute-start.13) | collective-permute-done | bytes 1007648 | tf_op jit(solution)/shard_map/ppermute | solution.py:486
  142.0 3.5 %shard_map.250 = (f32[2,320,384]{2,1,0:T(8,128)}, f32[2,8,384]{2,1,0:T(8,128)}, s16[336,384]{1,0:T(8,128)(2,1)}, s16[336,384]{1,0:T(8,128)(2,1)}) custom-call(f32[2,640,384]{2,1,0:T(8,128)} %get-tuple-element.79.keep_ref, f32[2,8,384]{2,1,0:T(8,128)} %get-tuple-element.80.extra_ref, s16[2,656,384]{2,1,0:T(8,128)(2,1)} %copy-done.5), custom_call_target="tpu_custom_call" | custom-call | tf_op jit(solution)/shard_map/pallas_call | solution.py:610
  146.3 6.9 %collective-permute-done.14.refs_0_ = s16[336,384]{1,0:T(8,128)(2,1)S(1)} collective-permute-done((s16[336,384]{1,0:T(8,128)(2,1)}, s16[336,384]{1,0:T(8,128)(2,1)S(1)}, u32[]{:S(2)}, u32[]{:S(2)}) %collective-permute-start.14) | collective-permute-done | bytes 258080 | tf_op jit(solution)/shard_map/ppermute | solution.py:486
  154.3 2.4 %shard_map.251 = (f32[2,160,384]{2,1,0:T(8,128)}, f32[2,8,384]{2,1,0:T(8,128)}, s16[176,384]{1,0:T(8,128)(2,1)}, s16[176,384]{1,0:T(8,128)(2,1)}) custom-call(f32[2,320,384]{2,1,0:T(8,128)} %get-tuple-element.82.keep_ref, f32[2,8,384]{2,1,0:T(8,128)} %get-tuple-element.83.extra_ref, s16[336,384]{1,0:T(8,128)(2,1)} %copy-done.13, s16[336,384]{1,0:T(8,128)(2,1)} %copy-done.14), custom_call_target="tpu_custom_call" | custom-call | tf_op jit(solution)/shard_map/pallas_call | solution.py:610
  157.4 3.3 %collective-permute-done.16.refs_0_ = s16[176,384]{1,0:T(8,128)(2,1)S(1)} collective-permute-done((s16[176,384]{1,0:T(8,128)(2,1)}, s16[176,384]{1,0:T(8,128)(2,1)S(1)}, u32[]{:S(2)}, u32[]{:S(2)}) %collective-permute-start.16) | collective-permute-done | bytes 135200 | tf_op jit(solution)/shard_map/ppermute | solution.py:486
  161.5 2.1 shard_map.252
  163.6 1.7 collective-permute-start.18
  165.3 1.1 collective-permute-start.19
  166.4 1.1 collective-permute-start.20
  167.6 3.1 %collective-permute-done.19.refs_1_ = s16[2,56,384]{2,1,0:T(8,128)(2,1)S(1)} collective-permute-done((s16[2,56,384]{2,1,0:T(8,128)(2,1)}, s16[2,56,384]{2,1,0:T(8,128)(2,1)S(1)}, u32[]{:S(2)}, u32[]{:S(2)}) %collective-permute-start.19) | collective-permute-done | bytes 86048 | tf_op jit(solution)/shard_map/ppermute | solution.py:486
  170.7 1.1 collective-permute-done.20.refs_2_
  172.5 1.8 shard_map.253
  174.3 1.3 collective-permute-start.21
  175.6 1.6 collective-permute-start.22
  177.2 1.2 collective-permute-start.23
  179.9 2.7 %collective-permute-done.23 = s16[2,48,384]{2,1,0:T(8,128)(2,1)S(1)} collective-permute-done((s16[2,48,384]{2,1,0:T(8,128)(2,1)}, s16[2,48,384]{2,1,0:T(8,128)(2,1)S(1)}, u32[]{:S(2)}, u32[]{:S(2)}) %collective-permute-start.23) | collective-permute-done | bytes 73760 | tf_op jit(solution)/shard_map/ppermute | solution.py:486
  182.7 2.8 %collective-permute-start.24 = (s16[192,384]{1,0:T(8,128)(2,1)S(1)}, s16[192,384]{1,0:T(8,128)(2,1)S(1)}, u32[]{:S(2)}, u32[]{:S(2)}) collective-permute-start(s16[192,384]{1,0:T(8,128)(2,1)S(1)} %get-tuple-element.121), channel_id=1, source_target_pairs={{0,2},{1,3},{2,0},{3,1},{4,6},{5,7},{6,4},{7,5},{8,10},{9,11},{10,... | collective-permute-start | bytes 442376 | tf_op jit(solution)/shard_map/ppermute | solution.py:486
  185.9 2.1 collective-permute-done.24
  190.1 4.8 %collective-permute-done.25 = s16[384,384]{1,0:T(8,128)(2,1)S(1)} collective-permute-done((s16[384,384]{1,0:T(8,128)(2,1)S(1)}, s16[384,384]{1,0:T(8,128)(2,1)S(1)}, u32[]{:S(2)}, u32[]{:S(2)}) %collective-permute-start.25) | collective-permute-done | bytes 294944 | tf_op jit(solution)/shard_map/ppermute | solution.py:486
  195.8 7.3 %collective-permute-start.28 = (s16[2,768,384]{2,1,0:T(8,128)(2,1)S(1)}, s16[2,768,384]{2,1,0:T(8,128)(2,1)S(1)}, u32[]{:S(2)}, u32[]{:S(2)}) collective-permute-start(s16[2,768,384]{2,1,0:T(8,128)(2,1)S(1)} %pad_add_fusion.1.near_ref), channel_id=1, source_target_pairs={{0,4},{4,0},{8,12},{12,8},{16,20},{20,16},{24,28},{28,24},{1,5},{5... | collective-permute-start | bytes 3538952 | tf_op jit(solution)/shard_map/ppermute | solution.py:486
  203.6 1.9 collective-permute-done.28.far_ref
  206.5 5.5 %shard_map.254 = (bf16[5,256,768]{2,1,0:T(8,128)(2,1)}, bf16[5,256,768]{2,1,0:T(8,128)(2,1)}, f32[96,256]{1,0:T(8,128)}, f32[1,1]{1,0:T(1,128)}, f32[1,768]{1,0:...) custom-call(s32[2]{0:T(128)} %pad_add_fusion.7.me_ref, s16[2,768,384]{2,1,0:T(8,128)(2,1)} %copy-done.1, ...), custom_call_target="tpu_custom_call" | custom-call | tf_op jit(solution)/shard_map/pallas_call | solution.py:699
  212.1 1.6 collective-permute-start.30
  213.7 1.8 collective-permute-start.31
  215.6 13.1 %shard_map.255 = (f32[5,96,768]{2,1,0:T(8,128)}, f32[5,96,768]{2,1,0:T(8,128)}, f32[5,96,768]{2,1,0:T(8,128)}, f32[5,96,768]{2,1,0:T(8,128)}) custom-call(s32[2]{0:T(128)} %pad_add_fusion.6.where_ref.owner_ref, bf16[5,256,768]{2,1,0:T(8,128)(2,1)} %get-tuple-element.99.high_ref, bf16[5,256,768]{2,1,0:T(8,128)(2,1)} %get-tuple-element.100.low_ref, ...), custom_call_target="tpu_custom_call" | custom-call | flops 8589934592 | bytes 33554432 | tf_op jit(solution)/shard_map/pallas_call | solution.py:784
  228.7 1.3 collective-permute-start.32
  232.6 4.9 %shard_map.256 = (f32[32,768]{1,0:T(8,128)}, f32[32,768]{1,0:T(8,128)}, f32[32,256]{1,0:T(8,128)}, f32[96,768]{1,0:T(8,128)}) custom-call(s32[2]{0:T(128)} %pad_add_fusion.6.where_ref.owner_ref, f32[4,96,256]{2,1,0:T(8,128)} %copy-done.2, f32[4,96,256]{2,1,0:T(8,128)} %copy-done.12, f32[32,768]{1,0:T(8,128)} %weight_ref.3, f32[32,256]{1,0:T(8,128)} %left_ref.3, ...), custom_call_target="tpu_custom_call" | custom-call | tf_op jit(solution)/shard_map/pallas_call | solution.py:831
  (143 shorter events, 26.9 us)
Async XLA Ops:
  0.6 7.2 %copy-start.21 = (s32[16,512]{1,0:T(8,128)S(1)}, s32[16,512]{1,0:T(8,128)}, u32[]{:S(2)}) copy-start(s32[16,512]{1,0:T(8,128)} %param.15) | copy-start | bytes 98308
  3.4 12.5 %collective-permute-start = (bf16[960,128]{1,0:T(8,128)(2,1)}, bf16[960,128]{1,0:T(8,128)(2,1)S(1)}, u32[]{:S(2)}, u32[]{:S(2)}) collective-permute-start(bf16[960,128]{1,0:T(8,128)(2,1)} %shard_map.246.refs_0_), channel_id=1, source_target_pairs={{0,8},{4,12},{8,0},{12,4},{16,24},{20,28},{24,16},{28,20},{1,9},{5... | collective-permute-start | bytes 737288 | tf_op jit(solution)/shard_map/ppermute | solution.py:486
  5.5 13.8 %collective-permute-start.1 = (bf16[960,128]{1,0:T(8,128)(2,1)}, bf16[960,128]{1,0:T(8,128)(2,1)S(1)}, u32[]{:S(2)}, u32[]{:S(2)}) collective-permute-start(bf16[960,128]{1,0:T(8,128)(2,1)} %shard_map.246.refs_0_), channel_id=1, source_target_pairs={{0,16},{4,20},{8,24},{12,28},{16,0},{20,4},{24,8},{28,12},{1,17},{... | collective-permute-start | bytes 737288 | tf_op jit(solution)/shard_map/ppermute | solution.py:486
  7.9 16.0 %collective-permute-start.2 = (bf16[960,128]{1,0:T(8,128)(2,1)}, bf16[960,128]{1,0:T(8,128)(2,1)S(1)}, u32[]{:S(2)}, u32[]{:S(2)}) collective-permute-start(bf16[960,128]{1,0:T(8,128)(2,1)} %shard_map.246.refs_0_), channel_id=1, source_target_pairs={{0,24},{4,28},{8,16},{12,20},{16,8},{20,12},{24,0},{28,4},{1,25},{... | collective-permute-start | bytes 737288 | tf_op jit(solution)/shard_map/ppermute | solution.py:486
  7.9 20.7 %collective-permute-start.4 = (s32[16,8]{1,0:T(8,128)S(1)}, s32[16,8]{1,0:T(8,128)S(1)}, u32[]{:S(2)}, u32[]{:S(2)}) collective-permute-start(s32[16,8]{1,0:T(8,128)S(1)} %get-tuple-element.132), channel_id=1, source_target_pairs={{0,1},{1,2},{2,3},{4,5},{5,6},{6,7},{8,9},{9,10},{10,11},{12,13},{... | collective-permute-start | bytes 1544 | tf_op jit(solution)/shard_map/ppermute | solution.py:430
  11.1 17.6 %collective-permute-start.5 = (s32[16,8]{1,0:T(8,128)S(1)}, s32[16,8]{1,0:T(8,128)S(1)}, u32[]{:S(2)}, u32[]{:S(2)}) collective-permute-start(s32[16,8]{1,0:T(8,128)S(1)} %get-tuple-element.133), channel_id=1, source_target_pairs={{1,0},{2,1},{3,2},{5,4},{6,5},{7,6},{9,8},{10,9},{11,10},{13,12},{... | collective-permute-start | bytes 1544 | tf_op jit(solution)/shard_map/ppermute | solution.py:431
  15.3 13.4 %copy-start.27 = (s32[16]{0:T(128)S(1)}, s32[16]{0:T(128)}, u32[]{:S(2)}) copy-start(s32[16]{0:T(128)} %param.16) | copy-start | bytes 196
  15.9 8.1 %copy-start.6 = (bf16[960,128]{1,0:T(8,128)(2,1)}, bf16[960,128]{1,0:T(8,128)(2,1)S(1)}, u32[]{:S(2)}) copy-start(bf16[960,128]{1,0:T(8,128)(2,1)S(1)} %collective-permute-done.refs_1_) | copy-start | bytes 737284
  15.9 14.5 %collective-permute-start.6 = (f32[16,1,768]{2,0,1:T(8,128)S(1)}, f32[16,1,768]{2,0,1:T(8,128)S(1)}, u32[]{:S(2)}, u32[]{:S(2)}) collective-permute-start(f32[16,1,768]{2,0,1:T(8,128)S(1)} %copy.44), channel_id=1, source_target_pairs={{0,1},{1,2},{2,3},{4,5},{5,6},{6,7},{8,9},{9,10},{10,11},{12,13},{... | collective-permute-start | bytes 147464 | tf_op jit(solution)/shard_map/ppermute | solution.py:430
  19.4 9.5 %copy-start.7 = (bf16[960,128]{1,0:T(8,128)(2,1)}, bf16[960,128]{1,0:T(8,128)(2,1)S(1)}, u32[]{:S(2)}) copy-start(bf16[960,128]{1,0:T(8,128)(2,1)S(1)} %collective-permute-done.1.refs_2_) | copy-start | bytes 737284
  19.4 11.2 %collective-permute-start.7 = (f32[16,1,768]{2,0,1:T(8,128)S(1)}, f32[16,1,768]{2,0,1:T(8,128)S(1)}, u32[]{:S(2)}, u32[]{:S(2)}) collective-permute-start(f32[16,1,768]{2,0,1:T(8,128)S(1)} %copy.43), channel_id=1, source_target_pairs={{1,0},{2,1},{3,2},{5,4},{6,5},{7,6},{9,8},{10,9},{11,10},{13,12},{... | collective-permute-start | bytes 147464 | tf_op jit(solution)/shard_map/ppermute | solution.py:431
  23.9 6.6 %copy-start.8 = (bf16[960,128]{1,0:T(8,128)(2,1)}, bf16[960,128]{1,0:T(8,128)(2,1)S(1)}, u32[]{:S(2)}) copy-start(bf16[960,128]{1,0:T(8,128)(2,1)S(1)} %collective-permute-done.2.refs_3_) | copy-start | bytes 737284
  24.0 7.7 %collective-permute-start.3 = (bf16[4,576,128]{2,1,0:T(8,128)(2,1)S(1)}, bf16[4,576,128]{2,1,0:T(8,128)(2,1)S(1)}, u32[]{:S(2)}, u32[]{:S(2)}) collective-permute-start(bf16[4,576,128]{2,1,0:T(8,128)(2,1)S(1)} %pad_maximum_fusion.1), channel_id=1, source_target_pairs={{0,4},{4,0},{8,12},{12,8},{16,20},{20,16},{24,28},{28,24},{1,5},{5... | collective-permute-start | bytes 1769480 | tf_op jit(solution)/shard_map/ppermute | solution.py:486
  35.6 5.1 %collective-permute-start.8 = (s16[4,144,128]{2,1,0:T(8,128)(2,1)}, s16[4,144,128]{2,1,0:T(8,128)(2,1)S(1)}, u32[]{:S(2)}, u32[]{:S(2)}) collective-permute-start(s16[4,144,128]{2,1,0:T(8,128)(2,1)} %get-tuple-element.69), channel_id=1, source_target_pairs={{0,1},{1,0},{2,3},{3,2},{4,5},{5,4},{6,7},{7,6},{8,9},{9,8},{10,11... | collective-permute-start | bytes 442376 | tf_op jit(solution)/shard_map/ppermute | solution.py:486
  37.9 7.2 %collective-permute-start.10 = (s16[4,144,128]{2,1,0:T(8,128)(2,1)}, s16[4,144,128]{2,1,0:T(8,128)(2,1)S(1)}, u32[]{:S(2)}, u32[]{:S(2)}) collective-permute-start(s16[4,144,128]{2,1,0:T(8,128)(2,1)} %get-tuple-element.70), channel_id=1, source_target_pairs={{0,2},{1,3},{2,0},{3,1},{4,6},{5,7},{6,4},{7,5},{8,10},{9,11},{10,... | collective-permute-start | bytes 442376 | tf_op jit(solution)/shard_map/ppermute | solution.py:486
  41.6 9.4 %collective-permute-start.9 = (s16[8,144,128]{2,1,0:T(8,128)(2,1)S(1)}, s16[8,144,128]{2,1,0:T(8,128)(2,1)S(1)}, u32[]{:S(2)}, u32[]{:S(2)}) collective-permute-start(s16[8,144,128]{2,1,0:T(8,128)(2,1)S(1)} %pad_add_fusion.2), channel_id=1, source_target_pairs={{0,2},{1,3},{2,0},{3,1},{4,6},{5,7},{6,4},{7,5},{8,10},{9,11},{10,... | collective-permute-start | bytes 884744 | tf_op jit(solution)/shard_map/ppermute | solution.py:486
  46.0 7.0 %collective-permute-start.11 = (s16[8,144,128]{2,1,0:T(8,128)(2,1)S(1)}, s16[8,144,128]{2,1,0:T(8,128)(2,1)S(1)}, u32[]{:S(2)}, u32[]{:S(2)}) collective-permute-start(s16[8,144,128]{2,1,0:T(8,128)(2,1)S(1)} %pad_add_fusion.3), channel_id=1, source_target_pairs={{0,1},{1,0},{2,3},{3,2},{4,5},{5,4},{6,7},{7,6},{8,9},{9,8},{10,11... | collective-permute-start | bytes 884744 | tf_op jit(solution)/shard_map/ppermute | solution.py:486
  46.9 4.2 %copy-start.10 = (s16[4,144,128]{2,1,0:T(8,128)(2,1)S(1)}, s16[4,144,128]{2,1,0:T(8,128)(2,1)}, u32[]{:S(2)}) copy-start(s16[4,144,128]{2,1,0:T(8,128)(2,1)} %get-tuple-element.69) | copy-start | bytes 442372
  46.9 6.2 %copy-start.9 = (s16[4,144,128]{2,1,0:T(8,128)(2,1)S(1)}, s16[4,144,128]{2,1,0:T(8,128)(2,1)}, u32[]{:S(2)}) copy-start(s16[4,144,128]{2,1,0:T(8,128)(2,1)} %get-tuple-element.70) | copy-start | bytes 442372
  53.2 5.1 %copy-start = (s16[2,16,144,128]{3,2,1,0:T(8,128)(2,1)}, s16[2,16,144,128]{3,2,1,0:T(8,128)(2,1)S(1)}, u32[]{:S(2)}) copy-start(s16[2,16,144,128]{3,2,1,0:T(8,128)(2,1)S(1)} %pad_add_fusion.near_ref) | copy-start | bytes 3538948
  53.2 5.1 %collective-permute-start.12 = (s16[2,16,144,128]{3,2,1,0:T(8,128)(2,1)S(1)}, s16[2,16,144,128]{3,2,1,0:T(8,128)(2,1)S(1)}, u32[]{:S(2)}, u32[]{:S(2)}) collective-permute-start(s16[2,16,144,128]{3,2,1,0:T(8,128)(2,1)S(1)} %pad_add_fusion.near_ref), channel_id=1, source_target_pairs={{0,4},{4,0},{8,12},{12,8},{16,20},{20,16},{24,28},{28,24},{1,5},{5... | collective-permute-start | bytes 3538952 | tf_op jit(solution)/shard_map/ppermute | solution.py:486
  138.0 3.0 %collective-permute-start.13 = (s16[2,656,384]{2,1,0:T(8,128)(2,1)}, s16[2,656,384]{2,1,0:T(8,128)(2,1)S(1)}, u32[]{:S(2)}, u32[]{:S(2)}) collective-permute-start(s16[2,656,384]{2,1,0:T(8,128)(2,1)} %get-tuple-element.81), channel_id=1, source_target_pairs={{0,4},{4,0},{8,12},{12,8},{16,20},{20,16},{24,28},{28,24},{1,5},{5... | collective-permute-start | bytes 3022856 | tf_op jit(solution)/shard_map/ppermute | solution.py:486
  145.5 7.6 %collective-permute-start.14 = (s16[336,384]{1,0:T(8,128)(2,1)}, s16[336,384]{1,0:T(8,128)(2,1)S(1)}, u32[]{:S(2)}, u32[]{:S(2)}) collective-permute-start(s16[336,384]{1,0:T(8,128)(2,1)} %get-tuple-element.84), channel_id=1, source_target_pairs={{0,1},{1,0},{2,3},{3,2},{4,5},{5,4},{6,7},{7,6},{8,9},{9,8},{10,11... | collective-permute-start | bytes 774152 | tf_op jit(solution)/shard_map/ppermute | solution.py:486
  146.3 7.3 %collective-permute-start.15 = (s16[336,384]{1,0:T(8,128)(2,1)}, s16[336,384]{1,0:T(8,128)(2,1)S(1)}, u32[]{:S(2)}, u32[]{:S(2)}) collective-permute-start(s16[336,384]{1,0:T(8,128)(2,1)} %get-tuple-element.85), channel_id=1, source_target_pairs={{0,2},{1,3},{2,0},{3,1},{4,6},{5,7},{6,4},{7,5},{8,10},{9,11},{10,... | collective-permute-start | bytes 774152 | tf_op jit(solution)/shard_map/ppermute | solution.py:486
  156.7 4.1 %collective-permute-start.16 = (s16[176,384]{1,0:T(8,128)(2,1)}, s16[176,384]{1,0:T(8,128)(2,1)S(1)}, u32[]{:S(2)}, u32[]{:S(2)}) collective-permute-start(s16[176,384]{1,0:T(8,128)(2,1)} %get-tuple-element.88), channel_id=1, source_target_pairs={{0,2},{1,3},{2,0},{3,1},{4,6},{5,7},{6,4},{7,5},{8,10},{9,11},{10,... | collective-permute-start | bytes 405512 | tf_op jit(solution)/shard_map/ppermute | solution.py:486
  156.7 4.1 %collective-permute-start.17 = (s16[176,384]{1,0:T(8,128)(2,1)}, s16[176,384]{1,0:T(8,128)(2,1)S(1)}, u32[]{:S(2)}, u32[]{:S(2)}) collective-permute-start(s16[176,384]{1,0:T(8,128)(2,1)} %get-tuple-element.89), channel_id=1, source_target_pairs={{0,1},{1,0},{2,3},{3,2},{4,5},{5,4},{6,7},{7,6},{8,9},{9,8},{10,11... | collective-permute-start | bytes 405512 | tf_op jit(solution)/shard_map/ppermute | solution.py:486
  163.6 4.0 %collective-permute-start.18 = (s16[2,56,384]{2,1,0:T(8,128)(2,1)}, s16[2,56,384]{2,1,0:T(8,128)(2,1)S(1)}, u32[]{:S(2)}, u32[]{:S(2)}) collective-permute-start(s16[2,56,384]{2,1,0:T(8,128)(2,1)} %get-tuple-element.92), channel_id=1, source_target_pairs={{0,8},{4,12},{8,0},{12,4},{16,24},{20,28},{24,16},{28,20},{1,9},{5... | collective-permute-start | bytes 258056 | tf_op jit(solution)/shard_map/ppermute | solution.py:486
  165.3 5.4 %collective-permute-start.19 = (s16[2,56,384]{2,1,0:T(8,128)(2,1)}, s16[2,56,384]{2,1,0:T(8,128)(2,1)S(1)}, u32[]{:S(2)}, u32[]{:S(2)}) collective-permute-start(s16[2,56,384]{2,1,0:T(8,128)(2,1)} %get-tuple-element.93), channel_id=1, source_target_pairs={{0,16},{4,20},{8,24},{12,28},{16,0},{20,4},{24,8},{28,12},{1,17},{... | collective-permute-start | bytes 258056 | tf_op jit(solution)/shard_map/ppermute | solution.py:486
  166.4 5.4 %collective-permute-start.20 = (s16[2,56,384]{2,1,0:T(8,128)(2,1)}, s16[2,56,384]{2,1,0:T(8,128)(2,1)S(1)}, u32[]{:S(2)}, u32[]{:S(2)}) collective-permute-start(s16[2,56,384]{2,1,0:T(8,128)(2,1)} %get-tuple-element.94), channel_id=1, source_target_pairs={{0,24},{4,28},{8,16},{12,20},{16,8},{20,12},{24,0},{28,4},{1,25},{... | collective-permute-start | bytes 258056 | tf_op jit(solution)/shard_map/ppermute | solution.py:486
  167.6 4.3 %copy-start.18 = (s16[2,56,384]{2,1,0:T(8,128)(2,1)}, s16[2,56,384]{2,1,0:T(8,128)(2,1)S(1)}, u32[]{:S(2)}) copy-start(s16[2,56,384]{2,1,0:T(8,128)(2,1)S(1)} %collective-permute-done.18.refs_0_) | copy-start | bytes 258052
  174.3 5.0 %collective-permute-start.21 = (s16[2,48,384]{2,1,0:T(8,128)(2,1)}, s16[2,48,384]{2,1,0:T(8,128)(2,1)S(1)}, u32[]{:S(2)}, u32[]{:S(2)}) collective-permute-start(s16[2,48,384]{2,1,0:T(8,128)(2,1)} %get-tuple-element.95), channel_id=1, source_target_pairs={{0,8},{4,12},{8,0},{12,4},{16,24},{20,28},{24,16},{28,20},{1,9},{5... | collective-permute-start | bytes 221192 | tf_op jit(solution)/shard_map/ppermute | solution.py:486
  175.6 4.3 %collective-permute-start.22 = (s16[2,48,384]{2,1,0:T(8,128)(2,1)}, s16[2,48,384]{2,1,0:T(8,128)(2,1)S(1)}, u32[]{:S(2)}, u32[]{:S(2)}) collective-permute-start(s16[2,48,384]{2,1,0:T(8,128)(2,1)} %get-tuple-element.95), channel_id=1, source_target_pairs={{0,16},{4,20},{8,24},{12,28},{16,0},{20,4},{24,8},{28,12},{1,17},{... | collective-permute-start | bytes 221192 | tf_op jit(solution)/shard_map/ppermute | solution.py:486
  177.2 5.4 %collective-permute-start.23 = (s16[2,48,384]{2,1,0:T(8,128)(2,1)}, s16[2,48,384]{2,1,0:T(8,128)(2,1)S(1)}, u32[]{:S(2)}, u32[]{:S(2)}) collective-permute-start(s16[2,48,384]{2,1,0:T(8,128)(2,1)} %get-tuple-element.95), channel_id=1, source_target_pairs={{0,24},{4,28},{8,16},{12,20},{16,8},{20,12},{24,0},{28,4},{1,25},{... | collective-permute-start | bytes 221192 | tf_op jit(solution)/shard_map/ppermute | solution.py:486
  182.7 5.3 %collective-permute-start.24 = (s16[192,384]{1,0:T(8,128)(2,1)S(1)}, s16[192,384]{1,0:T(8,128)(2,1)S(1)}, u32[]{:S(2)}, u32[]{:S(2)}) collective-permute-start(s16[192,384]{1,0:T(8,128)(2,1)S(1)} %get-tuple-element.121), channel_id=1, source_target_pairs={{0,2},{1,3},{2,0},{3,1},{4,6},{5,7},{6,4},{7,5},{8,10},{9,11},{10,... | collective-permute-start | bytes 442376 | tf_op jit(solution)/shard_map/ppermute | solution.py:486
  185.5 4.0 %collective-permute-start.26 = (s16[192,384]{1,0:T(8,128)(2,1)S(1)}, s16[192,384]{1,0:T(8,128)(2,1)S(1)}, u32[]{:S(2)}, u32[]{:S(2)}) collective-permute-start(s16[192,384]{1,0:T(8,128)(2,1)S(1)} %get-tuple-element.122), channel_id=1, source_target_pairs={{0,1},{1,0},{2,3},{3,2},{4,5},{5,4},{6,7},{7,6},{8,9},{9,8},{10,11... | collective-permute-start | bytes 442376 | tf_op jit(solution)/shard_map/ppermute | solution.py:486
  188.0 6.9 %collective-permute-start.25 = (s16[384,384]{1,0:T(8,128)(2,1)S(1)}, s16[384,384]{1,0:T(8,128)(2,1)S(1)}, u32[]{:S(2)}, u32[]{:S(2)}) collective-permute-start(s16[384,384]{1,0:T(8,128)(2,1)S(1)} %pad_add_fusion.4), channel_id=1, source_target_pairs={{0,1},{1,0},{2,3},{3,2},{4,5},{5,4},{6,7},{7,6},{8,9},{9,8},{10,11... | collective-permute-start | bytes 884744 | tf_op jit(solution)/shard_map/ppermute | solution.py:486
  189.5 6.1 %collective-permute-start.27 = (s16[384,384]{1,0:T(8,128)(2,1)S(1)}, s16[384,384]{1,0:T(8,128)(2,1)S(1)}, u32[]{:S(2)}, u32[]{:S(2)}) collective-permute-start(s16[384,384]{1,0:T(8,128)(2,1)S(1)} %pad_add_fusion.5), channel_id=1, source_target_pairs={{0,2},{1,3},{2,0},{3,1},{4,6},{5,7},{6,4},{7,5},{8,10},{9,11},{10,... | collective-permute-start | bytes 884744 | tf_op jit(solution)/shard_map/ppermute | solution.py:486
  195.6 7.4 %copy-start.23 = (f32[768]{0:T(1024)S(1)}, f32[768]{0:T(1024)}, u32[]{:S(2)}) copy-start(f32[768]{0:T(1024)} %param.29) | copy-start | bytes 9220
  195.7 9.8 %copy-start.1 = (s16[2,768,384]{2,1,0:T(8,128)(2,1)}, s16[2,768,384]{2,1,0:T(8,128)(2,1)S(1)}, u32[]{:S(2)}) copy-start(s16[2,768,384]{2,1,0:T(8,128)(2,1)S(1)} %pad_add_fusion.1.near_ref) | copy-start | bytes 3538948
  195.8 9.8 %collective-permute-start.28 = (s16[2,768,384]{2,1,0:T(8,128)(2,1)S(1)}, s16[2,768,384]{2,1,0:T(8,128)(2,1)S(1)}, u32[]{:S(2)}, u32[]{:S(2)}) collective-permute-start(s16[2,768,384]{2,1,0:T(8,128)(2,1)S(1)} %pad_add_fusion.1.near_ref), channel_id=1, source_target_pairs={{0,4},{4,0},{8,12},{12,8},{16,20},{20,16},{24,28},{28,24},{1,5},{5... | collective-permute-start | bytes 3538952 | tf_op jit(solution)/shard_map/ppermute | solution.py:486
  212.0 16.6 %collective-permute-start.29 = (f32[96,256]{1,0:T(8,128)}, f32[96,256]{1,0:T(8,128)S(1)}, u32[]{:S(2)}, u32[]{:S(2)}) collective-permute-start(f32[96,256]{1,0:T(8,128)} %get-tuple-element.98), channel_id=1, source_target_pairs={{0,8},{4,12},{8,0},{12,4},{16,24},{20,28},{24,16},{28,20},{1,9},{5... | collective-permute-start | bytes 294920 | tf_op jit(solution)/shard_map/ppermute | solution.py:486
  212.1 16.6 %collective-permute-start.30 = (f32[96,256]{1,0:T(8,128)}, f32[96,256]{1,0:T(8,128)S(1)}, u32[]{:S(2)}, u32[]{:S(2)}) collective-permute-start(f32[96,256]{1,0:T(8,128)} %get-tuple-element.98), channel_id=1, source_target_pairs={{0,16},{4,20},{8,24},{12,28},{16,0},{20,4},{24,8},{28,12},{1,17},{... | collective-permute-start | bytes 294920 | tf_op jit(solution)/shard_map/ppermute | solution.py:486
  213.7 14.9 %collective-permute-start.31 = (f32[96,256]{1,0:T(8,128)}, f32[96,256]{1,0:T(8,128)S(1)}, u32[]{:S(2)}, u32[]{:S(2)}) collective-permute-start(f32[96,256]{1,0:T(8,128)} %get-tuple-element.98), channel_id=1, source_target_pairs={{0,24},{4,28},{8,16},{12,20},{16,8},{20,12},{24,0},{28,4},{1,25},{... | collective-permute-start | bytes 294920 | tf_op jit(solution)/shard_map/ppermute | solution.py:486
  215.6 13.1 %copy-start.17 = (f32[96,256]{1,0:T(8,128)S(1)}, f32[96,256]{1,0:T(8,128)}, u32[]{:S(2)}) copy-start(f32[96,256]{1,0:T(8,128)} %get-tuple-element.98) | copy-start | bytes 294916
  215.6 14.4 %copy-start.26 = (f32[1,768]{1,0:T(1,128)S(1)}, f32[1,768]{1,0:T(1,128)}, u32[]{:S(2)}) copy-start(f32[1,768]{1,0:T(1,128)} %get-tuple-element.110) | copy-start | bytes 9220
  215.6 15.0 %copy-start.25 = (f32[1,768]{1,0:T(1,128)S(1)}, f32[1,768]{1,0:T(1,128)}, u32[]{:S(2)}) copy-start(f32[1,768]{1,0:T(1,128)} %get-tuple-element.113) | copy-start | bytes 9220
  215.6 15.7 %copy-start.24 = (f32[1,768]{1,0:T(1,128)S(1)}, f32[1,768]{1,0:T(1,128)}, u32[]{:S(2)}) copy-start(f32[1,768]{1,0:T(1,128)} %get-tuple-element.118) | copy-start | bytes 9220
  228.7 3.1 %collective-permute-start.32 = (f32[4,96,256]{2,1,0:T(8,128)S(1)}, f32[4,96,256]{2,1,0:T(8,128)S(1)}, u32[]{:S(2)}, u32[]{:S(2)}) collective-permute-start(f32[4,96,256]{2,1,0:T(8,128)S(1)} %pad_maximum_fusion.2.near_ref), channel_id=1, source_target_pairs={{0,4},{4,0},{8,12},{12,8},{16,20},{20,16},{24,28},{28,24},{1,5},{5... | collective-permute-start | bytes 1179656 | tf_op jit(solution)/shard_map/ppermute | solution.py:486
  (13 other events, 14.8 us)
